TPU v7x, 32 devices: a whole 2x2x4 slice. The times are simulated.
32 devices in a mesh: seq: 16 (over z, x, core), dp: 2 (over y).
Axes of the slice: x: 2, y: 2, z: 4, core: 2. Of those that a mesh axis runs over, the one named last changes fastest.
Arguments:
- activations: bfloat16 [2, 2048, 768], P('dp', 'seq'), may hold values from -6 to 6
- cotangent: bfloat16 [2, 2048, 768], P('dp', 'seq'), may hold values from -6 to 6
- weights: bfloat16 [3840, 768], P(('seq', 'dp')), may hold values from -0.09375 to 0.09375
- norm_gain: float32 [768], replicated, may hold values from 0.25 to 1.75
- pairing: int32 [768], replicated, may hold values from 0 to 767, as said below
Outputs:
- combined: bfloat16 [2, 2048, 768], P('dp', 'seq')
- grad_input: bfloat16 [2, 2048, 768], P('dp', 'seq')
- grad_kernel: float32 [3840, 768], P(('seq', 'dp'))
- grad_gain: float32 [768], P(('seq', 'dp'))
Inputs may be any that keep to these rules, and one draw needn't show every extreme that they name: pairing is an involution without fixed points: pairing[pairing[c]] = c != pairing[c].
All inputs are finite; a program needn't handle non-finite values.
Results may differ from a plain program's by a relative error of at most 0.0055.
Values may be sent and summed in bfloat16 or wider, within the bound.
No kernel may reach another device: no remote copies, remote signals or barrier semaphores. Data moves between devices by JAX's collectives and lax.ppermute only.
A program may use at most 192 MiB of HBM per device.

v0:
```python
import jax
import jax.numpy as jnp
from jax import lax
from jax.sharding import PartitionSpec as P

epsilon = 1e-06


def swapped(block, axis, bit):
    count = lax.axis_size(axis)
    route = []
    for low in range(count):
        high = low | 1 << bit
        if high != low and high < count:
            route += [(low, high), (high, low)]
    return lax.ppermute(block, axis, route)


def padded_2(block, sides, width):
    for axis, dim in sides:
        count = lax.axis_size(axis)
        forward = [(i, i + 1) for i in range(count - 1)]
        backward = [(target, source) for source, target in forward]
        low = lax.ppermute(
            lax.slice_in_dim(block, block.shape[dim] - width, None, axis=dim), axis, forward
        )
        high = lax.ppermute(lax.slice_in_dim(block, 0, width, axis=dim), axis, backward)
        block = jnp.concatenate([low, block, high], axis=dim)
    return block


def reversed_pair(block, pairing):
    return block[:, ::-1][:, :, pairing]


def mirror(stacked, levels):
    mirrored = stacked
    for bit_number in range(levels):
        mirrored = swapped(mirrored, "seq", bit_number)
    return mirrored


def per_device(activations, cotangent, weights, norm_gain, pairing):
    channels = activations.shape[2]
    positions = activations.shape[1]
    gathered = lax.all_gather(weights, ("seq", "dp"), axis=0, tiled=True)
    tap_count = gathered.shape[0] // channels
    kernel_plain = gathered.reshape(tap_count, channels, channels)
    half_cot = 0.5 * cotangent.astype(jnp.float32)
    levels = lax.axis_size("seq").bit_length() - 1
    mirrored = mirror(jnp.stack([activations, cotangent]), levels)
    inputs = [activations, reversed_pair(mirrored[0], pairing)]
    halves = [half_cot, 0.5 * reversed_pair(mirrored[1], pairing).astype(jnp.float32)]
    kernels = [kernel_plain, kernel_plain]
    gain_list = [norm_gain, norm_gain]
    padded = padded_2(jnp.stack(inputs), (("seq", 2),), 2)
    results = []
    windows_list = []
    grad_pres = []
    rms_list = []
    values_list = []
    for strand_index in range(2):
        values_pad = padded[strand_index].astype(jnp.float32)
        inverse_rms = lax.rsqrt(jnp.mean(values_pad * values_pad, -1, keepdims=True) + epsilon)
        normed = (values_pad * inverse_rms * gain_list[strand_index]).astype(jnp.bfloat16)
        windows = jnp.concatenate(
            [normed[:, offset : offset + positions] for offset in range(tap_count)], -1
        )
        flat_kernel = kernels[strand_index].reshape(tap_count * channels, channels)
        preact = jnp.einsum("btk,kd->btd", windows, flat_kernel, preferred_element_type=jnp.float32)
        values = values_pad[:, 2 : 2 + positions]
        results.append(values + jax.nn.gelu(preact))
        _, pullback = jax.vjp(jax.nn.gelu, preact)
        grad_pres.append(pullback(halves[strand_index])[0].astype(jnp.bfloat16))
        windows_list.append(windows)
        rms_list.append(inverse_rms[:, 2 : 2 + positions])
        values_list.append(values)
    grad_padded = padded_2(jnp.stack(grad_pres), (("seq", 2),), 2)
    grad_values = []
    kernel_terms = []
    gain_terms = []
    for strand_index in range(2):
        kernel_terms.append(
            jnp.einsum(
                "btk,btd->kd",
                windows_list[strand_index],
                grad_pres[strand_index],
                preferred_element_type=jnp.float32,
            )
        )
        grad_pad = grad_padded[strand_index]
        back_windows = jnp.concatenate(
            [
                grad_pad[:, tap_count - 1 - offset : tap_count - 1 - offset + positions]
                for offset in range(tap_count)
            ],
            -1,
        )
        kernel_t = kernels[strand_index].transpose(0, 2, 1).reshape(tap_count * channels, channels)
        grad_normed = jnp.einsum(
            "btk,kc->btc", back_windows, kernel_t, preferred_element_type=jnp.float32
        )
        values = values_list[strand_index]
        inverse_rms = rms_list[strand_index]
        gain_terms.append(jnp.sum(grad_normed * values * inverse_rms, (0, 1)))
        scaled = grad_normed * gain_list[strand_index]
        grad_values.append(
            halves[strand_index]
            + inverse_rms * scaled
            - values * inverse_rms**3 * jnp.mean(scaled * values, -1, keepdims=True)
        )
    returned = mirror(
        jnp.stack([results[1].astype(jnp.bfloat16), grad_values[1].astype(jnp.bfloat16)]), levels
    )
    out_round = reversed_pair(returned[0], pairing)
    grad_round = reversed_pair(returned[1], pairing)
    kernel_total = kernel_terms[0] + kernel_terms[1]
    gain_total = gain_terms[0] + gain_terms[1]
    combined = (0.5 * (results[0] + out_round.astype(jnp.float32))).astype(jnp.bfloat16)
    grad_input = (grad_values[0] + grad_round.astype(jnp.float32)).astype(jnp.bfloat16)
    grad_kernel, grad_gain = (
        lax.psum_scatter(kernel_total, ("seq", "dp"), scatter_dimension=0, tiled=True),
        lax.psum_scatter(gain_total, ("seq", "dp"), scatter_dimension=0, tiled=True),
    )
    return (combined, grad_input, grad_kernel, grad_gain)


def solution(mesh):
    placed = (P("dp", "seq", None), P("dp", "seq", None), P(("seq", "dp"), None), P(), P())
    return jax.shard_map(
        per_device,
        mesh=mesh,
        in_specs=placed,
        out_specs=(
            P("dp", "seq", None),
            P("dp", "seq", None),
            P(("seq", "dp"), None),
            P(("seq", "dp")),
        ),
        check_vma=False,
    )
```

profile of v0, /device:TPU:0, one launch (start us, length us, event | category | flops | bytes accessed | tf_op | source)
XLA Modules:
  0.0 276.2 jit_solution(13339643187793785478)
XLA Ops:
  7.2 0.7 all-gather.2.cloned.1.call-update
  8.0 1.1 pad_maximum_fusion
  9.0 0.5 collective-permute-start
  9.5 1.3 collective-permute-done
  10.9 2.9 %collective-permute-start.1 = (bf16[2,1,128,768]{3,2,1,0:T(8,128)(2,1)S(1)}, bf16[2,1,128,768]{3,2,1,0:T(8,128)(2,1)S(1)}, u32[]{:S(2)}, u32[]{:S(2)}) collective-permute-start(bf16[2,1,128,768]{3,2,1,0:T(8,128)(2,1)S(1)} %collective-permute-done), channel_id=1, source_target_pairs={{0,4},{4,0},{2,6},{6,2},{8,12},{12,8},{10,14},{14,10},{16,20},{20,... | collective-permute-start | bytes 1179656 | tf_op jit(solution)/shard_map/ppermute | solution.py:16
  13.8 9.4 %collective-permute-done.1 = bf16[2,1,128,768]{3,2,1,0:T(8,128)(2,1)S(1)} collective-permute-done((bf16[2,1,128,768]{3,2,1,0:T(8,128)(2,1)S(1)}, bf16[2,1,128,768]{3,2,1,0:T(8,128)(2,1)S(1)}, u32[]{:S(2)}, u32[]{:S(2)}) %collective-permute-start.1) | collective-permute-done | bytes 393248 | tf_op jit(solution)/shard_map/ppermute | solution.py:16
  23.2 1.8 collective-permute-start.2
  25.0 12.6 %collective-permute-done.2 = bf16[2,1,128,768]{3,2,1,0:T(8,128)(2,1)S(1)} collective-permute-done((bf16[2,1,128,768]{3,2,1,0:T(8,128)(2,1)S(1)}, bf16[2,1,128,768]{3,2,1,0:T(8,128)(2,1)S(1)}, u32[]{:S(2)}, u32[]{:S(2)}) %collective-permute-start.2) | collective-permute-done | bytes 393248 | tf_op jit(solution)/shard_map/ppermute | solution.py:16
  37.6 2.3 collective-permute-start.3
  39.9 0.7 compare_select_fusion
  40.6 23.9 %collective-permute-done.3 = bf16[2,1,128,768]{3,2,1,0:T(8,128)(2,1)S(1)} collective-permute-done((bf16[2,1,128,768]{3,2,1,0:T(8,128)(2,1)S(1)}, bf16[2,1,128,768]{3,2,1,0:T(8,128)(2,1)S(1)}, u32[]{:S(2)}, u32[]{:S(2)}) %collective-permute-start.3) | collective-permute-done | bytes 393248 | tf_op jit(solution)/shard_map/ppermute | solution.py:16
  64.6 0.2 rev.12
  64.8 0.2 copy.34
  65.0 1.9 gather_fusion
  67.0 0.7 fusion.48
  67.8 1.3 collective-permute-start.5
  69.1 3.0 %collective-permute-start.4 = (bf16[2,1,2,768]{3,2,1,0:T(2,128)(2,1)S(1)}, bf16[2,1,2,768]{3,2,1,0:T(2,128)(2,1)S(1)}, u32[]{:S(2)}, u32[]{:S(2)}) collective-permute-start(bf16[2,1,2,768]{3,2,1,0:T(2,128)(2,1)S(1)} %get-tuple-element.26), channel_id=1, source_target_pairs={{0,2},{2,4},{4,6},{6,8},{8,10},{10,12},{12,14},{14,16},{16,18},{18... | collective-permute-start | bytes 18440 | tf_op jit(solution)/shard_map/ppermute | solution.py:24
  72.1 0.2 rev.13
  72.5 1.9 gather_fusion.1
  74.7 0.2 multiply_reduce_fusion.1
  74.9 0.2 multiply_convert_fusion.1
  75.6 18.0 %all-gather.2.cloned.1.call-done = bf16[3840,768]{1,0:T(8,128)(2,1)} async-done(((bf16[120,768]{1,0:T(8,128)(2,1)}), bf16[3840,768]{1,0:T(8,128)(2,1)}) %all-gather.2.cloned.1.call-update) | async-done | bytes 5898256 | tf_op jit(solution)/shard_map/all_gather | solution.py:46
  93.6 4.8 %fusion.18 = (bf16[1,128,768]{2,1,0:T(8,128)(2,1)S(1)}, f32[128,768]{1,0:T(8,128)}) fusion(bf16[1,128,768]{2,1,0:T(8,128)(2,1)S(1)} %copy-done.1, bf16[3840,768]{1,0:T(8,128)(2,1)} %all-gather.2.cloned.1.call-done, bf16[1,128,3840]{2,1,0:T(8,128)(2,1)S(1)} %slice_dynamic-update-slice_fusion.15), kind=kOutput, calls=%fused_computation.35 | convolution fusion | flops 757137408 | bytes 7667712 | tf_op jit(solution)/shard_map/btk,kd->btd/dot_general | solution.py:70
  98.4 1.7 fusion.7
  100.1 1.2 fusion.25
  101.3 6.1 %convolution_add_fusion = f32[3840,768]{1,0:T(8,128)} fusion(f32[3840,768]{1,0:T(8,128)S(1)} %fusion.7, bf16[128,768]{1,0:T(8,128)(2,1)S(1)} %get-tuple-element.34, bf16[1,128,3840]{2,1,0:T(8,128)(2,1)S(1)} %slice_dynamic-update-slice_fusion.10), kind=kOutput, calls=%fused_computation.4 | convolution fusion | flops 757923840 | bytes 24772608 | tf_op jit(solution)/shard_map/btk,btd->kd/dot_general | solution.py:84
  107.6 1.3 collective-permute-start.7
  108.9 3.2 %collective-permute-start.6 = (bf16[2,1,2,768]{3,2,1,0:T(2,128)(2,1)S(1)}, bf16[2,1,2,768]{3,2,1,0:T(2,128)(2,1)S(1)}, u32[]{:S(2)}, u32[]{:S(2)}) collective-permute-start(bf16[2,1,2,768]{3,2,1,0:T(2,128)(2,1)S(1)} %get-tuple-element.22), channel_id=1, source_target_pairs={{0,2},{2,4},{4,6},{6,8},{8,10},{10,12},{12,14},{14,16},{16,18},{18... | collective-permute-start | bytes 18440 | tf_op jit(solution)/shard_map/ppermute | solution.py:24
  112.2 9.2 %copy.38 = bf16[5,768,768]{2,1,0:T(8,128)(2,1)} copy(bf16[5,768,768]{1,2,0:T(8,128)(2,1)} %bitcast.193) | data formatting | bytes 11796480 | tf_op jit(solution)/shard_map/transpose | solution.py:99
  121.8 4.3 %fusion.30 = (f32[768]{0:T(1024)S(1)}, f32[128]{0:T(128)S(1)}, f32[128,768]{1,0:T(8,128)S(1)}) fusion(f32[1,132,768]{2,1,0:T(8,128)S(1)} %get-tuple-element.17, f32[128]{0:T(128)S(1)} %get-tuple-element.33, f32[768]{0:T(1024)S(1)} %copy-done.3, bf16[3840,768]{1,0:T(8,128)(2,1)} %bitcast.189, bf16[1,128,3840]{2,1,0:T(8,128)(2,1)S(1)} %slice_dynamic-update-slice_fusion.5), kind=kOutput, calls=%fused_computation.51 | convolution fusion | flops 755563648 | bytes 7674880 | tf_op jit(solution)/shard_map/btk,kc->btc/dot_general | solution.py:100
  126.4 0.3 slice-done.1
  126.7 1.0 fusion
  127.7 0.5 fusion.47
  128.2 1.6 collective-permute-start.8
  129.8 1.4 collective-permute-done.8
  131.2 2.3 collective-permute-start.9
  133.5 9.6 %collective-permute-done.9 = bf16[2,1,128,768]{3,2,1,0:T(8,128)(2,1)S(1)} collective-permute-done((bf16[2,1,128,768]{3,2,1,0:T(8,128)(2,1)S(1)}, bf16[2,1,128,768]{3,2,1,0:T(8,128)(2,1)S(1)}, u32[]{:S(2)}, u32[]{:S(2)}) %collective-permute-start.9) | collective-permute-done | bytes 393248 | tf_op jit(solution)/shard_map/ppermute | solution.py:16
  143.1 2.1 collective-permute-start.10
  145.2 9.1 %collective-permute-done.10 = bf16[2,1,128,768]{3,2,1,0:T(8,128)(2,1)S(1)} collective-permute-done((bf16[2,1,128,768]{3,2,1,0:T(8,128)(2,1)S(1)}, bf16[2,1,128,768]{3,2,1,0:T(8,128)(2,1)S(1)}, u32[]{:S(2)}, u32[]{:S(2)}) %collective-permute-start.10) | collective-permute-done | bytes 393248 | tf_op jit(solution)/shard_map/ppermute | solution.py:16
  154.3 2.1 collective-permute-start.11
  156.3 58.8 %all-reduce = f32[768]{0:T(1024)S(1)} all-reduce(f32[768]{0:T(1024)S(1)} %add.100), channel_id=3, replica_groups=mesh['seq'=16,'dp'=2] {'seq','dp'}, use_global_device_ids=true, to_apply=%region_7.0.clone | all-reduce | flops 768 | bytes 6144
  215.1 0.6 dynamic-slice
  215.8 0.2 rev.15
  216.2 1.9 gather_fusion.3
  218.2 0.2 rev.14
  218.6 1.9 gather_fusion.2
  220.7 1.1 fusion.26
  221.8 47.6 %reduce-scatter.2.cloned.1.call-done = f32[120,768]{1,0:T(8,128)} async-done(((f32[3840,768]{1,0:T(8,128)}), f32[120,768]{1,0:T(8,128)}) %reduce-scatter.2.cloned.1.call-update) | async-done | bytes 368656 | tf_op jit(solution)/shard_map/reduce_scatter | solution.py:122
  (67 shorter events, 2.7 us)
Async XLA Ops:
  7.2 67.4 %copy-start = (bf16[1,128,768]{2,1,0:T(8,128)(2,1)S(1)}, bf16[1,128,768]{2,1,0:T(8,128)(2,1)}, u32[]{:S(2)}) copy-start(bf16[1,128,768]{2,1,0:T(8,128)(2,1)} %param.5) | copy-start | bytes 589828
  7.2 67.7 %copy-start.3 = (f32[768]{0:T(1024)S(1)}, f32[768]{0:T(1024)}, u32[]{:S(2)}) copy-start(f32[768]{0:T(1024)} %param.8) | copy-start | bytes 9220
  7.2 86.4 %all-gather.2.cloned.1.call-start = ((), (), s32[]{:S(2)}) async-start(), calls=%async_computation.1 | async-start | bytes 6082560 | tf_op jit(solution)/shard_map/all_gather | solution.py:46
  7.9 261.5 %reduce-scatter.2.cloned.1.call-start = ((), (), s32[]{:S(2)}) async-start(), calls=%async_computation.2 | async-start | bytes 12165120 | tf_op jit(solution)/shard_map/reduce_scatter | solution.py:122
  9.0 1.9 collective-permute-start
  10.9 12.3 %collective-permute-start.1 = (bf16[2,1,128,768]{3,2,1,0:T(8,128)(2,1)S(1)}, bf16[2,1,128,768]{3,2,1,0:T(8,128)(2,1)S(1)}, u32[]{:S(2)}, u32[]{:S(2)}) collective-permute-start(bf16[2,1,128,768]{3,2,1,0:T(8,128)(2,1)S(1)} %collective-permute-done), channel_id=1, source_target_pairs={{0,4},{4,0},{2,6},{6,2},{8,12},{12,8},{10,14},{14,10},{16,20},{20,... | collective-permute-start | bytes 1179656 | tf_op jit(solution)/shard_map/ppermute | solution.py:16
  23.2 14.4 %collective-permute-start.2 = (bf16[2,1,128,768]{3,2,1,0:T(8,128)(2,1)S(1)}, bf16[2,1,128,768]{3,2,1,0:T(8,128)(2,1)S(1)}, u32[]{:S(2)}, u32[]{:S(2)}) collective-permute-start(bf16[2,1,128,768]{3,2,1,0:T(8,128)(2,1)S(1)} %collective-permute-done.1), channel_id=1, source_target_pairs={{0,8},{8,0},{2,10},{10,2},{4,12},{12,4},{6,14},{14,6},{16,24},{24,... | collective-permute-start | bytes 1179656 | tf_op jit(solution)/shard_map/ppermute | solution.py:16
  37.6 26.9 %collective-permute-start.3 = (bf16[2,1,128,768]{3,2,1,0:T(8,128)(2,1)S(1)}, bf16[2,1,128,768]{3,2,1,0:T(8,128)(2,1)S(1)}, u32[]{:S(2)}, u32[]{:S(2)}) collective-permute-start(bf16[2,1,128,768]{3,2,1,0:T(8,128)(2,1)S(1)} %collective-permute-done.2), channel_id=1, source_target_pairs={{0,16},{16,0},{2,18},{18,2},{4,20},{20,4},{6,22},{22,6},{8,24},{24... | collective-permute-start | bytes 1179656 | tf_op jit(solution)/shard_map/ppermute | solution.py:16
  64.8 28.8 %copy-start.1 = (bf16[1,128,768]{2,1,0:T(8,128)(2,1)S(1)}, bf16[1,128,768]{2,1,0:T(8,128)(2,1)}, u32[]{:S(2)}) copy-start(bf16[1,128,768]{2,1,0:T(8,128)(2,1)} %param.6) | copy-start | bytes 589828
  67.8 6.8 %collective-permute-start.5 = (bf16[2,1,2,768]{3,2,1,0:T(2,128)(2,1)S(1)}, bf16[2,1,2,768]{3,2,1,0:T(2,128)(2,1)S(1)}, u32[]{:S(2)}, u32[]{:S(2)}) collective-permute-start(bf16[2,1,2,768]{3,2,1,0:T(2,128)(2,1)S(1)} %get-tuple-element.27), channel_id=1, source_target_pairs={{2,0},{4,2},{6,4},{8,6},{10,8},{12,10},{14,12},{16,14},{18,16},{20... | collective-permute-start | bytes 18440 | tf_op jit(solution)/shard_map/ppermute | solution.py:27
  69.1 5.5 %collective-permute-start.4 = (bf16[2,1,2,768]{3,2,1,0:T(2,128)(2,1)S(1)}, bf16[2,1,2,768]{3,2,1,0:T(2,128)(2,1)S(1)}, u32[]{:S(2)}, u32[]{:S(2)}) collective-permute-start(bf16[2,1,2,768]{3,2,1,0:T(2,128)(2,1)S(1)} %get-tuple-element.26), channel_id=1, source_target_pairs={{0,2},{2,4},{4,6},{6,8},{8,10},{10,12},{12,14},{14,16},{16,18},{18... | collective-permute-start | bytes 18440 | tf_op jit(solution)/shard_map/ppermute | solution.py:24
  93.6 6.5 %slice-start.2 = ((s8[5898240]{0:T(1024)(128)(4,1)}), s8[4194304]{0:T(1024)(128)(4,1)S(1)}, s32[]{:S(2)}) async-start(s8[5898240]{0:T(1024)(128)(4,1)} %bitcast.194), calls=%async_computation.5 | async-start | bytes 8388608
  98.4 1.7 slice-start.3
  107.6 13.8 %collective-permute-start.7 = (bf16[2,1,2,768]{3,2,1,0:T(2,128)(2,1)S(1)}, bf16[2,1,2,768]{3,2,1,0:T(2,128)(2,1)S(1)}, u32[]{:S(2)}, u32[]{:S(2)}) collective-permute-start(bf16[2,1,2,768]{3,2,1,0:T(2,128)(2,1)S(1)} %get-tuple-element.23), channel_id=1, source_target_pairs={{2,0},{4,2},{6,4},{8,6},{10,8},{12,10},{14,12},{16,14},{18,16},{20... | collective-permute-start | bytes 18440 | tf_op jit(solution)/shard_map/ppermute | solution.py:27
  108.9 12.5 %collective-permute-start.6 = (bf16[2,1,2,768]{3,2,1,0:T(2,128)(2,1)S(1)}, bf16[2,1,2,768]{3,2,1,0:T(2,128)(2,1)S(1)}, u32[]{:S(2)}, u32[]{:S(2)}) collective-permute-start(bf16[2,1,2,768]{3,2,1,0:T(2,128)(2,1)S(1)} %get-tuple-element.22), channel_id=1, source_target_pairs={{0,2},{2,4},{4,6},{6,8},{8,10},{10,12},{12,14},{14,16},{16,18},{18... | collective-permute-start | bytes 18440 | tf_op jit(solution)/shard_map/ppermute | solution.py:24
  121.6 4.8 %slice-start = ((s8[5898240]{0:T(1024)(128)(4,1)}), s8[4194304]{0:T(1024)(128)(4,1)S(1)}, s32[]{:S(2)}) async-start(s8[5898240]{0:T(1024)(128)(4,1)} %bitcast.190), calls=%async_computation.3 | async-start | bytes 8388608
  121.8 4.9 %slice-start.1 = ((s8[5898240]{0:T(1024)(128)(4,1)}), s8[1703936]{0:T(1024)(128)(4,1)S(1)}, s32[]{:S(2)}) async-start(s8[5898240]{0:T(1024)(128)(4,1)} %bitcast.190), calls=%async_computation.4 | async-start | bytes 3407872
  127.7 93.0 %copy-start.2 = (f32[128,768]{1,0:T(8,128)S(1)}, f32[128,768]{1,0:T(8,128)}, u32[]{:S(2)}) copy-start(f32[128,768]{1,0:T(8,128)} %get-tuple-element.37) | copy-start | bytes 1179652
  128.2 2.9 %collective-permute-start.8 = (bf16[2,1,128,768]{3,2,1,0:T(8,128)(2,1)S(1)}, bf16[2,1,128,768]{3,2,1,0:T(8,128)(2,1)S(1)}, u32[]{:S(2)}, u32[]{:S(2)}) collective-permute-start(bf16[2,1,128,768]{3,2,1,0:T(8,128)(2,1)S(1)} %pad_maximum_fusion.3), channel_id=1, source_target_pairs={{0,2},{2,0},{4,6},{6,4},{8,10},{10,8},{12,14},{14,12},{16,18},{18,... | collective-permute-start | bytes 1179656 | tf_op jit(solution)/shard_map/ppermute | solution.py:16
  131.2 11.9 %collective-permute-start.9 = (bf16[2,1,128,768]{3,2,1,0:T(8,128)(2,1)S(1)}, bf16[2,1,128,768]{3,2,1,0:T(8,128)(2,1)S(1)}, u32[]{:S(2)}, u32[]{:S(2)}) collective-permute-start(bf16[2,1,128,768]{3,2,1,0:T(8,128)(2,1)S(1)} %collective-permute-done.8), channel_id=1, source_target_pairs={{0,4},{4,0},{2,6},{6,2},{8,12},{12,8},{10,14},{14,10},{16,20},{20,... | collective-permute-start | bytes 1179656 | tf_op jit(solution)/shard_map/ppermute | solution.py:16
  143.1 11.2 %collective-permute-start.10 = (bf16[2,1,128,768]{3,2,1,0:T(8,128)(2,1)S(1)}, bf16[2,1,128,768]{3,2,1,0:T(8,128)(2,1)S(1)}, u32[]{:S(2)}, u32[]{:S(2)}) collective-permute-start(bf16[2,1,128,768]{3,2,1,0:T(8,128)(2,1)S(1)} %collective-permute-done.9), channel_id=1, source_target_pairs={{0,8},{8,0},{2,10},{10,2},{4,12},{12,4},{6,14},{14,6},{16,24},{24,... | collective-permute-start | bytes 1179656 | tf_op jit(solution)/shard_map/ppermute | solution.py:16
  154.3 61.5 %collective-permute-start.11 = (bf16[2,1,128,768]{3,2,1,0:T(8,128)(2,1)S(1)}, bf16[2,1,128,768]{3,2,1,0:T(8,128)(2,1)S(1)}, u32[]{:S(2)}, u32[]{:S(2)}) collective-permute-start(bf16[2,1,128,768]{3,2,1,0:T(8,128)(2,1)S(1)} %collective-permute-done.10), channel_id=1, source_target_pairs={{0,16},{16,0},{2,18},{18,2},{4,20},{20,4},{6,22},{22,6},{8,24},{24... | collective-permute-start | bytes 1179656 | tf_op jit(solution)/shard_map/ppermute | solution.py:16
Sparse Core Ops, SparseCore 0:
  10.9 82.6 all-gather.1
  107.6 161.7 reduce-scatter.1
where the time goes:
time: 277 us; the launch traced here: 276 us
  waiting for transfers between devices  134 us (48%)
  blocking collectives  58.8 us (21%)
  starting transfers between devices  24.5 us (9%)
  local copies, waits for them, and re-layouts  20.8 us (8%)
  matrix products  19 us (7%)
  between operations  14.5 us (5%)
  other arithmetic  4.92 us (2%)
    ppermute x8, waiting for transfers between devices, swapped(): return lax.ppermute(block, axis, route)  67.3 us
    unnamed x1, blocking collectives  58.8 us
    reduce_scatter x1, waiting for transfers between devices, per_device(): lax.psum_scatter(kernel_total, ('seq', 'dp'), scatter_dimension=0, tiled=...  47.6 us
    all_gather x1, waiting for transfers between devices, per_device(): gathered = lax.all_gather(weights, ('seq', 'dp'), axis=0, tiled=True)  18 us
    ppermute x8, starting transfers between devices, swapped(): return lax.ppermute(block, axis, route)  15.6 us
    transpose x1, local copies, waits for them, and re-layouts, per_device(): kernels[strand_index].transpose(0, 2, 1)  9.22 us
    gather x8, local copies, waits for them, and re-layouts, reversed_pair(): return block[:, ::-1][:, :, pairing]  8.09 us
    dot_general x2, matrix products, per_device(): jnp.einsum('btk,btd->kd', windows_list[strand_index], grad_pres[strand_in...  7.81 us
  transfers between devices with their start and end apart: 14, of which 9 were waited for; matrix products, arithmetic and copies ran while one was open for 11% of the time, Pallas kernels for 0%

commit v1 on v0

v1 whole, which is shorter than its diff:
```python
import jax
import jax.numpy as jnp
from jax import lax
from jax.sharding import Mesh, PartitionSpec as P

epsilon = 1e-06


def neighbours(block, axis, width):
    count = lax.axis_size(axis)
    forward = [(i, i + 1) for i in range(count - 1)]
    backward = [(target, source) for source, target in forward]
    low = lax.ppermute(block[-width:], axis, forward)
    high = lax.ppermute(block[:width], axis, backward)
    return low, high


def gelu_and_slope(preact):
    result, pullback = jax.vjp(jax.nn.gelu, preact)
    return result, pullback(jnp.ones_like(preact))[0]


def per_device(activations, cotangent, weights, norm_gain, pairing):
    ranks = lax.axis_size("rank")
    blocks = lax.axis_size("block")
    copies = lax.axis_size("dp")
    positions, channels = activations.shape[1:]
    rows = weights.shape[0]
    taps = rows * ranks * blocks * copies // channels
    part = channels // ranks
    half = taps // 2
    reach = 2 * half
    span = positions * ranks
    mine = lax.all_to_all(weights, "rank", split_axis=1, concat_axis=0, tiled=True)
    packed = mine.reshape(2, ranks * rows // 2, part).transpose(1, 0, 2).reshape(-1, 2 * part)
    gathered = lax.all_gather(packed, ("block", "dp"), axis=0, tiled=True)
    kernel = gathered.reshape(blocks, copies, ranks // 2, rows, 2, part)
    kernel = kernel.transpose(0, 4, 2, 1, 3, 5).reshape(taps, channels, part)
    kernel = kernel.transpose(1, 0, 2).reshape(channels, taps * part)
    swap = (pairing[None, :] == jnp.arange(channels, dtype=pairing.dtype)[:, None]).astype(jnp.bfloat16)
    values = activations[0]
    cot = cotangent[0]
    cot_swapped = jnp.dot(cot, swap)
    whole = jnp.broadcast_to(values, (ranks, positions, channels))
    slices = [t.reshape(positions, ranks, part).transpose(1, 0, 2) for t in (cot, cot_swapped)]
    message = jnp.concatenate([whole] + slices, -1).reshape(span, -1)
    message = lax.all_to_all(message, "rank", split_axis=0, concat_axis=0, tiled=True)
    low, high = neighbours(message, "block", reach)
    extended = jnp.concatenate([low, message, high], 0)
    group = extended[:, :channels]
    group_swapped = jnp.dot(group, swap)
    group = group.astype(jnp.float32)
    inverse_rms = lax.rsqrt(jnp.mean(group * group, -1, keepdims=True) + epsilon)
    normed = jnp.stack(
        [
            (group * inverse_rms * norm_gain).astype(jnp.bfloat16),
            (group_swapped.astype(jnp.float32) * inverse_rms * norm_gain).astype(jnp.bfloat16),
        ]
    )
    halves = 0.5 * extended[half:-half, channels:].astype(jnp.float32)
    terms = jnp.einsum("src,ce->sre", normed, kernel, preferred_element_type=jnp.float32)
    wide = span + reach
    tap_list = range(taps)
    gelus, shifted = [], []
    for strand in range(2):
        starts = [k if strand == 0 else reach - k for k in tap_list]
        preact = sum(
            terms[strand, starts[k] : starts[k] + wide, k * part : (k + 1) * part] for k in tap_list
        )
        result, slope = gelu_and_slope(preact)
        gelus.append(result[half : half + span].astype(jnp.bfloat16))
        grad_pre = (halves[:, strand * part : (strand + 1) * part] * slope).astype(jnp.bfloat16)
        shifted.append(
            jnp.concatenate([grad_pre[reach - s : reach - s + span] for s in starts], -1)
        )
    shifted = jnp.stack(shifted)
    inner = normed[:, reach : reach + span]
    kernel_term = jnp.einsum("src,sre->ce", inner, shifted, preferred_element_type=jnp.float32)
    gain_term = jnp.sum(kernel_term * kernel.astype(jnp.float32), -1) / norm_gain
    kernel_rows = kernel_term.astype(jnp.bfloat16).reshape(channels, taps, part).transpose(1, 0, 2)
    kernel_rows = kernel_rows.reshape(blocks, 2, ranks // 2, copies, rows, part)
    kernel_rows = kernel_rows.transpose(0, 3, 2, 4, 1, 5).reshape(blocks * copies, -1, 2 * part)
    gain_rows = gain_term.reshape(blocks, ranks, copies, -1).transpose(0, 2, 1, 3)
    gain_rows = gain_rows.reshape(blocks * copies, -1)
    gain_high = gain_rows.astype(jnp.bfloat16)
    gain_low = (gain_rows - gain_high.astype(jnp.float32)).astype(jnp.bfloat16)
    extra = jnp.concatenate([gain_high, gain_low], -1)
    gain_count = extra.shape[-1]
    extra_rows = -(-gain_count // (2 * part * 16)) * 16
    extra = jnp.pad(extra, ((0, 0), (0, extra_rows * 2 * part - gain_count)))
    outgoing = jnp.concatenate([kernel_rows, extra.reshape(blocks * copies, extra_rows, 2 * part)], 1)
    summed = lax.psum_scatter(outgoing, ("block", "dp"), scatter_dimension=0, tiled=True)[0]
    summed = summed.astype(jnp.float32)
    kernel_sum = summed[:-extra_rows].reshape(ranks // 2, rows, 2, part).transpose(2, 0, 1, 3)
    kernel_sum = kernel_sum.reshape(ranks, rows, part)
    gain_sum = summed[-extra_rows:].reshape(-1)[:gain_count].reshape(2, ranks, -1).sum(0)
    gain_sum = jnp.pad(gain_sum, ((0, 0), (0, part - gain_sum.shape[1])))
    last = jnp.concatenate([kernel_sum, gain_sum[:, None]], 1)
    last = lax.all_to_all(last, "rank", split_axis=0, concat_axis=0, tiled=True)
    grad_kernel = last[:, :rows].transpose(1, 0, 2).reshape(rows, channels)
    grad_gain = last[:, rows, : channels // (ranks * blocks * copies)].sum(0)
    kernel_swapped = jnp.dot(swap, kernel)
    grad_scaled = (
        jnp.einsum("re,ce->rc", shifted[0], kernel, preferred_element_type=jnp.float32) * norm_gain
        + jnp.einsum("re,ce->rc", shifted[1], kernel_swapped, preferred_element_type=jnp.float32)
        * norm_gain[pairing]
    )
    back = jnp.concatenate([grad_scaled.astype(jnp.bfloat16)] + gelus, -1)
    back = lax.all_to_all(back, "rank", split_axis=0, concat_axis=0, tiled=True)
    back = back.reshape(ranks, positions, -1)
    scaled = back[:, :, :channels].astype(jnp.float32).sum(0)
    gelu_plain = back[:, :, channels : channels + part].transpose(1, 0, 2).reshape(positions, channels)
    gelu_other = back[:, :, channels + part :].transpose(1, 0, 2).reshape(positions, channels)
    gelu_other = jnp.dot(gelu_other, swap).astype(jnp.float32)
    values = values.astype(jnp.float32)
    cot = cot.astype(jnp.float32)
    own_rms = lax.rsqrt(jnp.mean(values * values, -1, keepdims=True) + epsilon)
    reverse_out = (values + gelu_other).astype(jnp.bfloat16).astype(jnp.float32)
    combined = (0.5 * (values + gelu_plain.astype(jnp.float32) + reverse_out)).astype(jnp.bfloat16)
    grad_input = (
        cot + own_rms * scaled - values * own_rms**3 * jnp.mean(scaled * values, -1, keepdims=True)
    ).astype(jnp.bfloat16)
    return combined[None], grad_input[None], grad_kernel, grad_gain


def solution(mesh):
    seq, dp = mesh.shape["seq"], mesh.shape["dp"]
    ranks = 4
    grouped = Mesh(mesh.devices.reshape(seq // ranks, ranks, dp), ("block", "rank", "dp"))
    along = P("dp", ("block", "rank"), None)
    every = ("block", "rank", "dp")
    return jax.shard_map(
        per_device,
        mesh=grouped,
        in_specs=(along, along, P(every, None), P(), P()),
        out_specs=(along, along, P(every, None), P(every)),
        check_vma=False,
    )
```

time: 277 us -> 185 us (0.67)
  waiting for transfers between devices: 134 us -> 63.6 us
  blocking collectives: 58.8 us -> 27.6 us
  local copies, waits for them, and re-layouts: 20.8 us -> 38.8 us
  starting transfers between devices: 24.5 us -> 12.2 us
  other arithmetic: 4.92 us -> 9.25 us
    ppermute x12 -> x2, waiting for transfers between devices: 67.4 us -> 4.52 us  [the longest x1 4.52 us: neighbours(): high = lax.ppermute(block[:width], axis, backward)]
    unnamed x1 -> x0, blocking collectives: 58.8 us -> none
    all_to_all x0 -> x2, blocking collectives: none -> 27.6 us  [the longest x1 18.3 us: per_device(): lax.all_to_all(message, 'rank', split_axis=0, concat_axis=0, tiled=True)]
    all_to_all x0 -> x2, waiting for transfers between devices: none -> 20.7 us  [the longest x1 15.6 us: per_device(): back = lax.all_to_all(back, 'rank', split_axis=0, concat_axis=0, tiled=True)]
    ppermute x12 -> x2, starting transfers between devices: 24.4 us -> 4.95 us  [the longest x1 3.48 us: neighbours(): low = lax.ppermute(block[-width:], axis, forward)]
    reduce_scatter x1, waiting for transfers between devices: 47.6 us -> 29.3 us  [per_device(): lax.psum_scatter(outgoing, ('block', 'dp'), scatter_dimension=0, tiled=True)]
    reshape x0 -> x9, local copies, waits for them, and re-layouts: none -> 9.71 us  [the longest x1 3.31 us: per_device(): kernel = gathered.reshape(blocks, copies, ranks // 2, rows, 2, part)]
    all_gather x1, waiting for transfers between devices: 18 us -> 8.99 us  [per_device(): gathered = lax.all_gather(packed, ('block', 'dp'), axis=0, tiled=True)]
  transfers between devices with their start and end apart: 14 -> 6, of which waited for: 9 -> 5; matrix products, arithmetic and copies ran while one was open for 11% -> 12% of each run, Pallas kernels for 0% -> 0%
where the time goes in v1:
time: 185 us
  waiting for transfers between devices  63.6 us (34%)
  local copies, waits for them, and re-layouts  38.8 us (21%)
  blocking collectives  27.6 us (15%)
  matrix products  18.7 us (10%)
  between operations  14.5 us (8%)
  starting transfers between devices  12.2 us (7%)
  other arithmetic  9.25 us (5%)
    reduce_scatter x1, waiting for transfers between devices, per_device(): lax.psum_scatter(outgoing, ('block', 'dp'), scatter_dimension=0, tiled=True)  29.3 us
    all_to_all x1, blocking collectives, per_device(): lax.all_to_all(message, 'rank', split_axis=0, concat_axis=0, tiled=True)  18.3 us
    all_to_all x1, waiting for transfers between devices, per_device(): back = lax.all_to_all(back, 'rank', split_axis=0, concat_axis=0, tiled=True)  15.6 us
    all_to_all x1, blocking collectives, per_device(): lax.all_to_all(weights, 'rank', split_axis=1, concat_axis=0, tiled=True)  9.34 us
    all_gather x1, waiting for transfers between devices, per_device(): gathered = lax.all_gather(packed, ('block', 'dp'), axis=0, tiled=True)  8.99 us
    unnamed x42, local copies, waits for them, and re-layouts  5.64 us
    concatenate x2, local copies, waits for them, and re-layouts, per_device(): jnp.concatenate([grad_pre[reach - s:reach - s + span] for s in starts], -1)  5.25 us
    dot_general x1, matrix products, per_device(): jnp.einsum('src,sre->ce', inner, shifted, preferred_element_type=jnp.floa...  5.15 us
  transfers between devices with their start and end apart: 6, of which 5 were waited for; matrix products, arithmetic and copies ran while one was open for 12% of the time, Pallas kernels for 0%

profile of v1, /device:TPU:0, one launch (start us, length us, event | category | flops | bytes accessed | tf_op | source)
XLA Modules:
  0.0 184.7 jit_solution(4669085749540602701)
XLA Ops:
  7.2 1.1 copy.51
  8.4 9.3 %all_to_all.39 = bf16[120,4,192]{0,2,1:T(8,128)(2,1)S(1)} all-to-all(bf16[120,4,192]{0,2,1:T(8,128)(2,1)S(1)} %bitcast.120), channel_id=1, replica_groups=mesh['block'=4,'rank'=4,'dp'=2] {'rank'}, dimensions={1} | all-to-all | bytes 368640 | tf_op jit(solution)/shard_map/all_to_all | solution.py:34
  18.2 0.8 copy.54
  19.1 0.5 fusion.33
  20.5 1.3 concatenate.24
  21.8 18.3 %all_to_all.40 = bf16[4,128,1152]{2,1,0:T(8,128)(2,1)S(1)} all-to-all(bf16[4,128,1152]{2,1,0:T(8,128)(2,1)S(1)} %concatenate.24), channel_id=1, replica_groups=mesh['block'=4,'rank'=4,'dp'=2] {'rank'}, dimensions={0} | all-to-all | bytes 2359296 | tf_op jit(solution)/shard_map/all_to_all | solution.py:47
  40.1 3.5 %collective-permute-start = (bf16[4,1152]{1,0:T(4,128)(2,1)S(1)}, bf16[4,1152]{1,0:T(4,128)(2,1)S(1)}, u32[]{:S(2)}, u32[]{:S(2)}) collective-permute-start(bf16[4,1152]{1,0:T(4,128)(2,1)S(1)} %get-tuple-element.28), channel_id=1, source_target_pairs={{0,8},{8,16},{16,24},{1,9},{9,17},{17,25},{2,10},{10,18},{18,26},{... | collective-permute-start | bytes 27656 | tf_op jit(solution)/shard_map/ppermute | solution.py:13
  43.6 1.5 collective-permute-start.1
  45.1 4.5 %collective-permute-done.1 = bf16[4,1152]{1,0:T(4,128)(2,1)S(1)} collective-permute-done((bf16[4,1152]{1,0:T(4,128)(2,1)S(1)}, bf16[4,1152]{1,0:T(4,128)(2,1)S(1)}, u32[]{:S(2)}, u32[]{:S(2)}) %collective-permute-start.1) | collective-permute-done | bytes 9248 | tf_op jit(solution)/shard_map/ppermute | solution.py:14
  50.0 1.0 convert_multiply_fusion.2
  51.0 1.2 fusion.37
  52.2 1.9 %fusion.19 = bf16[1,520,768]{2,1,0:T(8,128)(2,1)} fusion(s32[768]{0:T(1024)S(1)} %copy-done.17, f32[768]{0:T(1024)S(1)} %copy-done, f32[520]{0:T(1024)S(1)} %add_rsqrt_fusion, bf16[4,1152]{1,0:T(4,128)(2,1)S(1)} %collective-permute-done.1, bf16[512,1152]{1,0:T(8,128)(2,1)S(1)} %bitcast.100, bf16[4,1152]{1,0:T(4,128)(2,1)S(1)} %collective-permute-done), kind=kOutput, calls=%fused_computation.29 | convolution fusion | flops 618000384 | bytes 2005024 | tf_op jit(solution)/shard_map/dot_general | solution.py:51
  54.1 9.0 %all-gather.2.cloned.1.call-done = bf16[1920,384]{1,0:T(8,128)(2,1)} async-done(((bf16[240,384]{1,0:T(8,128)(2,1)}), bf16[1920,384]{1,0:T(8,128)(2,1)}) %all-gather.2.cloned.1.call-update) | async-done | bytes 1474576 | tf_op jit(solution)/shard_map/all_gather | solution.py:36
  63.1 1.9 %copy.55 = bf16[1920,384]{0,1:T(8,128)(2,1)S(1)} copy(bf16[1920,384]{1,0:T(8,128)(2,1)} %all-gather.2.cloned.1.call-done) | data formatting | bytes 2949120 | tf_op jit(solution)/shard_map/all_gather | solution.py:36
  65.0 3.3 %reshape.160 = bf16[4,2,2,120,2,192]{3,2,1,0,5,4:T(2,128)(2,1)S(1)} reshape(bf16[1920,384]{0,1:T(8,128)(2,1)S(1)} %copy.55) | data formatting | bytes 2949120 | tf_op jit(solution)/shard_map/reshape | solution.py:37
  68.3 1.9 %copy.56 = bf16[4,2,2,2,120,192]{5,4,3,2,1,0:T(8,128)(2,1)S(1)} copy(bf16[4,2,2,2,120,192]{4,2,3,0,5,1:T(2,128)(2,1)S(1)} %bitcast.103) | data formatting | bytes 2949120 | tf_op jit(solution)/shard_map/transpose | solution.py:38
  70.2 0.9 copy.57
  71.1 3.8 %fusion.12 = f32[2,520,960]{2,1,0:T(8,128)S(1)} fusion(bf16[768,960,1]{0,1,2:T(8,128)(2,1)S(1)} %bitcast.111, bf16[1,520,768]{2,1,0:T(8,128)(2,1)} %fusion.19, bf16[1,520,768]{2,1,0:T(8,128)(2,1)} %fusion.37), kind=kOutput, calls=%fused_computation.18 | convolution fusion | flops 1534341120 | bytes 7065600 | tf_op jit(solution)/shard_map/src,ce->sre/dot_general | solution.py:61
  74.9 1.9 %add_multiply_fusion = (f32[516,192]{1,0:T(8,128)}, f32[516,192]{1,0:T(8,128)S(1)}, f32[516,192]{1,0:T(8,128)}, f32[516,192]{1,0:T(8,128)S(1)}) fusion(f32[2,520,960]{2,1,0:T(8,128)S(1)} %fusion.12), kind=kLoop, calls=%fused_computation.85 | loop fusion | flops 2179584 | bytes 5548032 | tf_op jit(solution)/shard_map/jvp()/mul | solution.py:19
  76.8 0.7 fusion.53
  77.5 1.3 fusion.72
  78.8 3.2 %concatenate.27 = bf16[512,960]{1,0:T(8,128)(2,1)} concatenate(bf16[512,192]{1,0:T(8,128)(2,1)} %get-tuple-element.36, bf16[512,192]{1,0:T(8,128)(2,1)} %get-tuple-element.35, bf16[512,192]{1,0:T(8,128)(2,1)} %get-tuple-element.34, bf16[512,192]{1,0:T(8,128)(2,1)S(1)} %get-tuple-element.33, bf16[512,192]{1,0:T(8,128)(2,1)S(1)} %get-tuple-element.32), dimensions={1} | concatenate | bytes 1966080 | tf_op jit(solution)/shard_map/concatenate | solution.py:74
  82.0 2.1 %concatenate.26 = bf16[512,960]{1,0:T(8,128)(2,1)} concatenate(bf16[512,192]{1,0:T(8,128)(2,1)S(1)} %get-tuple-element.48, bf16[512,192]{1,0:T(8,128)(2,1)S(1)} %get-tuple-element.49, bf16[512,192]{1,0:T(8,128)(2,1)S(1)} %get-tuple-element.50, bf16[512,192]{1,0:T(8,128)(2,1)S(1)} %get-tuple-element.51, bf16[512,192]{1,0:T(8,128)(2,1)S(1)} %get-tuple-element.52), dimensions={1} | concatenate | bytes 1966080 | tf_op jit(solution)/shard_map/concatenate | solution.py:74
  84.0 5.1 %fusion = (f32[768]{0:T(1024)S(1)}, bf16[768,960,1]{0,1,2:T(8,128)(2,1)}) fusion(bf16[768,5,192]{0,2,1:T(8,128)(2,1)S(1)} %copy.57, bf16[1,512,960]{2,1,0:T(8,128)(2,1)} %bitcast.115, bf16[1,512,960]{2,1,0:T(8,128)(2,1)} %bitcast.116, bf16[1,520,768]{2,1,0:T(8,128)(2,1)} %fusion.19, bf16[1,520,768]{2,1,0:T(8,128)(2,1)} %fusion.37), kind=kOutput, calls=%fused_computation.3 | convolution fusion | flops 1517026560 | bytes 6515712 | tf_op jit(solution)/shard_map/src,sre->ce/dot_general | solution.py:78
  89.5 0.7 copy.76
  90.1 2.6 %copy.64 = bf16[768,5,192]{2,0,1:T(8,128)(2,1)S(1)} copy(bf16[768,5,192]{0,2,1:T(8,128)(2,1)} %bitcast.114) | data formatting | bytes 2949120 | tf_op jit(solution)/shard_map/reshape | solution.py:80
  92.7 1.6 copy.65
  94.3 1.1 reshape.166
  95.3 1.3 copy.67
  96.6 1.6 pad_maximum_fusion
  98.4 3.4 %gather_fusion = f32[768]{0:T(1024)S(1)} fusion(f32[768]{0:T(1024)S(1)} %copy-done, s32[1024]{0:T(1024)S(1)} %pad_clamp_fusion), kind=kCustom, calls=%fused_computation | custom fusion | bytes 9216 | tf_op jit(solution)/shard_map/gather | solution.py:106
  102.1 1.1 copy-done.13
  103.5 2.1 %fusion.74 = f32[512,768]{1,0:T(8,128)} fusion(bf16[512,960]{1,0:T(8,128)(2,1)S(1)} %copy-done.15, bf16[768,960]{0,1:T(8,128)(2,1)S(1)} %bitcast.112), kind=kOutput, calls=%fused_computation.116 | convolution fusion | flops 754974720 | bytes 4030464 | tf_op jit(solution)/shard_map/re,ce->rc/dot_general | solution.py:104
  105.6 3.9 %add_convert_fusion = bf16[512,768]{1,0:T(8,128)(2,1)S(1)} fusion(f32[512,768]{1,0:T(8,128)} %fusion.74, bf16[512,960]{1,0:T(8,128)(2,1)} %concatenate.27, f32[768]{0:T(1024)S(1)} %gather_fusion, f32[768]{0:T(1024)S(1)} %copy-done, bf16[768,960]{0,1:T(8,128)(2,1)S(1)} %bitcast.113, s32[768]{0:T(1024)S(1)} %copy-done.17), kind=kOutput, calls=%fused_computation.28 | convolution fusion | flops 1889599488 | bytes 4826112 | tf_op jit(solution)/shard_map/re,ce->rc/dot_general | solution.py:105
  109.5 1.3 concatenate.28
  110.8 1.4 copy.58
  112.2 3.7 %all-to-all-start.2 = ((bf16[4,128,1152]{1,2,0:T(8,128)(2,1)}), bf16[4,128,1152]{1,2,0:T(8,128)(2,1)S(1)}, u32[]{:S(2)}, u32[]{:S(2)}) async-start(bf16[4,128,1152]{1,2,0:T(8,128)(2,1)} %copy.58), calls=%async_computation.2 | async-start | bytes 2359296 | tf_op jit(solution)/shard_map/all_to_all | solution.py:109
  116.1 15.6 %all-to-all-done.2 = bf16[4,128,1152]{1,2,0:T(8,128)(2,1)S(1)} async-done(((bf16[4,128,1152]{1,2,0:T(8,128)(2,1)}), bf16[4,128,1152]{1,2,0:T(8,128)(2,1)S(1)}, u32[]{:S(2)}, u32[]{:S(2)}) %all-to-all-start.2) | async-done | bytes 1179680 | tf_op jit(solution)/shard_map/all_to_all | solution.py:109
  132.3 29.3 %reduce-scatter.2.cloned.1.call-done = bf16[1,256,384]{1,2,0:T(8,128)(2,1)} async-done(((bf16[8,256,384]{1,2,0:T(8,128)(2,1)}), bf16[1,256,384]{1,2,0:T(8,128)(2,1)}) %reduce-scatter.2.cloned.1.call-update) | async-done | bytes 196624 | tf_op jit(solution)/shard_map/reduce_scatter | solution.py:92
  161.7 1.0 slice.190
  163.0 1.0 slice.189
  164.4 0.9 pad_maximum_fusion.3
  165.4 3.5 %all-to-all-start.3 = ((f32[4,121,192]{1,2,0:T(8,128)}), f32[4,121,192]{1,2,0:T(8,128)S(1)}, u32[]{:S(2)}, u32[]{:S(2)}) async-start(f32[4,121,192]{1,2,0:T(8,128)} %pad_maximum_fusion.3), calls=%async_computation.4 | async-start | bytes 786432 | tf_op jit(solution)/shard_map/all_to_all | solution.py:99
  169.1 0.8 copy.71
  169.9 1.3 fusion.36
  171.2 5.1 %all-to-all-done.3 = f32[4,121,192]{1,2,0:T(8,128)S(1)} async-done(((f32[4,121,192]{1,2,0:T(8,128)}), f32[4,121,192]{1,2,0:T(8,128)S(1)}, u32[]{:S(2)}, u32[]{:S(2)}) %all-to-all-start.3) | async-done | bytes 371744 | tf_op jit(solution)/shard_map/all_to_all | solution.py:99
  176.3 0.9 copy.72
  177.2 0.7 slice_reduce_fusion
  (75 shorter events, 4.4 us)
Async XLA Ops:
  7.2 11.9 %copy-start.17 = (s32[768]{0:T(1024)S(1)}, s32[768]{0:T(1024)}, u32[]{:S(2)}) copy-start(s32[768]{0:T(1024)} %param.9) | copy-start | bytes 9220
  7.2 11.9 %copy-start.16 = (bf16[1,128,768]{2,1,0:T(8,128)(2,1)S(1)}, bf16[1,128,768]{2,1,0:T(8,128)(2,1)}, u32[]{:S(2)}) copy-start(bf16[1,128,768]{2,1,0:T(8,128)(2,1)} %param.6) | copy-start | bytes 589828
  7.2 55.9 %all-gather.2.cloned.1.call-start = ((), (), s32[]{:S(2)}) async-start(), calls=%async_computation.5 | async-start | bytes 1658880 | tf_op jit(solution)/shard_map/all_gather | solution.py:36
  18.1 2.3 %copy-start.10 = (bf16[1,128,768]{2,1,0:T(8,128)(2,1)S(1)}, bf16[1,128,768]{2,1,0:T(8,128)(2,1)}, u32[]{:S(2)}) copy-start(bf16[1,128,768]{2,1,0:T(8,128)(2,1)} %param.5) | copy-start | bytes 589828
  19.0 142.7 %reduce-scatter.2.cloned.1.call-start = ((), (), s32[]{:S(2)}) async-start(), calls=%async_computation.6 | async-start | bytes 1769472 | tf_op jit(solution)/shard_map/reduce_scatter | solution.py:92
  19.8 0.7 copy-start.8
  40.1 5.0 %collective-permute-start = (bf16[4,1152]{1,0:T(4,128)(2,1)S(1)}, bf16[4,1152]{1,0:T(4,128)(2,1)S(1)}, u32[]{:S(2)}, u32[]{:S(2)}) collective-permute-start(bf16[4,1152]{1,0:T(4,128)(2,1)S(1)} %get-tuple-element.28), channel_id=1, source_target_pairs={{0,8},{8,16},{16,24},{1,9},{9,17},{17,25},{2,10},{10,18},{18,26},{... | collective-permute-start | bytes 27656 | tf_op jit(solution)/shard_map/ppermute | solution.py:13
  43.6 6.0 %collective-permute-start.1 = (bf16[4,1152]{1,0:T(4,128)(2,1)S(1)}, bf16[4,1152]{1,0:T(4,128)(2,1)S(1)}, u32[]{:S(2)}, u32[]{:S(2)}) collective-permute-start(bf16[4,1152]{1,0:T(4,128)(2,1)S(1)} %get-tuple-element.29), channel_id=1, source_target_pairs={{8,0},{16,8},{24,16},{9,1},{17,9},{25,17},{10,2},{18,10},{26,18},{... | collective-permute-start | bytes 27656 | tf_op jit(solution)/shard_map/ppermute | solution.py:14
  45.1 5.9 %copy-start = (f32[768]{0:T(1024)S(1)}, f32[768]{0:T(1024)}, u32[]{:S(2)}) copy-start(f32[768]{0:T(1024)} %param.8) | copy-start | bytes 9220
  71.1 13.0 %copy-start.12 = (bf16[768,5,192]{0,2,1:T(8,128)(2,1)}, bf16[768,5,192]{0,2,1:T(8,128)(2,1)S(1)}, u32[]{:S(2)}) copy-start(bf16[768,5,192]{0,2,1:T(8,128)(2,1)S(1)} %copy.57) | copy-start | bytes 4423684
  74.9 1.9 %copy-start.5 = (f32[516,384]{1,0:T(8,128)S(1)}, f32[516,384]{1,0:T(8,128)}, u32[]{:S(2)}) copy-start(f32[516,384]{1,0:T(8,128)} %convert_multiply_fusion.2) | copy-start | bytes 2377732
  76.8 2.0 %copy-start.1 = (f32[516,192]{1,0:T(8,128)}, f32[516,192]{1,0:T(8,128)S(1)}, u32[]{:S(2)}) copy-start(f32[516,192]{1,0:T(8,128)S(1)} %get-tuple-element.21) | copy-start | bytes 1188868
  76.8 2.0 %copy-start.3 = (f32[516,192]{1,0:T(8,128)}, f32[516,192]{1,0:T(8,128)S(1)}, u32[]{:S(2)}) copy-start(f32[516,192]{1,0:T(8,128)S(1)} %get-tuple-element.25) | copy-start | bytes 1188868
  98.3 3.5 %copy-start.2 = (f32[516,192]{1,0:T(8,128)S(1)}, f32[516,192]{1,0:T(8,128)}, u32[]{:S(2)}) copy-start(f32[516,192]{1,0:T(8,128)} %copy-done.1) | copy-start | bytes 1188868
  98.3 3.5 %copy-start.4 = (f32[516,192]{1,0:T(8,128)S(1)}, f32[516,192]{1,0:T(8,128)}, u32[]{:S(2)}) copy-start(f32[516,192]{1,0:T(8,128)} %copy-done.3) | copy-start | bytes 1188868
  98.3 3.5 %copy-start.6 = (f32[516,192]{1,0:T(8,128)S(1)}, f32[516,192]{1,0:T(8,128)}, u32[]{:S(2)}) copy-start(f32[516,192]{1,0:T(8,128)} %get-tuple-element.20) | copy-start | bytes 1188868
  98.4 3.5 %copy-start.7 = (f32[516,192]{1,0:T(8,128)S(1)}, f32[516,192]{1,0:T(8,128)}, u32[]{:S(2)}) copy-start(f32[516,192]{1,0:T(8,128)} %get-tuple-element.24) | copy-start | bytes 1188868
  101.8 1.4 copy-start.13
  101.8 1.7 copy-start.15
  103.5 2.1 %copy-start.14 = (bf16[768,5,192]{0,2,1:T(8,128)(2,1)S(1)}, bf16[768,5,192]{0,2,1:T(8,128)(2,1)}, u32[]{:S(2)}) copy-start(bf16[768,5,192]{0,2,1:T(8,128)(2,1)} %copy-done.12) | copy-start | bytes 4423684
  112.2 3.7 %copy-start.11 = (bf16[1,128,768]{2,1,0:T(8,128)(2,1)S(1)}, bf16[1,128,768]{2,1,0:T(8,128)(2,1)}, u32[]{:S(2)}) copy-start(bf16[1,128,768]{2,1,0:T(8,128)(2,1)} %param.5) | copy-start | bytes 589828
  112.2 19.5 %all-to-all-start.2 = ((bf16[4,128,1152]{1,2,0:T(8,128)(2,1)}), bf16[4,128,1152]{1,2,0:T(8,128)(2,1)S(1)}, u32[]{:S(2)}, u32[]{:S(2)}) async-start(bf16[4,128,1152]{1,2,0:T(8,128)(2,1)} %copy.58), calls=%async_computation.2 | async-start | bytes 2359296 | tf_op jit(solution)/shard_map/all_to_all | solution.py:109
  115.9 16.3 %copy-start.9 = (bf16[1,128,768]{1,2,0:T(8,128)(2,1)S(1)}, bf16[1,128,768]{1,2,0:T(8,128)(2,1)}, u32[]{:S(2)}) copy-start(bf16[1,128,768]{1,2,0:T(8,128)(2,1)} %copy-done.8) | copy-start | bytes 589828
  165.4 10.9 %all-to-all-start.3 = ((f32[4,121,192]{1,2,0:T(8,128)}), f32[4,121,192]{1,2,0:T(8,128)S(1)}, u32[]{:S(2)}, u32[]{:S(2)}) async-start(f32[4,121,192]{1,2,0:T(8,128)} %pad_maximum_fusion.3), calls=%async_computation.4 | async-start | bytes 786432 | tf_op jit(solution)/shard_map/all_to_all | solution.py:99
Sparse Core Ops, SparseCore 0:
  19.1 43.9 all-gather.1
  98.4 63.1 reduce-scatter.1

commit v2 on v1

v2 whole, which is shorter than its diff:
```python
import jax
import jax.numpy as jnp
from jax import lax
from jax.sharding import Mesh, PartitionSpec as P

epsilon = 1e-06
RANK = ("seq_rank", "dp_rank")
BLOCK = ("seq_block", "dp_block")


def neighbours(block, axis, width, dim):
    count = lax.axis_size(axis)
    forward = [(i, i + 1) for i in range(count - 1)]
    backward = [(target, source) for source, target in forward]
    size = block.shape[dim]
    low = lax.ppermute(lax.slice_in_dim(block, size - width, size, axis=dim), axis, forward)
    high = lax.ppermute(lax.slice_in_dim(block, 0, width, axis=dim), axis, backward)
    return low, high


def gathered_direct(block, axes):
    count = lax.axis_size(axes)
    me = lax.axis_index(axes)
    result = lax.dynamic_update_index_in_dim(
        jnp.zeros((count,) + block.shape, block.dtype), block, me, 0
    )
    for shift in range(1, count):
        other = lax.ppermute(block, axes, [(i, (i + shift) % count) for i in range(count)])
        result = lax.dynamic_update_index_in_dim(result, other, (me + count - shift) % count, 0)
    return result


def gelu_and_slope(preact):
    result, pullback = jax.vjp(jax.nn.gelu, preact)
    return result, pullback(jnp.ones_like(preact))[0]


def per_device(activations, cotangent, weights, norm_gain, pairing):
    seq_ranks = lax.axis_size("seq_rank")
    dp_ranks = lax.axis_size("dp_rank")
    seq_blocks = lax.axis_size("seq_block")
    dp_blocks = lax.axis_size("dp_block")
    ranks = seq_ranks * dp_ranks
    blocks = seq_blocks * dp_blocks
    positions, channels = activations.shape[1:]
    rows = weights.shape[0]
    taps = rows * ranks * blocks // channels
    part = channels // ranks
    half = taps // 2
    reach = 2 * half
    span = positions * seq_ranks
    mine = lax.all_to_all(weights.T.reshape(ranks, part, rows), RANK, 0, 0, tiled=True)
    mine = mine.transpose(1, 0, 2).reshape(part, ranks * rows)
    kernel = gathered_direct(mine, BLOCK)
    kernel = kernel.reshape(seq_blocks, dp_blocks, part, seq_ranks, dp_ranks, rows)
    kernel = kernel.transpose(2, 0, 3, 1, 4, 5).reshape(part, taps, channels)
    kernel = kernel.transpose(1, 0, 2).reshape(taps * part, channels)
    swap = (pairing[None, :] == jnp.arange(channels, dtype=pairing.dtype)[:, None]).astype(jnp.bfloat16)
    values = activations[0]
    cot = cotangent[0]
    cot_swapped = jnp.dot(cot, swap)
    whole = jnp.broadcast_to(values, (ranks, positions, channels))
    slices = [t.reshape(positions, ranks, part).transpose(1, 0, 2) for t in (cot, cot_swapped)]
    message = jnp.concatenate([whole] + slices, -1)
    message = lax.all_to_all(message, RANK, 0, 0, tiled=True)
    message = message.reshape(seq_ranks, dp_ranks, positions, -1).transpose(1, 0, 2, 3)
    message = message.reshape(dp_ranks, span, -1)
    low, high = neighbours(message, "seq_block", reach, 1)
    extended = jnp.concatenate([low, message, high], 1)
    group = extended[:, :, :channels]
    group_swapped = jnp.dot(group, swap)
    group = group.astype(jnp.float32)
    inverse_rms = lax.rsqrt(jnp.mean(group * group, -1, keepdims=True) + epsilon)
    normed = [
        (t.astype(jnp.float32) * inverse_rms * norm_gain).astype(jnp.bfloat16)
        for t in (group, group_swapped)
    ]
    halves = 0.5 * extended[:, half:-half, channels:].astype(jnp.float32)
    wide = span + reach
    gelus, shifted = [], []
    for strand in range(2):
        terms = jnp.einsum("brc,ec->bre", normed[strand], kernel, preferred_element_type=jnp.float32)
        starts = [k if strand == 0 else reach - k for k in range(taps)]
        preact = sum(
            terms[:, starts[k] : starts[k] + wide, k * part : (k + 1) * part] for k in range(taps)
        )
        result, slope = gelu_and_slope(preact)
        gelus.append(result[:, half : half + span].astype(jnp.bfloat16))
        grad_pre = (halves[:, :, strand * part : (strand + 1) * part] * slope).astype(jnp.bfloat16)
        shifted.append(
            jnp.concatenate([grad_pre[:, reach - s : reach - s + span] for s in starts], -1)
        )
    kernel_term = jnp.einsum(
        "sbre,sbrc->ec",
        jnp.stack(shifted),
        jnp.stack([n[:, reach : reach + span] for n in normed]),
        preferred_element_type=jnp.float32,
    )
    gain_term = jnp.sum(kernel_term * kernel.astype(jnp.float32), 0) / norm_gain
    outgoing = kernel_term.astype(jnp.bfloat16).reshape(taps, part, channels).transpose(1, 0, 2)
    outgoing = outgoing.reshape(part, seq_blocks, seq_ranks, dp_blocks, dp_ranks, rows)
    outgoing = outgoing.transpose(1, 3, 0, 2, 4, 5).reshape(blocks, part, ranks * rows)
    own_gain = channels // (ranks * blocks)
    gain_rows = gain_term.reshape(seq_blocks, seq_ranks, dp_blocks, dp_ranks, own_gain)
    gain_rows = gain_rows.transpose(0, 2, 1, 3, 4).reshape(blocks, 1, ranks, own_gain)
    gain_rows = jnp.pad(gain_rows, ((0, 0), (0, 0), (0, 0), (0, rows - own_gain)))
    gain_rows = gain_rows.reshape(blocks, 1, ranks * rows)
    gain_high = gain_rows.astype(jnp.bfloat16)
    gain_low = (gain_rows - gain_high.astype(jnp.float32)).astype(jnp.bfloat16)
    extra = jnp.pad(jnp.concatenate([gain_high, gain_low], 1), ((0, 0), (0, 14), (0, 0)))
    outgoing = jnp.concatenate([outgoing, extra], 1)
    terms = lax.all_to_all(outgoing, BLOCK, 0, 0, tiled=True)
    summed = terms.astype(jnp.float32).sum(0)
    gain_sum = summed[part : part + 1] + summed[part + 1 : part + 2]
    last = jnp.concatenate([summed[:part], jnp.pad(gain_sum, ((0, 7), (0, 0)))], 0)
    last = last.reshape(-1, ranks, rows).transpose(1, 0, 2)
    last = lax.all_to_all(last, RANK, 0, 0, tiled=True)
    grad_kernel = last[:, :part].reshape(channels, rows).T
    grad_gain = last[:, part, :own_gain].sum(0)
    kernel_swapped = jnp.dot(kernel, swap)
    grad_scaled = (
        jnp.einsum("bre,ec->brc", shifted[0], kernel, preferred_element_type=jnp.float32) * norm_gain
        + jnp.einsum("bre,ec->brc", shifted[1], kernel_swapped, preferred_element_type=jnp.float32)
        * norm_gain[pairing]
    )
    back = jnp.concatenate([grad_scaled.astype(jnp.bfloat16)] + gelus, -1)
    back = back.reshape(dp_ranks, seq_ranks, positions, -1).transpose(1, 0, 2, 3)
    back = back.reshape(ranks, positions, -1)
    back = lax.all_to_all(back, RANK, 0, 0, tiled=True)
    scaled = back[:, :, :channels].astype(jnp.float32).sum(0)
    gelu_plain = back[:, :, channels : channels + part].transpose(1, 0, 2).reshape(positions, channels)
    gelu_other = back[:, :, channels + part :].transpose(1, 0, 2).reshape(positions, channels)
    gelu_other = jnp.dot(gelu_other, swap).astype(jnp.float32)
    values = values.astype(jnp.float32)
    cot = cot.astype(jnp.float32)
    own_rms = lax.rsqrt(jnp.mean(values * values, -1, keepdims=True) + epsilon)
    reverse_out = (values + gelu_other).astype(jnp.bfloat16).astype(jnp.float32)
    combined = (0.5 * (values + gelu_plain.astype(jnp.float32) + reverse_out)).astype(jnp.bfloat16)
    grad_input = (
        cot + own_rms * scaled - values * own_rms**3 * jnp.mean(scaled * values, -1, keepdims=True)
    ).astype(jnp.bfloat16)
    return combined[None], grad_input[None], grad_kernel, grad_gain


def solution(mesh):
    seq, dp = mesh.shape["seq"], mesh.shape["dp"]
    seq_ranks, dp_ranks = 4, 2
    grouped = Mesh(
        mesh.devices.reshape(seq // seq_ranks, seq_ranks, dp // dp_ranks, dp_ranks),
        ("seq_block", "seq_rank", "dp_block", "dp_rank"),
    )
    along = P(("dp_block", "dp_rank"), ("seq_block", "seq_rank"), None)
    every = ("seq_block", "seq_rank", "dp_block", "dp_rank")
    return jax.shard_map(
        per_device,
        mesh=grouped,
        in_specs=(along, along, P(every, None), P(), P()),
        out_specs=(along, along, P(every, None), P(every)),
        check_vma=False,
    )
```

time: 185 us -> 157 us (0.85)
  blocking collectives: 27.6 us -> 0 us
  starting transfers between devices: 12.2 us -> 27.7 us
  between operations: 14.5 us -> 1.03 us
  waiting for transfers between devices: 63.6 us -> 50.2 us
  local copies, waits for them, and re-layouts: 38.8 us -> 45.6 us
  other arithmetic: 9.25 us -> 12.4 us
    reduce_scatter x1 -> x0, waiting for transfers between devices: 29.3 us -> none  [per_device(): lax.psum_scatter(outgoing, ('block', 'dp'), scatter_dimension=0, tiled=True)]
    all_to_all x2 -> x0, blocking collectives: 27.6 us -> none  [the longest x1 18.3 us: per_device(): lax.all_to_all(message, 'rank', split_axis=0, concat_axis=0, tiled=True)]
    all_to_all x2 -> x5, waiting for transfers between devices: 20.7 us -> 38.5 us  [the longest x1 22.7 us: per_device(): back = lax.all_to_all(back, RANK, 0, 0, tiled=True)]
    all_to_all x2 -> x5, starting transfers between devices: 7.12 us -> 20.3 us  [the longest x1 5.17 us: per_device(): lax.all_to_all(weights.T.reshape(ranks, part, rows), RANK, 0, 0, tiled=True)]
    all_gather x1 -> x0, waiting for transfers between devices: 8.99 us -> none  [per_device(): gathered = lax.all_gather(packed, ('block', 'dp'), axis=0, tiled=True)]
    ppermute x2 -> x5, waiting for transfers between devices: 4.52 us -> 11.7 us  [the longest x3 9.71 us: gathered_direct(): lax.ppermute(block, axes, [(i, (i + shift) % count) for i in range(count)])]
    broadcast_in_dim x2 -> x5, local copies, waits for them, and re-layouts: 0.19 us -> 5.38 us  [the longest x3 4.42 us: gathered_direct(): lax.dynamic_update_index_in_dim(result, other, (me + count - shift) % cou...]
    dynamic_update_slice x0 -> x4, local copies, waits for them, and re-layouts: none -> 3.92 us  [the longest x3 2.94 us: gathered_direct(): lax.dynamic_update_index_in_dim(result, other, (me + count - shift) % cou...]
  transfers between devices with their start and end apart: 6 -> 10, of which waited for: 5 -> 5; matrix products, arithmetic and copies ran while one was open for 12% -> 22% of each run, Pallas kernels for 0% -> 0%
where the time goes in v2:
time: 157 us; the launch traced here: 156 us
  waiting for transfers between devices  50.2 us (32%)
  local copies, waits for them, and re-layouts  45.6 us (29%)
  starting transfers between devices  27.7 us (18%)
  matrix products  19.4 us (12%)
  other arithmetic  12.4 us (8%)
    all_to_all x1, waiting for transfers between devices, per_device(): back = lax.all_to_all(back, RANK, 0, 0, tiled=True)  22.7 us
    all_to_all x1, waiting for transfers between devices, per_device(): terms = lax.all_to_all(outgoing, BLOCK, 0, 0, tiled=True)  12.5 us
    ppermute x3, waiting for transfers between devices, gathered_direct(): lax.ppermute(block, axes, [(i, (i + shift) % count) for i in range(count)])  9.71 us
    unnamed x31, local copies, waits for them, and re-layouts  9.14 us
    concatenate x2, local copies, waits for them, and re-layouts, per_device(): jnp.concatenate([grad_pre[:, reach - s:reach - s + span] for s in starts]...  6.01 us
    dot_general x1, matrix products, per_device(): jnp.einsum('bre,ec->brc', shifted[1], kernel_swapped, preferred_element_t...  5.36 us
    all_to_all x1, starting transfers between devices, per_device(): lax.all_to_all(weights.T.reshape(ranks, part, rows), RANK, 0, 0, tiled=True)  5.17 us
    dot_general x1, matrix products, per_device(): jnp.einsum('sbre,sbrc->ec', jnp.stack(shifted), jnp.stack([n[:, reach:rea...  4.85 us
  transfers between devices with their start and end apart: 10, of which 5 were waited for; matrix products, arithmetic and copies ran while one was open for 22% of the time, Pallas kernels for 0%

profile of v2, /device:TPU:0, one launch (start us, length us, event | category | flops | bytes accessed | tf_op | source)
XLA Modules:
  0.0 156.2 jit_solution(982009874103989281)
XLA Ops:
  0.6 1.7 %copy.59 = bf16[120,768]{0,1:T(8,128)(2,1)} copy(bf16[120,768]{1,0:T(8,128)(2,1)} %param.7) | data formatting | bytes 368640 | tf_op args[2]
  2.4 5.2 %all-to-all-start.1 = ((bf16[8,96,120]{2,1,0:T(8,128)(2,1)}), bf16[8,96,120]{2,1,0:T(8,128)(2,1)S(1)}, u32[]{:S(2)}, u32[]{:S(2)}) async-start(bf16[8,96,120]{2,1,0:T(8,128)(2,1)} %bitcast.11), calls=%async_computation.1 | async-start | bytes 393216 | tf_op jit(solution)/shard_map/all_to_all | solution.py:52
  7.5 1.1 copy.57
  8.6 1.1 copy.56
  9.7 1.5 fusion.30
  11.4 1.4 pad_maximum_fusion.3
  12.9 4.3 %all-to-all-start = ((bf16[8,128,960]{1,2,0:T(8,128)(2,1)}), bf16[8,128,960]{1,2,0:T(8,128)(2,1)S(1)}, u32[]{:S(2)}, u32[]{:S(2)}) async-start(bf16[8,128,960]{1,2,0:T(8,128)(2,1)} %pad_maximum_fusion.3), calls=%async_computation | async-start | bytes 3932160 | tf_op jit(solution)/shard_map/all_to_all | solution.py:65
  18.2 3.6 %collective-permute-start.4 = (bf16[96,960]{1,0:T(8,128)(2,1)}, bf16[96,960]{1,0:T(8,128)(2,1)}, u32[]{:S(2)}, u32[]{:S(2)}) collective-permute-start(bf16[96,960]{1,0:T(8,128)(2,1)} %reshape.172), channel_id=1, source_target_pairs={{0,24},{8,0},{16,8},{24,16},{1,25},{9,1},{17,9},{25,17},{2,26},{10... | collective-permute-start | bytes 552968 | tf_op jit(solution)/shard_map/ppermute | solution.py:28
  21.8 1.0 collective-permute-start.2
  22.8 3.2 %gather_fusion = f32[768]{0:T(1024)S(1)} fusion(f32[768]{0:T(1024)S(1)} %copy-done, s32[1024]{0:T(1024)S(1)} %pad_clamp_fusion), kind=kCustom, calls=%fused_computation | custom fusion | bytes 9216 | tf_op jit(solution)/shard_map/gather | solution.py:124
  27.0 1.0 constant_dynamic-update-slice_fusion.3
  28.0 1.8 %copy.65 = bf16[1,96,960]{1,2,0:T(8,128)(2,1)} copy(bf16[1,96,960]{2,1,0:T(8,128)(2,1)} %bitcast.16) | data formatting | bytes 368640 | tf_op jit(solution)/shard_map/jit(dynamic_update_index_in_dim)/broadcast_in_dim | solution.py:29
  29.7 9.7 %collective-permute-done.3 = bf16[96,960]{1,0:T(8,128)(2,1)} collective-permute-done((bf16[96,960]{1,0:T(8,128)(2,1)}, bf16[96,960]{1,0:T(8,128)(2,1)}, u32[]{:S(2)}, u32[]{:S(2)}) %collective-permute-start.3) | collective-permute-done | bytes 184352 | tf_op jit(solution)/shard_map/ppermute | solution.py:28
  39.4 1.8 %copy.64 = bf16[1,96,960]{1,2,0:T(8,128)(2,1)} copy(bf16[1,96,960]{2,1,0:T(8,128)(2,1)} %bitcast.15) | data formatting | bytes 368640 | tf_op jit(solution)/shard_map/jit(dynamic_update_index_in_dim)/broadcast_in_dim | solution.py:29
  43.1 1.0 constant_dynamic-update-slice_fusion.1
  44.1 1.3 copy-done.1
  45.4 2.9 %copy.58 = bf16[2,4,128,960]{3,2,1,0:T(8,128)(2,1)S(1)} copy(bf16[2,4,128,960]{2,3,0,1:T(8,128)(2,1)} %bitcast.115) | data formatting | bytes 3932160 | tf_op jit(solution)/shard_map/transpose | solution.py:66
  48.4 1.3 collective-permute-start
  49.6 1.5 collective-permute-start.1
  51.1 1.0 constant_dynamic-update-slice_fusion
  52.1 1.3 copy.66
  53.4 2.0 %collective-permute-done.1 = bf16[2,4,960]{2,1,0:T(4,128)(2,1)S(1)} collective-permute-done((bf16[2,4,960]{2,1,0:T(4,128)(2,1)S(1)}, bf16[2,4,960]{2,1,0:T(4,128)(2,1)S(1)}, u32[]{:S(2)}, u32[]{:S(2)}) %collective-permute-start.1) | collective-permute-done | bytes 15392 | tf_op jit(solution)/shard_map/ppermute | solution.py:17
  57.1 1.0 fusion.63
  58.1 1.7 %multiply_convert_fusion = bf16[2,520,768]{2,1,0:T(8,128)(2,1)S(1)} fusion(f32[768]{0:T(1024)S(1)} %copy-done, f32[2,520]{1,0:T(2,128)S(1)} %add_rsqrt_fusion, s32[768]{0:T(1024)S(1)} %copy-done.10, bf16[2,4,960]{2,1,0:T(4,128)(2,1)S(1)} %collective-permute-done.1, bf16[2,512,960]{2,1,0:T(8,128)(2,1)S(1)} %bitcast.112, ...), kind=kOutput, calls=%fused_computation.6 | convolution fusion | flops 1235410944 | bytes 3604544 | tf_op jit(solution)/shard_map/dot_general | solution.py:71
  59.8 2.5 %slice_bitcast_fusion = (bf16[1,2,512,768]{3,2,1,0:T(8,128)(2,1)}, bf16[1,2,512,768]{3,2,1,0:T(8,128)(2,1)}) fusion(bf16[2,520,768]{2,1,0:T(8,128)(2,1)S(1)} %multiply_convert_fusion, bf16[2,520,768]{2,1,0:T(8,128)(2,1)S(1)} %fusion.2), kind=kLoop, calls=%fused_computation.27 | loop fusion | bytes 6291456 | tf_op jit(solution)/shard_map/stack | solution.py:96
  62.3 1.0 fusion.65
  63.5 1.4 fusion.42
  64.9 1.4 fusion.61
  66.3 3.2 %concatenate.27 = bf16[2,512,480]{2,1,0:T(8,128)(2,1)} concatenate(bf16[2,512,96]{2,1,0:T(8,128)(2,1)} %get-tuple-element.36, bf16[2,512,96]{2,1,0:T(8,128)(2,1)S(1)} %get-tuple-element.35, bf16[2,512,96]{2,1,0:T(8,128)(2,1)S(1)} %get-tuple-element.34, bf16[2,512,96]{2,1,0:T(8,128)(2,1)S(1)} %get-tuple-element.33, bf16[2,512,96]{2,1,0:T(8,128)(2,1)S(1)} %get-tuple-element.32), dimensions={2} | concatenate | bytes 1966080 | tf_op jit(solution)/shard_map/concatenate | solution.py:91
  69.5 2.8 %concatenate.26 = bf16[2,512,480]{2,1,0:T(8,128)(2,1)S(1)} concatenate(bf16[2,512,96]{2,1,0:T(8,128)(2,1)S(1)} %get-tuple-element.48, bf16[2,512,96]{2,1,0:T(8,128)(2,1)} %get-tuple-element.49, bf16[2,512,96]{2,1,0:T(8,128)(2,1)} %get-tuple-element.50, bf16[2,512,96]{2,1,0:T(8,128)(2,1)} %get-tuple-element.51, bf16[2,512,96]{2,1,0:T(8,128)(2,1)} %get-tuple-element.52), dimensions={2} | concatenate | bytes 1966080 | tf_op jit(solution)/shard_map/concatenate | solution.py:91
  72.3 4.9 %fusion.15 = (f32[768]{0:T(1024)S(1)}, bf16[480,768,1,1]{1,0,3,2:T(8,128)(2,1)}) fusion(bf16[5,96,768]{2,1,0:T(8,128)(2,1)S(1)} %copy-done.2, bf16[1,2,512,768]{3,2,1,0:T(8,128)(2,1)} %get-tuple-element.53, bf16[1,2,512,768]{3,2,1,0:T(8,128)(2,1)} %get-tuple-element.54, bf16[1,2,512,480]{3,2,1,0:T(8,128)(2,1)} %bitcast.131, ...), kind=kOutput, calls=%fused_computation.31 | convolution fusion | flops 1513979136 | bytes 6589440 | tf_op jit(solution)/shard_map/sbre,sbrc->ec/dot_general | solution.py:93
  77.4 1.6 copy.76
  79.0 1.3 copy.77
  80.3 2.2 %fusion.34 = bf16[4,112,960]{2,1,0:T(8,128)(2,1)} fusion(bf16[4,2,960]{2,1,0:T(2,128)(2,1)S(1)} %copy.97, bf16[4,96,960]{2,1,0:T(8,128)(2,1)} %copy.77), kind=kLoop, calls=%fused_computation.48 | loop fusion | flops 2580480 | bytes 1612800 | tf_op jit(solution)/shard_map/concatenate | solution.py:111
  82.4 3.7 %all-to-all-start.3 = ((bf16[4,112,960]{2,1,0:T(8,128)(2,1)}), bf16[4,112,960]{2,1,0:T(8,128)(2,1)S(1)}, u32[]{:S(2)}, u32[]{:S(2)}) async-start(bf16[4,112,960]{2,1,0:T(8,128)(2,1)} %fusion.34), calls=%async_computation.3 | async-start | bytes 1835008 | tf_op jit(solution)/shard_map/all_to_all | solution.py:112
  86.2 1.0 add_multiply_fusion.1
  88.1 2.6 %fusion.64 = f32[2,512,768]{2,1,0:T(8,128)} fusion(bf16[2,512,480]{2,1,0:T(8,128)(2,1)S(1)} %concatenate.26, bf16[480,768,1]{1,0,2:T(8,128)(2,1)S(1)} %bitcast.123), kind=kOutput, calls=%fused_computation.114 | convolution fusion | flops 754974720 | bytes 4866048 | tf_op jit(solution)/shard_map/bre,ec->brc/dot_general | solution.py:122
  90.8 5.4 %add_convert_fusion = bf16[2,512,768]{2,1,0:T(8,128)(2,1)} fusion(f32[2,512,768]{2,1,0:T(8,128)} %fusion.64, bf16[2,512,480]{2,1,0:T(8,128)(2,1)} %concatenate.27, f32[768]{0:T(1024)S(1)} %gather_fusion, f32[768]{0:T(1024)S(1)} %copy-done, bf16[480,768]{1,0:T(8,128)(2,1)} %bitcast.120, s32[768]{0:T(1024)S(1)} %copy-done.10), kind=kOutput, calls=%fused_computation.11 | convolution fusion | flops 1324941312 | bytes 6448128 | tf_op jit(solution)/shard_map/bre,ec->brc/dot_general | solution.py:123
  96.1 12.5 %all-to-all-done.3 = bf16[4,112,960]{2,1,0:T(8,128)(2,1)S(1)} async-done(((bf16[4,112,960]{2,1,0:T(8,128)(2,1)}), bf16[4,112,960]{2,1,0:T(8,128)(2,1)S(1)}, u32[]{:S(2)}, u32[]{:S(2)}) %all-to-all-start.3) | async-done | bytes 860192 | tf_op jit(solution)/shard_map/all_to_all | solution.py:112
  109.3 1.0 copy.95
  110.3 1.2 add.160
  112.7 3.5 %all-to-all-start.4 = ((f32[8,104,120]{2,1,0:T(8,128)}), f32[8,104,120]{2,1,0:T(8,128)S(1)}, u32[]{:S(2)}, u32[]{:S(2)}) async-start(f32[8,104,120]{2,1,0:T(8,128)} %copy.81), calls=%async_computation.4 | async-start | bytes 851968 | tf_op jit(solution)/shard_map/all_to_all | solution.py:117
  116.4 1.2 copy-done.7
  118.0 2.5 %copy.69 = bf16[2,4,128,960]{2,3,0,1:T(8,128)(2,1)} copy(bf16[2,4,128,960]{3,2,1,0:T(8,128)(2,1)S(1)} %bitcast.114) | data formatting | bytes 3932160 | tf_op jit(solution)/shard_map/reshape | solution.py:127
  120.5 3.3 %all-to-all-done.4 = f32[8,104,120]{2,1,0:T(8,128)S(1)} async-done(((f32[8,104,120]{2,1,0:T(8,128)}), f32[8,104,120]{2,1,0:T(8,128)S(1)}, u32[]{:S(2)}, u32[]{:S(2)}) %all-to-all-start.4) | async-done | bytes 399392 | tf_op jit(solution)/shard_map/all_to_all | solution.py:117
  123.8 3.6 %all-to-all-start.2 = ((bf16[8,128,960]{1,2,0:T(8,128)(2,1)}), bf16[8,128,960]{1,2,0:T(8,128)(2,1)S(1)}, u32[]{:S(2)}, u32[]{:S(2)}) async-start(bf16[8,128,960]{1,2,0:T(8,128)(2,1)} %bitcast.116), calls=%async_computation.2 | async-start | bytes 3932160 | tf_op jit(solution)/shard_map/all_to_all | solution.py:129
  129.1 22.7 %all-to-all-done.2 = bf16[8,128,960]{1,2,0:T(8,128)(2,1)S(1)} async-done(((bf16[8,128,960]{1,2,0:T(8,128)(2,1)}), bf16[8,128,960]{1,2,0:T(8,128)(2,1)S(1)}, u32[]{:S(2)}, u32[]{:S(2)}) %all-to-all-start.2) | async-done | bytes 1966112 | tf_op jit(solution)/shard_map/all_to_all | solution.py:129
  154.9 1.3 fusion.33
  (70 shorter events, 14.2 us)
Async XLA Ops:
  2.4 10.5 %all-to-all-start.1 = ((bf16[8,96,120]{2,1,0:T(8,128)(2,1)}), bf16[8,96,120]{2,1,0:T(8,128)(2,1)S(1)}, u32[]{:S(2)}, u32[]{:S(2)}) async-start(bf16[8,96,120]{2,1,0:T(8,128)(2,1)} %bitcast.11), calls=%async_computation.1 | async-start | bytes 393216 | tf_op jit(solution)/shard_map/all_to_all | solution.py:52
  12.9 4.3 %copy-start.10 = (s32[768]{0:T(1024)S(1)}, s32[768]{0:T(1024)}, u32[]{:S(2)}) copy-start(s32[768]{0:T(1024)} %param.9) | copy-start | bytes 9220
  12.9 9.9 %copy-start = (f32[768]{0:T(1024)S(1)}, f32[768]{0:T(1024)}, u32[]{:S(2)}) copy-start(f32[768]{0:T(1024)} %param.8) | copy-start | bytes 9220
  12.9 31.2 %all-to-all-start = ((bf16[8,128,960]{1,2,0:T(8,128)(2,1)}), bf16[8,128,960]{1,2,0:T(8,128)(2,1)S(1)}, u32[]{:S(2)}, u32[]{:S(2)}) async-start(bf16[8,128,960]{1,2,0:T(8,128)(2,1)} %pad_maximum_fusion.3), calls=%async_computation | async-start | bytes 3932160 | tf_op jit(solution)/shard_map/all_to_all | solution.py:65
  18.2 9.8 %collective-permute-start.4 = (bf16[96,960]{1,0:T(8,128)(2,1)}, bf16[96,960]{1,0:T(8,128)(2,1)}, u32[]{:S(2)}, u32[]{:S(2)}) collective-permute-start(bf16[96,960]{1,0:T(8,128)(2,1)} %reshape.172), channel_id=1, source_target_pairs={{0,24},{8,0},{16,8},{24,16},{1,25},{9,1},{17,9},{25,17},{2,26},{10... | collective-permute-start | bytes 552968 | tf_op jit(solution)/shard_map/ppermute | solution.py:28
  21.8 17.7 %collective-permute-start.3 = (bf16[96,960]{1,0:T(8,128)(2,1)}, bf16[96,960]{1,0:T(8,128)(2,1)}, u32[]{:S(2)}, u32[]{:S(2)}) collective-permute-start(bf16[96,960]{1,0:T(8,128)(2,1)} %reshape.172), channel_id=1, source_target_pairs={{0,16},{8,24},{16,0},{24,8},{1,17},{9,25},{17,1},{25,9},{2,18},{10... | collective-permute-start | bytes 552968 | tf_op jit(solution)/shard_map/ppermute | solution.py:28
  21.8 19.5 %collective-permute-start.2 = (bf16[96,960]{1,0:T(8,128)(2,1)}, bf16[96,960]{1,0:T(8,128)(2,1)S(1)}, u32[]{:S(2)}, u32[]{:S(2)}) collective-permute-start(bf16[96,960]{1,0:T(8,128)(2,1)} %reshape.172), channel_id=1, source_target_pairs={{0,8},{8,16},{16,24},{24,0},{1,9},{9,17},{17,25},{25,1},{2,10},{10... | collective-permute-start | bytes 552968 | tf_op jit(solution)/shard_map/ppermute | solution.py:28
  44.1 1.3 copy-start.1
  48.4 5.0 %collective-permute-start = (bf16[2,4,960]{2,1,0:T(4,128)(2,1)S(1)}, bf16[2,4,960]{2,1,0:T(4,128)(2,1)S(1)}, u32[]{:S(2)}, u32[]{:S(2)}) collective-permute-start(bf16[2,4,960]{2,1,0:T(4,128)(2,1)S(1)} %get-tuple-element.24), channel_id=1, source_target_pairs={{0,8},{8,16},{16,24},{1,9},{9,17},{17,25},{2,10},{10,18},{18,26},{... | collective-permute-start | bytes 46088 | tf_op jit(solution)/shard_map/ppermute | solution.py:16
  49.6 5.7 %collective-permute-start.1 = (bf16[2,4,960]{2,1,0:T(4,128)(2,1)S(1)}, bf16[2,4,960]{2,1,0:T(4,128)(2,1)S(1)}, u32[]{:S(2)}, u32[]{:S(2)}) collective-permute-start(bf16[2,4,960]{2,1,0:T(4,128)(2,1)S(1)} %get-tuple-element.25), channel_id=1, source_target_pairs={{8,0},{16,8},{24,16},{9,1},{17,9},{25,17},{10,2},{18,10},{26,18},{... | collective-permute-start | bytes 46088 | tf_op jit(solution)/shard_map/ppermute | solution.py:17
  56.0 1.1 copy-start.2
  82.4 26.2 %all-to-all-start.3 = ((bf16[4,112,960]{2,1,0:T(8,128)(2,1)}), bf16[4,112,960]{2,1,0:T(8,128)(2,1)S(1)}, u32[]{:S(2)}, u32[]{:S(2)}) async-start(bf16[4,112,960]{2,1,0:T(8,128)(2,1)} %fusion.34), calls=%async_computation.3 | async-start | bytes 1835008 | tf_op jit(solution)/shard_map/all_to_all | solution.py:112
  86.2 2.0 %copy-start.3 = (bf16[5,96,768]{2,1,0:T(8,128)(2,1)S(1)}, bf16[5,96,768]{2,1,0:T(8,128)(2,1)}, u32[]{:S(2)}) copy-start(bf16[5,96,768]{2,1,0:T(8,128)(2,1)} %copy.66) | copy-start | bytes 2211844
  110.3 5.8 %copy-start.4 = (f32[2,516,96]{2,1,0:T(8,128)S(1)}, f32[2,516,96]{2,1,0:T(8,128)}, u32[]{:S(2)}) copy-start(f32[2,516,96]{2,1,0:T(8,128)} %add_multiply_fusion.1) | copy-start | bytes 1188868
  110.3 5.8 %copy-start.5 = (f32[2,516,96]{2,1,0:T(8,128)S(1)}, f32[2,516,96]{2,1,0:T(8,128)}, u32[]{:S(2)}) copy-start(f32[2,516,96]{2,1,0:T(8,128)} %add_multiply_fusion) | copy-start | bytes 1188868
  112.7 11.2 %all-to-all-start.4 = ((f32[8,104,120]{2,1,0:T(8,128)}), f32[8,104,120]{2,1,0:T(8,128)S(1)}, u32[]{:S(2)}, u32[]{:S(2)}) async-start(f32[8,104,120]{2,1,0:T(8,128)} %copy.81), calls=%async_computation.4 | async-start | bytes 851968 | tf_op jit(solution)/shard_map/all_to_all | solution.py:117
  116.1 1.4 copy-start.7
  120.5 6.9 %copy-start.6 = (bf16[1,128,768]{2,1,0:T(8,128)(2,1)S(1)}, bf16[1,128,768]{2,1,0:T(8,128)(2,1)}, u32[]{:S(2)}) copy-start(bf16[1,128,768]{2,1,0:T(8,128)(2,1)} %param.5) | copy-start | bytes 589828
  123.8 27.9 %all-to-all-start.2 = ((bf16[8,128,960]{1,2,0:T(8,128)(2,1)}), bf16[8,128,960]{1,2,0:T(8,128)(2,1)S(1)}, u32[]{:S(2)}, u32[]{:S(2)}) async-start(bf16[8,128,960]{1,2,0:T(8,128)(2,1)} %bitcast.116), calls=%async_computation.2 | async-start | bytes 3932160 | tf_op jit(solution)/shard_map/all_to_all | solution.py:129
  153.6 1.3 copy-start.8
  153.6 1.3 copy-start.9

commit v3 on v2

v3 whole, which is shorter than its diff:
```python
import jax
import jax.numpy as jnp
from jax import lax
from jax.experimental import pallas as pl
from jax.experimental.pallas import tpu as pltpu
from jax.sharding import Mesh, PartitionSpec as P

epsilon = 1e-06
RANK = ("seq_rank", "dp_rank")
BLOCK = ("seq_block", "dp_block")
EVERY = ("seq_block", "seq_rank", "dp_block", "dp_rank")
LANES = 128
HALO = 16
EXTRA = 16
VMEM = pl.BlockSpec(memory_space=pltpu.VMEM)
SMEM = pl.BlockSpec(memory_space=pltpu.SMEM)
bf16 = jnp.bfloat16
f32 = jnp.float32


def called(body, outs, args, scratch=(), specs=None, flops=0, moved=0):
    return pl.pallas_call(
        body,
        out_shape=outs,
        in_specs=specs or [VMEM] * len(args),
        out_specs=jax.tree.map(lambda _: VMEM, outs),
        scratch_shapes=list(scratch),
        compiler_params=pltpu.CompilerParams(vmem_limit_bytes=50 * 2**20),
        cost_estimate=pl.CostEstimate(flops=flops, bytes_accessed=moved, transcendentals=0),
    )(*args)


def shape_of(shape, dtype):
    return jax.ShapeDtypeStruct(shape, dtype)


def dot(a, b, contract):
    return lax.dot_general(a, b, (contract, ((), ())), preferred_element_type=f32)


def gelu_and_slope(x):
    inner = 0.7978845608028654 * (x + 0.044715 * (x * x * x))
    bend = jnp.tanh(inner)
    half_sum = 0.5 * (1.0 + bend)
    slope = half_sum + (0.5 * x) * (1.0 - bend * bend) * (
        0.7978845608028654 * (1.0 + 0.134145 * (x * x))
    )
    return x * half_sum, slope


def pack_message(values_ref, cot_ref, plain_ref, other_ref, message_ref):
    ranks = message_ref.shape[0]
    channels = values_ref.shape[1]
    cot = cot_ref[...]
    pieces = [dot(cot, ref[...], ((1,), (0,))).astype(bf16) for ref in (plain_ref, other_ref)]
    for j in range(ranks):
        message_ref[j, :, :channels] = values_ref[...]
        for n, piece in enumerate(pieces):
            start = channels + n * LANES
            message_ref[j, :, start : start + LANES] = piece[:, j * LANES : (j + 1) * LANES]


def prepare(message_ref, low_ref, high_ref, gain_ref, swap_ref, normed_ref, grads_ref):
    dp_ranks = low_ref.shape[0]
    ranks, positions = message_ref.shape[:2]
    channels = gain_ref.shape[1]

    def put(block, b, start):
        count = block.shape[0]
        x = block[:, :channels]
        other = dot(x, swap_ref[...], ((1,), (0,)))
        x = x.astype(f32)
        rms = lax.rsqrt(jnp.mean(x * x, -1, keepdims=True) + epsilon)
        normed_ref[b, pl.ds(start, count), :] = (x * rms * gain_ref[...]).astype(bf16)
        normed_ref[dp_ranks + b, pl.ds(start, count), :] = (other * rms * gain_ref[...]).astype(bf16)
        for n in range(2):
            lane = channels + n * LANES
            grads_ref[n * dp_ranks + b, pl.ds(start, count), :] = 0.5 * block[:, lane : lane + LANES].astype(f32)

    for b in range(dp_ranks):
        put(low_ref[b], b, 0)
        for i in range(ranks // dp_ranks):
            put(message_ref[i * dp_ranks + b], b, HALO + i * positions)
        put(high_ref[b], b, HALO + (ranks // dp_ranks) * positions)


def main_body(sizes, me_ref, own_ref, *refs):
    seq_blocks, dp_blocks, seq_ranks, dp_ranks = sizes
    blocks = seq_blocks * dp_blocks
    others = refs[: blocks - 1]
    normed_ref, grads_ref, gain_ref = refs[blocks - 1 : blocks + 2]
    shifted_ref, kernel_ref, gelu_ref, out_ref = refs[blocks + 2 : blocks + 6]
    pieces, terms, bent, slopes, total = refs[blocks + 6 :]
    part, rows = own_ref.shape[1:]
    strands, long, channels = normed_ref.shape
    taps = kernel_ref.shape[0] // LANES
    half = taps // 2
    reach = 2 * half
    span = long - 2 * HALO
    wide = bent.shape[0]
    me = me_ref[0]
    pieces[me] = own_ref[...]
    for shift in range(1, blocks):
        pieces[lax.rem(me + blocks - shift, blocks)] = others[shift - 1][...]
    kernel_ref[...] = jnp.zeros_like(kernel_ref)
    owners = [
        (sb * dp_blocks + db, sr * dp_ranks + dr)
        for sb in range(seq_blocks)
        for sr in range(seq_ranks)
        for db in range(dp_blocks)
        for dr in range(dp_ranks)
    ]

    def runs(owner):
        first, last = owner * rows, (owner + 1) * rows
        while first < last:
            tap, channel = divmod(first, channels)
            count = min(last - first, channels - channel)
            yield tap, channel, count, first - owner * rows
            first += count

    for owner, (block, rank) in enumerate(owners):
        for tap, channel, count, offset in runs(owner):
            kernel_ref[tap * LANES : tap * LANES + part, channel : channel + count] = pieces[
                block, rank, :, offset : offset + count
            ]
    for strand in range(strands):
        terms[...] = dot(normed_ref[strand], kernel_ref[...], ((1,), (1,)))
        forward = strand < dp_ranks
        preact = jnp.zeros((wide, LANES), f32)
        for k in range(taps):
            start = HALO - reach + k if forward else HALO - k
            preact += terms[start : start + wide, k * LANES : (k + 1) * LANES]
        result, slope = gelu_and_slope(preact)
        bent[...] = result
        gelu_ref[strand] = bent[half : half + span, :].astype(bf16)
        slopes[...] = grads_ref[strand, HALO - half : HALO - half + wide, :] * slope
        edge = jnp.zeros((HALO, taps * LANES), bf16)
        shifted_ref[strand, :HALO, :] = edge
        shifted_ref[strand, HALO + span :, :] = edge
        for k in range(taps):
            start = reach - k if forward else k
            shifted_ref[strand, HALO : HALO + span, k * LANES : (k + 1) * LANES] = slopes[
                start : start + span, :
            ].astype(bf16)
    total[...] = dot(
        shifted_ref[...].reshape(strands * long, taps * LANES),
        normed_ref[...].reshape(strands * long, channels),
        ((0,), (0,)),
    )
    gain = jnp.sum(total[...] * kernel_ref[...].astype(f32), 0, keepdims=True) / gain_ref[...]
    gain_high = gain.astype(bf16).astype(f32)
    row = lax.broadcasted_iota(jnp.int32, (EXTRA, channels), 0)
    extra = jnp.where(row == 0, gain_high, jnp.where(row == 1, gain - gain_high, 0.0))
    own_gain = channels // len(owners)
    for owner in range(len(owners)):
        for tap, channel, count, offset in runs(owner):
            out_ref[owner, :part, offset : offset + count] = total[
                tap * LANES : tap * LANES + part, channel : channel + count
            ].astype(bf16)
        out_ref[owner, part:, :] = jnp.zeros((EXTRA, rows), bf16)
        out_ref[owner, part:, :own_gain] = extra[
            :, owner * own_gain : (owner + 1) * own_gain
        ].astype(bf16)


def input_gradient(rank_ref, shifted_ref, kernel_ref, swap_ref, gain_ref, swapped_gain_ref, gelu_ref, *refs):
    outs, scaled = refs[:-1], refs[-1]
    ranks = len(outs)
    strands, long, _ = shifted_ref.shape
    dp_ranks = strands // 2
    span = long - 2 * HALO
    positions = outs[0].shape[0]
    channels = gain_ref.shape[1]
    kernel = kernel_ref[...]
    swapped = dot(kernel, swap_ref[...], ((1,), (0,))).astype(bf16)
    for b in range(dp_ranks):
        scaled[b] = (
            dot(shifted_ref[b, HALO : HALO + span, :], kernel, ((1,), (0,))) * gain_ref[...]
            + dot(shifted_ref[dp_ranks + b, HALO : HALO + span, :], swapped, ((1,), (0,)))
            * swapped_gain_ref[...]
        ).astype(bf16)
    for shift in range(ranks):
        target = lax.bitwise_xor(rank_ref[0], shift)
        b = lax.rem(target, dp_ranks)
        start = pl.multiple_of(lax.div(target, dp_ranks) * positions, positions)
        outs[shift][:, :channels] = scaled[b, pl.ds(start, positions), :]
        for n in range(2):
            lane = channels + n * LANES
            outs[shift][:, lane : lane + LANES] = gelu_ref[n * dp_ranks + b, pl.ds(start, positions), :]


def finish(rank_ref, values_ref, cot_ref, plain_ref, other_ref, *refs):
    blocks, (combined_ref, grad_ref, gelus) = refs[:-3], refs[-3:]
    channels = values_ref.shape[1]
    scaled = jnp.zeros(values_ref.shape, f32)
    for shift, block in enumerate(blocks):
        source = lax.bitwise_xor(rank_ref[0], shift)
        scaled += block[:, :channels].astype(f32)
        for n in range(2):
            lane = channels + n * LANES
            gelus[n, source] = block[:, lane : lane + LANES]
    plain = jnp.zeros(values_ref.shape, f32)
    other = jnp.zeros(values_ref.shape, f32)
    joined = [jnp.concatenate([gelus[n, j] for j in range(len(blocks))], -1) for n in range(2)]
    plain = dot(joined[0], plain_ref[...], ((1,), (1,)))
    other = dot(joined[1], other_ref[...], ((1,), (1,)))
    values = values_ref[...].astype(f32)
    rms = lax.rsqrt(jnp.mean(values * values, -1, keepdims=True) + epsilon)
    reverse_out = (values + other).astype(bf16).astype(f32)
    combined_ref[...] = (0.5 * (values + plain + reverse_out)).astype(bf16)
    along = jnp.mean(scaled * values, -1, keepdims=True)
    grad_ref[...] = (cot_ref[...].astype(f32) + rms * scaled - values * (rms * rms * rms * along)).astype(bf16)


def shifted_pairs(count, shift):
    return [(i, (i + shift) % count) for i in range(count)]


def flipped_pairs(count, mask):
    return [(i, i ^ mask) for i in range(count)]


def per_device(activations, cotangent, weights, norm_gain, pairing):
    seq_ranks = lax.axis_size("seq_rank")
    dp_ranks = lax.axis_size("dp_rank")
    seq_blocks = lax.axis_size("seq_block")
    dp_blocks = lax.axis_size("dp_block")
    ranks = seq_ranks * dp_ranks
    blocks = seq_blocks * dp_blocks
    owners = ranks * blocks
    positions, channels = activations.shape[1:]
    rows = weights.shape[0]
    taps = rows * owners // channels
    part = channels // ranks
    span = positions * seq_ranks
    long = span + 2 * HALO
    reach = taps - taps % 2
    wide = -(-(span + reach) // 8) * 8
    strands = 2 * dp_ranks
    width = channels + 2 * LANES
    me = lax.axis_index(BLOCK).reshape(1)
    rank = lax.axis_index(RANK).reshape(1)
    values, cot = activations[0], cotangent[0]
    mine = lax.all_to_all(weights.T.reshape(ranks, part, rows), RANK, 0, 0, tiled=True)
    other_kernels = [
        lax.ppermute(mine, BLOCK, shifted_pairs(blocks, shift)) for shift in range(1, blocks)
    ]
    slot = jnp.arange(ranks * LANES)
    inside = slot % LANES < part
    channel_of = jnp.where(inside, slot // LANES * part + slot % LANES, 0).astype(jnp.int32)
    channel_list = jnp.arange(channels, dtype=jnp.int32)[:, None]
    plain_map = ((channel_list == channel_of) & inside).astype(bf16)
    other_map = ((channel_list == pairing[channel_of]) & inside).astype(bf16)
    swap = (channel_list == pairing).astype(bf16)
    gain = norm_gain.reshape(1, channels)
    swapped_gain = norm_gain[pairing].reshape(1, channels)
    message = called(
        pack_message,
        shape_of((ranks, positions, width), bf16),
        (values, cot, plain_map, other_map),
    )
    message = lax.all_to_all(message, RANK, 0, 0, tiled=True)
    by_seq = message.reshape(seq_ranks, dp_ranks, positions, width)
    forward = [(i, i + 1) for i in range(seq_blocks - 1)]
    backward = [(target, source) for source, target in forward]
    low = lax.ppermute(by_seq[-1, :, -HALO:], "seq_block", forward)
    high = lax.ppermute(by_seq[0, :, :HALO], "seq_block", backward)
    normed, grads = called(
        prepare,
        (shape_of((strands, long, channels), bf16), shape_of((strands, long, LANES), f32)),
        (message, low, high, gain, swap),
    )
    main_args = (me, mine, *other_kernels, normed, grads, gain)
    sizes = (seq_blocks, dp_blocks, seq_ranks, dp_ranks)
    shifted, kernel, gelus, outgoing = called(
        lambda *refs: main_body(sizes, *refs),
        (
            shape_of((strands, long, taps * LANES), bf16),
            shape_of((taps * LANES, channels), bf16),
            shape_of((strands, span, LANES), bf16),
            shape_of((owners, part + EXTRA, rows), bf16),
        ),
        main_args,
        scratch=[
            pltpu.VMEM((blocks, ranks, part, rows), bf16),
            pltpu.VMEM((long, taps * LANES), f32),
            pltpu.VMEM((wide, LANES), f32),
            pltpu.VMEM((wide, LANES), f32),
            pltpu.VMEM((taps * LANES, channels), f32),
        ],
        specs=[SMEM] + [VMEM] * (len(main_args) - 1),
        flops=4 * strands * long * taps * LANES * channels,
    )
    terms = lax.all_to_all(outgoing, EVERY, 0, 0, tiled=True)
    back = called(
        input_gradient,
        tuple(shape_of((positions, width), bf16) for _ in range(ranks)),
        (rank, shifted, kernel, swap, gain, swapped_gain, gelus),
        scratch=[pltpu.VMEM((dp_ranks, span, channels), bf16)],
        specs=[SMEM] + [VMEM] * 6,
        flops=2 * strands * span * taps * LANES * channels,
    )
    returned = [back[0]] + [
        lax.ppermute(back[mask], RANK, flipped_pairs(ranks, mask)) for mask in range(1, ranks)
    ]
    combined, grad_input = called(
        finish,
        (shape_of((positions, channels), bf16), shape_of((positions, channels), bf16)),
        (rank, values, cot, plain_map, other_map, *returned),
        scratch=[pltpu.VMEM((2, ranks, positions, LANES), bf16)],
        specs=[SMEM] + [VMEM] * (4 + ranks),
    )
    summed = terms.reshape(seq_blocks, seq_ranks, dp_blocks, dp_ranks, -1, rows).astype(f32).sum((0, 2))
    summed = summed.reshape(ranks, -1, rows)
    grad_kernel = summed[:, :part].reshape(channels, rows).T
    grad_gain = summed[:, part : part + 2, : channels // owners].sum((0, 1))
    return combined[None], grad_input[None], grad_kernel, grad_gain


def solution(mesh):
    seq, dp = mesh.shape["seq"], mesh.shape["dp"]
    seq_ranks, dp_ranks = 4, 2
    grouped = Mesh(mesh.devices.reshape(seq // seq_ranks, seq_ranks, dp // dp_ranks, dp_ranks), EVERY)
    along = P(("dp_block", "dp_rank"), ("seq_block", "seq_rank"), None)
    return jax.shard_map(
        per_device,
        mesh=grouped,
        in_specs=(along, along, P(EVERY, None), P(), P()),
        out_specs=(along, along, P(EVERY, None), P(EVERY)),
        check_vma=False,
    )
```

time: 157 us -> 126 us (0.80)
  local copies, waits for them, and re-layouts: 45.6 us -> 16.8 us
  Pallas kernels: 0 us -> 26.9 us
  matrix products: 19.4 us -> 0 us
  other arithmetic: 12.4 us -> 2.44 us
  starting transfers between devices: 27.7 us -> 33.1 us
  waiting for transfers between devices: 50.2 us -> 45.5 us
    all_to_all x3 -> x1, waiting for transfers between devices: 38.5 us -> 0.01 us  [per_device(): terms = lax.all_to_all(outgoing, EVERY, 0, 0, tiled=True)]
    pallas_call x0 -> x5, Pallas kernels: none -> 26.9 us  [called(): pl.pallas_call(body, out_shape=outs, in_specs=specs or [VMEM] * len(args)...]
    all_to_all x1, waiting for transfers between devices: 0.01 us -> 19.9 us  [per_device(): message = lax.all_to_all(message, RANK, 0, 0, tiled=True)]
    dot_general x7 -> x0, matrix products: 17.9 us -> none  [the longest x1 5.36 us: per_device(): jnp.einsum('bre,ec->brc', shifted[1], kernel_swapped, preferred_element_t...]
    ppermute x5 -> x12, waiting for transfers between devices: 11.7 us -> 25.6 us  [the longest x7 21.2 us: per_device(): lax.ppermute(back[mask], RANK, flipped_pairs(ranks, mask))]
    ppermute x5 -> x12, starting transfers between devices: 7.38 us -> 19.4 us  [the longest x7 8.46 us: per_device(): lax.ppermute(back[mask], RANK, flipped_pairs(ranks, mask))]
    all_to_all x3 -> x1, starting transfers between devices: 10.8 us -> 4.03 us  [per_device(): terms = lax.all_to_all(outgoing, EVERY, 0, 0, tiled=True)]
    reshape x5 -> x2, local copies, waits for them, and re-layouts: 6.32 us -> 0.01 us  [the longest x1 0.01 us: per_device(): gain = norm_gain.reshape(1, channels)]
  transfers between devices with their start and end apart: 10 -> 15, of which waited for: 5 -> 6; matrix products, arithmetic and copies ran while one was open for 22% -> 9% of each run, Pallas kernels for 0% -> 13%
where the time goes in v3:
time: 126 us
  waiting for transfers between devices  45.5 us (36%)
  starting transfers between devices  33.1 us (26%)
  Pallas kernels  26.9 us (21%)
  local copies, waits for them, and re-layouts  16.8 us (13%)
  other arithmetic  2.44 us (2%)
    pallas_call x5, Pallas kernels, called(): pl.pallas_call(body, out_shape=outs, in_specs=specs or [VMEM] * len(args)...  26.9 us
    ppermute x7, waiting for transfers between devices, per_device(): lax.ppermute(back[mask], RANK, flipped_pairs(ranks, mask))  21.2 us
    all_to_all x1, waiting for transfers between devices, per_device(): message = lax.all_to_all(message, RANK, 0, 0, tiled=True)  19.9 us
    ppermute x7, starting transfers between devices, per_device(): lax.ppermute(back[mask], RANK, flipped_pairs(ranks, mask))  8.46 us
    ppermute x3, starting transfers between devices, per_device(): lax.ppermute(mine, BLOCK, shifted_pairs(blocks, shift))  5.89 us
    unnamed x25, local copies, waits for them, and re-layouts  5.84 us
    all_to_all x1, starting transfers between devices, per_device(): lax.all_to_all(weights.T.reshape(ranks, part, rows), RANK, 0, 0, tiled=True)  5.17 us
    gather x1, local copies, waits for them, and re-layouts, per_device(): other_map = ((channel_list == pairing[channel_of]) & inside).astype(bf16)  4.53 us
  transfers between devices with their start and end apart: 15, of which 6 were waited for; matrix products, arithmetic and copies ran while one was open for 9% of the time, Pallas kernels for 13%

profile of v3, /device:TPU:0, one launch (start us, length us, event | category | flops | bytes accessed | tf_op | source)
XLA Modules:
  0.0 125.7 jit_solution(4809989427870865281)
XLA Ops:
  0.6 1.7 %copy.10 = bf16[768,120]{1,0:T(8,128)(2,1)} copy(bf16[768,120]{0,1:T(8,128)(2,1)} %bitcast.28) | data formatting | bytes 368640 | tf_op jit(solution)/shard_map/transpose | solution.py:245
  2.4 5.2 %all-to-all-start = ((bf16[8,96,120]{2,1,0:T(8,128)(2,1)}), bf16[8,96,120]{2,1,0:T(8,128)(2,1)}, u32[]{:S(2)}, u32[]{:S(2)}) async-start(bf16[8,96,120]{2,1,0:T(8,128)(2,1)} %bitcast.6), calls=%async_computation | async-start | bytes 393216 | tf_op jit(solution)/shard_map/all_to_all | solution.py:245
  7.6 4.5 %gather_fusion = s32[1024]{0:T(1024)S(1)} fusion(s32[768]{0:T(1024)S(1)} %copy-done.10, s32[1024]{0:T(1024)S(1)} %broadcast_clamp_fusion), kind=kCustom, calls=%fused_computation | custom fusion | bytes 12288 | tf_op jit(solution)/shard_map/gather | solution.py:254
  12.2 0.0 copy-start.3
  12.2 0.0 copy-start.4
  12.2 1.3 fusion.3
  13.5 2.0 %shard_map.84 = bf16[8,128,1024]{2,1,0:T(8,128)(2,1)} custom-call(bf16[128,768]{1,0:T(8,128)(2,1)S(1)} %bitcast.20, bf16[128,768]{1,0:T(8,128)(2,1)S(1)} %bitcast.22, bf16[768,1024]{1,0:T(8,128)(2,1)S(1)} %get-tuple-element.43.plain_ref, bf16[768,1024]{1,0:T(8,128)(2,1)S(1)} %get-tuple-element.42.other_ref), custom_call_target="tpu_custom_call" | custom-call | tf_op jit(solution)/shard_map/pallas_call | solution.py:22
  15.5 0.0 all-to-all-done.refs_1_
  15.5 4.5 %all-to-all-start.1 = ((bf16[8,128,1024]{2,1,0:T(8,128)(2,1)}), bf16[8,128,1024]{2,1,0:T(8,128)(2,1)}, u32[]{:S(2)}, u32[]{:S(2)}) async-start(bf16[8,128,1024]{2,1,0:T(8,128)(2,1)} %shard_map.84), calls=%async_computation.1 | async-start | bytes 4194304 | tf_op jit(solution)/shard_map/all_to_all | solution.py:263
  20.0 1.9 %collective-permute-start = (bf16[8,96,120]{2,1,0:T(8,128)(2,1)}, bf16[8,96,120]{2,1,0:T(8,128)(2,1)S(1)}, u32[]{:S(2)}, u32[]{:S(2)}) collective-permute-start(bf16[8,96,120]{2,1,0:T(8,128)(2,1)} %all-to-all-done.refs_1_), channel_id=1, source_target_pairs={{0,8},{8,16},{16,24},{24,0},{1,9},{9,17},{17,25},{25,1},{2,10},{10... | collective-permute-start | bytes 552968 | tf_op jit(solution)/shard_map/ppermute | solution.py:247
  21.9 2.6 %collective-permute-start.1 = (bf16[8,96,120]{2,1,0:T(8,128)(2,1)}, bf16[8,96,120]{2,1,0:T(8,128)(2,1)}, u32[]{:S(2)}, u32[]{:S(2)}) collective-permute-start(bf16[8,96,120]{2,1,0:T(8,128)(2,1)} %all-to-all-done.refs_1_), channel_id=1, source_target_pairs={{0,16},{8,24},{16,0},{24,8},{1,17},{9,25},{17,1},{25,9},{2,18},{10... | collective-permute-start | bytes 552968 | tf_op jit(solution)/shard_map/ppermute | solution.py:247
  24.5 1.4 %collective-permute-start.2 = (bf16[8,96,120]{2,1,0:T(8,128)(2,1)}, bf16[8,96,120]{2,1,0:T(8,128)(2,1)}, u32[]{:S(2)}, u32[]{:S(2)}) collective-permute-start(bf16[8,96,120]{2,1,0:T(8,128)(2,1)} %all-to-all-done.refs_1_), channel_id=1, source_target_pairs={{0,24},{8,0},{16,8},{24,16},{1,25},{9,1},{17,9},{25,17},{2,26},{10... | collective-permute-start | bytes 552968 | tf_op jit(solution)/shard_map/ppermute | solution.py:247
  25.9 19.9 %all-to-all-done.1.message_ref = bf16[8,128,1024]{2,1,0:T(8,128)(2,1)} async-done(((bf16[8,128,1024]{2,1,0:T(8,128)(2,1)}), bf16[8,128,1024]{2,1,0:T(8,128)(2,1)}, u32[]{:S(2)}, u32[]{:S(2)}) %all-to-all-start.1) | async-done | bytes 2097184 | tf_op jit(solution)/shard_map/all_to_all | solution.py:263
  45.8 1.5 %slice_bitcast_fusion = (bf16[2,16,1024]{2,1,0:T(8,128)(2,1)S(1)}, bf16[2,16,1024]{2,1,0:T(8,128)(2,1)}) fusion(bf16[4,2,128,1024]{3,2,1,0:T(8,128)(2,1)} %bitcast.7), kind=kLoop, calls=%fused_computation.11 | loop fusion | bytes 262144 | tf_op jit(solution)/shard_map/squeeze | solution.py:268
  47.3 3.8 %collective-permute-start.3 = (bf16[2,16,1024]{2,1,0:T(8,128)(2,1)}, bf16[2,16,1024]{2,1,0:T(8,128)(2,1)S(1)}, u32[]{:S(2)}, u32[]{:S(2)}) collective-permute-start(bf16[2,16,1024]{2,1,0:T(8,128)(2,1)} %get-tuple-element.41), channel_id=1, source_target_pairs={{0,8},{8,16},{16,24},{1,9},{9,17},{17,25},{2,10},{10,18},{18,26},{... | collective-permute-start | bytes 196616 | tf_op jit(solution)/shard_map/ppermute | solution.py:267
  51.1 1.3 %collective-permute-start.4 = (bf16[2,16,1024]{2,1,0:T(8,128)(2,1)S(1)}, bf16[2,16,1024]{2,1,0:T(8,128)(2,1)S(1)}, u32[]{:S(2)}, u32[]{:S(2)}) collective-permute-start(bf16[2,16,1024]{2,1,0:T(8,128)(2,1)S(1)} %get-tuple-element.40), channel_id=1, source_target_pairs={{8,0},{16,8},{24,16},{9,1},{17,9},{25,17},{10,2},{18,10},{26,18},{... | collective-permute-start | bytes 196616 | tf_op jit(solution)/shard_map/ppermute | solution.py:268
  52.4 0.4 fusion.4.swap_ref
  52.9 0.4 collective-permute-done.3.low_ref
  53.3 4.0 %collective-permute-done.4.high_ref = bf16[2,16,1024]{2,1,0:T(8,128)(2,1)S(1)} collective-permute-done((bf16[2,16,1024]{2,1,0:T(8,128)(2,1)S(1)}, bf16[2,16,1024]{2,1,0:T(8,128)(2,1)S(1)}, u32[]{:S(2)}, u32[]{:S(2)}) %collective-permute-start.4) | collective-permute-done | bytes 65568 | tf_op jit(solution)/shard_map/ppermute | solution.py:268
  57.3 5.6 %shard_map.85 = (bf16[4,544,768]{2,1,0:T(8,128)(2,1)}, f32[4,544,128]{2,1,0:T(8,128)S(1)}) custom-call(bf16[8,128,1024]{2,1,0:T(8,128)(2,1)} %all-to-all-done.1.message_ref, bf16[2,16,1024]{2,1,0:T(8,128)(2,1)S(1)} %collective-permute-done.3.low_ref, bf16[2,16,1024]{2,1,0:T(8,128)(2,1)S(1)} %collective-permute-done.4.high_ref, ...), custom_call_target="tpu_custom_call" | custom-call | tf_op jit(solution)/shard_map/pallas_call | solution.py:22
  62.9 1.0 copy-done.5
  63.9 0.0 collective-permute-done.refs_2_
  63.9 0.0 collective-permute-done.1.refs_3_
  63.9 0.0 collective-permute-done.2.refs_4_
  63.9 10.1 %shard_map.86 = (bf16[4,544,640]{2,1,0:T(8,128)(2,1)}, bf16[640,768]{1,0:T(8,128)(2,1)S(1)}, bf16[4,512,128]{2,1,0:T(8,128)(2,1)S(1)}, bf16[32,112,120]{2,1,0:T(8,128)(2,1)S(1)}) custom-call(s32[1]{0:T(128)} %bitcast.4.refs_0_, bf16[8,96,120]{2,1,0:T(8,128)(2,1)} %all-to-all-done.refs_1_, bf16[8,96,120]{2,1,0:T(8,128)(2,1)S(1)} %collective-permute-done.refs_2_, ...), custom_call_target="tpu_custom_call" | custom-call | flops 4278190080 | tf_op jit(solution)/shard_map/pallas_call | solution.py:22
  73.9 0.9 copy-done.2
  74.9 1.0 copy-done.6
  75.9 0.8 copy-done.8
  76.7 4.0 %all-to-all-start.2 = ((bf16[32,112,120]{2,1,0:T(8,128)(2,1)}), bf16[32,112,120]{2,1,0:T(8,128)(2,1)S(1)}, u32[]{:S(2)}, u32[]{:S(2)}) async-start(bf16[32,112,120]{2,1,0:T(8,128)(2,1)} %copy-done.2), calls=%async_computation.2 | async-start | bytes 1835008 | tf_op jit(solution)/shard_map/all_to_all | solution.py:295
  80.7 3.2 %gather_fusion.1 = f32[768]{0:T(1024)S(1)} fusion(f32[768]{0:T(1024)S(1)} %copy-done.11, s32[1024]{0:T(1024)S(1)} %pad_clamp_fusion), kind=kCustom, calls=%fused_computation.1 | custom fusion | bytes 9216 | tf_op jit(solution)/shard_map/gather | solution.py:257
  84.0 1.2 copy-done.7
  85.2 5.7 %shard_map.87 = (bf16[128,1024]{1,0:T(8,128)(2,1)S(1)}, bf16[128,1024]{1,0:T(8,128)(2,1)S(1)}, bf16[128,1024]{1,0:T(8,128)(2,1)S(1)}, bf16[128,1024]{1,0:T(8,128...) custom-call(s32[1]{0:T(128)} %bitcast.rank_ref, ...), custom_call_target="tpu_custom_call" | custom-call | flops 2013265920 | tf_op jit(solution)/shard_map/pallas_call | solution.py:22
  90.9 1.4 %collective-permute-start.10 = (bf16[128,1024]{1,0:T(8,128)(2,1)S(1)}, bf16[128,1024]{1,0:T(8,128)(2,1)S(1)}, u32[]{:S(2)}, u32[]{:S(2)}) collective-permute-start(bf16[128,1024]{1,0:T(8,128)(2,1)S(1)} %get-tuple-element.31), channel_id=1, source_target_pairs={{0,6},{1,7},{2,4},{3,5},{4,2},{5,3},{6,0},{7,1},{8,14},{9,15},{10,... | collective-permute-start | bytes 786440 | tf_op jit(solution)/shard_map/ppermute | solution.py:305
  92.3 1.4 %collective-permute-start.11 = (bf16[128,1024]{1,0:T(8,128)(2,1)S(1)}, bf16[128,1024]{1,0:T(8,128)(2,1)S(1)}, u32[]{:S(2)}, u32[]{:S(2)}) collective-permute-start(bf16[128,1024]{1,0:T(8,128)(2,1)S(1)} %get-tuple-element.32), channel_id=1, source_target_pairs={{0,7},{1,6},{2,5},{3,4},{4,3},{5,2},{6,1},{7,0},{8,15},{9,14},{10,... | collective-permute-start | bytes 786440 | tf_op jit(solution)/shard_map/ppermute | solution.py:305
  93.7 0.4 collective-permute-start.5
  94.2 0.0 collective-permute-start.6
  94.2 1.7 %collective-permute-start.7 = (bf16[128,1024]{1,0:T(8,128)(2,1)S(1)}, bf16[128,1024]{1,0:T(8,128)(2,1)S(1)}, u32[]{:S(2)}, u32[]{:S(2)}) collective-permute-start(bf16[128,1024]{1,0:T(8,128)(2,1)S(1)} %get-tuple-element.28), channel_id=1, source_target_pairs={{0,3},{1,2},{2,1},{3,0},{4,7},{5,6},{6,5},{7,4},{8,11},{9,10},{10,... | collective-permute-start | bytes 786440 | tf_op jit(solution)/shard_map/ppermute | solution.py:305
  95.9 6.0 %collective-permute-done.10.refs_6_ = bf16[128,1024]{1,0:T(8,128)(2,1)S(1)} collective-permute-done((bf16[128,1024]{1,0:T(8,128)(2,1)S(1)}, bf16[128,1024]{1,0:T(8,128)(2,1)S(1)}, u32[]{:S(2)}, u32[]{:S(2)}) %collective-permute-start.10) | collective-permute-done | bytes 262176 | tf_op jit(solution)/shard_map/ppermute | solution.py:305
  101.8 1.4 %collective-permute-start.8 = (bf16[128,1024]{1,0:T(8,128)(2,1)S(1)}, bf16[128,1024]{1,0:T(8,128)(2,1)S(1)}, u32[]{:S(2)}, u32[]{:S(2)}) collective-permute-start(bf16[128,1024]{1,0:T(8,128)(2,1)S(1)} %get-tuple-element.29), channel_id=1, source_target_pairs={{0,4},{1,5},{2,6},{3,7},{4,0},{5,1},{6,2},{7,3},{8,12},{9,13},{10,... | collective-permute-start | bytes 786440 | tf_op jit(solution)/shard_map/ppermute | solution.py:305
  103.2 5.1 %collective-permute-done.11.refs_7_ = bf16[128,1024]{1,0:T(8,128)(2,1)S(1)} collective-permute-done((bf16[128,1024]{1,0:T(8,128)(2,1)S(1)}, bf16[128,1024]{1,0:T(8,128)(2,1)S(1)}, u32[]{:S(2)}, u32[]{:S(2)}) %collective-permute-start.11) | collective-permute-done | bytes 262176 | tf_op jit(solution)/shard_map/ppermute | solution.py:305
  108.4 2.1 %collective-permute-start.9 = (bf16[128,1024]{1,0:T(8,128)(2,1)S(1)}, bf16[128,1024]{1,0:T(8,128)(2,1)S(1)}, u32[]{:S(2)}, u32[]{:S(2)}) collective-permute-start(bf16[128,1024]{1,0:T(8,128)(2,1)S(1)} %get-tuple-element.30), channel_id=1, source_target_pairs={{0,5},{1,4},{2,7},{3,6},{4,1},{5,0},{6,3},{7,2},{8,13},{9,12},{10,... | collective-permute-start | bytes 786440 | tf_op jit(solution)/shard_map/ppermute | solution.py:305
  110.5 0.0 collective-permute-done.5.refs_1_
  110.5 0.0 collective-permute-done.6.refs_2_
  110.5 10.0 %collective-permute-done.7.refs_3_ = bf16[128,1024]{1,0:T(8,128)(2,1)S(1)} collective-permute-done((bf16[128,1024]{1,0:T(8,128)(2,1)S(1)}, bf16[128,1024]{1,0:T(8,128)(2,1)S(1)}, u32[]{:S(2)}, u32[]{:S(2)}) %collective-permute-start.7) | collective-permute-done | bytes 262176 | tf_op jit(solution)/shard_map/ppermute | solution.py:305
  120.5 3.5 %shard_map.88 = (bf16[128,768]{1,0:T(8,128)(2,1)}, bf16[128,768]{1,0:T(8,128)(2,1)}) custom-call(s32[1]{0:T(128)} %bitcast.rank_ref, bf16[128,768]{1,0:T(8,128)(2,1)S(1)} %bitcast.21, bf16[128,768]{1,0:T(8,128)(2,1)S(1)} %bitcast.23, bf16[768,1024]{1,0:T(8,128)(2,1)S(1)} %get-tuple-element.43.plain_ref, bf16[768,1024]{1,0:T(8,128)(2,1)} %copy-done, ...), custom_call_target="tpu_custom_call" | custom-call | tf_op jit(solution)/shard_map/pallas_call | solution.py:22
  124.1 0.2 convert_reduce_fusion
  124.3 0.5 slice_reduce_fusion
  124.8 0.9 copy.11
  (29 shorter events, 0.1 us)
Async XLA Ops:
  0.6 7.0 %copy-start.10 = (s32[768]{0:T(1024)S(1)}, s32[768]{0:T(1024)}, u32[]{:S(2)}) copy-start(s32[768]{0:T(1024)} %param.9) | copy-start | bytes 9220
  2.4 13.1 %all-to-all-start = ((bf16[8,96,120]{2,1,0:T(8,128)(2,1)}), bf16[8,96,120]{2,1,0:T(8,128)(2,1)}, u32[]{:S(2)}, u32[]{:S(2)}) async-start(bf16[8,96,120]{2,1,0:T(8,128)(2,1)} %bitcast.6), calls=%async_computation | async-start | bytes 393216 | tf_op jit(solution)/shard_map/all_to_all | solution.py:245
  12.2 1.3 %copy-start.3 = (bf16[1,128,768]{2,1,0:T(8,128)(2,1)S(1)}, bf16[1,128,768]{2,1,0:T(8,128)(2,1)}, u32[]{:S(2)}) copy-start(bf16[1,128,768]{2,1,0:T(8,128)(2,1)} %param.5) | copy-start | bytes 589828
  12.2 1.3 %copy-start.4 = (bf16[1,128,768]{2,1,0:T(8,128)(2,1)S(1)}, bf16[1,128,768]{2,1,0:T(8,128)(2,1)}, u32[]{:S(2)}) copy-start(bf16[1,128,768]{2,1,0:T(8,128)(2,1)} %param.6) | copy-start | bytes 589828
  13.4 2.0 %copy-start = (bf16[768,1024]{1,0:T(8,128)(2,1)}, bf16[768,1024]{1,0:T(8,128)(2,1)S(1)}, u32[]{:S(2)}) copy-start(bf16[768,1024]{1,0:T(8,128)(2,1)S(1)} %get-tuple-element.42.other_ref) | copy-start | bytes 4718596
  15.5 37.3 %copy-start.11 = (f32[768]{0:T(1024)S(1)}, f32[768]{0:T(1024)}, u32[]{:S(2)}) copy-start(f32[768]{0:T(1024)} %param.8) | copy-start | bytes 9220
  15.5 30.3 %all-to-all-start.1 = ((bf16[8,128,1024]{2,1,0:T(8,128)(2,1)}), bf16[8,128,1024]{2,1,0:T(8,128)(2,1)}, u32[]{:S(2)}, u32[]{:S(2)}) async-start(bf16[8,128,1024]{2,1,0:T(8,128)(2,1)} %shard_map.84), calls=%async_computation.1 | async-start | bytes 4194304 | tf_op jit(solution)/shard_map/all_to_all | solution.py:263
  20.0 43.9 %collective-permute-start = (bf16[8,96,120]{2,1,0:T(8,128)(2,1)}, bf16[8,96,120]{2,1,0:T(8,128)(2,1)S(1)}, u32[]{:S(2)}, u32[]{:S(2)}) collective-permute-start(bf16[8,96,120]{2,1,0:T(8,128)(2,1)} %all-to-all-done.refs_1_), channel_id=1, source_target_pairs={{0,8},{8,16},{16,24},{24,0},{1,9},{9,17},{17,25},{25,1},{2,10},{10... | collective-permute-start | bytes 552968 | tf_op jit(solution)/shard_map/ppermute | solution.py:247
  21.9 41.9 %collective-permute-start.1 = (bf16[8,96,120]{2,1,0:T(8,128)(2,1)}, bf16[8,96,120]{2,1,0:T(8,128)(2,1)}, u32[]{:S(2)}, u32[]{:S(2)}) collective-permute-start(bf16[8,96,120]{2,1,0:T(8,128)(2,1)} %all-to-all-done.refs_1_), channel_id=1, source_target_pairs={{0,16},{8,24},{16,0},{24,8},{1,17},{9,25},{17,1},{25,9},{2,18},{10... | collective-permute-start | bytes 552968 | tf_op jit(solution)/shard_map/ppermute | solution.py:247
  24.5 39.3 %collective-permute-start.2 = (bf16[8,96,120]{2,1,0:T(8,128)(2,1)}, bf16[8,96,120]{2,1,0:T(8,128)(2,1)}, u32[]{:S(2)}, u32[]{:S(2)}) collective-permute-start(bf16[8,96,120]{2,1,0:T(8,128)(2,1)} %all-to-all-done.refs_1_), channel_id=1, source_target_pairs={{0,24},{8,0},{16,8},{24,16},{1,25},{9,1},{17,9},{25,17},{2,26},{10... | collective-permute-start | bytes 552968 | tf_op jit(solution)/shard_map/ppermute | solution.py:247
  47.3 6.0 %collective-permute-start.3 = (bf16[2,16,1024]{2,1,0:T(8,128)(2,1)}, bf16[2,16,1024]{2,1,0:T(8,128)(2,1)S(1)}, u32[]{:S(2)}, u32[]{:S(2)}) collective-permute-start(bf16[2,16,1024]{2,1,0:T(8,128)(2,1)} %get-tuple-element.41), channel_id=1, source_target_pairs={{0,8},{8,16},{16,24},{1,9},{9,17},{17,25},{2,10},{10,18},{18,26},{... | collective-permute-start | bytes 196616 | tf_op jit(solution)/shard_map/ppermute | solution.py:267
  51.1 6.2 %collective-permute-start.4 = (bf16[2,16,1024]{2,1,0:T(8,128)(2,1)S(1)}, bf16[2,16,1024]{2,1,0:T(8,128)(2,1)S(1)}, u32[]{:S(2)}, u32[]{:S(2)}) collective-permute-start(bf16[2,16,1024]{2,1,0:T(8,128)(2,1)S(1)} %get-tuple-element.40), channel_id=1, source_target_pairs={{8,0},{16,8},{24,16},{9,1},{17,9},{25,17},{10,2},{18,10},{26,18},{... | collective-permute-start | bytes 196616 | tf_op jit(solution)/shard_map/ppermute | solution.py:268
  52.8 21.1 %copy-start.1 = (bf16[768,768]{1,0:T(8,128)(2,1)}, bf16[768,768]{1,0:T(8,128)(2,1)S(1)}, u32[]{:S(2)}) copy-start(bf16[768,768]{1,0:T(8,128)(2,1)S(1)} %fusion.4.swap_ref) | copy-start | bytes 3538948
  62.9 1.0 copy-start.5
  73.9 0.9 copy-start.2
  74.9 1.0 copy-start.6
  75.9 0.8 copy-start.8
  76.7 47.4 %all-to-all-start.2 = ((bf16[32,112,120]{2,1,0:T(8,128)(2,1)}), bf16[32,112,120]{2,1,0:T(8,128)(2,1)S(1)}, u32[]{:S(2)}, u32[]{:S(2)}) async-start(bf16[32,112,120]{2,1,0:T(8,128)(2,1)} %copy-done.2), calls=%async_computation.2 | async-start | bytes 1835008 | tf_op jit(solution)/shard_map/all_to_all | solution.py:295
  80.7 3.2 %copy-start.9 = (bf16[4,512,128]{2,1,0:T(8,128)(2,1)S(1)}, bf16[4,512,128]{2,1,0:T(8,128)(2,1)}, u32[]{:S(2)}) copy-start(bf16[4,512,128]{2,1,0:T(8,128)(2,1)} %copy-done.8) | copy-start | bytes 1572868
  84.0 1.2 copy-start.7
  90.9 11.0 %collective-permute-start.10 = (bf16[128,1024]{1,0:T(8,128)(2,1)S(1)}, bf16[128,1024]{1,0:T(8,128)(2,1)S(1)}, u32[]{:S(2)}, u32[]{:S(2)}) collective-permute-start(bf16[128,1024]{1,0:T(8,128)(2,1)S(1)} %get-tuple-element.31), channel_id=1, source_target_pairs={{0,6},{1,7},{2,4},{3,5},{4,2},{5,3},{6,0},{7,1},{8,14},{9,15},{10,... | collective-permute-start | bytes 786440 | tf_op jit(solution)/shard_map/ppermute | solution.py:305
  92.3 16.0 %collective-permute-start.11 = (bf16[128,1024]{1,0:T(8,128)(2,1)S(1)}, bf16[128,1024]{1,0:T(8,128)(2,1)S(1)}, u32[]{:S(2)}, u32[]{:S(2)}) collective-permute-start(bf16[128,1024]{1,0:T(8,128)(2,1)S(1)} %get-tuple-element.32), channel_id=1, source_target_pairs={{0,7},{1,6},{2,5},{3,4},{4,3},{5,2},{6,1},{7,0},{8,15},{9,14},{10,... | collective-permute-start | bytes 786440 | tf_op jit(solution)/shard_map/ppermute | solution.py:305
  93.7 16.8 %collective-permute-start.5 = (bf16[128,1024]{1,0:T(8,128)(2,1)S(1)}, bf16[128,1024]{1,0:T(8,128)(2,1)S(1)}, u32[]{:S(2)}, u32[]{:S(2)}) collective-permute-start(bf16[128,1024]{1,0:T(8,128)(2,1)S(1)} %get-tuple-element.26), channel_id=1, source_target_pairs={{0,1},{1,0},{2,3},{3,2},{4,5},{5,4},{6,7},{7,6},{8,9},{9,8},{10,11... | collective-permute-start | bytes 786440 | tf_op jit(solution)/shard_map/ppermute | solution.py:305
  94.2 16.3 %collective-permute-start.6 = (bf16[128,1024]{1,0:T(8,128)(2,1)S(1)}, bf16[128,1024]{1,0:T(8,128)(2,1)S(1)}, u32[]{:S(2)}, u32[]{:S(2)}) collective-permute-start(bf16[128,1024]{1,0:T(8,128)(2,1)S(1)} %get-tuple-element.27), channel_id=1, source_target_pairs={{0,2},{1,3},{2,0},{3,1},{4,6},{5,7},{6,4},{7,5},{8,10},{9,11},{10,... | collective-permute-start | bytes 786440 | tf_op jit(solution)/shard_map/ppermute | solution.py:305
  94.2 26.4 %collective-permute-start.7 = (bf16[128,1024]{1,0:T(8,128)(2,1)S(1)}, bf16[128,1024]{1,0:T(8,128)(2,1)S(1)}, u32[]{:S(2)}, u32[]{:S(2)}) collective-permute-start(bf16[128,1024]{1,0:T(8,128)(2,1)S(1)} %get-tuple-element.28), channel_id=1, source_target_pairs={{0,3},{1,2},{2,1},{3,0},{4,7},{5,6},{6,5},{7,4},{8,11},{9,10},{10,... | collective-permute-start | bytes 786440 | tf_op jit(solution)/shard_map/ppermute | solution.py:305
  101.8 18.7 %collective-permute-start.8 = (bf16[128,1024]{1,0:T(8,128)(2,1)S(1)}, bf16[128,1024]{1,0:T(8,128)(2,1)S(1)}, u32[]{:S(2)}, u32[]{:S(2)}) collective-permute-start(bf16[128,1024]{1,0:T(8,128)(2,1)S(1)} %get-tuple-element.29), channel_id=1, source_target_pairs={{0,4},{1,5},{2,6},{3,7},{4,0},{5,1},{6,2},{7,3},{8,12},{9,13},{10,... | collective-permute-start | bytes 786440 | tf_op jit(solution)/shard_map/ppermute | solution.py:305
  108.4 12.2 %collective-permute-start.9 = (bf16[128,1024]{1,0:T(8,128)(2,1)S(1)}, bf16[128,1024]{1,0:T(8,128)(2,1)S(1)}, u32[]{:S(2)}, u32[]{:S(2)}) collective-permute-start(bf16[128,1024]{1,0:T(8,128)(2,1)S(1)} %get-tuple-element.30), channel_id=1, source_target_pairs={{0,5},{1,4},{2,7},{3,6},{4,1},{5,0},{6,3},{7,2},{8,13},{9,12},{10,... | collective-permute-start | bytes 786440 | tf_op jit(solution)/shard_map/ppermute | solution.py:305

commit v4 on v3

--- a/solution.py
+++ b/solution.py
@@ -18,14 +18,14 @@
 f32 = jnp.float32
 
 
-def called(body, outs, args, scratch=(), specs=None, flops=0, moved=0):
+def called(body, outs, args, vmem, scratch=(), specs=None, flops=0, moved=0):
     return pl.pallas_call(
         body,
         out_shape=outs,
         in_specs=specs or [VMEM] * len(args),
         out_specs=jax.tree.map(lambda _: VMEM, outs),
         scratch_shapes=list(scratch),
-        compiler_params=pltpu.CompilerParams(vmem_limit_bytes=50 * 2**20),
+        compiler_params=pltpu.CompilerParams(vmem_limit_bytes=vmem * 2**20),
         cost_estimate=pl.CostEstimate(flops=flops, bytes_accessed=moved, transcendentals=0),
     )(*args)
 
@@ -60,43 +60,47 @@
             message_ref[j, :, start : start + LANES] = piece[:, j * LANES : (j + 1) * LANES]
 
 
-def prepare(message_ref, low_ref, high_ref, gain_ref, swap_ref, normed_ref, grads_ref):
-    dp_ranks = low_ref.shape[0]
+def normalize(x, gain, swap):
+    other = dot(x, swap, ((1,), (0,)))
+    x = x.astype(f32)
+    rms = lax.rsqrt(jnp.mean(x * x, -1, keepdims=True) + epsilon)
+    return [(t * rms * gain).astype(bf16) for t in (x, other)]
+
+
+def prepare(message_ref, gain_ref, swap_ref, normed_ref, grads_ref, swapped_gain_ref):
     ranks, positions = message_ref.shape[:2]
+    dp_ranks = normed_ref.shape[0] // 2
     channels = gain_ref.shape[1]
-
-    def put(block, b, start):
-        count = block.shape[0]
-        x = block[:, :channels]
-        other = dot(x, swap_ref[...], ((1,), (0,)))
-        x = x.astype(f32)
-        rms = lax.rsqrt(jnp.mean(x * x, -1, keepdims=True) + epsilon)
-        normed_ref[b, pl.ds(start, count), :] = (x * rms * gain_ref[...]).astype(bf16)
-        normed_ref[dp_ranks + b, pl.ds(start, count), :] = (other * rms * gain_ref[...]).astype(bf16)
-        for n in range(2):
+    for rank in range(ranks):
+        b, start = rank % dp_ranks, rank // dp_ranks * positions
+        for n, normed in enumerate(normalize(message_ref[rank, :, :channels], gain_ref[...], swap_ref[...])):
+            normed_ref[n * dp_ranks + b, start : start + positions, :] = normed
             lane = channels + n * LANES
-            grads_ref[n * dp_ranks + b, pl.ds(start, count), :] = 0.5 * block[:, lane : lane + LANES].astype(f32)
-
-    for b in range(dp_ranks):
-        put(low_ref[b], b, 0)
-        for i in range(ranks // dp_ranks):
-            put(message_ref[i * dp_ranks + b], b, HALO + i * positions)
-        put(high_ref[b], b, HALO + (ranks // dp_ranks) * positions)
+            grads_ref[n * dp_ranks + b, start : start + positions, :] = (
+                0.5 * message_ref[rank, :, lane : lane + LANES].astype(f32)
+            ).astype(bf16)
+    gain = gain_ref[...]
+    first = gain.astype(bf16).astype(f32)
+    second = (gain - first).astype(bf16).astype(f32)
+    third = gain - first - second
+    row = lax.broadcasted_iota(jnp.int32, (HALO, channels), 0)
+    parts = jnp.where(row == 0, first, jnp.where(row == 1, second, jnp.where(row == 2, third, 0.0)))
+    swapped = dot(parts.astype(bf16), swap_ref[...], ((1,), (0,)))
+    swapped_gain_ref[...] = swapped[0:1] + swapped[1:2] + swapped[2:3]
 
 
 def main_body(sizes, me_ref, own_ref, *refs):
     seq_blocks, dp_blocks, seq_ranks, dp_ranks = sizes
     blocks = seq_blocks * dp_blocks
     others = refs[: blocks - 1]
-    normed_ref, grads_ref, gain_ref = refs[blocks - 1 : blocks + 2]
-    shifted_ref, kernel_ref, gelu_ref, out_ref = refs[blocks + 2 : blocks + 6]
-    pieces, terms, bent, slopes, total = refs[blocks + 6 :]
+    normed_ref, grads_ref, low_ref, high_ref, gain_ref, swap_ref = refs[blocks - 1 : blocks + 5]
+    shifted_ref, kernel_ref, gelu_ref, out_ref = refs[blocks + 5 : blocks + 9]
+    pieces, terms, halves, bent, slopes, total = refs[blocks + 9 :]
     part, rows = own_ref.shape[1:]
-    strands, long, channels = normed_ref.shape
+    strands, span, channels = normed_ref.shape
     taps = kernel_ref.shape[0] // LANES
     half = taps // 2
     reach = 2 * half
-    span = long - 2 * HALO
     wide = bent.shape[0]
     me = me_ref[0]
     pieces[me] = own_ref[...]
@@ -124,9 +128,23 @@
             kernel_ref[tap * LANES : tap * LANES + part, channel : channel + count] = pieces[
                 block, rank, :, offset : offset + count
             ]
+    edges = [ref[b] for ref in (low_ref, high_ref) for b in range(dp_ranks)]
+    edges = jnp.concatenate(edges, 0)
+    edge_normed = jnp.concatenate(normalize(edges[:, :channels], gain_ref[...], swap_ref[...]), 0)
+    edge_terms = dot(edge_normed, kernel_ref[...], ((1,), (1,)))
     for strand in range(strands):
-        terms[...] = dot(normed_ref[strand], kernel_ref[...], ((1,), (1,)))
         forward = strand < dp_ranks
+        n, b = divmod(strand, dp_ranks)
+        terms[HALO : HALO + span, :] = dot(normed_ref[strand], kernel_ref[...], ((1,), (1,)))
+        halves[HALO : HALO + span, :] = grads_ref[strand].astype(f32)
+        for side, start in enumerate((0, HALO + span)):
+            edge = (side * dp_ranks + b) * HALO
+            first = n * 2 * dp_ranks * HALO + edge
+            terms[start : start + HALO, :] = edge_terms[first : first + HALO]
+            lane = channels + n * LANES
+            halves[start : start + HALO, :] = 0.5 * edges[
+                edge : edge + HALO, lane : lane + LANES
+            ].astype(f32)
         preact = jnp.zeros((wide, LANES), f32)
         for k in range(taps):
             start = HALO - reach + k if forward else HALO - k
@@ -134,18 +152,15 @@
         result, slope = gelu_and_slope(preact)
         bent[...] = result
         gelu_ref[strand] = bent[half : half + span, :].astype(bf16)
-        slopes[...] = grads_ref[strand, HALO - half : HALO - half + wide, :] * slope
-        edge = jnp.zeros((HALO, taps * LANES), bf16)
-        shifted_ref[strand, :HALO, :] = edge
-        shifted_ref[strand, HALO + span :, :] = edge
+        slopes[...] = halves[HALO - half : HALO - half + wide, :] * slope
         for k in range(taps):
             start = reach - k if forward else k
-            shifted_ref[strand, HALO : HALO + span, k * LANES : (k + 1) * LANES] = slopes[
+            shifted_ref[strand, :, k * LANES : (k + 1) * LANES] = slopes[
                 start : start + span, :
             ].astype(bf16)
     total[...] = dot(
-        shifted_ref[...].reshape(strands * long, taps * LANES),
-        normed_ref[...].reshape(strands * long, channels),
+        shifted_ref[...].reshape(strands * span, taps * LANES),
+        normed_ref[...].reshape(strands * span, channels),
         ((0,), (0,)),
     )
     gain = jnp.sum(total[...] * kernel_ref[...].astype(f32), 0, keepdims=True) / gain_ref[...]
@@ -164,45 +179,62 @@
         ].astype(bf16)
 
 
-def input_gradient(rank_ref, shifted_ref, kernel_ref, swap_ref, gain_ref, swapped_gain_ref, gelu_ref, *refs):
-    outs, scaled = refs[:-1], refs[-1]
-    ranks = len(outs)
-    strands, long, _ = shifted_ref.shape
+def chip_masks(ranks, core):
+    return [mask for mask in range(ranks) if not mask & core]
+
+
+def input_gradient(
+    rank_ref, shifted_ref, kernel_ref, swap_ref, gain_ref, swapped_gain_ref, gelu_ref, own_ref, cross_ref, scaled
+):
+    strands = shifted_ref.shape[0]
     dp_ranks = strands // 2
-    span = long - 2 * HALO
-    positions = outs[0].shape[0]
+    chips, positions, _ = own_ref.shape
     channels = gain_ref.shape[1]
     kernel = kernel_ref[...]
     swapped = dot(kernel, swap_ref[...], ((1,), (0,))).astype(bf16)
     for b in range(dp_ranks):
         scaled[b] = (
-            dot(shifted_ref[b, HALO : HALO + span, :], kernel, ((1,), (0,))) * gain_ref[...]
-            + dot(shifted_ref[dp_ranks + b, HALO : HALO + span, :], swapped, ((1,), (0,)))
-            * swapped_gain_ref[...]
+            dot(shifted_ref[b], kernel, ((1,), (0,))) * gain_ref[...]
+            + dot(shifted_ref[dp_ranks + b], swapped, ((1,), (0,))) * swapped_gain_ref[...]
         ).astype(bf16)
-    for shift in range(ranks):
-        target = lax.bitwise_xor(rank_ref[0], shift)
-        b = lax.rem(target, dp_ranks)
-        start = pl.multiple_of(lax.div(target, dp_ranks) * positions, positions)
-        outs[shift][:, :channels] = scaled[b, pl.ds(start, positions), :]
-        for n in range(2):
-            lane = channels + n * LANES
-            outs[shift][:, lane : lane + LANES] = gelu_ref[n * dp_ranks + b, pl.ds(start, positions), :]
-
-
-def finish(rank_ref, values_ref, cot_ref, plain_ref, other_ref, *refs):
-    blocks, (combined_ref, grad_ref, gelus) = refs[:-3], refs[-3:]
+    for m, mask in enumerate(chip_masks(2 * chips, dp_ranks)):
+        for out, flip in ((own_ref, mask), (cross_ref, mask | dp_ranks)):
+            target = lax.bitwise_xor(rank_ref[0], flip)
+            b = lax.rem(target, dp_ranks)
+            start = pl.multiple_of(lax.div(target, dp_ranks) * positions, positions)
+            out[m, :, :channels] = scaled[b, pl.ds(start, positions), :]
+            for n in range(2):
+                lane = channels + n * LANES
+                out[m, :, lane : lane + LANES] = gelu_ref[n * dp_ranks + b, pl.ds(start, positions), :]
+
+
+def chip_sum(part, own_ref, crossed_ref, *outs):
+    channels = own_ref.shape[2] - 2 * LANES
+    for m, out in enumerate(outs):
+        out[:, :channels] = (
+            own_ref[m, :, :channels].astype(f32) + crossed_ref[m, :, :channels].astype(f32)
+        ).astype(bf16)
+        for c, ref in enumerate((own_ref, crossed_ref)):
+            for n in range(2):
+                lane = channels + n * LANES
+                start = channels + (2 * c + n) * part
+                out[:, start : start + part] = ref[m, :, lane : lane + part]
+
+
+def finish(part, core, rank_ref, values_ref, cot_ref, plain_ref, other_ref, *refs):
+    arrived, (combined_ref, grad_ref, gelus) = refs[:-3], refs[-3:]
     channels = values_ref.shape[1]
+    ranks = gelus.shape[1]
+    gelus[...] = jnp.zeros_like(gelus)
     scaled = jnp.zeros(values_ref.shape, f32)
-    for shift, block in enumerate(blocks):
-        source = lax.bitwise_xor(rank_ref[0], shift)
+    for mask, block in zip(chip_masks(ranks, core), arrived):
         scaled += block[:, :channels].astype(f32)
-        for n in range(2):
-            lane = channels + n * LANES
-            gelus[n, source] = block[:, lane : lane + LANES]
-    plain = jnp.zeros(values_ref.shape, f32)
-    other = jnp.zeros(values_ref.shape, f32)
-    joined = [jnp.concatenate([gelus[n, j] for j in range(len(blocks))], -1) for n in range(2)]
+        for c in range(2):
+            source = lax.bitwise_xor(rank_ref[0], mask | c * core)
+            for n in range(2):
+                start = channels + (2 * c + n) * part
+                gelus[n, source, :, :part] = block[:, start : start + part]
+    joined = [jnp.concatenate([gelus[n, j] for j in range(ranks)], -1) for n in range(2)]
     plain = dot(joined[0], plain_ref[...], ((1,), (1,)))
     other = dot(joined[1], other_ref[...], ((1,), (1,)))
     values = values_ref[...].astype(f32)
@@ -246,19 +278,18 @@
     other_kernels = [
         lax.ppermute(mine, BLOCK, shifted_pairs(blocks, shift)) for shift in range(1, blocks)
     ]
-    slot = jnp.arange(ranks * LANES)
-    inside = slot % LANES < part
-    channel_of = jnp.where(inside, slot // LANES * part + slot % LANES, 0).astype(jnp.int32)
-    channel_list = jnp.arange(channels, dtype=jnp.int32)[:, None]
-    plain_map = ((channel_list == channel_of) & inside).astype(bf16)
-    other_map = ((channel_list == pairing[channel_of]) & inside).astype(bf16)
-    swap = (channel_list == pairing).astype(bf16)
+    slot = jnp.arange(ranks * LANES, dtype=jnp.int32)
+    channel_of = jnp.where(slot % LANES < part, slot // LANES * part + slot % LANES, -1)
+    channel_list = jnp.arange(channels, dtype=jnp.int32)
+    plain_map = (channel_list[:, None] == channel_of).astype(bf16)
+    other_map = (pairing[:, None] == channel_of).astype(bf16)
+    swap = (pairing[:, None] == channel_list).astype(bf16)
     gain = norm_gain.reshape(1, channels)
-    swapped_gain = norm_gain[pairing].reshape(1, channels)
     message = called(
         pack_message,
         shape_of((ranks, positions, width), bf16),
         (values, cot, plain_map, other_map),
+        16,
     )
     message = lax.all_to_all(message, RANK, 0, 0, tiled=True)
     by_seq = message.reshape(seq_ranks, dp_ranks, positions, width)
@@ -266,50 +297,72 @@
     backward = [(target, source) for source, target in forward]
     low = lax.ppermute(by_seq[-1, :, -HALO:], "seq_block", forward)
     high = lax.ppermute(by_seq[0, :, :HALO], "seq_block", backward)
-    normed, grads = called(
+    normed, grads, swapped_gain = called(
         prepare,
-        (shape_of((strands, long, channels), bf16), shape_of((strands, long, LANES), f32)),
-        (message, low, high, gain, swap),
-    )
-    main_args = (me, mine, *other_kernels, normed, grads, gain)
+        (
+            shape_of((strands, span, channels), bf16),
+            shape_of((strands, span, LANES), bf16),
+            shape_of((1, channels), f32),
+        ),
+        (message, gain, swap),
+        16,
+        flops=2 * ranks * positions * channels * channels,
+        moved=ranks * positions * (width + 2 * channels) * 2,
+    )
+    main_args = (me, mine, *other_kernels, normed, grads, low, high, gain, swap)
     sizes = (seq_blocks, dp_blocks, seq_ranks, dp_ranks)
     shifted, kernel, gelus, outgoing = called(
         lambda *refs: main_body(sizes, *refs),
         (
-            shape_of((strands, long, taps * LANES), bf16),
+            shape_of((strands, span, taps * LANES), bf16),
             shape_of((taps * LANES, channels), bf16),
             shape_of((strands, span, LANES), bf16),
             shape_of((owners, part + EXTRA, rows), bf16),
         ),
         main_args,
+        32,
         scratch=[
             pltpu.VMEM((blocks, ranks, part, rows), bf16),
             pltpu.VMEM((long, taps * LANES), f32),
+            pltpu.VMEM((long, LANES), f32),
             pltpu.VMEM((wide, LANES), f32),
             pltpu.VMEM((wide, LANES), f32),
             pltpu.VMEM((taps * LANES, channels), f32),
         ],
         specs=[SMEM] + [VMEM] * (len(main_args) - 1),
-        flops=4 * strands * long * taps * LANES * channels,
+        flops=4 * strands * span * taps * LANES * channels,
     )
     terms = lax.all_to_all(outgoing, EVERY, 0, 0, tiled=True)
-    back = called(
+    core = dp_ranks
+    masks = chip_masks(ranks, core)
+    halves = shape_of((len(masks), positions, width), bf16)
+    own, cross = called(
         input_gradient,
-        tuple(shape_of((positions, width), bf16) for _ in range(ranks)),
+        (halves, halves),
         (rank, shifted, kernel, swap, gain, swapped_gain, gelus),
+        16,
         scratch=[pltpu.VMEM((dp_ranks, span, channels), bf16)],
         specs=[SMEM] + [VMEM] * 6,
         flops=2 * strands * span * taps * LANES * channels,
     )
-    returned = [back[0]] + [
-        lax.ppermute(back[mask], RANK, flipped_pairs(ranks, mask)) for mask in range(1, ranks)
-    ]
+    crossed = lax.ppermute(cross, RANK, flipped_pairs(ranks, core))
+    leaving = called(
+        lambda *refs: chip_sum(part, *refs),
+        tuple(shape_of((positions, channels + 4 * part), bf16) for _ in masks),
+        (own, crossed),
+        8,
+    )
+    arrived = leaving[:1] + tuple(
+        lax.ppermute(block, RANK, flipped_pairs(ranks, mask))
+        for block, mask in zip(leaving[1:], masks[1:])
+    )
     combined, grad_input = called(
-        finish,
+        lambda *refs: finish(part, core, *refs),
         (shape_of((positions, channels), bf16), shape_of((positions, channels), bf16)),
-        (rank, values, cot, plain_map, other_map, *returned),
+        (rank, values, cot, plain_map, other_map, *arrived),
+        16,
         scratch=[pltpu.VMEM((2, ranks, positions, LANES), bf16)],
-        specs=[SMEM] + [VMEM] * (4 + ranks),
+        specs=[SMEM] + [VMEM] * (4 + len(arrived)),
     )
     summed = terms.reshape(seq_blocks, seq_ranks, dp_blocks, dp_ranks, -1, rows).astype(f32).sum((0, 2))
     summed = summed.reshape(ranks, -1, rows)

time: 126 us -> 107 us (0.85)
  Pallas kernels: 26.9 us -> 18.3 us
  waiting for transfers between devices: 45.5 us -> 39 us
  starting transfers between devices: 33.1 us -> 28.2 us
  other arithmetic: 2.44 us -> 4.82 us
    pallas_call x5 -> x6, Pallas kernels: 26.9 us -> 18.3 us  [called(): pl.pallas_call(body, out_shape=outs, in_specs=specs or [VMEM] * len(args)...]
    gather x2 -> x0, local copies, waits for them, and re-layouts: 7.72 us -> none  [the longest x1 4.53 us: per_device(): other_map = ((channel_list == pairing[channel_of]) & inside).astype(bf16)]
    unnamed x25 -> x31, local copies, waits for them, and re-layouts: 5.84 us -> 12.9 us
    ppermute x7 -> x4, starting transfers between devices: 8.46 us -> 3.63 us  [the longest x3 3.55 us: per_device(): lax.ppermute(block, RANK, flipped_pairs(ranks, mask))]
    ppermute x1, waiting for transfers between devices: 3.96 us -> 0.01 us  [per_device(): high = lax.ppermute(by_seq[0, :, :HALO], 'seq_block', backward)]
    ppermute x7 -> x4, waiting for transfers between devices: 21.2 us -> 17.5 us  [the longest x3 14.8 us: per_device(): lax.ppermute(block, RANK, flipped_pairs(ranks, mask))]
    all_to_all x1, waiting for transfers between devices: 0.01 us -> 1.8 us  [per_device(): lax.all_to_all(weights.T.reshape(ranks, part, rows), RANK, 0, 0, tiled=True)]
  transfers between devices with their start and end apart: 15 -> 12, of which waited for: 6 -> 6; matrix products, arithmetic and copies ran while one was open for 9% -> 4% of each run, Pallas kernels for 13% -> 10%
where the time goes in v4:
time: 107 us
  waiting for transfers between devices  39 us (36%)
  starting transfers between devices  28.2 us (26%)
  Pallas kernels  18.3 us (17%)
  local copies, waits for them, and re-layouts  15.6 us (15%)
  other arithmetic  4.82 us (5%)
    all_to_all x1, waiting for transfers between devices, per_device(): message = lax.all_to_all(message, RANK, 0, 0, tiled=True)  19.7 us
    pallas_call x6, Pallas kernels, called(): pl.pallas_call(body, out_shape=outs, in_specs=specs or [VMEM] * len(args)...  18.3 us
    ppermute x3, waiting for transfers between devices, per_device(): lax.ppermute(block, RANK, flipped_pairs(ranks, mask))  14.8 us
    unnamed x31, local copies, waits for them, and re-layouts  12.9 us
    all_to_all x1, starting transfers between devices, per_device(): lax.all_to_all(weights.T.reshape(ranks, part, rows), RANK, 0, 0, tiled=True)  5.17 us
    ppermute x3, starting transfers between devices, per_device(): lax.ppermute(mine, BLOCK, shifted_pairs(blocks, shift))  4.81 us
    ppermute x1, starting transfers between devices, per_device(): low = lax.ppermute(by_seq[-1, :, -HALO:], 'seq_block', forward)  4.55 us
    all_to_all x1, starting transfers between devices, per_device(): message = lax.all_to_all(message, RANK, 0, 0, tiled=True)  4.35 us
  transfers between devices with their start and end apart: 12, of which 6 were waited for; matrix products, arithmetic and copies ran while one was open for 4% of the time, Pallas kernels for 10%

profile of v4, /device:TPU:0, one launch (start us, length us, event | category | flops | bytes accessed | tf_op | source)
XLA Modules:
  0.0 106.7 jit_solution(776322942084545471)
XLA Ops:
  0.7 1.8 %copy.10 = bf16[768,120]{1,0:T(8,128)(2,1)} copy(bf16[768,120]{0,1:T(8,128)(2,1)} %bitcast.26) | data formatting | bytes 368640 | tf_op jit(solution)/shard_map/transpose | solution.py:277
  2.4 5.2 %all-to-all-start = ((bf16[8,96,120]{2,1,0:T(8,128)(2,1)}), bf16[8,96,120]{2,1,0:T(8,128)(2,1)}, u32[]{:S(2)}, u32[]{:S(2)}) async-start(bf16[8,96,120]{2,1,0:T(8,128)(2,1)} %bitcast.5), calls=%async_computation | async-start | bytes 393216 | tf_op jit(solution)/shard_map/all_to_all | solution.py:277
  7.6 1.6 %compare_convert_fusion = (bf16[768,1024]{1,0:T(8,128)(2,1)S(1)}, bf16[768,1024]{1,0:T(8,128)(2,1)S(1)}) fusion(s32[1024]{0:T(1024)S(1)} %fusion.10, s32[768]{0:T(1024)} %param.9), kind=kLoop, calls=%fused_computation.2 | loop fusion | flops 3145728 | bytes 3152896 | tf_op jit(solution)/shard_map/convert_element_type | solution.py:285
  9.2 0.6 shard_map.84
  9.9 1.4 %copy-done = bf16[8,128,1024]{2,1,0:T(8,128)(2,1)} copy-done((bf16[8,128,1024]{2,1,0:T(8,128)(2,1)}, bf16[8,128,1024]{2,1,0:T(8,128)(2,1)S(1)}, u32[]{:S(2)}) %copy-start) | copy-done | bytes 2097176
  11.2 1.8 %all-to-all-done.refs_1_ = bf16[8,96,120]{2,1,0:T(8,128)(2,1)} async-done(((bf16[8,96,120]{2,1,0:T(8,128)(2,1)}), bf16[8,96,120]{2,1,0:T(8,128)(2,1)}, u32[]{:S(2)}, u32[]{:S(2)}) %all-to-all-start) | async-done | bytes 184352 | tf_op jit(solution)/shard_map/all_to_all | solution.py:277
  13.0 4.4 %all-to-all-start.1 = ((bf16[8,128,1024]{2,1,0:T(8,128)(2,1)}), bf16[8,128,1024]{2,1,0:T(8,128)(2,1)}, u32[]{:S(2)}, u32[]{:S(2)}) async-start(bf16[8,128,1024]{2,1,0:T(8,128)(2,1)} %copy-done), calls=%async_computation.1 | async-start | bytes 4194304 | tf_op jit(solution)/shard_map/all_to_all | solution.py:294
  17.4 0.0 copy-done.14
  17.4 1.3 %fusion.1.swap_ref.refs_10_ = bf16[768,768]{1,0:T(8,128)(2,1)} fusion(s32[768]{0:T(1024)S(1)} %copy-done.13), kind=kLoop, calls=%fused_computation.4 | loop fusion | flops 1179648 | bytes 1182720 | tf_op jit(solution)/shard_map/convert_element_type | solution.py:286
  18.7 3.8 %collective-permute-start.2 = (bf16[8,96,120]{2,1,0:T(8,128)(2,1)}, bf16[8,96,120]{2,1,0:T(8,128)(2,1)}, u32[]{:S(2)}, u32[]{:S(2)}) collective-permute-start(bf16[8,96,120]{2,1,0:T(8,128)(2,1)} %all-to-all-done.refs_1_), channel_id=1, source_target_pairs={{0,24},{8,0},{16,8},{24,16},{1,25},{9,1},{17,9},{25,17},{2,26},{10... | collective-permute-start | bytes 552968 | tf_op jit(solution)/shard_map/ppermute | solution.py:279
  22.5 0.0 collective-permute-start.1
  22.5 1.0 collective-permute-start
  23.5 19.7 %all-to-all-done.1.message_ref = bf16[8,128,1024]{2,1,0:T(8,128)(2,1)} async-done(((bf16[8,128,1024]{2,1,0:T(8,128)(2,1)}), bf16[8,128,1024]{2,1,0:T(8,128)(2,1)}, u32[]{:S(2)}, u32[]{:S(2)}) %all-to-all-start.1) | async-done | bytes 2097184 | tf_op jit(solution)/shard_map/all_to_all | solution.py:294
  43.2 0.9 slice_bitcast_fusion
  44.1 1.3 %collective-permute-start.4 = (bf16[2,16,1024]{2,1,0:T(8,128)(2,1)S(1)}, bf16[2,16,1024]{2,1,0:T(8,128)(2,1)S(1)}, u32[]{:S(2)}, u32[]{:S(2)}) collective-permute-start(bf16[2,16,1024]{2,1,0:T(8,128)(2,1)S(1)} %get-tuple-element.38), channel_id=1, source_target_pairs={{8,0},{16,8},{24,16},{9,1},{17,9},{25,17},{10,2},{18,10},{26,18},{... | collective-permute-start | bytes 196616 | tf_op jit(solution)/shard_map/ppermute | solution.py:299
  45.4 4.5 %collective-permute-start.3 = (bf16[2,16,1024]{2,1,0:T(8,128)(2,1)S(1)}, bf16[2,16,1024]{2,1,0:T(8,128)(2,1)S(1)}, u32[]{:S(2)}, u32[]{:S(2)}) collective-permute-start(bf16[2,16,1024]{2,1,0:T(8,128)(2,1)S(1)} %get-tuple-element.39), channel_id=1, source_target_pairs={{0,8},{8,16},{16,24},{1,9},{9,17},{17,25},{2,10},{10,18},{18,26},{... | collective-permute-start | bytes 196616 | tf_op jit(solution)/shard_map/ppermute | solution.py:298
  49.9 1.3 %copy-done.1 = bf16[768,768]{1,0:T(8,128)(2,1)S(1)} copy-done((bf16[768,768]{1,0:T(8,128)(2,1)S(1)}, bf16[768,768]{1,0:T(8,128)(2,1)}, u32[]{:S(2)}) %copy-start.1) | copy-done | bytes 1179672
  51.2 3.4 %shard_map.85 = (bf16[4,512,768]{2,1,0:T(8,128)(2,1)S(1)}, bf16[4,512,128]{2,1,0:T(8,128)(2,1)S(1)}, f32[1,768]{1,0:T(1,128)S(1)}) custom-call(bf16[8,128,1024]{2,1,0:T(8,128)(2,1)} %all-to-all-done.1.message_ref, f32[1,768]{1,0:T(1,128)S(1)} %reshape.73.gain_ref.refs_9_, bf16[768,768]{1,0:T(8,128)(2,1)S(1)} %copy-done.1), custom_call_target="tpu_custom_call" | custom-call | flops 1207959552 | bytes 5242880 | tf_op jit(solution)/shard_map/pallas_call | solution.py:22
  54.6 0.0 collective-permute-done.2.refs_4_
  54.6 0.0 collective-permute-done.1.refs_3_
  54.6 0.0 collective-permute-done.refs_2_
  54.6 0.0 collective-permute-done.4.refs_8_
  54.6 0.0 collective-permute-done.3.refs_7_
  54.6 7.9 %shard_map.86 = (bf16[4,512,640]{2,1,0:T(8,128)(2,1)S(1)}, bf16[640,768]{1,0:T(8,128)(2,1)S(1)}, bf16[4,512,128]{2,1,0:T(8,128)(2,1)S(1)}, bf16[32,112,120]{2,1,0:T(8,128)(2,1)S(1)}) custom-call(s32[1]{0:T(128)} %bitcast.3.refs_0_, bf16[8,96,120]{2,1,0:T(8,128)(2,1)} %all-to-all-done.refs_1_, bf16[8,96,120]{2,1,0:T(8,128)(2,1)} %collective-permute-done.refs_2_, ...), custom_call_target="tpu_custom_call" | custom-call | flops 4026531840 | tf_op jit(solution)/shard_map/pallas_call | solution.py:22
  62.5 0.9 copy-done.4
  63.4 1.5 %copy-done.7 = bf16[4,512,640]{2,1,0:T(8,128)(2,1)} copy-done((bf16[4,512,640]{2,1,0:T(8,128)(2,1)}, bf16[4,512,640]{2,1,0:T(8,128)(2,1)S(1)}, u32[]{:S(2)}) %copy-start.7) | copy-done | bytes 2621464
  64.9 0.9 copy-done.9
  65.9 0.8 copy-done.11
  66.7 4.3 %all-to-all-start.2 = ((bf16[32,112,120]{2,1,0:T(8,128)(2,1)}), bf16[32,112,120]{2,1,0:T(8,128)(2,1)}, u32[]{:S(2)}, u32[]{:S(2)}) async-start(bf16[32,112,120]{2,1,0:T(8,128)(2,1)} %copy-done.4), calls=%async_computation.2 | async-start | bytes 1835008 | tf_op jit(solution)/shard_map/all_to_all | solution.py:335
  71.0 1.3 %copy-done.3 = bf16[768,768]{1,0:T(8,128)(2,1)S(1)} copy-done((bf16[768,768]{1,0:T(8,128)(2,1)S(1)}, bf16[768,768]{1,0:T(8,128)(2,1)}, u32[]{:S(2)}) %copy-start.3) | copy-done | bytes 1179672
  72.3 1.7 %copy-done.8 = bf16[4,512,640]{2,1,0:T(8,128)(2,1)S(1)} copy-done((bf16[4,512,640]{2,1,0:T(8,128)(2,1)S(1)}, bf16[4,512,640]{2,1,0:T(8,128)(2,1)}, u32[]{:S(2)}) %copy-start.8) | copy-done | bytes 2621464
  74.1 1.2 %copy-done.10 = bf16[640,768]{1,0:T(8,128)(2,1)S(1)} copy-done((bf16[640,768]{1,0:T(8,128)(2,1)S(1)}, bf16[640,768]{1,0:T(8,128)(2,1)}, u32[]{:S(2)}) %copy-start.10) | copy-done | bytes 983064
  75.3 1.0 copy-done.12
  76.3 3.6 %shard_map.87 = (bf16[4,128,1024]{2,1,0:T(8,128)(2,1)S(1)}, bf16[4,128,1024]{2,1,0:T(8,128)(2,1)S(1)}) custom-call(s32[1]{0:T(128)} %bitcast.rank_ref.refs_0_, bf16[4,512,640]{2,1,0:T(8,128)(2,1)S(1)} %copy-done.8, bf16[640,768]{1,0:T(8,128)(2,1)S(1)} %copy-done.10, bf16[768,768]{1,0:T(8,128)(2,1)S(1)} %copy-done.3, f32[1,768]{1,0:T(1,128)S(1)} %reshape.73.gain_ref.refs_9_, ...), custom_call_target="tpu_custom_call" | custom-call | flops 2013265920 | tf_op jit(solution)/shard_map/pallas_call | solution.py:22
  79.9 0.1 collective-permute-start.5
  80.0 2.6 %collective-permute-done.5.refs_1_ = bf16[4,128,1024]{2,1,0:T(8,128)(2,1)S(1)} collective-permute-done((bf16[4,128,1024]{2,1,0:T(8,128)(2,1)S(1)}, bf16[4,128,1024]{2,1,0:T(8,128)(2,1)S(1)}, u32[]{:S(2)}, u32[]{:S(2)}) %collective-permute-start.5) | collective-permute-done | bytes 1048608 | tf_op jit(solution)/shard_map/ppermute | solution.py:348
  82.7 0.5 shard_map.88
  83.2 1.6 %collective-permute-start.6 = (bf16[128,1152]{1,0:T(8,128)(2,1)S(1)}, bf16[128,1152]{1,0:T(8,128)(2,1)S(1)}, u32[]{:S(2)}, u32[]{:S(2)}) collective-permute-start(bf16[128,1152]{1,0:T(8,128)(2,1)S(1)} %get-tuple-element.28), channel_id=1, source_target_pairs={{0,1},{1,0},{2,3},{3,2},{4,5},{5,4},{6,7},{7,6},{8,9},{9,8},{10,11... | collective-permute-start | bytes 884744 | tf_op jit(solution)/shard_map/ppermute | solution.py:356
  84.8 1.5 %collective-permute-start.7 = (bf16[128,1152]{1,0:T(8,128)(2,1)S(1)}, bf16[128,1152]{1,0:T(8,128)(2,1)S(1)}, u32[]{:S(2)}, u32[]{:S(2)}) collective-permute-start(bf16[128,1152]{1,0:T(8,128)(2,1)S(1)} %get-tuple-element.29), channel_id=1, source_target_pairs={{0,4},{1,5},{2,6},{3,7},{4,0},{5,1},{6,2},{7,3},{8,12},{9,13},{10,... | collective-permute-start | bytes 884744 | tf_op jit(solution)/shard_map/ppermute | solution.py:356
  86.2 0.5 collective-permute-start.8
  86.7 8.1 %collective-permute-done.6.refs_6_ = bf16[128,1152]{1,0:T(8,128)(2,1)S(1)} collective-permute-done((bf16[128,1152]{1,0:T(8,128)(2,1)S(1)}, bf16[128,1152]{1,0:T(8,128)(2,1)S(1)}, u32[]{:S(2)}, u32[]{:S(2)}) %collective-permute-start.6) | collective-permute-done | bytes 294944 | tf_op jit(solution)/shard_map/ppermute | solution.py:356
  94.8 1.4 %collective-permute-done.7.refs_7_ = bf16[128,1152]{1,0:T(8,128)(2,1)S(1)} collective-permute-done((bf16[128,1152]{1,0:T(8,128)(2,1)S(1)}, bf16[128,1152]{1,0:T(8,128)(2,1)S(1)}, u32[]{:S(2)}, u32[]{:S(2)}) %collective-permute-start.7) | collective-permute-done | bytes 294944 | tf_op jit(solution)/shard_map/ppermute | solution.py:356
  96.2 5.4 %collective-permute-done.8.refs_8_ = bf16[128,1152]{1,0:T(8,128)(2,1)S(1)} collective-permute-done((bf16[128,1152]{1,0:T(8,128)(2,1)S(1)}, bf16[128,1152]{1,0:T(8,128)(2,1)S(1)}, u32[]{:S(2)}, u32[]{:S(2)}) %collective-permute-start.8) | collective-permute-done | bytes 294944 | tf_op jit(solution)/shard_map/ppermute | solution.py:356
  101.6 2.3 %shard_map.89 = (bf16[128,768]{1,0:T(8,128)(2,1)}, bf16[128,768]{1,0:T(8,128)(2,1)}) custom-call(s32[1]{0:T(128)} %bitcast.rank_ref.refs_0_, bf16[128,768]{1,0:T(8,128)(2,1)S(1)} %bitcast.20, bf16[128,768]{1,0:T(8,128)(2,1)S(1)} %bitcast.22, bf16[768,1024]{1,0:T(8,128)(2,1)S(1)} %get-tuple-element.41.plain_ref.refs_3_, ...), custom_call_target="tpu_custom_call" | custom-call | tf_op jit(solution)/shard_map/pallas_call | solution.py:22
  103.8 0.0 all-to-all-done.2
  103.8 1.4 %convert_reduce_fusion = f32[4,2,112,120]{3,2,1,0:T(8,128)S(1)} fusion(bf16[4,4,2,112,120]{4,3,2,1,0:T(8,128)(2,1)} %bitcast.15), kind=kLoop, calls=%fused_computation.5 | loop fusion | flops 752640 | bytes 1290240 | tf_op jit(solution)/shard_map/reduce_sum | solution.py:367
  105.3 0.5 slice_reduce_fusion
  105.8 0.9 copy.11
  (22 shorter events, 0.1 us)
Async XLA Ops:
  0.6 8.6 %copy-start.6 = (bf16[1,128,768]{2,1,0:T(8,128)(2,1)S(1)}, bf16[1,128,768]{2,1,0:T(8,128)(2,1)}, u32[]{:S(2)}) copy-start(bf16[1,128,768]{2,1,0:T(8,128)(2,1)} %param.6) | copy-start | bytes 589828
  0.6 8.6 %copy-start.5 = (bf16[1,128,768]{2,1,0:T(8,128)(2,1)S(1)}, bf16[1,128,768]{2,1,0:T(8,128)(2,1)}, u32[]{:S(2)}) copy-start(bf16[1,128,768]{2,1,0:T(8,128)(2,1)} %param.5) | copy-start | bytes 589828
  2.4 10.6 %all-to-all-start = ((bf16[8,96,120]{2,1,0:T(8,128)(2,1)}), bf16[8,96,120]{2,1,0:T(8,128)(2,1)}, u32[]{:S(2)}, u32[]{:S(2)}) async-start(bf16[8,96,120]{2,1,0:T(8,128)(2,1)} %bitcast.5), calls=%async_computation | async-start | bytes 393216 | tf_op jit(solution)/shard_map/all_to_all | solution.py:277
  9.9 1.4 %copy-start = (bf16[8,128,1024]{2,1,0:T(8,128)(2,1)}, bf16[8,128,1024]{2,1,0:T(8,128)(2,1)S(1)}, u32[]{:S(2)}) copy-start(bf16[8,128,1024]{2,1,0:T(8,128)(2,1)S(1)} %shard_map.84) | copy-start | bytes 6291460
  11.2 6.2 %copy-start.14 = (f32[768]{0:T(1024)S(1)}, f32[768]{0:T(1024)}, u32[]{:S(2)}) copy-start(f32[768]{0:T(1024)} %param.8) | copy-start | bytes 9220
  11.2 6.2 %copy-start.13 = (s32[768]{0:T(1024)S(1)}, s32[768]{0:T(1024)}, u32[]{:S(2)}) copy-start(s32[768]{0:T(1024)} %param.9) | copy-start | bytes 9220
  13.0 30.1 %all-to-all-start.1 = ((bf16[8,128,1024]{2,1,0:T(8,128)(2,1)}), bf16[8,128,1024]{2,1,0:T(8,128)(2,1)}, u32[]{:S(2)}, u32[]{:S(2)}) async-start(bf16[8,128,1024]{2,1,0:T(8,128)(2,1)} %copy-done), calls=%async_computation.1 | async-start | bytes 4194304 | tf_op jit(solution)/shard_map/all_to_all | solution.py:294
  18.7 35.9 %collective-permute-start.2 = (bf16[8,96,120]{2,1,0:T(8,128)(2,1)}, bf16[8,96,120]{2,1,0:T(8,128)(2,1)}, u32[]{:S(2)}, u32[]{:S(2)}) collective-permute-start(bf16[8,96,120]{2,1,0:T(8,128)(2,1)} %all-to-all-done.refs_1_), channel_id=1, source_target_pairs={{0,24},{8,0},{16,8},{24,16},{1,25},{9,1},{17,9},{25,17},{2,26},{10... | collective-permute-start | bytes 552968 | tf_op jit(solution)/shard_map/ppermute | solution.py:279
  22.5 32.1 %collective-permute-start.1 = (bf16[8,96,120]{2,1,0:T(8,128)(2,1)}, bf16[8,96,120]{2,1,0:T(8,128)(2,1)}, u32[]{:S(2)}, u32[]{:S(2)}) collective-permute-start(bf16[8,96,120]{2,1,0:T(8,128)(2,1)} %all-to-all-done.refs_1_), channel_id=1, source_target_pairs={{0,16},{8,24},{16,0},{24,8},{1,17},{9,25},{17,1},{25,9},{2,18},{10... | collective-permute-start | bytes 552968 | tf_op jit(solution)/shard_map/ppermute | solution.py:279
  22.5 32.1 %collective-permute-start = (bf16[8,96,120]{2,1,0:T(8,128)(2,1)}, bf16[8,96,120]{2,1,0:T(8,128)(2,1)}, u32[]{:S(2)}, u32[]{:S(2)}) collective-permute-start(bf16[8,96,120]{2,1,0:T(8,128)(2,1)} %all-to-all-done.refs_1_), channel_id=1, source_target_pairs={{0,8},{8,16},{16,24},{24,0},{1,9},{9,17},{17,25},{25,1},{2,10},{10... | collective-permute-start | bytes 552968 | tf_op jit(solution)/shard_map/ppermute | solution.py:279
  44.1 10.5 %collective-permute-start.4 = (bf16[2,16,1024]{2,1,0:T(8,128)(2,1)S(1)}, bf16[2,16,1024]{2,1,0:T(8,128)(2,1)S(1)}, u32[]{:S(2)}, u32[]{:S(2)}) collective-permute-start(bf16[2,16,1024]{2,1,0:T(8,128)(2,1)S(1)} %get-tuple-element.38), channel_id=1, source_target_pairs={{8,0},{16,8},{24,16},{9,1},{17,9},{25,17},{10,2},{18,10},{26,18},{... | collective-permute-start | bytes 196616 | tf_op jit(solution)/shard_map/ppermute | solution.py:299
  45.4 9.2 %collective-permute-start.3 = (bf16[2,16,1024]{2,1,0:T(8,128)(2,1)S(1)}, bf16[2,16,1024]{2,1,0:T(8,128)(2,1)S(1)}, u32[]{:S(2)}, u32[]{:S(2)}) collective-permute-start(bf16[2,16,1024]{2,1,0:T(8,128)(2,1)S(1)} %get-tuple-element.39), channel_id=1, source_target_pairs={{0,8},{8,16},{16,24},{1,9},{9,17},{17,25},{2,10},{10,18},{18,26},{... | collective-permute-start | bytes 196616 | tf_op jit(solution)/shard_map/ppermute | solution.py:298
  49.9 1.3 %copy-start.1 = (bf16[768,768]{1,0:T(8,128)(2,1)S(1)}, bf16[768,768]{1,0:T(8,128)(2,1)}, u32[]{:S(2)}) copy-start(bf16[768,768]{1,0:T(8,128)(2,1)} %fusion.1.swap_ref.refs_10_) | copy-start | bytes 3538948
  51.2 3.4 %copy-start.2 = (bf16[768,768]{1,0:T(8,128)(2,1)S(1)}, bf16[768,768]{1,0:T(8,128)(2,1)}, u32[]{:S(2)}) copy-start(bf16[768,768]{1,0:T(8,128)(2,1)} %fusion.1.swap_ref.refs_10_) | copy-start | bytes 3538948
  62.5 0.9 copy-start.4
  63.4 1.5 %copy-start.7 = (bf16[4,512,640]{2,1,0:T(8,128)(2,1)}, bf16[4,512,640]{2,1,0:T(8,128)(2,1)S(1)}, u32[]{:S(2)}) copy-start(bf16[4,512,640]{2,1,0:T(8,128)(2,1)S(1)} %get-tuple-element.21.shifted_ref) | copy-start | bytes 7864324
  64.9 0.9 copy-start.9
  65.9 0.8 copy-start.11
  66.7 37.2 %all-to-all-start.2 = ((bf16[32,112,120]{2,1,0:T(8,128)(2,1)}), bf16[32,112,120]{2,1,0:T(8,128)(2,1)}, u32[]{:S(2)}, u32[]{:S(2)}) async-start(bf16[32,112,120]{2,1,0:T(8,128)(2,1)} %copy-done.4), calls=%async_computation.2 | async-start | bytes 1835008 | tf_op jit(solution)/shard_map/all_to_all | solution.py:335
  71.0 1.3 %copy-start.3 = (bf16[768,768]{1,0:T(8,128)(2,1)S(1)}, bf16[768,768]{1,0:T(8,128)(2,1)}, u32[]{:S(2)}) copy-start(bf16[768,768]{1,0:T(8,128)(2,1)} %fusion.1.swap_ref.refs_10_) | copy-start | bytes 3538948
  72.3 1.7 %copy-start.8 = (bf16[4,512,640]{2,1,0:T(8,128)(2,1)S(1)}, bf16[4,512,640]{2,1,0:T(8,128)(2,1)}, u32[]{:S(2)}) copy-start(bf16[4,512,640]{2,1,0:T(8,128)(2,1)} %copy-done.7) | copy-start | bytes 7864324
  74.0 1.2 %copy-start.10 = (bf16[640,768]{1,0:T(8,128)(2,1)S(1)}, bf16[640,768]{1,0:T(8,128)(2,1)}, u32[]{:S(2)}) copy-start(bf16[640,768]{1,0:T(8,128)(2,1)} %copy-done.9) | copy-start | bytes 2949124
  75.3 1.0 copy-start.12
  79.9 2.7 %collective-permute-start.5 = (bf16[4,128,1024]{2,1,0:T(8,128)(2,1)S(1)}, bf16[4,128,1024]{2,1,0:T(8,128)(2,1)S(1)}, u32[]{:S(2)}, u32[]{:S(2)}) collective-permute-start(bf16[4,128,1024]{2,1,0:T(8,128)(2,1)S(1)} %get-tuple-element.26), channel_id=1, source_target_pairs={{0,2},{1,3},{2,0},{3,1},{4,6},{5,7},{6,4},{7,5},{8,10},{9,11},{10,... | collective-permute-start | bytes 3145736 | tf_op jit(solution)/shard_map/ppermute | solution.py:348
  83.2 11.7 %collective-permute-start.6 = (bf16[128,1152]{1,0:T(8,128)(2,1)S(1)}, bf16[128,1152]{1,0:T(8,128)(2,1)S(1)}, u32[]{:S(2)}, u32[]{:S(2)}) collective-permute-start(bf16[128,1152]{1,0:T(8,128)(2,1)S(1)} %get-tuple-element.28), channel_id=1, source_target_pairs={{0,1},{1,0},{2,3},{3,2},{4,5},{5,4},{6,7},{7,6},{8,9},{9,8},{10,11... | collective-permute-start | bytes 884744 | tf_op jit(solution)/shard_map/ppermute | solution.py:356
  84.8 11.4 %collective-permute-start.7 = (bf16[128,1152]{1,0:T(8,128)(2,1)S(1)}, bf16[128,1152]{1,0:T(8,128)(2,1)S(1)}, u32[]{:S(2)}, u32[]{:S(2)}) collective-permute-start(bf16[128,1152]{1,0:T(8,128)(2,1)S(1)} %get-tuple-element.29), channel_id=1, source_target_pairs={{0,4},{1,5},{2,6},{3,7},{4,0},{5,1},{6,2},{7,3},{8,12},{9,13},{10,... | collective-permute-start | bytes 884744 | tf_op jit(solution)/shard_map/ppermute | solution.py:356
  86.2 15.3 %collective-permute-start.8 = (bf16[128,1152]{1,0:T(8,128)(2,1)S(1)}, bf16[128,1152]{1,0:T(8,128)(2,1)S(1)}, u32[]{:S(2)}, u32[]{:S(2)}) collective-permute-start(bf16[128,1152]{1,0:T(8,128)(2,1)S(1)} %get-tuple-element.30), channel_id=1, source_target_pairs={{0,5},{1,4},{2,7},{3,6},{4,1},{5,0},{6,3},{7,2},{8,13},{9,12},{10,... | collective-permute-start | bytes 884744 | tf_op jit(solution)/shard_map/ppermute | solution.py:356

commit v5 on v4

v5 whole, which is shorter than its diff:
```python
import jax
import jax.numpy as jnp
from jax import lax
from jax.experimental import pallas as pl
from jax.experimental.pallas import tpu as pltpu
from jax.sharding import Mesh, PartitionSpec as P

epsilon = 1e-06
RANK = ("seq_rank", "dp_rank")
BLOCK = ("seq_block", "dp_block")
EVERY = ("seq_block", "seq_rank", "dp_block", "dp_rank")
LANES = 128
HALO = 16
EXTRA = 16
VMEM = pl.BlockSpec(memory_space=pltpu.VMEM)
SMEM = pl.BlockSpec(memory_space=pltpu.SMEM)
bf16 = jnp.bfloat16
f32 = jnp.float32


def called(body, outs, args, vmem, scratch=(), specs=None, flops=0, moved=0):
    return pl.pallas_call(
        body,
        out_shape=outs,
        in_specs=specs or [VMEM] * len(args),
        out_specs=jax.tree.map(lambda _: VMEM, outs),
        scratch_shapes=list(scratch),
        compiler_params=pltpu.CompilerParams(vmem_limit_bytes=vmem * 2**20),
        cost_estimate=pl.CostEstimate(flops=flops, bytes_accessed=moved, transcendentals=0),
    )(*args)


def shape_of(shape, dtype):
    return jax.ShapeDtypeStruct(shape, dtype)


def dot(a, b, contract):
    return lax.dot_general(a, b, (contract, ((), ())), preferred_element_type=f32)


def gelu_and_slope(x):
    inner = 0.7978845608028654 * (x + 0.044715 * (x * x * x))
    bend = jnp.tanh(inner)
    half_sum = 0.5 * (1.0 + bend)
    slope = half_sum + (0.5 * x) * (1.0 - bend * bend) * (
        0.7978845608028654 * (1.0 + 0.134145 * (x * x))
    )
    return x * half_sum, slope


def chip_masks(ranks, core):
    return [mask for mask in range(ranks) if not mask & core]


def pack_messages(core, rank_ref, values_ref, cot_ref, edge_ref, plain_ref, other_ref, *refs):
    home_ref, cross_ref, leaving, slices = refs[0], refs[1], refs[2:-1], refs[-1]
    positions, channels = values_ref.shape
    ranks = slices.shape[0]
    here, edge = slice(0, positions), slice(positions, None)
    for rows, source in ((here, cot_ref[...]), (edge, edge_ref[:, channels:])):
        for n, ref in enumerate((plain_ref, other_ref)):
            piece = dot(source, ref[...], ((1,), (0,))).astype(bf16)
            for j in range(ranks):
                slices[j, rows, n * LANES : (n + 1) * LANES] = piece[:, j * LANES : (j + 1) * LANES]
    rank = rank_ref[0]
    two = 2 * LANES
    starts = [(home_ref, 0), (cross_ref, two)] + [(out, two) for out in leaving]
    for out, start in starts:
        out[here, start : start + channels] = values_ref[...]
        out[edge, start : start + channels] = edge_ref[:, :channels]
    home_ref[:, channels:] = slices[rank]
    cross_ref[:, :two] = slices[lax.bitwise_xor(rank, core)]
    for mask, out in zip(chip_masks(ranks, core)[1:], leaving):
        out[:, :two] = slices[lax.bitwise_xor(rank, mask | core)]
        out[:, two + channels :] = slices[lax.bitwise_xor(rank, mask)]


def normalize(x, gain, swap):
    other = dot(x, swap, ((1,), (0,)))
    x = x.astype(f32)
    rms = lax.rsqrt(jnp.mean(x * x, -1, keepdims=True) + epsilon)
    return [(t * rms * gain).astype(bf16) for t in (x, other)]


def prepare(core, rank_ref, home_ref, home_crossed_ref, crossed_ref, *refs):
    arrived = refs[:-7]
    gain_ref, swap_ref, normed_ref, grads_ref, edge_normed_ref, edge_grads_ref, swapped_gain_ref = refs[-7:]
    dp_ranks = normed_ref.shape[0] // 2
    channels = gain_ref.shape[1]
    masks = chip_masks(2 * (len(arrived) + 1), core)
    seq_ranks = 2 * len(masks) // dp_ranks
    positions = home_ref.shape[0] - HALO
    two = 2 * LANES
    blocks = [(0, home_ref, 0, channels), (core, home_crossed_ref, two, 0)]
    for m, mask in enumerate(masks[1:]):
        blocks.append((mask, arrived[m], two, two + channels))
        blocks.append((mask | core, crossed_ref.at[m], two, 0))
    for flip, ref, lane, grad_lane in blocks:
        source = lax.bitwise_xor(rank_ref[0], flip)
        b, i = lax.rem(source, dp_ranks), lax.div(source, dp_ranks)
        start = pl.multiple_of(i * positions, positions)
        side = jnp.where(i == 0, 0, jnp.where(i == seq_ranks - 1, 1, 2))
        both = normalize(ref[:, lane : lane + channels], gain_ref[...], swap_ref[...])
        for n, normed in enumerate(both):
            first = grad_lane + n * LANES
            grads = (0.5 * ref[:, first : first + LANES].astype(f32)).astype(bf16)
            index = n * dp_ranks + b
            normed_ref[index, pl.ds(start, positions), :] = normed[:positions]
            grads_ref[index, pl.ds(start, positions), :] = grads[:positions]
            edge_normed_ref[side, index] = normed[positions:]
            edge_grads_ref[side, index] = grads[positions:]
    gain = gain_ref[...]
    first = gain.astype(bf16).astype(f32)
    second = (gain - first).astype(bf16).astype(f32)
    third = gain - first - second
    row = lax.broadcasted_iota(jnp.int32, (HALO, channels), 0)
    parts = jnp.where(row == 0, first, jnp.where(row == 1, second, jnp.where(row == 2, third, 0.0)))
    swapped = dot(parts.astype(bf16), swap_ref[...], ((1,), (0,)))
    swapped_gain_ref[...] = swapped[0:1] + swapped[1:2] + swapped[2:3]


def main_body(rank_ref, pieces_ref, normed_ref, grads_ref, edge_normed_ref, edge_grads_ref, *refs):
    gain_ref, swapped_gain_ref, swap_ref, out_ref, own_ref, cross_ref = refs[:6]
    kernel_ref, shifted, gelus, terms, halves, bent, slopes, total, scaled = refs[6:]
    owners, part, rows = pieces_ref.shape
    strands, span, channels = normed_ref.shape
    dp_ranks = strands // 2
    taps = kernel_ref.shape[0] // LANES
    half = taps // 2
    reach = 2 * half
    wide = bent.shape[0]

    def runs(owner):
        first, last = owner * rows, (owner + 1) * rows
        while first < last:
            tap, channel = divmod(first, channels)
            count = min(last - first, channels - channel)
            yield tap, channel, count, first - owner * rows
            first += count

    kernel_ref[...] = jnp.zeros_like(kernel_ref)
    for owner in range(owners):
        for tap, channel, count, offset in runs(owner):
            kernel_ref[tap * LANES : tap * LANES + part, channel : channel + count] = pieces_ref[
                owner, :, offset : offset + count
            ]
    kernel = kernel_ref[...]
    edge_normed = jnp.concatenate([edge_normed_ref[side, s] for side in range(2) for s in range(strands)], 0)
    edge_terms = dot(edge_normed, kernel, ((1,), (1,)))
    for strand in range(strands):
        forward = strand < dp_ranks
        terms[HALO : HALO + span, :] = dot(normed_ref[strand], kernel, ((1,), (1,)))
        halves[HALO : HALO + span, :] = grads_ref[strand].astype(f32)
        for side, start in enumerate((0, HALO + span)):
            first = (side * strands + strand) * HALO
            terms[start : start + HALO, :] = edge_terms[first : first + HALO]
            halves[start : start + HALO, :] = edge_grads_ref[side, strand].astype(f32)
        preact = jnp.zeros((wide, LANES), f32)
        for k in range(taps):
            start = HALO - reach + k if forward else HALO - k
            preact += terms[start : start + wide, k * LANES : (k + 1) * LANES]
        result, slope = gelu_and_slope(preact)
        bent[...] = result
        gelus[strand] = bent[half : half + span, :].astype(bf16)
        slopes[...] = halves[HALO - half : HALO - half + wide, :] * slope
        for k in range(taps):
            start = reach - k if forward else k
            shifted[strand, :, k * LANES : (k + 1) * LANES] = slopes[start : start + span, :].astype(bf16)
    total[...] = dot(
        shifted[...].reshape(strands * span, taps * LANES),
        normed_ref[...].reshape(strands * span, channels),
        ((0,), (0,)),
    )
    gain = jnp.sum(total[...] * kernel.astype(f32), 0, keepdims=True) / gain_ref[...]
    gain_high = gain.astype(bf16).astype(f32)
    row = lax.broadcasted_iota(jnp.int32, (EXTRA, channels), 0)
    extra = jnp.where(row == 0, gain_high, jnp.where(row == 1, gain - gain_high, 0.0))
    own_gain = channels // owners
    for owner in range(owners):
        for tap, channel, count, offset in runs(owner):
            out_ref[owner, :part, offset : offset + count] = total[
                tap * LANES : tap * LANES + part, channel : channel + count
            ].astype(bf16)
        out_ref[owner, part:, :] = jnp.zeros((EXTRA, rows), bf16)
        out_ref[owner, part:, :own_gain] = extra[
            :, owner * own_gain : (owner + 1) * own_gain
        ].astype(bf16)
    swapped = dot(kernel, swap_ref[...], ((1,), (0,))).astype(bf16)
    for b in range(dp_ranks):
        scaled[b] = (
            dot(shifted[b], kernel, ((1,), (0,))) * gain_ref[...]
            + dot(shifted[dp_ranks + b], swapped, ((1,), (0,))) * swapped_gain_ref[...]
        ).astype(bf16)
    chips, positions, _ = own_ref.shape
    for m, mask in enumerate(chip_masks(2 * chips, dp_ranks)):
        for out, flip in ((own_ref, mask), (cross_ref, mask | dp_ranks)):
            target = lax.bitwise_xor(rank_ref[0], flip)
            b = lax.rem(target, dp_ranks)
            start = pl.multiple_of(lax.div(target, dp_ranks) * positions, positions)
            out[m, :, :channels] = scaled[b, pl.ds(start, positions), :]
            for n in range(2):
                lane = channels + n * LANES
                out[m, :, lane : lane + LANES] = gelus[n * dp_ranks + b, pl.ds(start, positions), :]


def chip_sum(part, own_ref, crossed_ref, *outs):
    channels = own_ref.shape[2] - 2 * LANES
    for m, out in enumerate(outs):
        out[:, :channels] = (
            own_ref[m, :, :channels].astype(f32) + crossed_ref[m, :, :channels].astype(f32)
        ).astype(bf16)
        for c, ref in enumerate((own_ref, crossed_ref)):
            for n in range(2):
                lane = channels + n * LANES
                start = channels + (2 * c + n) * part
                out[:, start : start + part] = ref[m, :, lane : lane + part]


def finish(part, core, rank_ref, values_ref, cot_ref, plain_ref, other_ref, *refs):
    arrived, (combined_ref, grad_ref, gelus) = refs[:-3], refs[-3:]
    channels = values_ref.shape[1]
    ranks = gelus.shape[1]
    gelus[...] = jnp.zeros_like(gelus)
    scaled = jnp.zeros(values_ref.shape, f32)
    for mask, block in zip(chip_masks(ranks, core), arrived):
        scaled += block[:, :channels].astype(f32)
        for c in range(2):
            source = lax.bitwise_xor(rank_ref[0], mask | c * core)
            for n in range(2):
                start = channels + (2 * c + n) * part
                gelus[n, source, :, :part] = block[:, start : start + part]
    joined = [jnp.concatenate([gelus[n, j] for j in range(ranks)], -1) for n in range(2)]
    plain = dot(joined[0], plain_ref[...], ((1,), (1,)))
    other = dot(joined[1], other_ref[...], ((1,), (1,)))
    values = values_ref[...].astype(f32)
    rms = lax.rsqrt(jnp.mean(values * values, -1, keepdims=True) + epsilon)
    reverse_out = (values + other).astype(bf16).astype(f32)
    combined_ref[...] = (0.5 * (values + plain + reverse_out)).astype(bf16)
    along = jnp.mean(scaled * values, -1, keepdims=True)
    grad_ref[...] = (cot_ref[...].astype(f32) + rms * scaled - values * (rms * rms * rms * along)).astype(bf16)


def collect(owner_of, terms_ref, kernel_ref, gain_ref, joined):
    _, height, rows = terms_ref.shape
    part = height - EXTRA
    joined[...] = jnp.zeros_like(joined)
    gain = jnp.zeros((1, rows), f32)
    for rank, owners in enumerate(owner_of):
        total = terms_ref[owners[0]].astype(f32)
        for owner in owners[1:]:
            total += terms_ref[owner].astype(f32)
        joined[rank * part : (rank + 1) * part, :rows] = total[:part]
        gain += total[part : part + 1] + total[part + 1 : part + 2]
    kernel_ref[...] = joined[...].T[:rows]
    gain_ref[...] = gain[:, : gain_ref.shape[1]]


def flipped_pairs(count, mask):
    return [(i, i ^ mask) for i in range(count)]


def per_device(activations, cotangent, weights, norm_gain, pairing):
    seq_ranks = lax.axis_size("seq_rank")
    dp_ranks = lax.axis_size("dp_rank")
    seq_blocks = lax.axis_size("seq_block")
    dp_blocks = lax.axis_size("dp_block")
    ranks = seq_ranks * dp_ranks
    owners = ranks * seq_blocks * dp_blocks
    positions, channels = activations.shape[1:]
    rows = weights.shape[0]
    taps = rows * owners // channels
    part = channels // ranks
    span = positions * seq_ranks
    long = span + 2 * HALO
    reach = taps - taps % 2
    wide = -(-(span + reach) // 8) * 8
    strands = 2 * dp_ranks
    width = channels + 2 * LANES
    rank = lax.axis_index(RANK).reshape(1)
    values, cot = activations[0], cotangent[0]
    along = ("seq_block", "seq_rank")
    ends = [(b * seq_ranks - 1, b * seq_ranks) for b in range(1, seq_blocks)]
    both = jnp.concatenate([values, cot], -1)
    low = lax.ppermute(both[-HALO:], along, ends)
    high = lax.ppermute(both[:HALO], along, [(target, source) for source, target in ends])
    slices = weights.T.reshape(1, seq_ranks, 1, dp_ranks, part, rows)
    slices = jnp.broadcast_to(slices, (seq_blocks, seq_ranks, dp_blocks, dp_ranks, part, rows))
    pieces = lax.all_to_all(slices.reshape(owners, part, rows), EVERY, 0, 0, tiled=True)
    slot = jnp.arange(ranks * LANES, dtype=jnp.int32)
    channel_of = jnp.where(slot % LANES < part, slot // LANES * part + slot % LANES, -1)
    channel_list = jnp.arange(channels, dtype=jnp.int32)
    plain_map = (channel_list[:, None] == channel_of).astype(bf16)
    other_map = (pairing[:, None] == channel_of).astype(bf16)
    swap = (pairing[:, None] == channel_list).astype(bf16)
    gain = norm_gain.reshape(1, channels)
    core = dp_ranks
    masks = chip_masks(ranks, core)
    block = positions + HALO
    home, cross, *leaving = called(
        lambda *refs: pack_messages(core, *refs),
        (shape_of((block, width), bf16),) * 2
        + tuple(shape_of((block, width + 2 * LANES), bf16) for _ in masks[1:]),
        (rank, values, cot, low + high, plain_map, other_map),
        16,
        scratch=[pltpu.VMEM((ranks, block, 2 * LANES), bf16)],
        specs=[SMEM] + [VMEM] * 5,
    )
    arrived = [
        lax.ppermute(message, RANK, flipped_pairs(ranks, mask))
        for message, mask in zip(leaving, masks[1:])
    ]
    home_crossed = lax.ppermute(cross, RANK, flipped_pairs(ranks, core))
    crossed = lax.ppermute(
        jnp.stack([message[:, :width] for message in arrived]), RANK, flipped_pairs(ranks, core)
    )
    normed, grads, edge_normed, edge_grads, swapped_gain = called(
        lambda *refs: prepare(core, *refs),
        (
            shape_of((strands, span, channels), bf16),
            shape_of((strands, span, LANES), bf16),
            shape_of((3, strands, HALO, channels), bf16),
            shape_of((3, strands, HALO, LANES), bf16),
            shape_of((1, channels), f32),
        ),
        (rank, home, home_crossed, crossed, *arrived, gain, swap),
        16,
        specs=[SMEM] + [VMEM] * (5 + len(arrived)),
        flops=2 * ranks * positions * channels * channels,
        moved=ranks * positions * (width + 2 * channels) * 2,
    )
    sent = shape_of((len(masks), positions, width), bf16)
    outgoing, own, cross = called(
        main_body,
        (shape_of((owners, part + EXTRA, rows), bf16), sent, sent),
        (rank, pieces, normed, grads, edge_normed, edge_grads, gain, swapped_gain, swap),
        32,
        scratch=[
            pltpu.VMEM((taps * LANES, channels), bf16),
            pltpu.VMEM((strands, span, taps * LANES), bf16),
            pltpu.VMEM((strands, span, LANES), bf16),
            pltpu.VMEM((long, taps * LANES), f32),
            pltpu.VMEM((long, LANES), f32),
            pltpu.VMEM((wide, LANES), f32),
            pltpu.VMEM((wide, LANES), f32),
            pltpu.VMEM((taps * LANES, channels), f32),
            pltpu.VMEM((dp_ranks, span, channels), bf16),
        ],
        specs=[SMEM] + [VMEM] * 8,
        flops=6 * strands * span * taps * LANES * channels,
    )
    terms = lax.all_to_all(outgoing, EVERY, 0, 0, tiled=True)
    crossed = lax.ppermute(cross, RANK, flipped_pairs(ranks, core))
    leaving = called(
        lambda *refs: chip_sum(part, *refs),
        tuple(shape_of((positions, channels + 4 * part), bf16) for _ in masks),
        (own, crossed),
        8,
    )
    arrived = leaving[:1] + tuple(
        lax.ppermute(message, RANK, flipped_pairs(ranks, mask))
        for message, mask in zip(leaving[1:], masks[1:])
    )
    combined, grad_input = called(
        lambda *refs: finish(part, core, *refs),
        (shape_of((positions, channels), bf16), shape_of((positions, channels), bf16)),
        (rank, values, cot, plain_map, other_map, *arrived),
        16,
        scratch=[pltpu.VMEM((2, ranks, positions, LANES), bf16)],
        specs=[SMEM] + [VMEM] * (4 + len(arrived)),
    )
    order = [
        [
            ((sb * seq_ranks + sr) * dp_blocks + db) * dp_ranks + dr
            for sb in range(seq_blocks)
            for db in range(dp_blocks)
        ]
        for sr in range(seq_ranks)
        for dr in range(dp_ranks)
    ]
    grad_kernel, grad_gain = called(
        lambda *refs: collect(order, *refs),
        (shape_of((rows, channels), f32), shape_of((1, channels // owners), f32)),
        (terms,),
        16,
        scratch=[pltpu.VMEM((channels, -(-rows // LANES) * LANES), f32)],
    )
    return combined[None], grad_input[None], grad_kernel, grad_gain[0]


def solution(mesh):
    seq, dp = mesh.shape["seq"], mesh.shape["dp"]
    seq_ranks, dp_ranks = 4, 2
    grouped = Mesh(mesh.devices.reshape(seq // seq_ranks, seq_ranks, dp // dp_ranks, dp_ranks), EVERY)
    along = P(("dp_block", "dp_rank"), ("seq_block", "seq_rank"), None)
    return jax.shard_map(
        per_device,
        mesh=grouped,
        in_specs=(along, along, P(EVERY, None), P(), P()),
        out_specs=(along, along, P(EVERY, None), P(EVERY)),
        check_vma=False,
    )
```

time: 107 us -> 116 us (1.084)
  local copies, waits for them, and re-layouts: 15.6 us -> 22.8 us
  Pallas kernels: 18.3 us -> 20.7 us
    all_to_all x2 -> x1, waiting for transfers between devices: 21.5 us -> 0.01 us  [per_device(): lax.all_to_all(slices.reshape(owners, part, rows), EVERY, 0, 0, tiled=True)]
    ppermute x8 -> x10, waiting for transfers between devices: 14.8 us -> 36.2 us  [the longest x6 34.1 us: per_device(): lax.ppermute(message, RANK, flipped_pairs(ranks, mask))]
    unnamed x31 -> x47, local copies, waits for them, and re-layouts: 12.9 us -> 18.8 us
    pallas_call x6, Pallas kernels: 18.3 us -> 20.7 us  [called(): pl.pallas_call(body, out_shape=outs, in_specs=specs or [VMEM] * len(args)...]
    another operation x0 -> x3, local copies, waits for them, and re-layouts: none -> 1.99 us  [per_device(): jnp.stack([message[:, :width] for message in arrived])]
    broadcast_in_dim x0 -> x1, local copies, waits for them, and re-layouts: none -> 1.98 us  [per_device(): jnp.broadcast_to(slices, (seq_blocks, seq_ranks, dp_blocks, dp_ranks, par...]
    reduce_sum x2 -> x0, other arithmetic: 1.95 us -> none  [the longest x1 1.41 us: per_device(): terms.reshape(seq_blocks, seq_ranks, dp_blocks, dp_ranks, -1, rows)]
    transpose x1 -> x0, local copies, waits for them, and re-layouts: 1.79 us -> none  [per_device(): weights.T.reshape(ranks, part, rows)]
  transfers between devices with their start and end apart: 12 -> 13, of which waited for: 6 -> 6; matrix products, arithmetic and copies ran while one was open for 4% -> 7% of each run, Pallas kernels for 10% -> 5%
where the time goes in v5:
time: 116 us; the launch traced here: 115 us
  waiting for transfers between devices  38.8 us (33%)
  starting transfers between devices  27.9 us (24%)
  local copies, waits for them, and re-layouts  22.8 us (20%)
  Pallas kernels  20.7 us (18%)
  other arithmetic  4.27 us (4%)
    ppermute x6, waiting for transfers between devices, per_device(): lax.ppermute(message, RANK, flipped_pairs(ranks, mask))  34.1 us
    pallas_call x6, Pallas kernels, called(): pl.pallas_call(body, out_shape=outs, in_specs=specs or [VMEM] * len(args)...  20.7 us
    unnamed x47, local copies, waits for them, and re-layouts  18.8 us
    ppermute x6, starting transfers between devices, per_device(): lax.ppermute(message, RANK, flipped_pairs(ranks, mask))  10.5 us
    all_to_all x1, starting transfers between devices, per_device(): lax.all_to_all(slices.reshape(owners, part, rows), EVERY, 0, 0, tiled=True)  10 us
    all_to_all x1, starting transfers between devices, per_device(): terms = lax.all_to_all(outgoing, EVERY, 0, 0, tiled=True)  4.06 us
    ppermute x1, waiting for transfers between devices, per_device(): crossed = lax.ppermute(cross, RANK, flipped_pairs(ranks, core))  2.68 us
  transfers between devices with their start and end apart: 13, of which 6 were waited for; matrix products, arithmetic and copies ran while one was open for 7% of the time, Pallas kernels for 5%

profile of v5, /device:TPU:0, one launch (start us, length us, event | category | flops | bytes accessed | tf_op | source)
XLA Modules:
  0.0 115.4 jit_solution(9338224881660135479)
XLA Ops:
  0.7 1.5 %pad_maximum_fusion.1 = (bf16[16,1536]{1,0:T(8,128)(2,1)}, bf16[16,1536]{1,0:T(8,128)(2,1)}) fusion(bf16[128,768]{1,0:T(8,128)(2,1)} %bitcast.19, bf16[128,768]{1,0:T(8,128)(2,1)} %bitcast.16), kind=kLoop, calls=%fused_computation.9 | loop fusion | flops 196608 | bytes 491520 | tf_op jit(solution)/shard_map/concatenate | solution.py:283
  2.1 1.3 %collective-permute-start.1 = (bf16[16,1536]{1,0:T(8,128)(2,1)}, bf16[16,1536]{1,0:T(8,128)(2,1)}, u32[]{:S(2)}, u32[]{:S(2)}) collective-permute-start(bf16[16,1536]{1,0:T(8,128)(2,1)} %get-tuple-element.46), channel_id=1, source_target_pairs={{8,6},{16,14},{24,22},{9,7},{17,15},{25,23}} | collective-permute-start | bytes 147464 | tf_op jit(solution)/shard_map/ppermute | solution.py:285
  3.4 1.3 %collective-permute-start = (bf16[16,1536]{1,0:T(8,128)(2,1)}, bf16[16,1536]{1,0:T(8,128)(2,1)}, u32[]{:S(2)}, u32[]{:S(2)}) collective-permute-start(bf16[16,1536]{1,0:T(8,128)(2,1)} %get-tuple-element.47), channel_id=1, source_target_pairs={{6,8},{14,16},{22,24},{7,9},{15,17},{23,25}} | collective-permute-start | bytes 147464 | tf_op jit(solution)/shard_map/ppermute | solution.py:284
  4.7 1.6 %compare_convert_fusion = (bf16[768,1024]{1,0:T(8,128)(2,1)S(1)}, bf16[768,1024]{1,0:T(8,128)(2,1)S(1)}) fusion(s32[1024]{0:T(1024)S(1)} %fusion.10, s32[768]{0:T(1024)} %param.9), kind=kLoop, calls=%fused_computation.2 | loop fusion | flops 3145728 | bytes 3152896 | tf_op jit(solution)/shard_map/convert_element_type | solution.py:293
  6.3 0.8 add.41.refs_3_
  7.1 1.9 %shard_map.84 = (bf16[144,1024]{1,0:T(8,128)(2,1)S(1)}, bf16[144,1024]{1,0:T(8,128)(2,1)S(1)}, bf16[144,1280]{1,0:T(8,128)(2,1)}, bf16[144,1280]{1,0:T(8,128)(2,1)}, bf16[144,1280]{1,0:T(8,128)(2,1)S(1)}) custom-call(s32[1]{0:T(128)} %bitcast.refs_0_.rank_ref, bf16[128,768]{1,0:T(8,128)(2,1)S(1)} %bitcast.17, bf16[128,768]{1,0:T(8,128)(2,1)S(1)} %bitcast.20, ...), custom_call_target="tpu_custom_call" | custom-call | tf_op jit(solution)/shard_map/pallas_call | solution.py:22
  9.0 0.7 copy-done.8
  9.8 0.7 copy-done.9
  10.5 0.7 copy-done.11
  11.2 3.0 %collective-permute-start.3 = (bf16[144,1280]{1,0:T(8,128)(2,1)}, bf16[144,1280]{1,0:T(8,128)(2,1)}, u32[]{:S(2)}, u32[]{:S(2)}) collective-permute-start(bf16[144,1280]{1,0:T(8,128)(2,1)} %get-tuple-element.27), channel_id=1, source_target_pairs={{0,1},{1,0},{2,3},{3,2},{4,5},{5,4},{6,7},{7,6},{8,9},{9,8},{10,11... | collective-permute-start | bytes 1105928 | tf_op jit(solution)/shard_map/ppermute | solution.py:309
  14.1 1.5 %collective-permute-start.4 = (bf16[144,1280]{1,0:T(8,128)(2,1)}, bf16[144,1280]{1,0:T(8,128)(2,1)}, u32[]{:S(2)}, u32[]{:S(2)}) collective-permute-start(bf16[144,1280]{1,0:T(8,128)(2,1)} %get-tuple-element.28), channel_id=1, source_target_pairs={{0,4},{1,5},{2,6},{3,7},{4,0},{5,1},{6,2},{7,3},{8,12},{9,13},{10,... | collective-permute-start | bytes 1105928 | tf_op jit(solution)/shard_map/ppermute | solution.py:309
  15.6 1.7 %copy.10 = bf16[120,768]{0,1:T(8,128)(2,1)} copy(bf16[120,768]{1,0:T(8,128)(2,1)} %param.7) | data formatting | bytes 368640 | tf_op args[2]
  17.4 2.0 %broadcast_in_dim.11 = bf16[4,4,1,2,96,120]{5,4,3,1,0,2:T(8,128)(2,1)} broadcast(bf16[4,2,96,120]{3,2,1,0:T(8,128)(2,1)} %bitcast.23), dimensions={1,3,4,5} | broadcast | bytes 921600 | tf_op jit(solution)/shard_map/broadcast_in_dim | solution.py:287
  19.3 10.0 %all-to-all-start = ((bf16[32,96,120]{2,1,0:T(8,128)(2,1)}), bf16[32,96,120]{2,1,0:T(8,128)(2,1)}, u32[]{:S(2)}, u32[]{:S(2)}) async-start(bf16[32,96,120]{2,1,0:T(8,128)(2,1)} %bitcast.22), calls=%async_computation | async-start | bytes 1572864 | tf_op jit(solution)/shard_map/all_to_all | solution.py:288
  29.4 2.5 %collective-permute-start.5 = (bf16[144,1280]{1,0:T(8,128)(2,1)}, bf16[144,1280]{1,0:T(8,128)(2,1)S(1)}, u32[]{:S(2)}, u32[]{:S(2)}) collective-permute-start(bf16[144,1280]{1,0:T(8,128)(2,1)} %copy-done.8), channel_id=1, source_target_pairs={{0,5},{1,4},{2,7},{3,6},{4,1},{5,0},{6,3},{7,2},{8,13},{9,12},{10,... | collective-permute-start | bytes 1105928 | tf_op jit(solution)/shard_map/ppermute | solution.py:309
  31.9 1.0 slice_bitcast_fusion.2
  32.9 1.0 slice_bitcast_fusion.1
  33.9 15.7 %collective-permute-done.5.refs_6_ = bf16[144,1280]{1,0:T(8,128)(2,1)S(1)} collective-permute-done((bf16[144,1280]{1,0:T(8,128)(2,1)}, bf16[144,1280]{1,0:T(8,128)(2,1)S(1)}, u32[]{:S(2)}, u32[]{:S(2)}) %collective-permute-start.5) | collective-permute-done | bytes 368672 | tf_op jit(solution)/shard_map/ppermute | solution.py:309
  49.8 0.5 collective-permute-start.2
  50.3 0.3 fusion.1.refs_8_.refs_2_
  50.6 2.1 %collective-permute-done.2.refs_2_ = bf16[144,1024]{1,0:T(8,128)(2,1)S(1)} collective-permute-done((bf16[144,1024]{1,0:T(8,128)(2,1)S(1)}, bf16[144,1024]{1,0:T(8,128)(2,1)S(1)}, u32[]{:S(2)}, u32[]{:S(2)}) %collective-permute-start.2) | collective-permute-done | bytes 294944 | tf_op jit(solution)/shard_map/ppermute | solution.py:312
  52.7 3.5 %shard_map.85 = (bf16[4,512,768]{2,1,0:T(8,128)(2,1)S(1)}, bf16[4,512,128]{2,1,0:T(8,128)(2,1)S(1)}, bf16[3,4,16,768]{3,2,1,0:T(8,128)(2,1)S(1)}, bf16[3,4,16,128]{3,2,1,0:T(8,128)(2,1)S(1)}, f32[1,768]{1,0:T(1,128)S(1)}) custom-call(s32[1]{0:T(128)} %bitcast.refs_0_.rank_ref, bf16[144,1024]{1,0:T(8,128)(2,1)S(1)} %copy-done.10, ...), custom_call_target="tpu_custom_call" | custom-call | flops 1207959552 | bytes 5242880 | tf_op jit(solution)/shard_map/pallas_call | solution.py:22
  56.2 1.0 copy-done.2
  57.2 1.6 %copy-done.13 = bf16[4,512,768]{2,1,0:T(8,128)(2,1)} copy-done((bf16[4,512,768]{2,1,0:T(8,128)(2,1)}, bf16[4,512,768]{2,1,0:T(8,128)(2,1)S(1)}, u32[]{:S(2)}) %copy-start.13) | copy-done | bytes 3145752
  58.9 0.8 copy-done.15
  59.7 0.7 copy-done.17
  60.4 0.6 copy-done.19
  61.0 1.3 %copy-done.3 = bf16[768,768]{1,0:T(8,128)(2,1)S(1)} copy-done((bf16[768,768]{1,0:T(8,128)(2,1)S(1)}, bf16[768,768]{1,0:T(8,128)(2,1)}, u32[]{:S(2)}) %copy-start.3) | copy-done | bytes 1179672
  62.3 1.9 %copy-done.14 = bf16[4,512,768]{2,1,0:T(8,128)(2,1)S(1)} copy-done((bf16[4,512,768]{2,1,0:T(8,128)(2,1)S(1)}, bf16[4,512,768]{2,1,0:T(8,128)(2,1)}, u32[]{:S(2)}) %copy-start.14) | copy-done | bytes 3145752
  64.2 1.0 copy-done.16
  65.2 1.0 copy-done.18
  66.2 0.8 copy-done.20
  67.0 10.4 %shard_map.86 = (bf16[32,112,120]{2,1,0:T(8,128)(2,1)S(1)}, bf16[4,128,1024]{2,1,0:T(8,128)(2,1)S(1)}, bf16[4,128,1024]{2,1,0:T(8,128)(2,1)S(1)}) custom-call(s32[1]{0:T(128)} %bitcast.refs_0_.rank_ref, bf16[32,96,120]{2,1,0:T(8,128)(2,1)} %all-to-all-done.pieces_ref, bf16[4,512,768]{2,1,0:T(8,128)(2,1)S(1)} %copy-done.14, ...), custom_call_target="tpu_custom_call" | custom-call | flops 6039797760 | tf_op jit(solution)/shard_map/pallas_call | solution.py:22
  77.4 1.0 copy-done.4
  78.4 0.9 copy-done.6
  79.3 1.0 copy-done.7
  80.3 4.1 %all-to-all-start.1 = ((bf16[32,112,120]{2,1,0:T(8,128)(2,1)}), bf16[32,112,120]{2,1,0:T(8,128)(2,1)}, u32[]{:S(2)}, u32[]{:S(2)}) async-start(bf16[32,112,120]{2,1,0:T(8,128)(2,1)} %copy-done.6), calls=%async_computation.1 | async-start | bytes 1835008 | tf_op jit(solution)/shard_map/all_to_all | solution.py:351
  84.6 2.7 %collective-permute-done.7.refs_1_ = bf16[4,128,1024]{2,1,0:T(8,128)(2,1)S(1)} collective-permute-done((bf16[4,128,1024]{2,1,0:T(8,128)(2,1)}, bf16[4,128,1024]{2,1,0:T(8,128)(2,1)S(1)}, u32[]{:S(2)}, u32[]{:S(2)}) %collective-permute-start.7) | collective-permute-done | bytes 1048608 | tf_op jit(solution)/shard_map/ppermute | solution.py:352
  87.3 1.2 %copy-done.5 = bf16[4,128,1024]{2,1,0:T(8,128)(2,1)S(1)} copy-done((bf16[4,128,1024]{2,1,0:T(8,128)(2,1)S(1)}, bf16[4,128,1024]{2,1,0:T(8,128)(2,1)}, u32[]{:S(2)}) %copy-start.5) | copy-done | bytes 1048600
  88.5 0.5 shard_map.87
  89.0 1.8 %collective-permute-start.8 = (bf16[128,1152]{1,0:T(8,128)(2,1)S(1)}, bf16[128,1152]{1,0:T(8,128)(2,1)S(1)}, u32[]{:S(2)}, u32[]{:S(2)}) collective-permute-start(bf16[128,1152]{1,0:T(8,128)(2,1)S(1)} %get-tuple-element.38), channel_id=1, source_target_pairs={{0,1},{1,0},{2,3},{3,2},{4,5},{5,4},{6,7},{7,6},{8,9},{9,8},{10,11... | collective-permute-start | bytes 884744 | tf_op jit(solution)/shard_map/ppermute | solution.py:360
  90.8 1.5 %collective-permute-start.9 = (bf16[128,1152]{1,0:T(8,128)(2,1)S(1)}, bf16[128,1152]{1,0:T(8,128)(2,1)S(1)}, u32[]{:S(2)}, u32[]{:S(2)}) collective-permute-start(bf16[128,1152]{1,0:T(8,128)(2,1)S(1)} %get-tuple-element.39), channel_id=1, source_target_pairs={{0,4},{1,5},{2,6},{3,7},{4,0},{5,1},{6,2},{7,3},{8,12},{9,13},{10,... | collective-permute-start | bytes 884744 | tf_op jit(solution)/shard_map/ppermute | solution.py:360
  92.3 0.3 collective-permute-start.10
  92.6 10.0 %collective-permute-done.8.refs_6_ = bf16[128,1152]{1,0:T(8,128)(2,1)S(1)} collective-permute-done((bf16[128,1152]{1,0:T(8,128)(2,1)S(1)}, bf16[128,1152]{1,0:T(8,128)(2,1)S(1)}, u32[]{:S(2)}, u32[]{:S(2)}) %collective-permute-start.8) | collective-permute-done | bytes 294944 | tf_op jit(solution)/shard_map/ppermute | solution.py:360
  102.6 1.9 %collective-permute-done.9.refs_7_ = bf16[128,1152]{1,0:T(8,128)(2,1)S(1)} collective-permute-done((bf16[128,1152]{1,0:T(8,128)(2,1)S(1)}, bf16[128,1152]{1,0:T(8,128)(2,1)S(1)}, u32[]{:S(2)}, u32[]{:S(2)}) %collective-permute-start.9) | collective-permute-done | bytes 294944 | tf_op jit(solution)/shard_map/ppermute | solution.py:360
  104.4 6.5 %collective-permute-done.10.refs_8_ = bf16[128,1152]{1,0:T(8,128)(2,1)S(1)} collective-permute-done((bf16[128,1152]{1,0:T(8,128)(2,1)S(1)}, bf16[128,1152]{1,0:T(8,128)(2,1)S(1)}, u32[]{:S(2)}, u32[]{:S(2)}) %collective-permute-start.10) | collective-permute-done | bytes 294944 | tf_op jit(solution)/shard_map/ppermute | solution.py:360
  110.9 2.3 %shard_map.88 = (bf16[128,768]{1,0:T(8,128)(2,1)}, bf16[128,768]{1,0:T(8,128)(2,1)}) custom-call(s32[1]{0:T(128)} %bitcast.refs_0_.rank_ref, bf16[128,768]{1,0:T(8,128)(2,1)S(1)} %bitcast.18, bf16[128,768]{1,0:T(8,128)(2,1)S(1)} %bitcast.21, bf16[768,1024]{1,0:T(8,128)(2,1)S(1)} %get-tuple-element.49.refs_4_.refs_3_, ...), custom_call_target="tpu_custom_call" | custom-call | tf_op jit(solution)/shard_map/pallas_call | solution.py:22
  113.2 2.1 %shard_map.89 = (f32[120,768]{1,0:T(8,128)}, f32[1,24]{1,0:T(1,128)}) custom-call(bf16[32,112,120]{2,1,0:T(8,128)(2,1)} %all-to-all-done.1.refs_0_), custom_call_target="tpu_custom_call" | custom-call | tf_op jit(solution)/shard_map/pallas_call | solution.py:22
  (42 shorter events, 0.5 us)
Async XLA Ops:
  0.6 6.5 %copy-start.1 = (bf16[1,128,768]{2,1,0:T(8,128)(2,1)S(1)}, bf16[1,128,768]{2,1,0:T(8,128)(2,1)}, u32[]{:S(2)}) copy-start(bf16[1,128,768]{2,1,0:T(8,128)(2,1)} %param.6) | copy-start | bytes 589828
  0.6 6.5 %copy-start = (bf16[1,128,768]{2,1,0:T(8,128)(2,1)S(1)}, bf16[1,128,768]{2,1,0:T(8,128)(2,1)}, u32[]{:S(2)}) copy-start(bf16[1,128,768]{2,1,0:T(8,128)(2,1)} %param.5) | copy-start | bytes 589828
  2.1 4.1 %collective-permute-start.1 = (bf16[16,1536]{1,0:T(8,128)(2,1)}, bf16[16,1536]{1,0:T(8,128)(2,1)}, u32[]{:S(2)}, u32[]{:S(2)}) collective-permute-start(bf16[16,1536]{1,0:T(8,128)(2,1)} %get-tuple-element.46), channel_id=1, source_target_pairs={{8,6},{16,14},{24,22},{9,7},{17,15},{25,23}} | collective-permute-start | bytes 147464 | tf_op jit(solution)/shard_map/ppermute | solution.py:285
  3.4 2.9 %collective-permute-start = (bf16[16,1536]{1,0:T(8,128)(2,1)}, bf16[16,1536]{1,0:T(8,128)(2,1)}, u32[]{:S(2)}, u32[]{:S(2)}) collective-permute-start(bf16[16,1536]{1,0:T(8,128)(2,1)} %get-tuple-element.47), channel_id=1, source_target_pairs={{6,8},{14,16},{22,24},{7,9},{15,17},{23,25}} | collective-permute-start | bytes 147464 | tf_op jit(solution)/shard_map/ppermute | solution.py:284
  9.0 0.7 copy-start.8
  9.8 0.7 copy-start.9
  10.5 0.7 copy-start.11
  11.2 20.7 %collective-permute-start.3 = (bf16[144,1280]{1,0:T(8,128)(2,1)}, bf16[144,1280]{1,0:T(8,128)(2,1)}, u32[]{:S(2)}, u32[]{:S(2)}) collective-permute-start(bf16[144,1280]{1,0:T(8,128)(2,1)} %get-tuple-element.27), channel_id=1, source_target_pairs={{0,1},{1,0},{2,3},{3,2},{4,5},{5,4},{6,7},{7,6},{8,9},{9,8},{10,11... | collective-permute-start | bytes 1105928 | tf_op jit(solution)/shard_map/ppermute | solution.py:309
  14.1 18.7 %collective-permute-start.4 = (bf16[144,1280]{1,0:T(8,128)(2,1)}, bf16[144,1280]{1,0:T(8,128)(2,1)}, u32[]{:S(2)}, u32[]{:S(2)}) collective-permute-start(bf16[144,1280]{1,0:T(8,128)(2,1)} %get-tuple-element.28), channel_id=1, source_target_pairs={{0,4},{1,5},{2,6},{3,7},{4,0},{5,1},{6,2},{7,3},{8,12},{9,13},{10,... | collective-permute-start | bytes 1105928 | tf_op jit(solution)/shard_map/ppermute | solution.py:309
  19.3 31.0 %copy-start.22 = (f32[768]{0:T(1024)S(1)}, f32[768]{0:T(1024)}, u32[]{:S(2)}) copy-start(f32[768]{0:T(1024)} %param.8) | copy-start | bytes 9220
  19.3 31.0 %copy-start.21 = (s32[768]{0:T(1024)S(1)}, s32[768]{0:T(1024)}, u32[]{:S(2)}) copy-start(s32[768]{0:T(1024)} %param.9) | copy-start | bytes 9220
  19.3 41.7 %all-to-all-start = ((bf16[32,96,120]{2,1,0:T(8,128)(2,1)}), bf16[32,96,120]{2,1,0:T(8,128)(2,1)}, u32[]{:S(2)}, u32[]{:S(2)}) async-start(bf16[32,96,120]{2,1,0:T(8,128)(2,1)} %bitcast.22), calls=%async_computation | async-start | bytes 1572864 | tf_op jit(solution)/shard_map/all_to_all | solution.py:288
  29.4 20.5 %copy-start.12 = (bf16[144,1024]{1,0:T(8,128)(2,1)S(1)}, bf16[144,1024]{1,0:T(8,128)(2,1)}, u32[]{:S(2)}) copy-start(bf16[144,1024]{1,0:T(8,128)(2,1)} %copy-done.11) | copy-start | bytes 884740
  29.4 23.3 %copy-start.10 = (bf16[144,1024]{1,0:T(8,128)(2,1)S(1)}, bf16[144,1024]{1,0:T(8,128)(2,1)}, u32[]{:S(2)}) copy-start(bf16[144,1024]{1,0:T(8,128)(2,1)} %copy-done.9) | copy-start | bytes 884740
  29.4 20.2 %collective-permute-start.5 = (bf16[144,1280]{1,0:T(8,128)(2,1)}, bf16[144,1280]{1,0:T(8,128)(2,1)S(1)}, u32[]{:S(2)}, u32[]{:S(2)}) collective-permute-start(bf16[144,1280]{1,0:T(8,128)(2,1)} %copy-done.8), channel_id=1, source_target_pairs={{0,5},{1,4},{2,7},{3,6},{4,1},{5,0},{6,3},{7,2},{8,13},{9,12},{10,... | collective-permute-start | bytes 1105928 | tf_op jit(solution)/shard_map/ppermute | solution.py:309
  49.7 2.9 %collective-permute-start.6 = (bf16[3,144,1024]{2,1,0:T(8,128)(2,1)S(1)}, bf16[3,144,1024]{2,1,0:T(8,128)(2,1)S(1)}, u32[]{:S(2)}, u32[]{:S(2)}) collective-permute-start(bf16[3,144,1024]{2,1,0:T(8,128)(2,1)S(1)} %pad_maximum_fusion), channel_id=1, source_target_pairs={{0,2},{1,3},{2,0},{3,1},{4,6},{5,7},{6,4},{7,5},{8,10},{9,11},{10,... | collective-permute-start | bytes 2654216 | tf_op jit(solution)/shard_map/ppermute | solution.py:313
  49.8 2.8 %collective-permute-start.2 = (bf16[144,1024]{1,0:T(8,128)(2,1)S(1)}, bf16[144,1024]{1,0:T(8,128)(2,1)S(1)}, u32[]{:S(2)}, u32[]{:S(2)}) collective-permute-start(bf16[144,1024]{1,0:T(8,128)(2,1)S(1)} %copy-done.12), channel_id=1, source_target_pairs={{0,2},{1,3},{2,0},{3,1},{4,6},{5,7},{6,4},{7,5},{8,10},{9,11},{10,... | collective-permute-start | bytes 884744 | tf_op jit(solution)/shard_map/ppermute | solution.py:312
  56.2 1.0 copy-start.2
  57.2 1.7 %copy-start.13 = (bf16[4,512,768]{2,1,0:T(8,128)(2,1)}, bf16[4,512,768]{2,1,0:T(8,128)(2,1)S(1)}, u32[]{:S(2)}) copy-start(bf16[4,512,768]{2,1,0:T(8,128)(2,1)S(1)} %get-tuple-element.30.normed_ref) | copy-start | bytes 9437188
  58.9 0.8 copy-start.15
  59.7 0.7 copy-start.17
  60.4 0.6 copy-start.19
  61.0 1.3 %copy-start.3 = (bf16[768,768]{1,0:T(8,128)(2,1)S(1)}, bf16[768,768]{1,0:T(8,128)(2,1)}, u32[]{:S(2)}) copy-start(bf16[768,768]{1,0:T(8,128)(2,1)} %copy-done.2) | copy-start | bytes 3538948
  62.3 1.9 %copy-start.14 = (bf16[4,512,768]{2,1,0:T(8,128)(2,1)S(1)}, bf16[4,512,768]{2,1,0:T(8,128)(2,1)}, u32[]{:S(2)}) copy-start(bf16[4,512,768]{2,1,0:T(8,128)(2,1)} %copy-done.13) | copy-start | bytes 9437188
  64.2 1.0 copy-start.16
  65.2 1.0 copy-start.18
  66.2 0.8 copy-start.20
  77.4 1.0 copy-start.4
  78.4 0.9 copy-start.6
  79.3 1.0 copy-start.7
  80.3 32.9 %all-to-all-start.1 = ((bf16[32,112,120]{2,1,0:T(8,128)(2,1)}), bf16[32,112,120]{2,1,0:T(8,128)(2,1)}, u32[]{:S(2)}, u32[]{:S(2)}) async-start(bf16[32,112,120]{2,1,0:T(8,128)(2,1)} %copy-done.6), calls=%async_computation.1 | async-start | bytes 1835008 | tf_op jit(solution)/shard_map/all_to_all | solution.py:351
  84.4 2.9 %collective-permute-start.7 = (bf16[4,128,1024]{2,1,0:T(8,128)(2,1)}, bf16[4,128,1024]{2,1,0:T(8,128)(2,1)S(1)}, u32[]{:S(2)}, u32[]{:S(2)}) collective-permute-start(bf16[4,128,1024]{2,1,0:T(8,128)(2,1)} %copy-done.7), channel_id=1, source_target_pairs={{0,2},{1,3},{2,0},{3,1},{4,6},{5,7},{6,4},{7,5},{8,10},{9,11},{10,... | collective-permute-start | bytes 3145736 | tf_op jit(solution)/shard_map/ppermute | solution.py:352
  87.3 1.2 %copy-start.5 = (bf16[4,128,1024]{2,1,0:T(8,128)(2,1)S(1)}, bf16[4,128,1024]{2,1,0:T(8,128)(2,1)}, u32[]{:S(2)}) copy-start(bf16[4,128,1024]{2,1,0:T(8,128)(2,1)} %copy-done.4) | copy-start | bytes 3145732
  89.0 13.5 %collective-permute-start.8 = (bf16[128,1152]{1,0:T(8,128)(2,1)S(1)}, bf16[128,1152]{1,0:T(8,128)(2,1)S(1)}, u32[]{:S(2)}, u32[]{:S(2)}) collective-permute-start(bf16[128,1152]{1,0:T(8,128)(2,1)S(1)} %get-tuple-element.38), channel_id=1, source_target_pairs={{0,1},{1,0},{2,3},{3,2},{4,5},{5,4},{6,7},{7,6},{8,9},{9,8},{10,11... | collective-permute-start | bytes 884744 | tf_op jit(solution)/shard_map/ppermute | solution.py:360
  90.8 13.6 %collective-permute-start.9 = (bf16[128,1152]{1,0:T(8,128)(2,1)S(1)}, bf16[128,1152]{1,0:T(8,128)(2,1)S(1)}, u32[]{:S(2)}, u32[]{:S(2)}) collective-permute-start(bf16[128,1152]{1,0:T(8,128)(2,1)S(1)} %get-tuple-element.39), channel_id=1, source_target_pairs={{0,4},{1,5},{2,6},{3,7},{4,0},{5,1},{6,2},{7,3},{8,12},{9,13},{10,... | collective-permute-start | bytes 884744 | tf_op jit(solution)/shard_map/ppermute | solution.py:360
  92.3 18.7 %collective-permute-start.10 = (bf16[128,1152]{1,0:T(8,128)(2,1)S(1)}, bf16[128,1152]{1,0:T(8,128)(2,1)S(1)}, u32[]{:S(2)}, u32[]{:S(2)}) collective-permute-start(bf16[128,1152]{1,0:T(8,128)(2,1)S(1)} %get-tuple-element.40), channel_id=1, source_target_pairs={{0,5},{1,4},{2,7},{3,6},{4,1},{5,0},{6,3},{7,2},{8,13},{9,12},{10,... | collective-permute-start | bytes 884744 | tf_op jit(solution)/shard_map/ppermute | solution.py:360

commit v6 on v5

--- a/solution.py
+++ b/solution.py
@@ -14,16 +14,17 @@
 EXTRA = 16
 VMEM = pl.BlockSpec(memory_space=pltpu.VMEM)
 SMEM = pl.BlockSpec(memory_space=pltpu.SMEM)
+HBM = pl.BlockSpec(memory_space=pltpu.HBM)
 bf16 = jnp.bfloat16
 f32 = jnp.float32
 
 
-def called(body, outs, args, vmem, scratch=(), specs=None, flops=0, moved=0):
+def called(body, outs, args, vmem, scratch=(), specs=None, out_specs=None, flops=0, moved=0):
     return pl.pallas_call(
         body,
         out_shape=outs,
         in_specs=specs or [VMEM] * len(args),
-        out_specs=jax.tree.map(lambda _: VMEM, outs),
+        out_specs=out_specs or jax.tree.map(lambda _: VMEM, outs),
         scratch_shapes=list(scratch),
         compiler_params=pltpu.CompilerParams(vmem_limit_bytes=vmem * 2**20),
         cost_estimate=pl.CostEstimate(flops=flops, bytes_accessed=moved, transcendentals=0),
@@ -48,18 +49,33 @@
     return x * half_sum, slope
 
 
+def slot_maps(part, slots, pairing):
+    shape = (slots, pairing.shape[1])
+    slot = lax.broadcasted_iota(jnp.int32, shape, 0)
+    lane = lax.bitwise_and(slot, LANES - 1)
+    channel_of = jnp.where(lane < part, lax.div(slot, LANES) * part + lane, -1)
+    channel = lax.broadcasted_iota(jnp.int32, shape, 1)
+    return [jnp.where(channel_of == c, 1.0, 0.0).astype(bf16) for c in (channel, pairing)]
+
+
+def swap_map(pairing):
+    channels = pairing.shape[1]
+    row = lax.broadcasted_iota(jnp.int32, (channels, channels), 0)
+    return jnp.where(row == pairing, 1.0, 0.0).astype(bf16)
+
+
 def chip_masks(ranks, core):
     return [mask for mask in range(ranks) if not mask & core]
 
 
-def pack_messages(core, rank_ref, values_ref, cot_ref, edge_ref, plain_ref, other_ref, *refs):
+def pack_messages(part, core, rank_ref, values_ref, cot_ref, edge_ref, pairing_ref, *refs):
     home_ref, cross_ref, leaving, slices = refs[0], refs[1], refs[2:-1], refs[-1]
     positions, channels = values_ref.shape
     ranks = slices.shape[0]
     here, edge = slice(0, positions), slice(positions, None)
-    for rows, source in ((here, cot_ref[...]), (edge, edge_ref[:, channels:])):
-        for n, ref in enumerate((plain_ref, other_ref)):
-            piece = dot(source, ref[...], ((1,), (0,))).astype(bf16)
+    for n, map_of in enumerate(slot_maps(part, ranks * LANES, pairing_ref[...])):
+        for rows, source in ((here, cot_ref[...]), (edge, edge_ref[:, channels:])):
+            piece = dot(source, map_of, ((1,), (1,))).astype(bf16)
             for j in range(ranks):
                 slices[j, rows, n * LANES : (n + 1) * LANES] = piece[:, j * LANES : (j + 1) * LANES]
     rank = rank_ref[0]
@@ -75,6 +91,13 @@
         out[:, two + channels :] = slices[lax.bitwise_xor(rank, mask)]
 
 
+def stack_crossing(cross_ref, *refs):
+    out_ref = refs[-1]
+    width = out_ref.shape[2]
+    for m, ref in enumerate((cross_ref,) + refs[:-1]):
+        out_ref[m] = ref[:, :width]
+
+
 def normalize(x, gain, swap):
     other = dot(x, swap, ((1,), (0,)))
     x = x.astype(f32)
@@ -82,25 +105,25 @@
     return [(t * rms * gain).astype(bf16) for t in (x, other)]
 
 
-def prepare(core, rank_ref, home_ref, home_crossed_ref, crossed_ref, *refs):
+def prepare(core, rank_ref, home_ref, crossed_ref, *refs):
     arrived = refs[:-7]
-    gain_ref, swap_ref, normed_ref, grads_ref, edge_normed_ref, edge_grads_ref, swapped_gain_ref = refs[-7:]
+    gain_ref, pairing_ref, normed_ref, grads_ref, edge_normed_ref, edge_grads_ref, swapped_gain_ref = refs[-7:]
     dp_ranks = normed_ref.shape[0] // 2
     channels = gain_ref.shape[1]
     masks = chip_masks(2 * (len(arrived) + 1), core)
     seq_ranks = 2 * len(masks) // dp_ranks
     positions = home_ref.shape[0] - HALO
     two = 2 * LANES
-    blocks = [(0, home_ref, 0, channels), (core, home_crossed_ref, two, 0)]
-    for m, mask in enumerate(masks[1:]):
-        blocks.append((mask, arrived[m], two, two + channels))
-        blocks.append((mask | core, crossed_ref.at[m], two, 0))
+    swap = swap_map(pairing_ref[...])
+    blocks = [(0, home_ref, 0, channels)]
+    blocks += [(mask, ref, two, two + channels) for mask, ref in zip(masks[1:], arrived)]
+    blocks += [(mask | core, crossed_ref.at[m], two, 0) for m, mask in enumerate(masks)]
     for flip, ref, lane, grad_lane in blocks:
         source = lax.bitwise_xor(rank_ref[0], flip)
         b, i = lax.rem(source, dp_ranks), lax.div(source, dp_ranks)
         start = pl.multiple_of(i * positions, positions)
         side = jnp.where(i == 0, 0, jnp.where(i == seq_ranks - 1, 1, 2))
-        both = normalize(ref[:, lane : lane + channels], gain_ref[...], swap_ref[...])
+        both = normalize(ref[:, lane : lane + channels], gain_ref[...], swap)
         for n, normed in enumerate(both):
             first = grad_lane + n * LANES
             grads = (0.5 * ref[:, first : first + LANES].astype(f32)).astype(bf16)
@@ -115,16 +138,19 @@
     third = gain - first - second
     row = lax.broadcasted_iota(jnp.int32, (HALO, channels), 0)
     parts = jnp.where(row == 0, first, jnp.where(row == 1, second, jnp.where(row == 2, third, 0.0)))
-    swapped = dot(parts.astype(bf16), swap_ref[...], ((1,), (0,)))
+    swapped = dot(parts.astype(bf16), swap, ((1,), (0,)))
     swapped_gain_ref[...] = swapped[0:1] + swapped[1:2] + swapped[2:3]
 
 
-def main_body(rank_ref, pieces_ref, normed_ref, grads_ref, edge_normed_ref, edge_grads_ref, *refs):
-    gain_ref, swapped_gain_ref, swap_ref, out_ref, own_ref, cross_ref = refs[:6]
-    kernel_ref, shifted, gelus, terms, halves, bent, slopes, total, scaled = refs[6:]
-    owners, part, rows = pieces_ref.shape
+def main_body(sizes, place_ref, near_ref, far_ref, normed_ref, grads_ref, edge_normed_ref, edge_grads_ref, *refs):
+    gain_ref, swapped_gain_ref, pairing_ref, sent_ref, own_ref, cross_ref = refs[:6]
+    pieces, kernel_ref, shifted, gelus, terms, halves, bent, slopes, total, scaled = refs[6:16]
+    out_ref, own, cross, sems = refs[16:]
+    seq_blocks, dp_blocks, seq_ranks, dp_ranks = sizes
+    rank, me = place_ref[0], place_ref[1]
+    owners = seq_blocks * dp_blocks * seq_ranks * dp_ranks
+    part, rows = near_ref.shape[2:]
     strands, span, channels = normed_ref.shape
-    dp_ranks = strands // 2
     taps = kernel_ref.shape[0] // LANES
     half = taps // 2
     reach = 2 * half
@@ -138,11 +164,21 @@
             yield tap, channel, count, first - owner * rows
             first += count
 
+    for ref, first in ((near_ref, 0), (far_ref, near_ref.shape[0])):
+        for j in range(ref.shape[0]):
+            pieces[lax.bitwise_xor(me, first + j)] = ref[j]
     kernel_ref[...] = jnp.zeros_like(kernel_ref)
-    for owner in range(owners):
+    places = [
+        (sb * dp_blocks + db, sr * dp_ranks + dr)
+        for sb in range(seq_blocks)
+        for sr in range(seq_ranks)
+        for db in range(dp_blocks)
+        for dr in range(dp_ranks)
+    ]
+    for owner, (source, piece) in enumerate(places):
         for tap, channel, count, offset in runs(owner):
-            kernel_ref[tap * LANES : tap * LANES + part, channel : channel + count] = pieces_ref[
-                owner, :, offset : offset + count
+            kernel_ref[tap * LANES : tap * LANES + part, channel : channel + count] = pieces[
+                source, piece, :, offset : offset + count
             ]
     kernel = kernel_ref[...]
     edge_normed = jnp.concatenate([edge_normed_ref[side, s] for side in range(2) for s in range(strands)], 0)
@@ -185,22 +221,28 @@
         out_ref[owner, part:, :own_gain] = extra[
             :, owner * own_gain : (owner + 1) * own_gain
         ].astype(bf16)
-    swapped = dot(kernel, swap_ref[...], ((1,), (0,))).astype(bf16)
+    copies = [pltpu.make_async_copy(out_ref, sent_ref, sems.at[0])]
+    copies[0].start()
+    swapped = dot(kernel, swap_map(pairing_ref[...]), ((1,), (0,))).astype(bf16)
     for b in range(dp_ranks):
         scaled[b] = (
             dot(shifted[b], kernel, ((1,), (0,))) * gain_ref[...]
             + dot(shifted[dp_ranks + b], swapped, ((1,), (0,))) * swapped_gain_ref[...]
         ).astype(bf16)
-    chips, positions, _ = own_ref.shape
-    for m, mask in enumerate(chip_masks(2 * chips, dp_ranks)):
-        for out, flip in ((own_ref, mask), (cross_ref, mask | dp_ranks)):
-            target = lax.bitwise_xor(rank_ref[0], flip)
+    chips, positions, _ = own.shape
+    for c, (out, ref) in enumerate(((cross, cross_ref), (own, own_ref))):
+        for m, mask in enumerate(chip_masks(2 * chips, dp_ranks)):
+            target = lax.bitwise_xor(rank, mask if c else mask | dp_ranks)
             b = lax.rem(target, dp_ranks)
             start = pl.multiple_of(lax.div(target, dp_ranks) * positions, positions)
             out[m, :, :channels] = scaled[b, pl.ds(start, positions), :]
             for n in range(2):
                 lane = channels + n * LANES
                 out[m, :, lane : lane + LANES] = gelus[n * dp_ranks + b, pl.ds(start, positions), :]
+        copies.append(pltpu.make_async_copy(out, ref, sems.at[1 + c]))
+        copies[-1].start()
+    for copy in copies:
+        copy.wait()
 
 
 def chip_sum(part, own_ref, crossed_ref, *outs):
@@ -216,7 +258,7 @@
                 out[:, start : start + part] = ref[m, :, lane : lane + part]
 
 
-def finish(part, core, rank_ref, values_ref, cot_ref, plain_ref, other_ref, *refs):
+def finish(part, core, rank_ref, values_ref, cot_ref, pairing_ref, *refs):
     arrived, (combined_ref, grad_ref, gelus) = refs[:-3], refs[-3:]
     channels = values_ref.shape[1]
     ranks = gelus.shape[1]
@@ -230,8 +272,8 @@
                 start = channels + (2 * c + n) * part
                 gelus[n, source, :, :part] = block[:, start : start + part]
     joined = [jnp.concatenate([gelus[n, j] for j in range(ranks)], -1) for n in range(2)]
-    plain = dot(joined[0], plain_ref[...], ((1,), (1,)))
-    other = dot(joined[1], other_ref[...], ((1,), (1,)))
+    maps = slot_maps(part, ranks * LANES, pairing_ref[...])
+    plain, other = [dot(j, m, ((1,), (0,))) for j, m in zip(joined, maps)]
     values = values_ref[...].astype(f32)
     rms = lax.rsqrt(jnp.mean(values * values, -1, keepdims=True) + epsilon)
     reverse_out = (values + other).astype(bf16).astype(f32)
@@ -277,42 +319,42 @@
     strands = 2 * dp_ranks
     width = channels + 2 * LANES
     rank = lax.axis_index(RANK).reshape(1)
+    place = jnp.concatenate([rank, lax.axis_index(BLOCK).reshape(1)])
     values, cot = activations[0], cotangent[0]
+    slices = lax.all_to_all(weights.T.reshape(ranks, part, rows), RANK, 0, 0, tiled=True)
+    far = slices[None]
+    stages = [1 << bit for bit in range((seq_blocks * dp_blocks).bit_length() - 1)]
+    for mask in stages:
+        near = far if mask == 1 else jnp.concatenate([near, far])
+        far = lax.ppermute(near, BLOCK, flipped_pairs(seq_blocks * dp_blocks, mask))
+    slices, values, cot = lax.optimization_barrier((slices, values, cot))
     along = ("seq_block", "seq_rank")
     ends = [(b * seq_ranks - 1, b * seq_ranks) for b in range(1, seq_blocks)]
     both = jnp.concatenate([values, cot], -1)
     low = lax.ppermute(both[-HALO:], along, ends)
     high = lax.ppermute(both[:HALO], along, [(target, source) for source, target in ends])
-    slices = weights.T.reshape(1, seq_ranks, 1, dp_ranks, part, rows)
-    slices = jnp.broadcast_to(slices, (seq_blocks, seq_ranks, dp_blocks, dp_ranks, part, rows))
-    pieces = lax.all_to_all(slices.reshape(owners, part, rows), EVERY, 0, 0, tiled=True)
-    slot = jnp.arange(ranks * LANES, dtype=jnp.int32)
-    channel_of = jnp.where(slot % LANES < part, slot // LANES * part + slot % LANES, -1)
-    channel_list = jnp.arange(channels, dtype=jnp.int32)
-    plain_map = (channel_list[:, None] == channel_of).astype(bf16)
-    other_map = (pairing[:, None] == channel_of).astype(bf16)
-    swap = (pairing[:, None] == channel_list).astype(bf16)
+    pairing = pairing.reshape(1, channels)
     gain = norm_gain.reshape(1, channels)
     core = dp_ranks
     masks = chip_masks(ranks, core)
     block = positions + HALO
     home, cross, *leaving = called(
-        lambda *refs: pack_messages(core, *refs),
+        lambda *refs: pack_messages(part, core, *refs),
         (shape_of((block, width), bf16),) * 2
         + tuple(shape_of((block, width + 2 * LANES), bf16) for _ in masks[1:]),
-        (rank, values, cot, low + high, plain_map, other_map),
+        (rank, values, cot, low + high, pairing),
         16,
         scratch=[pltpu.VMEM((ranks, block, 2 * LANES), bf16)],
-        specs=[SMEM] + [VMEM] * 5,
+        specs=[SMEM] + [VMEM] * 4,
     )
     arrived = [
         lax.ppermute(message, RANK, flipped_pairs(ranks, mask))
         for message, mask in zip(leaving, masks[1:])
     ]
-    home_crossed = lax.ppermute(cross, RANK, flipped_pairs(ranks, core))
-    crossed = lax.ppermute(
-        jnp.stack([message[:, :width] for message in arrived]), RANK, flipped_pairs(ranks, core)
-    )
+    crossing = called(
+        stack_crossing, shape_of((len(masks), block, width), bf16), (cross, *arrived), 8
+    )
+    crossed = lax.ppermute(crossing, RANK, flipped_pairs(ranks, core))
     normed, grads, edge_normed, edge_grads, swapped_gain = called(
         lambda *refs: prepare(core, *refs),
         (
@@ -322,19 +364,22 @@
             shape_of((3, strands, HALO, LANES), bf16),
             shape_of((1, channels), f32),
         ),
-        (rank, home, home_crossed, crossed, *arrived, gain, swap),
+        (rank, home, crossed, *arrived, gain, pairing),
         16,
-        specs=[SMEM] + [VMEM] * (5 + len(arrived)),
+        specs=[SMEM] + [VMEM] * (4 + len(arrived)),
         flops=2 * ranks * positions * channels * channels,
         moved=ranks * positions * (width + 2 * channels) * 2,
     )
-    sent = shape_of((len(masks), positions, width), bf16)
+    sent = (owners, part + EXTRA, rows)
+    halves = (len(masks), positions, width)
+    sizes = (seq_blocks, dp_blocks, seq_ranks, dp_ranks)
     outgoing, own, cross = called(
-        main_body,
-        (shape_of((owners, part + EXTRA, rows), bf16), sent, sent),
-        (rank, pieces, normed, grads, edge_normed, edge_grads, gain, swapped_gain, swap),
-        32,
+        lambda *refs: main_body(sizes, *refs),
+        tuple(pltpu.HBM(shape, bf16) for shape in (sent, halves, halves)),
+        (place, near, far, normed, grads, edge_normed, edge_grads, gain, swapped_gain, pairing),
+        40,
         scratch=[
+            pltpu.VMEM((seq_blocks * dp_blocks, ranks, part, rows), bf16),
             pltpu.VMEM((taps * LANES, channels), bf16),
             pltpu.VMEM((strands, span, taps * LANES), bf16),
             pltpu.VMEM((strands, span, LANES), bf16),
@@ -344,8 +389,13 @@
             pltpu.VMEM((wide, LANES), f32),
             pltpu.VMEM((taps * LANES, channels), f32),
             pltpu.VMEM((dp_ranks, span, channels), bf16),
+            pltpu.VMEM(sent, bf16),
+            pltpu.VMEM(halves, bf16),
+            pltpu.VMEM(halves, bf16),
+            pltpu.SemaphoreType.DMA((3,)),
         ],
-        specs=[SMEM] + [VMEM] * 8,
+        specs=[SMEM] + [VMEM] * 9,
+        out_specs=(HBM,) * 3,
         flops=6 * strands * span * taps * LANES * channels,
     )
     terms = lax.all_to_all(outgoing, EVERY, 0, 0, tiled=True)
@@ -363,10 +413,10 @@
     combined, grad_input = called(
         lambda *refs: finish(part, core, *refs),
         (shape_of((positions, channels), bf16), shape_of((positions, channels), bf16)),
-        (rank, values, cot, plain_map, other_map, *arrived),
+        (rank, values, cot, pairing, *arrived),
         16,
         scratch=[pltpu.VMEM((2, ranks, positions, LANES), bf16)],
-        specs=[SMEM] + [VMEM] * (4 + len(arrived)),
+        specs=[SMEM] + [VMEM] * (3 + len(arrived)),
     )
     order = [
         [

time: 116 us -> 115 us (level)
  local copies, waits for them, and re-layouts: 22.8 us -> 2.14 us
  waiting for transfers between devices: 38.8 us -> 53.1 us
  blocking collectives: 0 us -> 10.4 us
  other arithmetic: 4.27 us -> 0.18 us
    unnamed x47 -> x13, local copies, waits for them, and re-layouts: 18.8 us -> 0.97 us
    ppermute x2 -> x3, waiting for transfers between devices: 2.06 us -> 18.1 us  [the longest x2 18.1 us: per_device(): far = lax.ppermute(near, BLOCK, flipped_pairs(seq_blocks * dp_blocks, mask))]
    ppermute x2 -> x3, starting transfers between devices: 0.56 us -> 14.3 us  [the longest x2 9.87 us: per_device(): far = lax.ppermute(near, BLOCK, flipped_pairs(seq_blocks * dp_blocks, mask))]
    all_to_all x0 -> x1, blocking collectives: none -> 10.4 us  [per_device(): lax.all_to_all(weights.T.reshape(ranks, part, rows), RANK, 0, 0, tiled=True)]
    all_to_all x1 -> x0, starting transfers between devices: 10 us -> none  [per_device(): lax.all_to_all(slices.reshape(owners, part, rows), EVERY, 0, 0, tiled=True)]
    ppermute x6, starting transfers between devices: 10.5 us -> 7.11 us  [per_device(): lax.ppermute(message, RANK, flipped_pairs(ranks, mask))]
    another operation x3 -> x0, local copies, waits for them, and re-layouts: 1.99 us -> none  [per_device(): jnp.stack([message[:, :width] for message in arrived])]
    broadcast_in_dim x1 -> x0, local copies, waits for them, and re-layouts: 1.98 us -> none  [per_device(): jnp.broadcast_to(slices, (seq_blocks, seq_ranks, dp_blocks, dp_ranks, par...]
  transfers between devices with their start and end apart: 13 -> 13, of which waited for: 6 -> 8; matrix products, arithmetic and copies ran while one was open for 7% -> 0% of each run, Pallas kernels for 5% -> 5%
where the time goes in v6:
time: 115 us
  waiting for transfers between devices  53.1 us (46%)
  starting transfers between devices  27.1 us (24%)
  Pallas kernels  20.8 us (18%)
  blocking collectives  10.4 us (9%)
  local copies, waits for them, and re-layouts  2.14 us (2%)
    ppermute x6, waiting for transfers between devices, per_device(): lax.ppermute(message, RANK, flipped_pairs(ranks, mask))  32.4 us
    pallas_call x7, Pallas kernels, called(): pl.pallas_call(body, out_shape=outs, in_specs=specs or [VMEM] * len(args)...  20.8 us
    ppermute x2, waiting for transfers between devices, per_device(): far = lax.ppermute(near, BLOCK, flipped_pairs(seq_blocks * dp_blocks, mask))  18.1 us
    all_to_all x1, blocking collectives, per_device(): lax.all_to_all(weights.T.reshape(ranks, part, rows), RANK, 0, 0, tiled=True)  10.4 us
    ppermute x2, starting transfers between devices, per_device(): far = lax.ppermute(near, BLOCK, flipped_pairs(seq_blocks * dp_blocks, mask))  9.87 us
    ppermute x6, starting transfers between devices, per_device(): lax.ppermute(message, RANK, flipped_pairs(ranks, mask))  7.11 us
    ppermute x1, starting transfers between devices, per_device(): crossed = lax.ppermute(crossing, RANK, flipped_pairs(ranks, core))  4.47 us
    all_to_all x1, starting transfers between devices, per_device(): terms = lax.all_to_all(outgoing, EVERY, 0, 0, tiled=True)  4.03 us
  transfers between devices with their start and end apart: 13, of which 8 were waited for; matrix products, arithmetic and copies ran while one was open for 0% of the time, Pallas kernels for 5%

profile of v6, /device:TPU:0, one launch (start us, length us, event | category | flops | bytes accessed | tf_op | source)
XLA Modules:
  0.0 114.5 jit_solution(6035350713670669401)
XLA Ops:
  0.6 0.0 copy-start.1
  0.6 0.0 copy-start
  0.7 0.0 copy-start.4
  0.7 1.1 copy.9
  1.8 10.4 %all_to_all.10 = bf16[8,96,120]{2,1,0:T(8,128)(2,1)} all-to-all(bf16[8,96,120]{2,1,0:T(8,128)(2,1)S(1)} %bitcast.16), channel_id=1, replica_groups=mesh['seq_block'=4,'seq_rank'=4,'dp_block'=1,'dp_rank'=2] {'seq_rank','d..., dimensions={0} | all-to-all | bytes 368640 | tf_op jit(solution)/shard_map/all_to_all | solution.py:324
  12.2 0.9 constant_dynamic-update-slice_fusion.1
  13.2 0.0 copy-done.1
  13.2 0.7 collective-permute-start.3
  13.9 0.7 collective-permute-start.2
  14.6 0.0 copy-done.4
  14.6 0.0 collective-permute-done.3
  14.6 0.0 collective-permute-done.2
  14.6 0.0 copy-done
  14.6 1.9 %shard_map.84 = (bf16[144,1024]{1,0:T(8,128)(2,1)S(1)}, bf16[144,1024]{1,0:T(8,128)(2,1)S(1)}, bf16[144,1280]{1,0:T(8,128)(2,1)S(1)}, bf16[144,1280]{1,0:T(8,128)(2,1)S(1)}, bf16[144,1280]{1,0:T(8,128)(2,1)S(1)}) custom-call(s32[1]{0:T(128)} %bitcast.refs_0_, bf16[128,768]{1,0:T(8,128)(2,1)S(1)} %bitcast.11, bf16[128,768]{1,0:T(8,128)(2,1)S(1)} %bitcast.14, ...), custom_call_target="tpu_custom_call" | custom-call | tf_op jit(solution)/shard_map/pallas_call | solution.py:23
  16.6 1.5 %collective-permute-start.4 = (bf16[144,1280]{1,0:T(8,128)(2,1)S(1)}, bf16[144,1280]{1,0:T(8,128)(2,1)S(1)}, u32[]{:S(2)}, u32[]{:S(2)}) collective-permute-start(bf16[144,1280]{1,0:T(8,128)(2,1)S(1)} %get-tuple-element.31), channel_id=1, source_target_pairs={{0,1},{1,0},{2,3},{3,2},{4,5},{5,4},{6,7},{7,6},{8,9},{9,8},{10,11... | collective-permute-start | bytes 1105928 | tf_op jit(solution)/shard_map/ppermute | solution.py:351
  18.1 0.6 collective-permute-start.5
  18.7 1.5 %collective-permute-start.6 = (bf16[144,1280]{1,0:T(8,128)(2,1)S(1)}, bf16[144,1280]{1,0:T(8,128)(2,1)S(1)}, u32[]{:S(2)}, u32[]{:S(2)}) collective-permute-start(bf16[144,1280]{1,0:T(8,128)(2,1)S(1)} %get-tuple-element.33), channel_id=1, source_target_pairs={{0,5},{1,4},{2,7},{3,6},{4,1},{5,0},{6,3},{7,2},{8,13},{9,12},{10,... | collective-permute-start | bytes 1105928 | tf_op jit(solution)/shard_map/ppermute | solution.py:351
  20.2 10.1 %collective-permute-done.4.refs_0_.refs_3_ = bf16[144,1280]{1,0:T(8,128)(2,1)S(1)} collective-permute-done((bf16[144,1280]{1,0:T(8,128)(2,1)S(1)}, bf16[144,1280]{1,0:T(8,128)(2,1)S(1)}, u32[]{:S(2)}, u32[]{:S(2)}) %collective-permute-start.4) | collective-permute-done | bytes 368672 | tf_op jit(solution)/shard_map/ppermute | solution.py:351
  30.2 0.0 collective-permute-done.5.refs_1_.refs_4_
  30.2 2.7 %collective-permute-done.6.refs_2_.refs_5_ = bf16[144,1280]{1,0:T(8,128)(2,1)S(1)} collective-permute-done((bf16[144,1280]{1,0:T(8,128)(2,1)S(1)}, bf16[144,1280]{1,0:T(8,128)(2,1)S(1)}, u32[]{:S(2)}, u32[]{:S(2)}) %collective-permute-start.6) | collective-permute-done | bytes 368672 | tf_op jit(solution)/shard_map/ppermute | solution.py:351
  32.9 0.1 shard_map.85
  33.0 4.5 %collective-permute-start.7 = (bf16[4,144,1024]{2,1,0:T(8,128)(2,1)S(1)}, bf16[4,144,1024]{2,1,0:T(8,128)(2,1)}, u32[]{:S(2)}, u32[]{:S(2)}) collective-permute-start(bf16[4,144,1024]{2,1,0:T(8,128)(2,1)S(1)} %shard_map.85), channel_id=1, source_target_pairs={{0,2},{1,3},{2,0},{3,1},{4,6},{5,7},{6,4},{7,5},{8,10},{9,11},{10,... | collective-permute-start | bytes 3538952 | tf_op jit(solution)/shard_map/ppermute | solution.py:357
  37.5 0.0 copy-done.3
  37.5 7.0 %collective-permute-start = (bf16[1,8,96,120]{3,2,1,0:T(8,128)(2,1)S(1)}, bf16[1,8,96,120]{3,2,1,0:T(8,128)(2,1)S(1)}, u32[]{:S(2)}, u32[]{:S(2)}) collective-permute-start(bf16[1,8,96,120]{3,2,1,0:T(8,128)(2,1)S(1)} %bitcast.17), channel_id=1, source_target_pairs={{0,8},{8,0},{16,24},{24,16},{1,9},{9,1},{17,25},{25,17},{2,10},{10... | collective-permute-start | bytes 552968 | tf_op jit(solution)/shard_map/ppermute | solution.py:329
  44.5 4.8 %collective-permute-done = bf16[1,8,96,120]{3,2,1,0:T(8,128)(2,1)S(1)} collective-permute-done((bf16[1,8,96,120]{3,2,1,0:T(8,128)(2,1)S(1)}, bf16[1,8,96,120]{3,2,1,0:T(8,128)(2,1)S(1)}, u32[]{:S(2)}, u32[]{:S(2)}) %collective-permute-start) | collective-permute-done | bytes 184352 | tf_op jit(solution)/shard_map/ppermute | solution.py:329
  49.3 0.1 pad_maximum_fusion.refs_1_
  49.4 2.8 %collective-permute-start.1 = (bf16[2,8,96,120]{3,2,1,0:T(8,128)(2,1)S(1)}, bf16[2,8,96,120]{3,2,1,0:T(8,128)(2,1)}, u32[]{:S(2)}, u32[]{:S(2)}) collective-permute-start(bf16[2,8,96,120]{3,2,1,0:T(8,128)(2,1)S(1)} %pad_maximum_fusion.refs_1_), channel_id=1, source_target_pairs={{0,16},{8,24},{16,0},{24,8},{1,17},{9,25},{17,1},{25,9},{2,18},{10... | collective-permute-start | bytes 1105928 | tf_op jit(solution)/shard_map/ppermute | solution.py:329
  52.2 0.0 copy-done.5
  52.2 0.1 pad_add_fusion.refs_0_
  52.3 0.0 collective-permute-done.7.refs_2_
  52.3 3.5 %shard_map.86 = (bf16[4,512,768]{2,1,0:T(8,128)(2,1)S(1)}, bf16[4,512,128]{2,1,0:T(8,128)(2,1)S(1)}, bf16[3,4,16,768]{3,2,1,0:T(8,128)(2,1)S(1)}, bf16[3,4,16,128]{3,2,1,0:T(8,128)(2,1)S(1)}, f32[1,768]{1,0:T(1,128)S(1)}) custom-call(s32[1]{0:T(128)} %bitcast.refs_0_, bf16[144,1024]{1,0:T(8,128)(2,1)S(1)} %get-tuple-element.29.refs_1_, ...), custom_call_target="tpu_custom_call" | custom-call | flops 1207959552 | bytes 5242880 | tf_op jit(solution)/shard_map/pallas_call | solution.py:23
  55.8 13.3 %collective-permute-done.1.refs_2_ = bf16[2,8,96,120]{3,2,1,0:T(8,128)(2,1)} collective-permute-done((bf16[2,8,96,120]{3,2,1,0:T(8,128)(2,1)S(1)}, bf16[2,8,96,120]{3,2,1,0:T(8,128)(2,1)}, u32[]{:S(2)}, u32[]{:S(2)}) %collective-permute-start.1) | collective-permute-done | bytes 368672 | tf_op jit(solution)/shard_map/ppermute | solution.py:329
  69.1 12.0 %shard_map.87 = (bf16[32,112,120]{2,1,0:T(8,128)(2,1)}, bf16[4,128,1024]{2,1,0:T(8,128)(2,1)}, bf16[4,128,1024]{2,1,0:T(8,128)(2,1)}) custom-call(s32[2]{0:T(128)S(1)} %pad_add_fusion.refs_0_, bf16[2,8,96,120]{3,2,1,0:T(8,128)(2,1)S(1)} %pad_maximum_fusion.refs_1_, bf16[2,8,96,120]{3,2,1,0:T(8,128)(2,1)} %collective-permute-done.1.refs_2_, ...), custom_call_target="tpu_custom_call" | custom-call | flops 6039797760 | tf_op jit(solution)/shard_map/pallas_call | solution.py:23
  81.1 0.0 copy-start.2
  81.1 4.0 %all-to-all-start.1 = ((bf16[32,112,120]{2,1,0:T(8,128)(2,1)}), bf16[32,112,120]{2,1,0:T(8,128)(2,1)S(1)}, u32[]{:S(2)}, u32[]{:S(2)}) async-start(bf16[32,112,120]{2,1,0:T(8,128)(2,1)} %get-tuple-element.47), calls=%async_computation.1 | async-start | bytes 1835008 | tf_op jit(solution)/shard_map/all_to_all | solution.py:401
  85.1 0.3 collective-permute-start.8
  85.4 2.6 %collective-permute-done.8.refs_1_ = bf16[4,128,1024]{2,1,0:T(8,128)(2,1)S(1)} collective-permute-done((bf16[4,128,1024]{2,1,0:T(8,128)(2,1)}, bf16[4,128,1024]{2,1,0:T(8,128)(2,1)S(1)}, u32[]{:S(2)}, u32[]{:S(2)}) %collective-permute-start.8) | collective-permute-done | bytes 1048608 | tf_op jit(solution)/shard_map/ppermute | solution.py:402
  88.1 0.0 copy-done.2
  88.1 0.5 shard_map.88
  88.6 1.8 %collective-permute-start.9 = (bf16[128,1152]{1,0:T(8,128)(2,1)S(1)}, bf16[128,1152]{1,0:T(8,128)(2,1)S(1)}, u32[]{:S(2)}, u32[]{:S(2)}) collective-permute-start(bf16[128,1152]{1,0:T(8,128)(2,1)S(1)} %get-tuple-element.42), channel_id=1, source_target_pairs={{0,1},{1,0},{2,3},{3,2},{4,5},{5,4},{6,7},{7,6},{8,9},{9,8},{10,11... | collective-permute-start | bytes 884744 | tf_op jit(solution)/shard_map/ppermute | solution.py:410
  90.4 1.5 %collective-permute-start.10 = (bf16[128,1152]{1,0:T(8,128)(2,1)S(1)}, bf16[128,1152]{1,0:T(8,128)(2,1)S(1)}, u32[]{:S(2)}, u32[]{:S(2)}) collective-permute-start(bf16[128,1152]{1,0:T(8,128)(2,1)S(1)} %get-tuple-element.43), channel_id=1, source_target_pairs={{0,4},{1,5},{2,6},{3,7},{4,0},{5,1},{6,2},{7,3},{8,12},{9,13},{10,... | collective-permute-start | bytes 884744 | tf_op jit(solution)/shard_map/ppermute | solution.py:410
  91.9 0.3 collective-permute-start.11
  92.2 10.7 %collective-permute-done.9.refs_5_ = bf16[128,1152]{1,0:T(8,128)(2,1)S(1)} collective-permute-done((bf16[128,1152]{1,0:T(8,128)(2,1)S(1)}, bf16[128,1152]{1,0:T(8,128)(2,1)S(1)}, u32[]{:S(2)}, u32[]{:S(2)}) %collective-permute-start.9) | collective-permute-done | bytes 294944 | tf_op jit(solution)/shard_map/ppermute | solution.py:410
  102.8 2.0 %collective-permute-done.10.refs_6_ = bf16[128,1152]{1,0:T(8,128)(2,1)S(1)} collective-permute-done((bf16[128,1152]{1,0:T(8,128)(2,1)S(1)}, bf16[128,1152]{1,0:T(8,128)(2,1)S(1)}, u32[]{:S(2)}, u32[]{:S(2)}) %collective-permute-start.10) | collective-permute-done | bytes 294944 | tf_op jit(solution)/shard_map/ppermute | solution.py:410
  104.8 6.9 %collective-permute-done.11.refs_7_ = bf16[128,1152]{1,0:T(8,128)(2,1)S(1)} collective-permute-done((bf16[128,1152]{1,0:T(8,128)(2,1)S(1)}, bf16[128,1152]{1,0:T(8,128)(2,1)S(1)}, u32[]{:S(2)}, u32[]{:S(2)}) %collective-permute-start.11) | collective-permute-done | bytes 294944 | tf_op jit(solution)/shard_map/ppermute | solution.py:410
  111.8 1.8 %shard_map.89 = (bf16[128,768]{1,0:T(8,128)(2,1)}, bf16[128,768]{1,0:T(8,128)(2,1)}) custom-call(s32[1]{0:T(128)} %bitcast.refs_0_, bf16[128,768]{1,0:T(8,128)(2,1)S(1)} %bitcast.12, bf16[128,768]{1,0:T(8,128)(2,1)S(1)} %bitcast.15, s32[1,768]{1,0:T(1,128)S(1)} %reshape.25.refs_4_.refs_7_.refs_9_.refs_3_, bf16[128,1152]{1,0:T(8,128)(2,1)S(1)} %get-tuple-element.41.refs_4_, ...), custom_call_target="tpu_custom_call" | custom-call | tf_op jit(solution)/shard_map/pallas_call | solution.py:23
  113.6 0.0 all-to-all-done.1.refs_0_
  113.6 1.0 shard_map.90
  (7 shorter events, 0.1 us)
Async XLA Ops:
  0.6 12.5 %copy-start.1 = (bf16[1,128,768]{2,1,0:T(8,128)(2,1)S(1)}, bf16[1,128,768]{2,1,0:T(8,128)(2,1)}, u32[]{:S(2)}) copy-start(bf16[1,128,768]{2,1,0:T(8,128)(2,1)} %param.6) | copy-start | bytes 589828
  0.6 14.0 %copy-start = (bf16[1,128,768]{2,1,0:T(8,128)(2,1)S(1)}, bf16[1,128,768]{2,1,0:T(8,128)(2,1)}, u32[]{:S(2)}) copy-start(bf16[1,128,768]{2,1,0:T(8,128)(2,1)} %param.5) | copy-start | bytes 589828
  0.7 13.9 %copy-start.4 = (s32[768]{0:T(1024)S(1)}, s32[768]{0:T(1024)}, u32[]{:S(2)}) copy-start(s32[768]{0:T(1024)} %param.9) | copy-start | bytes 9220
  13.2 1.4 %collective-permute-start.3 = (bf16[16,1536]{1,0:T(8,128)(2,1)S(1)}, bf16[16,1536]{1,0:T(8,128)(2,1)S(1)}, u32[]{:S(2)}, u32[]{:S(2)}) collective-permute-start(bf16[16,1536]{1,0:T(8,128)(2,1)S(1)} %get-tuple-element.50), channel_id=1, source_target_pairs={{8,6},{16,14},{24,22},{9,7},{17,15},{25,23}} | collective-permute-start | bytes 147464 | tf_op jit(solution)/shard_map/ppermute | solution.py:335
  13.9 0.7 collective-permute-start.2
  16.6 13.6 %collective-permute-start.4 = (bf16[144,1280]{1,0:T(8,128)(2,1)S(1)}, bf16[144,1280]{1,0:T(8,128)(2,1)S(1)}, u32[]{:S(2)}, u32[]{:S(2)}) collective-permute-start(bf16[144,1280]{1,0:T(8,128)(2,1)S(1)} %get-tuple-element.31), channel_id=1, source_target_pairs={{0,1},{1,0},{2,3},{3,2},{4,5},{5,4},{6,7},{7,6},{8,9},{9,8},{10,11... | collective-permute-start | bytes 1105928 | tf_op jit(solution)/shard_map/ppermute | solution.py:351
  18.1 12.1 %collective-permute-start.5 = (bf16[144,1280]{1,0:T(8,128)(2,1)S(1)}, bf16[144,1280]{1,0:T(8,128)(2,1)S(1)}, u32[]{:S(2)}, u32[]{:S(2)}) collective-permute-start(bf16[144,1280]{1,0:T(8,128)(2,1)S(1)} %get-tuple-element.32), channel_id=1, source_target_pairs={{0,4},{1,5},{2,6},{3,7},{4,0},{5,1},{6,2},{7,3},{8,12},{9,13},{10,... | collective-permute-start | bytes 1105928 | tf_op jit(solution)/shard_map/ppermute | solution.py:351
  18.7 14.2 %collective-permute-start.6 = (bf16[144,1280]{1,0:T(8,128)(2,1)S(1)}, bf16[144,1280]{1,0:T(8,128)(2,1)S(1)}, u32[]{:S(2)}, u32[]{:S(2)}) collective-permute-start(bf16[144,1280]{1,0:T(8,128)(2,1)S(1)} %get-tuple-element.33), channel_id=1, source_target_pairs={{0,5},{1,4},{2,7},{3,6},{4,1},{5,0},{6,3},{7,2},{8,13},{9,12},{10,... | collective-permute-start | bytes 1105928 | tf_op jit(solution)/shard_map/ppermute | solution.py:351
  32.9 4.6 %copy-start.3 = (bf16[8,96,120]{2,1,0:T(8,128)(2,1)S(1)}, bf16[8,96,120]{2,1,0:T(8,128)(2,1)}, u32[]{:S(2)}) copy-start(bf16[8,96,120]{2,1,0:T(8,128)(2,1)} %all_to_all.10) | copy-start | bytes 552964
  32.9 19.3 %copy-start.5 = (f32[768]{0:T(1024)S(1)}, f32[768]{0:T(1024)}, u32[]{:S(2)}) copy-start(f32[768]{0:T(1024)} %param.8) | copy-start | bytes 9220
  33.0 19.3 %collective-permute-start.7 = (bf16[4,144,1024]{2,1,0:T(8,128)(2,1)S(1)}, bf16[4,144,1024]{2,1,0:T(8,128)(2,1)}, u32[]{:S(2)}, u32[]{:S(2)}) collective-permute-start(bf16[4,144,1024]{2,1,0:T(8,128)(2,1)S(1)} %shard_map.85), channel_id=1, source_target_pairs={{0,2},{1,3},{2,0},{3,1},{4,6},{5,7},{6,4},{7,5},{8,10},{9,11},{10,... | collective-permute-start | bytes 3538952 | tf_op jit(solution)/shard_map/ppermute | solution.py:357
  37.5 11.8 %collective-permute-start = (bf16[1,8,96,120]{3,2,1,0:T(8,128)(2,1)S(1)}, bf16[1,8,96,120]{3,2,1,0:T(8,128)(2,1)S(1)}, u32[]{:S(2)}, u32[]{:S(2)}) collective-permute-start(bf16[1,8,96,120]{3,2,1,0:T(8,128)(2,1)S(1)} %bitcast.17), channel_id=1, source_target_pairs={{0,8},{8,0},{16,24},{24,16},{1,9},{9,1},{17,25},{25,17},{2,10},{10... | collective-permute-start | bytes 552968 | tf_op jit(solution)/shard_map/ppermute | solution.py:329
  49.4 19.7 %collective-permute-start.1 = (bf16[2,8,96,120]{3,2,1,0:T(8,128)(2,1)S(1)}, bf16[2,8,96,120]{3,2,1,0:T(8,128)(2,1)}, u32[]{:S(2)}, u32[]{:S(2)}) collective-permute-start(bf16[2,8,96,120]{3,2,1,0:T(8,128)(2,1)S(1)} %pad_maximum_fusion.refs_1_), channel_id=1, source_target_pairs={{0,16},{8,24},{16,0},{24,8},{1,17},{9,25},{17,1},{25,9},{2,18},{10... | collective-permute-start | bytes 1105928 | tf_op jit(solution)/shard_map/ppermute | solution.py:329
  81.1 7.0 %copy-start.2 = (bf16[4,128,1024]{2,1,0:T(8,128)(2,1)S(1)}, bf16[4,128,1024]{2,1,0:T(8,128)(2,1)}, u32[]{:S(2)}) copy-start(bf16[4,128,1024]{2,1,0:T(8,128)(2,1)} %get-tuple-element.39.refs_0_) | copy-start | bytes 3145732
  81.1 32.5 %all-to-all-start.1 = ((bf16[32,112,120]{2,1,0:T(8,128)(2,1)}), bf16[32,112,120]{2,1,0:T(8,128)(2,1)S(1)}, u32[]{:S(2)}, u32[]{:S(2)}) async-start(bf16[32,112,120]{2,1,0:T(8,128)(2,1)} %get-tuple-element.47), calls=%async_computation.1 | async-start | bytes 1835008 | tf_op jit(solution)/shard_map/all_to_all | solution.py:401
  85.1 2.9 %collective-permute-start.8 = (bf16[4,128,1024]{2,1,0:T(8,128)(2,1)}, bf16[4,128,1024]{2,1,0:T(8,128)(2,1)S(1)}, u32[]{:S(2)}, u32[]{:S(2)}) collective-permute-start(bf16[4,128,1024]{2,1,0:T(8,128)(2,1)} %get-tuple-element.40), channel_id=1, source_target_pairs={{0,2},{1,3},{2,0},{3,1},{4,6},{5,7},{6,4},{7,5},{8,10},{9,11},{10,... | collective-permute-start | bytes 3145736 | tf_op jit(solution)/shard_map/ppermute | solution.py:402
  88.6 14.2 %collective-permute-start.9 = (bf16[128,1152]{1,0:T(8,128)(2,1)S(1)}, bf16[128,1152]{1,0:T(8,128)(2,1)S(1)}, u32[]{:S(2)}, u32[]{:S(2)}) collective-permute-start(bf16[128,1152]{1,0:T(8,128)(2,1)S(1)} %get-tuple-element.42), channel_id=1, source_target_pairs={{0,1},{1,0},{2,3},{3,2},{4,5},{5,4},{6,7},{7,6},{8,9},{9,8},{10,11... | collective-permute-start | bytes 884744 | tf_op jit(solution)/shard_map/ppermute | solution.py:410
  90.4 14.4 %collective-permute-start.10 = (bf16[128,1152]{1,0:T(8,128)(2,1)S(1)}, bf16[128,1152]{1,0:T(8,128)(2,1)S(1)}, u32[]{:S(2)}, u32[]{:S(2)}) collective-permute-start(bf16[128,1152]{1,0:T(8,128)(2,1)S(1)} %get-tuple-element.43), channel_id=1, source_target_pairs={{0,4},{1,5},{2,6},{3,7},{4,0},{5,1},{6,2},{7,3},{8,12},{9,13},{10,... | collective-permute-start | bytes 884744 | tf_op jit(solution)/shard_map/ppermute | solution.py:410
  91.9 19.9 %collective-permute-start.11 = (bf16[128,1152]{1,0:T(8,128)(2,1)S(1)}, bf16[128,1152]{1,0:T(8,128)(2,1)S(1)}, u32[]{:S(2)}, u32[]{:S(2)}) collective-permute-start(bf16[128,1152]{1,0:T(8,128)(2,1)S(1)} %get-tuple-element.44), channel_id=1, source_target_pairs={{0,5},{1,4},{2,7},{3,6},{4,1},{5,0},{6,3},{7,2},{8,13},{9,12},{10,... | collective-permute-start | bytes 884744 | tf_op jit(solution)/shard_map/ppermute | solution.py:410

commit v7 on v6

--- a/solution.py
+++ b/solution.py
@@ -27,7 +27,7 @@
         out_specs=out_specs or jax.tree.map(lambda _: VMEM, outs),
         scratch_shapes=list(scratch),
         compiler_params=pltpu.CompilerParams(vmem_limit_bytes=vmem * 2**20),
-        cost_estimate=pl.CostEstimate(flops=flops, bytes_accessed=moved, transcendentals=0),
+        cost_estimate=pl.CostEstimate(flops=0, bytes_accessed=0, transcendentals=0),
     )(*args)
 
 
@@ -327,7 +327,6 @@
     for mask in stages:
         near = far if mask == 1 else jnp.concatenate([near, far])
         far = lax.ppermute(near, BLOCK, flipped_pairs(seq_blocks * dp_blocks, mask))
-    slices, values, cot = lax.optimization_barrier((slices, values, cot))
     along = ("seq_block", "seq_rank")
     ends = [(b * seq_ranks - 1, b * seq_ranks) for b in range(1, seq_blocks)]
     both = jnp.concatenate([values, cot], -1)
@@ -351,6 +350,7 @@
         lax.ppermute(message, RANK, flipped_pairs(ranks, mask))
         for message, mask in zip(leaving, masks[1:])
     ]
+    far, cross = lax.optimization_barrier((far, cross))
     crossing = called(
         stack_crossing, shape_of((len(masks), block, width), bf16), (cross, *arrived), 8
     )

time: 115 us -> 95.9 us (0.83)
  waiting for transfers between devices: 53.1 us -> 41.1 us
  starting transfers between devices: 27.1 us -> 20.3 us
    ppermute x6, waiting for transfers between devices: 32.4 us -> 24.6 us  [per_device(): lax.ppermute(message, RANK, flipped_pairs(ranks, mask))]
    ppermute x2, waiting for transfers between devices: 18.1 us -> 10.7 us  [per_device(): far = lax.ppermute(near, BLOCK, flipped_pairs(seq_blocks * dp_blocks, mask))]
    ppermute x1, starting transfers between devices: 4.47 us -> 0.01 us  [per_device(): crossed = lax.ppermute(crossing, RANK, flipped_pairs(ranks, core))]
    ppermute x1, waiting for transfers between devices: 0.01 us -> 2.97 us  [per_device(): crossed = lax.ppermute(crossing, RANK, flipped_pairs(ranks, core))]
    all_to_all x1, starting transfers between devices: 4.03 us -> 2.78 us  [per_device(): terms = lax.all_to_all(outgoing, EVERY, 0, 0, tiled=True)]
  transfers between devices with their start and end apart: 13 -> 13, of which waited for: 8 -> 8; matrix products, arithmetic and copies ran while one was open for 0% -> 1% of each run, Pallas kernels for 5% -> 4%
where the time goes in v7:
time: 95.9 us; the launch traced here: 95.5 us
  waiting for transfers between devices  41.1 us (43%)
  starting transfers between devices  20.3 us (21%)
  Pallas kernels  20.1 us (21%)
  blocking collectives  10.3 us (11%)
  local copies, waits for them, and re-layouts  1.93 us (2%)
  other arithmetic  0.98 us (1%)
    ppermute x6, waiting for transfers between devices, per_device(): lax.ppermute(message, RANK, flipped_pairs(ranks, mask))  24.6 us
    pallas_call x7, Pallas kernels, called(): pl.pallas_call(body, out_shape=outs, in_specs=specs or [VMEM] * len(args)...  20.1 us
    ppermute x2, waiting for transfers between devices, per_device(): far = lax.ppermute(near, BLOCK, flipped_pairs(seq_blocks * dp_blocks, mask))  10.7 us
    all_to_all x1, blocking collectives, per_device(): lax.all_to_all(weights.T.reshape(ranks, part, rows), RANK, 0, 0, tiled=True)  10.3 us
    ppermute x2, starting transfers between devices, per_device(): far = lax.ppermute(near, BLOCK, flipped_pairs(seq_blocks * dp_blocks, mask))  8.95 us
    ppermute x6, starting transfers between devices, per_device(): lax.ppermute(message, RANK, flipped_pairs(ranks, mask))  7.04 us
    ppermute x1, waiting for transfers between devices, per_device(): crossed = lax.ppermute(crossing, RANK, flipped_pairs(ranks, core))  2.97 us
    all_to_all x1, starting transfers between devices, per_device(): terms = lax.all_to_all(outgoing, EVERY, 0, 0, tiled=True)  2.78 us
  transfers between devices with their start and end apart: 13, of which 8 were waited for; matrix products, arithmetic and copies ran while one was open for 1% of the time, Pallas kernels for 4%

profile of v7, /device:TPU:0, one launch (start us, length us, event | category | flops | bytes accessed | tf_op | source)
XLA Modules:
  0.0 95.5 jit_solution(9260541862045109366)
XLA Ops:
  0.6 0.0 copy-start.1
  0.6 0.0 copy-start
  0.7 0.0 copy-start.5
  0.7 1.1 %copy.9 = bf16[768,120]{1,0:T(8,128)(2,1)S(1)} copy(bf16[768,120]{0,1:T(8,128)(2,1)} %bitcast.19) | data formatting | bytes 368640 | tf_op jit(solution)/shard_map/transpose | solution.py:324
  1.8 10.3 %all_to_all.10 = bf16[8,96,120]{2,1,0:T(8,128)(2,1)S(1)} all-to-all(bf16[8,96,120]{2,1,0:T(8,128)(2,1)S(1)} %bitcast.16), channel_id=1, replica_groups=mesh['seq_block'=4,'seq_rank'=4,'dp_block'=1,'dp_rank'=2] {'seq_rank','d..., dimensions={0} | all-to-all | bytes 368640 | tf_op jit(solution)/shard_map/all_to_all | solution.py:324
  12.1 1.6 %collective-permute-start = (bf16[1,8,96,120]{3,2,1,0:T(8,128)(2,1)S(1)}, bf16[1,8,96,120]{3,2,1,0:T(8,128)(2,1)S(1)}, u32[]{:S(2)}, u32[]{:S(2)}) collective-permute-start(bf16[1,8,96,120]{3,2,1,0:T(8,128)(2,1)S(1)} %bitcast.17), channel_id=1, source_target_pairs={{0,8},{8,0},{16,24},{24,16},{1,9},{9,1},{17,25},{25,17},{2,10},{10... | collective-permute-start | bytes 552968 | tf_op jit(solution)/shard_map/ppermute | solution.py:329
  13.7 0.8 pad_maximum_fusion.1
  14.5 0.7 collective-permute-start.3
  15.2 0.7 collective-permute-start.2
  15.8 0.0 copy-done.5
  15.9 0.0 collective-permute-done.3
  15.9 0.0 collective-permute-done.2
  15.9 0.0 copy-done.1
  15.9 0.0 copy-done
  15.9 1.9 %shard_map.84 = (bf16[144,1024]{1,0:T(8,128)(2,1)S(1)}, bf16[144,1024]{1,0:T(8,128)(2,1)S(1)}, bf16[144,1280]{1,0:T(8,128)(2,1)S(1)}, bf16[144,1280]{1,0:T(8,128)(2,1)S(1)}, bf16[144,1280]{1,0:T(8,128)(2,1)S(1)}) custom-call(s32[1]{0:T(128)} %bitcast.refs_0_, bf16[128,768]{1,0:T(8,128)(2,1)S(1)} %bitcast.11, bf16[128,768]{1,0:T(8,128)(2,1)S(1)} %bitcast.14, ...), custom_call_target="tpu_custom_call" | custom-call | tf_op jit(solution)/shard_map/pallas_call | solution.py:23
  17.9 1.5 %collective-permute-done = bf16[1,8,96,120]{3,2,1,0:T(8,128)(2,1)S(1)} collective-permute-done((bf16[1,8,96,120]{3,2,1,0:T(8,128)(2,1)S(1)}, bf16[1,8,96,120]{3,2,1,0:T(8,128)(2,1)S(1)}, u32[]{:S(2)}, u32[]{:S(2)}) %collective-permute-start) | collective-permute-done | bytes 184352 | tf_op jit(solution)/shard_map/ppermute | solution.py:329
  19.4 0.1 pad_maximum_fusion.refs_1_
  19.5 7.4 %collective-permute-start.1 = (bf16[2,8,96,120]{3,2,1,0:T(8,128)(2,1)S(1)}, bf16[2,8,96,120]{3,2,1,0:T(8,128)(2,1)S(1)}, u32[]{:S(2)}, u32[]{:S(2)}) collective-permute-start(bf16[2,8,96,120]{3,2,1,0:T(8,128)(2,1)S(1)} %pad_maximum_fusion.refs_1_), channel_id=1, source_target_pairs={{0,16},{8,24},{16,0},{24,8},{1,17},{9,25},{17,1},{25,9},{2,18},{10... | collective-permute-start | bytes 1105928 | tf_op jit(solution)/shard_map/ppermute | solution.py:329
  26.8 1.5 %collective-permute-start.4 = (bf16[144,1280]{1,0:T(8,128)(2,1)S(1)}, bf16[144,1280]{1,0:T(8,128)(2,1)S(1)}, u32[]{:S(2)}, u32[]{:S(2)}) collective-permute-start(bf16[144,1280]{1,0:T(8,128)(2,1)S(1)} %get-tuple-element.31), channel_id=1, source_target_pairs={{0,1},{1,0},{2,3},{3,2},{4,5},{5,4},{6,7},{7,6},{8,9},{9,8},{10,11... | collective-permute-start | bytes 1105928 | tf_op jit(solution)/shard_map/ppermute | solution.py:350
  28.3 0.0 collective-permute-start.5
  28.3 2.0 %collective-permute-start.6 = (bf16[144,1280]{1,0:T(8,128)(2,1)S(1)}, bf16[144,1280]{1,0:T(8,128)(2,1)S(1)}, u32[]{:S(2)}, u32[]{:S(2)}) collective-permute-start(bf16[144,1280]{1,0:T(8,128)(2,1)S(1)} %get-tuple-element.33), channel_id=1, source_target_pairs={{0,5},{1,4},{2,7},{3,6},{4,1},{5,0},{6,3},{7,2},{8,13},{9,12},{10,... | collective-permute-start | bytes 1105928 | tf_op jit(solution)/shard_map/ppermute | solution.py:350
  30.3 9.2 %collective-permute-done.1.refs_2_ = bf16[2,8,96,120]{3,2,1,0:T(8,128)(2,1)S(1)} collective-permute-done((bf16[2,8,96,120]{3,2,1,0:T(8,128)(2,1)S(1)}, bf16[2,8,96,120]{3,2,1,0:T(8,128)(2,1)S(1)}, u32[]{:S(2)}, u32[]{:S(2)}) %collective-permute-start.1) | collective-permute-done | bytes 368672 | tf_op jit(solution)/shard_map/ppermute | solution.py:329
  39.6 0.7 copy-done.3
  40.3 0.0 collective-permute-done.4.refs_0_.refs_3_
  40.3 0.0 collective-permute-done.5.refs_1_.refs_4_
  40.3 5.1 %collective-permute-done.6.refs_2_.refs_5_ = bf16[144,1280]{1,0:T(8,128)(2,1)S(1)} collective-permute-done((bf16[144,1280]{1,0:T(8,128)(2,1)S(1)}, bf16[144,1280]{1,0:T(8,128)(2,1)S(1)}, u32[]{:S(2)}, u32[]{:S(2)}) %collective-permute-start.6) | collective-permute-done | bytes 368672 | tf_op jit(solution)/shard_map/ppermute | solution.py:350
  45.4 1.1 %shard_map.85 = bf16[4,144,1024]{2,1,0:T(8,128)(2,1)} custom-call(bf16[144,1024]{1,0:T(8,128)(2,1)S(1)} %get-tuple-element.30.cross_ref, bf16[144,1280]{1,0:T(8,128)(2,1)S(1)} %collective-permute-done.4.refs_0_.refs_3_, bf16[144,1280]{1,0:T(8,128)(2,1)S(1)} %collective-permute-done.5.refs_1_.refs_4_, bf16[144,1280]{1,0:T(8,128)(2,1)S(1)} %collective-permute-done.6.refs_2_.refs_5_), custom_call_target="tpu_custom_call" | custom-call | tf_op jit(solution)/shard_map/pallas_call | solution.py:23
  46.5 0.0 collective-permute-start.7
  46.6 0.0 copy-done.6
  46.6 0.1 pad_add_fusion.refs_0_
  46.6 3.0 %collective-permute-done.7.refs_2_ = bf16[4,144,1024]{2,1,0:T(8,128)(2,1)S(1)} collective-permute-done((bf16[4,144,1024]{2,1,0:T(8,128)(2,1)}, bf16[4,144,1024]{2,1,0:T(8,128)(2,1)S(1)}, u32[]{:S(2)}, u32[]{:S(2)}) %collective-permute-start.7) | collective-permute-done | bytes 1179680 | tf_op jit(solution)/shard_map/ppermute | solution.py:357
  49.6 2.3 %shard_map.86 = (bf16[4,512,768]{2,1,0:T(8,128)(2,1)S(1)}, bf16[4,512,128]{2,1,0:T(8,128)(2,1)S(1)}, bf16[3,4,16,768]{3,2,1,0:T(8,128)(2,1)S(1)}, bf16[3,4,16,128]{3,2,1,0:T(8,128)(2,1)S(1)}, f32[1,768]{1,0:T(1,128)S(1)}) custom-call(s32[1]{0:T(128)} %bitcast.refs_0_, bf16[144,1024]{1,0:T(8,128)(2,1)S(1)} %get-tuple-element.29.refs_1_, ...), custom_call_target="tpu_custom_call" | custom-call | tf_op jit(solution)/shard_map/pallas_call | solution.py:23
  51.9 0.0 copy-done.4
  51.9 11.5 %shard_map.87 = (bf16[32,112,120]{2,1,0:T(8,128)(2,1)}, bf16[4,128,1024]{2,1,0:T(8,128)(2,1)}, bf16[4,128,1024]{2,1,0:T(8,128)(2,1)}) custom-call(s32[2]{0:T(128)S(1)} %pad_add_fusion.refs_0_, bf16[2,8,96,120]{3,2,1,0:T(8,128)(2,1)S(1)} %pad_maximum_fusion.refs_1_, bf16[2,8,96,120]{3,2,1,0:T(8,128)(2,1)S(1)} %copy-done.4, ...), custom_call_target="tpu_custom_call" | custom-call | tf_op jit(solution)/shard_map/pallas_call | solution.py:23
  63.4 0.0 copy-start.2
  63.4 2.8 %all-to-all-start.1 = ((bf16[32,112,120]{2,1,0:T(8,128)(2,1)}), bf16[32,112,120]{2,1,0:T(8,128)(2,1)S(1)}, u32[]{:S(2)}, u32[]{:S(2)}) async-start(bf16[32,112,120]{2,1,0:T(8,128)(2,1)} %get-tuple-element.47), calls=%async_computation.1 | async-start | bytes 1835008 | tf_op jit(solution)/shard_map/all_to_all | solution.py:401
  66.2 0.2 collective-permute-start.8
  66.4 2.7 %collective-permute-done.8.refs_1_ = bf16[4,128,1024]{2,1,0:T(8,128)(2,1)S(1)} collective-permute-done((bf16[4,128,1024]{2,1,0:T(8,128)(2,1)}, bf16[4,128,1024]{2,1,0:T(8,128)(2,1)S(1)}, u32[]{:S(2)}, u32[]{:S(2)}) %collective-permute-start.8) | collective-permute-done | bytes 1048608 | tf_op jit(solution)/shard_map/ppermute | solution.py:402
  69.2 0.5 shard_map.88
  69.7 1.7 %collective-permute-start.9 = (bf16[128,1152]{1,0:T(8,128)(2,1)S(1)}, bf16[128,1152]{1,0:T(8,128)(2,1)S(1)}, u32[]{:S(2)}, u32[]{:S(2)}) collective-permute-start(bf16[128,1152]{1,0:T(8,128)(2,1)S(1)} %get-tuple-element.42), channel_id=1, source_target_pairs={{0,1},{1,0},{2,3},{3,2},{4,5},{5,4},{6,7},{7,6},{8,9},{9,8},{10,11... | collective-permute-start | bytes 884744 | tf_op jit(solution)/shard_map/ppermute | solution.py:410
  71.4 1.5 %collective-permute-start.10 = (bf16[128,1152]{1,0:T(8,128)(2,1)S(1)}, bf16[128,1152]{1,0:T(8,128)(2,1)S(1)}, u32[]{:S(2)}, u32[]{:S(2)}) collective-permute-start(bf16[128,1152]{1,0:T(8,128)(2,1)S(1)} %get-tuple-element.43), channel_id=1, source_target_pairs={{0,4},{1,5},{2,6},{3,7},{4,0},{5,1},{6,2},{7,3},{8,12},{9,13},{10,... | collective-permute-start | bytes 884744 | tf_op jit(solution)/shard_map/ppermute | solution.py:410
  72.9 0.4 collective-permute-start.11
  73.2 10.6 %collective-permute-done.9.refs_5_ = bf16[128,1152]{1,0:T(8,128)(2,1)S(1)} collective-permute-done((bf16[128,1152]{1,0:T(8,128)(2,1)S(1)}, bf16[128,1152]{1,0:T(8,128)(2,1)S(1)}, u32[]{:S(2)}, u32[]{:S(2)}) %collective-permute-start.9) | collective-permute-done | bytes 294944 | tf_op jit(solution)/shard_map/ppermute | solution.py:410
  83.9 2.0 %collective-permute-done.10.refs_6_ = bf16[128,1152]{1,0:T(8,128)(2,1)S(1)} collective-permute-done((bf16[128,1152]{1,0:T(8,128)(2,1)S(1)}, bf16[128,1152]{1,0:T(8,128)(2,1)S(1)}, u32[]{:S(2)}, u32[]{:S(2)}) %collective-permute-start.10) | collective-permute-done | bytes 294944 | tf_op jit(solution)/shard_map/ppermute | solution.py:410
  85.8 6.9 %collective-permute-done.11.refs_7_ = bf16[128,1152]{1,0:T(8,128)(2,1)S(1)} collective-permute-done((bf16[128,1152]{1,0:T(8,128)(2,1)S(1)}, bf16[128,1152]{1,0:T(8,128)(2,1)S(1)}, u32[]{:S(2)}, u32[]{:S(2)}) %collective-permute-start.11) | collective-permute-done | bytes 294944 | tf_op jit(solution)/shard_map/ppermute | solution.py:410
  92.8 1.8 %shard_map.89 = (bf16[128,768]{1,0:T(8,128)(2,1)}, bf16[128,768]{1,0:T(8,128)(2,1)}) custom-call(s32[1]{0:T(128)} %bitcast.refs_0_, bf16[128,768]{1,0:T(8,128)(2,1)S(1)} %bitcast.12, bf16[128,768]{1,0:T(8,128)(2,1)S(1)} %bitcast.15, s32[1,768]{1,0:T(1,128)S(1)} %reshape.24.refs_4_.refs_7_.refs_9_.refs_3_, bf16[128,1152]{1,0:T(8,128)(2,1)S(1)} %get-tuple-element.41.refs_4_, ...), custom_call_target="tpu_custom_call" | custom-call | tf_op jit(solution)/shard_map/pallas_call | solution.py:23
  94.6 0.0 all-to-all-done.1.refs_0_
  94.6 1.0 %shard_map.90 = (f32[120,768]{1,0:T(8,128)}, f32[1,24]{1,0:T(1,128)}) custom-call(bf16[32,112,120]{2,1,0:T(8,128)(2,1)S(1)} %all-to-all-done.1.refs_0_), custom_call_target="tpu_custom_call" | custom-call | tf_op jit(solution)/shard_map/pallas_call | solution.py:23
  (7 shorter events, 0.0 us)
Async XLA Ops:
  0.6 15.3 %copy-start.1 = (bf16[1,128,768]{2,1,0:T(8,128)(2,1)S(1)}, bf16[1,128,768]{2,1,0:T(8,128)(2,1)}, u32[]{:S(2)}) copy-start(bf16[1,128,768]{2,1,0:T(8,128)(2,1)} %param.6) | copy-start | bytes 589828
  0.6 15.3 %copy-start = (bf16[1,128,768]{2,1,0:T(8,128)(2,1)S(1)}, bf16[1,128,768]{2,1,0:T(8,128)(2,1)}, u32[]{:S(2)}) copy-start(bf16[1,128,768]{2,1,0:T(8,128)(2,1)} %param.5) | copy-start | bytes 589828
  0.7 15.2 %copy-start.5 = (s32[768]{0:T(1024)S(1)}, s32[768]{0:T(1024)}, u32[]{:S(2)}) copy-start(s32[768]{0:T(1024)} %param.9) | copy-start | bytes 9220
  12.1 7.3 %collective-permute-start = (bf16[1,8,96,120]{3,2,1,0:T(8,128)(2,1)S(1)}, bf16[1,8,96,120]{3,2,1,0:T(8,128)(2,1)S(1)}, u32[]{:S(2)}, u32[]{:S(2)}) collective-permute-start(bf16[1,8,96,120]{3,2,1,0:T(8,128)(2,1)S(1)} %bitcast.17), channel_id=1, source_target_pairs={{0,8},{8,0},{16,24},{24,16},{1,9},{9,1},{17,25},{25,17},{2,10},{10... | collective-permute-start | bytes 552968 | tf_op jit(solution)/shard_map/ppermute | solution.py:329
  14.5 1.4 %collective-permute-start.3 = (bf16[16,1536]{1,0:T(8,128)(2,1)S(1)}, bf16[16,1536]{1,0:T(8,128)(2,1)S(1)}, u32[]{:S(2)}, u32[]{:S(2)}) collective-permute-start(bf16[16,1536]{1,0:T(8,128)(2,1)S(1)} %get-tuple-element.50), channel_id=1, source_target_pairs={{8,6},{16,14},{24,22},{9,7},{17,15},{25,23}} | collective-permute-start | bytes 147464 | tf_op jit(solution)/shard_map/ppermute | solution.py:334
  15.2 0.7 collective-permute-start.2
  19.5 20.1 %collective-permute-start.1 = (bf16[2,8,96,120]{3,2,1,0:T(8,128)(2,1)S(1)}, bf16[2,8,96,120]{3,2,1,0:T(8,128)(2,1)S(1)}, u32[]{:S(2)}, u32[]{:S(2)}) collective-permute-start(bf16[2,8,96,120]{3,2,1,0:T(8,128)(2,1)S(1)} %pad_maximum_fusion.refs_1_), channel_id=1, source_target_pairs={{0,16},{8,24},{16,0},{24,8},{1,17},{9,25},{17,1},{25,9},{2,18},{10... | collective-permute-start | bytes 1105928 | tf_op jit(solution)/shard_map/ppermute | solution.py:329
  26.8 13.5 %collective-permute-start.4 = (bf16[144,1280]{1,0:T(8,128)(2,1)S(1)}, bf16[144,1280]{1,0:T(8,128)(2,1)S(1)}, u32[]{:S(2)}, u32[]{:S(2)}) collective-permute-start(bf16[144,1280]{1,0:T(8,128)(2,1)S(1)} %get-tuple-element.31), channel_id=1, source_target_pairs={{0,1},{1,0},{2,3},{3,2},{4,5},{5,4},{6,7},{7,6},{8,9},{9,8},{10,11... | collective-permute-start | bytes 1105928 | tf_op jit(solution)/shard_map/ppermute | solution.py:350
  28.3 12.0 %collective-permute-start.5 = (bf16[144,1280]{1,0:T(8,128)(2,1)S(1)}, bf16[144,1280]{1,0:T(8,128)(2,1)S(1)}, u32[]{:S(2)}, u32[]{:S(2)}) collective-permute-start(bf16[144,1280]{1,0:T(8,128)(2,1)S(1)} %get-tuple-element.32), channel_id=1, source_target_pairs={{0,4},{1,5},{2,6},{3,7},{4,0},{5,1},{6,2},{7,3},{8,12},{9,13},{10,... | collective-permute-start | bytes 1105928 | tf_op jit(solution)/shard_map/ppermute | solution.py:350
  28.3 17.1 %collective-permute-start.6 = (bf16[144,1280]{1,0:T(8,128)(2,1)S(1)}, bf16[144,1280]{1,0:T(8,128)(2,1)S(1)}, u32[]{:S(2)}, u32[]{:S(2)}) collective-permute-start(bf16[144,1280]{1,0:T(8,128)(2,1)S(1)} %get-tuple-element.33), channel_id=1, source_target_pairs={{0,5},{1,4},{2,7},{3,6},{4,1},{5,0},{6,3},{7,2},{8,13},{9,12},{10,... | collective-permute-start | bytes 1105928 | tf_op jit(solution)/shard_map/ppermute | solution.py:350
  39.5 0.7 copy-start.3
  40.3 6.3 %copy-start.6 = (f32[768]{0:T(1024)S(1)}, f32[768]{0:T(1024)}, u32[]{:S(2)}) copy-start(f32[768]{0:T(1024)} %param.8) | copy-start | bytes 9220
  46.5 3.1 %collective-permute-start.7 = (bf16[4,144,1024]{2,1,0:T(8,128)(2,1)}, bf16[4,144,1024]{2,1,0:T(8,128)(2,1)S(1)}, u32[]{:S(2)}, u32[]{:S(2)}) collective-permute-start(bf16[4,144,1024]{2,1,0:T(8,128)(2,1)} %shard_map.85), channel_id=1, source_target_pairs={{0,2},{1,3},{2,0},{3,1},{4,6},{5,7},{6,4},{7,5},{8,10},{9,11},{10,... | collective-permute-start | bytes 3538952 | tf_op jit(solution)/shard_map/ppermute | solution.py:357
  49.6 2.3 %copy-start.4 = (bf16[2,8,96,120]{3,2,1,0:T(8,128)(2,1)S(1)}, bf16[2,8,96,120]{3,2,1,0:T(8,128)(2,1)}, u32[]{:S(2)}) copy-start(bf16[2,8,96,120]{3,2,1,0:T(8,128)(2,1)} %copy-done.3) | copy-start | bytes 1105924
  63.4 5.7 %copy-start.2 = (bf16[4,128,1024]{2,1,0:T(8,128)(2,1)S(1)}, bf16[4,128,1024]{2,1,0:T(8,128)(2,1)}, u32[]{:S(2)}) copy-start(bf16[4,128,1024]{2,1,0:T(8,128)(2,1)} %get-tuple-element.39.refs_0_) | copy-start | bytes 3145732
  63.4 31.2 %all-to-all-start.1 = ((bf16[32,112,120]{2,1,0:T(8,128)(2,1)}), bf16[32,112,120]{2,1,0:T(8,128)(2,1)S(1)}, u32[]{:S(2)}, u32[]{:S(2)}) async-start(bf16[32,112,120]{2,1,0:T(8,128)(2,1)} %get-tuple-element.47), calls=%async_computation.1 | async-start | bytes 1835008 | tf_op jit(solution)/shard_map/all_to_all | solution.py:401
  66.2 2.9 %collective-permute-start.8 = (bf16[4,128,1024]{2,1,0:T(8,128)(2,1)}, bf16[4,128,1024]{2,1,0:T(8,128)(2,1)S(1)}, u32[]{:S(2)}, u32[]{:S(2)}) collective-permute-start(bf16[4,128,1024]{2,1,0:T(8,128)(2,1)} %get-tuple-element.40), channel_id=1, source_target_pairs={{0,2},{1,3},{2,0},{3,1},{4,6},{5,7},{6,4},{7,5},{8,10},{9,11},{10,... | collective-permute-start | bytes 3145736 | tf_op jit(solution)/shard_map/ppermute | solution.py:402
  69.7 14.2 %collective-permute-start.9 = (bf16[128,1152]{1,0:T(8,128)(2,1)S(1)}, bf16[128,1152]{1,0:T(8,128)(2,1)S(1)}, u32[]{:S(2)}, u32[]{:S(2)}) collective-permute-start(bf16[128,1152]{1,0:T(8,128)(2,1)S(1)} %get-tuple-element.42), channel_id=1, source_target_pairs={{0,1},{1,0},{2,3},{3,2},{4,5},{5,4},{6,7},{7,6},{8,9},{9,8},{10,11... | collective-permute-start | bytes 884744 | tf_op jit(solution)/shard_map/ppermute | solution.py:410
  71.4 14.4 %collective-permute-start.10 = (bf16[128,1152]{1,0:T(8,128)(2,1)S(1)}, bf16[128,1152]{1,0:T(8,128)(2,1)S(1)}, u32[]{:S(2)}, u32[]{:S(2)}) collective-permute-start(bf16[128,1152]{1,0:T(8,128)(2,1)S(1)} %get-tuple-element.43), channel_id=1, source_target_pairs={{0,4},{1,5},{2,6},{3,7},{4,0},{5,1},{6,2},{7,3},{8,12},{9,13},{10,... | collective-permute-start | bytes 884744 | tf_op jit(solution)/shard_map/ppermute | solution.py:410
  72.9 19.9 %collective-permute-start.11 = (bf16[128,1152]{1,0:T(8,128)(2,1)S(1)}, bf16[128,1152]{1,0:T(8,128)(2,1)S(1)}, u32[]{:S(2)}, u32[]{:S(2)}) collective-permute-start(bf16[128,1152]{1,0:T(8,128)(2,1)S(1)} %get-tuple-element.44), channel_id=1, source_target_pairs={{0,5},{1,4},{2,7},{3,6},{4,1},{5,0},{6,3},{7,2},{8,13},{9,12},{10,... | collective-permute-start | bytes 884744 | tf_op jit(solution)/shard_map/ppermute | solution.py:410

commit v8 on v7

--- a/solution.py
+++ b/solution.py
@@ -19,7 +19,7 @@
 f32 = jnp.float32
 
 
-def called(body, outs, args, vmem, scratch=(), specs=None, out_specs=None, flops=0, moved=0):
+def called(body, outs, args, vmem, scratch=(), specs=None, out_specs=None):
     return pl.pallas_call(
         body,
         out_shape=outs,
@@ -143,15 +143,20 @@
 
 
 def main_body(sizes, place_ref, near_ref, far_ref, normed_ref, grads_ref, edge_normed_ref, edge_grads_ref, *refs):
-    gain_ref, swapped_gain_ref, pairing_ref, sent_ref, own_ref, cross_ref = refs[:6]
-    pieces, kernel_ref, shifted, gelus, terms, halves, bent, slopes, total, scaled = refs[6:16]
-    out_ref, own, cross, sems = refs[16:]
     seq_blocks, dp_blocks, seq_ranks, dp_ranks = sizes
-    rank, me = place_ref[0], place_ref[1]
-    owners = seq_blocks * dp_blocks * seq_ranks * dp_ranks
+    blocks = seq_blocks * dp_blocks
+    gain_ref, shifted_out, kernel_out, gelu_out, leaving_out = refs[:5]
+    pieces, padded, terms, halves, bent, slopes, total, shifted_ref, kernel_ref, gelu_ref, leaving, sems = refs[5:]
+    copies = []
+
+    def send(source, target):
+        copies.append(pltpu.make_async_copy(source, target, sems.at[len(copies)]))
+        copies[-1].start()
+
+    me = place_ref[1]
     part, rows = near_ref.shape[2:]
     strands, span, channels = normed_ref.shape
-    taps = kernel_ref.shape[0] // LANES
+    taps = kernel_ref.shape[0] // part
     half = taps // 2
     reach = 2 * half
     wide = bent.shape[0]
@@ -167,7 +172,6 @@
     for ref, first in ((near_ref, 0), (far_ref, near_ref.shape[0])):
         for j in range(ref.shape[0]):
             pieces[lax.bitwise_xor(me, first + j)] = ref[j]
-    kernel_ref[...] = jnp.zeros_like(kernel_ref)
     places = [
         (sb * dp_blocks + db, sr * dp_ranks + dr)
         for sb in range(seq_blocks)
@@ -177,10 +181,14 @@
     ]
     for owner, (source, piece) in enumerate(places):
         for tap, channel, count, offset in runs(owner):
-            kernel_ref[tap * LANES : tap * LANES + part, channel : channel + count] = pieces[
+            kernel_ref[tap * part : (tap + 1) * part, channel : channel + count] = pieces[
                 source, piece, :, offset : offset + count
             ]
-    kernel = kernel_ref[...]
+    send(kernel_ref, kernel_out)
+    padded[...] = jnp.zeros_like(padded)
+    for k in range(taps):
+        padded[k * LANES : k * LANES + part, :] = kernel_ref[k * part : (k + 1) * part, :]
+    kernel = padded[...]
     edge_normed = jnp.concatenate([edge_normed_ref[side, s] for side in range(2) for s in range(strands)], 0)
     edge_terms = dot(edge_normed, kernel, ((1,), (1,)))
     for strand in range(strands):
@@ -197,52 +205,70 @@
             preact += terms[start : start + wide, k * LANES : (k + 1) * LANES]
         result, slope = gelu_and_slope(preact)
         bent[...] = result
-        gelus[strand] = bent[half : half + span, :].astype(bf16)
+        gelu_ref[strand] = bent[half : half + span, :].astype(bf16)
         slopes[...] = halves[HALO - half : HALO - half + wide, :] * slope
         for k in range(taps):
             start = reach - k if forward else k
-            shifted[strand, :, k * LANES : (k + 1) * LANES] = slopes[start : start + span, :].astype(bf16)
+            shifted_ref[strand, :, k * part : (k + 1) * part] = slopes[start : start + span, :part].astype(bf16)
+        send(shifted_ref.at[strand], shifted_out.at[strand])
+    send(gelu_ref, gelu_out)
     total[...] = dot(
-        shifted[...].reshape(strands * span, taps * LANES),
+        shifted_ref[...].reshape(strands * span, taps * part),
         normed_ref[...].reshape(strands * span, channels),
         ((0,), (0,)),
     )
-    gain = jnp.sum(total[...] * kernel.astype(f32), 0, keepdims=True) / gain_ref[...]
+    gain = jnp.sum(total[...] * kernel_ref[...].astype(f32), 0, keepdims=True) / gain_ref[...]
     gain_high = gain.astype(bf16).astype(f32)
     row = lax.broadcasted_iota(jnp.int32, (EXTRA, channels), 0)
     extra = jnp.where(row == 0, gain_high, jnp.where(row == 1, gain - gain_high, 0.0))
-    own_gain = channels // owners
-    for owner in range(owners):
+    own_gain = channels // len(places)
+    for owner in range(len(places)):
         for tap, channel, count, offset in runs(owner):
-            out_ref[owner, :part, offset : offset + count] = total[
-                tap * LANES : tap * LANES + part, channel : channel + count
+            leaving[owner, :part, offset : offset + count] = total[
+                tap * part : (tap + 1) * part, channel : channel + count
             ].astype(bf16)
-        out_ref[owner, part:, :] = jnp.zeros((EXTRA, rows), bf16)
-        out_ref[owner, part:, :own_gain] = extra[
+        leaving[owner, part:, :] = jnp.zeros((EXTRA, rows), bf16)
+        leaving[owner, part:, :own_gain] = extra[
             :, owner * own_gain : (owner + 1) * own_gain
         ].astype(bf16)
-    copies = [pltpu.make_async_copy(out_ref, sent_ref, sems.at[0])]
-    copies[0].start()
+    send(leaving, leaving_out)
+    for copy in copies:
+        copy.wait()
+
+
+def input_gradient(
+    place_ref, shifted_ref, kernel_ref, gelu_ref, gain_ref, swapped_gain_ref, pairing_ref, own_ref, cross_ref, *scratch
+):
+    scaled, shifted, kernel_in, gelus, sems = scratch
+    strands = shifted_ref.shape[0]
+    moves = [(kernel_ref, kernel_in)]
+    moves += [(shifted_ref.at[n], shifted.at[n]) for n in range(strands)]
+    moves += [(gelu_ref, gelus)]
+    copies = [pltpu.make_async_copy(*move, sems.at[n]) for n, move in enumerate(moves)]
+    for copy in copies:
+        copy.start()
+    dp_ranks = strands // 2
+    chips, positions, _ = own_ref.shape
+    channels = gain_ref.shape[1]
+    copies[0].wait()
+    kernel = kernel_in[...]
     swapped = dot(kernel, swap_map(pairing_ref[...]), ((1,), (0,))).astype(bf16)
+    for copy in copies[1:]:
+        copy.wait()
     for b in range(dp_ranks):
         scaled[b] = (
             dot(shifted[b], kernel, ((1,), (0,))) * gain_ref[...]
             + dot(shifted[dp_ranks + b], swapped, ((1,), (0,))) * swapped_gain_ref[...]
         ).astype(bf16)
-    chips, positions, _ = own.shape
-    for c, (out, ref) in enumerate(((cross, cross_ref), (own, own_ref))):
-        for m, mask in enumerate(chip_masks(2 * chips, dp_ranks)):
-            target = lax.bitwise_xor(rank, mask if c else mask | dp_ranks)
+    for m, mask in enumerate(chip_masks(2 * chips, dp_ranks)):
+        for out, flip in ((own_ref, mask), (cross_ref, mask | dp_ranks)):
+            target = lax.bitwise_xor(place_ref[0], flip)
             b = lax.rem(target, dp_ranks)
             start = pl.multiple_of(lax.div(target, dp_ranks) * positions, positions)
             out[m, :, :channels] = scaled[b, pl.ds(start, positions), :]
             for n in range(2):
                 lane = channels + n * LANES
                 out[m, :, lane : lane + LANES] = gelus[n * dp_ranks + b, pl.ds(start, positions), :]
-        copies.append(pltpu.make_async_copy(out, ref, sems.at[1 + c]))
-        copies[-1].start()
-    for copy in copies:
-        copy.wait()
 
 
 def chip_sum(part, own_ref, crossed_ref, *outs):
@@ -321,17 +347,20 @@
     rank = lax.axis_index(RANK).reshape(1)
     place = jnp.concatenate([rank, lax.axis_index(BLOCK).reshape(1)])
     values, cot = activations[0], cotangent[0]
-    slices = lax.all_to_all(weights.T.reshape(ranks, part, rows), RANK, 0, 0, tiled=True)
-    far = slices[None]
-    stages = [1 << bit for bit in range((seq_blocks * dp_blocks).bit_length() - 1)]
-    for mask in stages:
-        near = far if mask == 1 else jnp.concatenate([near, far])
-        far = lax.ppermute(near, BLOCK, flipped_pairs(seq_blocks * dp_blocks, mask))
     along = ("seq_block", "seq_rank")
     ends = [(b * seq_ranks - 1, b * seq_ranks) for b in range(1, seq_blocks)]
     both = jnp.concatenate([values, cot], -1)
-    low = lax.ppermute(both[-HALO:], along, ends)
-    high = lax.ppermute(both[:HALO], along, [(target, source) for source, target in ends])
+    edge = jnp.where(lax.axis_index("seq_rank") == 0, both[:HALO], both[-HALO:])
+    edge = lax.ppermute(edge, along, ends + [(target, source) for source, target in ends])
+    edge, weights = lax.optimization_barrier((edge, weights))
+    blocks = seq_blocks * dp_blocks
+    slices = lax.all_to_all(weights.T.reshape(ranks, part, rows), RANK, 0, 0, tiled=True)
+    far = slices[None]
+    stages = [1 << bit for bit in range(blocks.bit_length() - 1)]
+    for mask in stages[:-1]:
+        near = far if mask == 1 else jnp.concatenate([near, far])
+        far = lax.ppermute(near, BLOCK, flipped_pairs(blocks, mask))
+    near = jnp.concatenate([near, far])
     pairing = pairing.reshape(1, channels)
     gain = norm_gain.reshape(1, channels)
     core = dp_ranks
@@ -341,7 +370,7 @@
         lambda *refs: pack_messages(part, core, *refs),
         (shape_of((block, width), bf16),) * 2
         + tuple(shape_of((block, width + 2 * LANES), bf16) for _ in masks[1:]),
-        (rank, values, cot, low + high, pairing),
+        (rank, values, cot, edge, pairing),
         16,
         scratch=[pltpu.VMEM((ranks, block, 2 * LANES), bf16)],
         specs=[SMEM] + [VMEM] * 4,
@@ -350,6 +379,7 @@
         lax.ppermute(message, RANK, flipped_pairs(ranks, mask))
         for message, mask in zip(leaving, masks[1:])
     ]
+    far = lax.ppermute(near, BLOCK, flipped_pairs(blocks, stages[-1]))
     far, cross = lax.optimization_barrier((far, cross))
     crossing = called(
         stack_crossing, shape_of((len(masks), block, width), bf16), (cross, *arrived), 8
@@ -367,38 +397,46 @@
         (rank, home, crossed, *arrived, gain, pairing),
         16,
         specs=[SMEM] + [VMEM] * (4 + len(arrived)),
-        flops=2 * ranks * positions * channels * channels,
-        moved=ranks * positions * (width + 2 * channels) * 2,
-    )
-    sent = (owners, part + EXTRA, rows)
-    halves = (len(masks), positions, width)
+    )
     sizes = (seq_blocks, dp_blocks, seq_ranks, dp_ranks)
-    outgoing, own, cross = called(
+    shapes = (
+        (strands, span, taps * part),
+        (taps * part, channels),
+        (strands, span, LANES),
+        (owners, part + EXTRA, rows),
+    )
+    shifted, kernel, gelus, outgoing = called(
         lambda *refs: main_body(sizes, *refs),
-        tuple(pltpu.HBM(shape, bf16) for shape in (sent, halves, halves)),
-        (place, near, far, normed, grads, edge_normed, edge_grads, gain, swapped_gain, pairing),
+        tuple(pltpu.HBM(shape, bf16) for shape in shapes),
+        (place, near, far, normed, grads, edge_normed, edge_grads, gain),
         40,
         scratch=[
-            pltpu.VMEM((seq_blocks * dp_blocks, ranks, part, rows), bf16),
+            pltpu.VMEM((blocks, ranks, part, rows), bf16),
             pltpu.VMEM((taps * LANES, channels), bf16),
-            pltpu.VMEM((strands, span, taps * LANES), bf16),
-            pltpu.VMEM((strands, span, LANES), bf16),
             pltpu.VMEM((long, taps * LANES), f32),
             pltpu.VMEM((long, LANES), f32),
             pltpu.VMEM((wide, LANES), f32),
             pltpu.VMEM((wide, LANES), f32),
-            pltpu.VMEM((taps * LANES, channels), f32),
-            pltpu.VMEM((dp_ranks, span, channels), bf16),
-            pltpu.VMEM(sent, bf16),
-            pltpu.VMEM(halves, bf16),
-            pltpu.VMEM(halves, bf16),
-            pltpu.SemaphoreType.DMA((3,)),
-        ],
-        specs=[SMEM] + [VMEM] * 9,
-        out_specs=(HBM,) * 3,
-        flops=6 * strands * span * taps * LANES * channels,
+            pltpu.VMEM((taps * part, channels), f32),
+        ]
+        + [pltpu.VMEM(shape, bf16) for shape in shapes]
+        + [pltpu.SemaphoreType.DMA((strands + 3,))],
+        specs=[SMEM] + [VMEM] * 7,
+        out_specs=(HBM,) * 4,
     )
     terms = lax.all_to_all(outgoing, EVERY, 0, 0, tiled=True)
+    halves = shape_of((len(masks), positions, width), bf16)
+    kept = [pltpu.with_memory_space_constraint(x, pltpu.HBM) for x in (shifted, kernel, gelus)]
+    own, cross = called(
+        input_gradient,
+        (halves, halves),
+        (place, *kept, gain, swapped_gain, pairing),
+        24,
+        scratch=[pltpu.VMEM((dp_ranks, span, channels), bf16)]
+        + [pltpu.VMEM(shape, bf16) for shape in shapes[:3]]
+        + [pltpu.SemaphoreType.DMA((strands + 2,))],
+        specs=[SMEM] + [HBM] * 3 + [VMEM] * 3,
+    )
     crossed = lax.ppermute(cross, RANK, flipped_pairs(ranks, core))
     leaving = called(
         lambda *refs: chip_sum(part, *refs),

time: 95.9 us -> 95.6 us (level)
  starting transfers between devices: 20.3 us -> 14.8 us
  blocking collectives: 10.3 us -> 15.4 us
  waiting for transfers between devices: 41.1 us -> 38.1 us
  local copies, waits for them, and re-layouts: 1.93 us -> 3.65 us
  Pallas kernels: 20.1 us -> 21.5 us
    ppermute x6, waiting for transfers between devices: 24.6 us -> 17.4 us  [per_device(): lax.ppermute(message, RANK, flipped_pairs(ranks, mask))]
    ppermute x4 -> x3, starting transfers between devices: 10.3 us -> 4.89 us  [the longest x1 2.65 us: per_device(): far = lax.ppermute(near, BLOCK, flipped_pairs(blocks, stages[-1]))]
    all_to_all x1, blocking collectives: 10.3 us -> 15.4 us  [per_device(): lax.all_to_all(weights.T.reshape(ranks, part, rows), RANK, 0, 0, tiled=True)]
    ppermute x4 -> x3, waiting for transfers between devices: 10.7 us -> 15.1 us  [the longest x1 13.9 us: per_device(): far = lax.ppermute(near, BLOCK, flipped_pairs(blocks, stages[-1]))]
    pallas_call x7 -> x8, Pallas kernels: 20.1 us -> 21.5 us  [called(): pl.pallas_call(body, out_shape=outs, in_specs=specs or [VMEM] * len(args)...]
    unnamed x14 -> x10, local copies, waits for them, and re-layouts: 0.78 us -> 1.87 us
  transfers between devices with their start and end apart: 13 -> 12, of which waited for: 8 -> 8; matrix products, arithmetic and copies ran while one was open for 1% -> 1% of each run, Pallas kernels for 4% -> 10%
where the time goes in v8:
time: 95.6 us; the launch traced here: 95.2 us
  waiting for transfers between devices  38.1 us (40%)
  Pallas kernels  21.5 us (22%)
  blocking collectives  15.4 us (16%)
  starting transfers between devices  14.8 us (15%)
  local copies, waits for them, and re-layouts  3.65 us (4%)
  other arithmetic  0.98 us (1%)
    pallas_call x8, Pallas kernels, called(): pl.pallas_call(body, out_shape=outs, in_specs=specs or [VMEM] * len(args)...  21.5 us
    ppermute x6, waiting for transfers between devices, per_device(): lax.ppermute(message, RANK, flipped_pairs(ranks, mask))  17.4 us
    all_to_all x1, blocking collectives, per_device(): lax.all_to_all(weights.T.reshape(ranks, part, rows), RANK, 0, 0, tiled=True)  15.4 us
    ppermute x1, waiting for transfers between devices, per_device(): far = lax.ppermute(near, BLOCK, flipped_pairs(blocks, stages[-1]))  13.9 us
    ppermute x6, starting transfers between devices, per_device(): lax.ppermute(message, RANK, flipped_pairs(ranks, mask))  7.04 us
    ppermute x1, waiting for transfers between devices, per_device(): crossed = lax.ppermute(crossing, RANK, flipped_pairs(ranks, core))  2.97 us
    all_to_all x1, starting transfers between devices, per_device(): terms = lax.all_to_all(outgoing, EVERY, 0, 0, tiled=True)  2.83 us
    ppermute x1, starting transfers between devices, per_device(): far = lax.ppermute(near, BLOCK, flipped_pairs(blocks, stages[-1]))  2.65 us
  transfers between devices with their start and end apart: 12, of which 8 were waited for; matrix products, arithmetic and copies ran while one was open for 1% of the time, Pallas kernels for 10%

profile of v8, /device:TPU:0, one launch (start us, length us, event | category | flops | bytes accessed | tf_op | source)
XLA Modules:
  0.0 95.2 jit_solution(8468094520135625808)
XLA Ops:
  0.6 0.8 fusion
  1.4 0.7 collective-permute-start
  2.1 0.0 collective-permute-done.refs_3_
  2.1 1.1 %copy.9 = bf16[768,120]{1,0:T(8,128)(2,1)S(1)} copy(bf16[768,120]{0,1:T(8,128)(2,1)} %bitcast.19) | data formatting | bytes 368640 | tf_op jit(solution)/shard_map/transpose | solution.py:357
  3.2 0.0 copy-start.4
  3.2 15.4 %all_to_all.10 = bf16[8,96,120]{2,1,0:T(8,128)(2,1)S(1)} all-to-all(bf16[8,96,120]{2,1,0:T(8,128)(2,1)S(1)} %bitcast.16), channel_id=1, replica_groups=mesh['seq_block'=4,'seq_rank'=4,'dp_block'=1,'dp_rank'=2] {'seq_rank','d..., dimensions={0} | all-to-all | bytes 368640 | tf_op jit(solution)/shard_map/all_to_all | solution.py:357
  18.6 1.6 %collective-permute-start.1 = (bf16[1,8,96,120]{3,2,1,0:T(8,128)(2,1)S(1)}, bf16[1,8,96,120]{3,2,1,0:T(8,128)(2,1)S(1)}, u32[]{:S(2)}, u32[]{:S(2)}) collective-permute-start(bf16[1,8,96,120]{3,2,1,0:T(8,128)(2,1)S(1)} %bitcast.17), channel_id=1, source_target_pairs={{0,8},{8,0},{16,24},{24,16},{1,9},{9,1},{17,25},{25,17},{2,10},{10... | collective-permute-start | bytes 552968 | tf_op jit(solution)/shard_map/ppermute | solution.py:362
  20.2 0.7 reshape.24.refs_4_.refs_7_.pairing_ref.refs_3_
  20.9 0.0 copy-start
  20.9 0.9 copy-done
  21.8 0.0 copy-start.2
  21.8 0.9 copy-done.2
  22.7 1.9 %shard_map.84 = (bf16[144,1024]{1,0:T(8,128)(2,1)S(1)}, bf16[144,1024]{1,0:T(8,128)(2,1)S(1)}, bf16[144,1280]{1,0:T(8,128)(2,1)S(1)}, bf16[144,1280]{1,0:T(8,128)(2,1)S(1)}, bf16[144,1280]{1,0:T(8,128)(2,1)S(1)}) custom-call(s32[1]{0:T(128)} %bitcast.refs_0_, bf16[128,768]{1,0:T(8,128)(2,1)S(1)} %bitcast.11, bf16[128,768]{1,0:T(8,128)(2,1)S(1)} %bitcast.14, ...), custom_call_target="tpu_custom_call" | custom-call | tf_op jit(solution)/shard_map/pallas_call | solution.py:23
  24.7 1.2 %collective-permute-done.1 = bf16[1,8,96,120]{3,2,1,0:T(8,128)(2,1)S(1)} collective-permute-done((bf16[1,8,96,120]{3,2,1,0:T(8,128)(2,1)S(1)}, bf16[1,8,96,120]{3,2,1,0:T(8,128)(2,1)S(1)}, u32[]{:S(2)}, u32[]{:S(2)}) %collective-permute-start.1) | collective-permute-done | bytes 184352 | tf_op jit(solution)/shard_map/ppermute | solution.py:362
  25.9 0.1 pad_maximum_fusion.refs_1_
  26.0 2.7 %collective-permute-start.2 = (bf16[2,8,96,120]{3,2,1,0:T(8,128)(2,1)S(1)}, bf16[2,8,96,120]{3,2,1,0:T(8,128)(2,1)S(1)}, u32[]{:S(2)}, u32[]{:S(2)}) collective-permute-start(bf16[2,8,96,120]{3,2,1,0:T(8,128)(2,1)S(1)} %pad_maximum_fusion.refs_1_), channel_id=1, source_target_pairs={{0,16},{8,24},{16,0},{24,8},{1,17},{9,25},{17,1},{25,9},{2,18},{10... | collective-permute-start | bytes 1105928 | tf_op jit(solution)/shard_map/ppermute | solution.py:382
  28.6 0.6 collective-permute-start.3
  29.3 0.6 collective-permute-start.4
  29.9 2.2 %collective-permute-start.5 = (bf16[144,1280]{1,0:T(8,128)(2,1)S(1)}, bf16[144,1280]{1,0:T(8,128)(2,1)S(1)}, u32[]{:S(2)}, u32[]{:S(2)}) collective-permute-start(bf16[144,1280]{1,0:T(8,128)(2,1)S(1)} %get-tuple-element.40), channel_id=1, source_target_pairs={{0,5},{1,4},{2,7},{3,6},{4,1},{5,0},{6,3},{7,2},{8,13},{9,12},{10,... | collective-permute-start | bytes 1105928 | tf_op jit(solution)/shard_map/ppermute | solution.py:379
  32.1 13.9 %collective-permute-done.2.refs_2_ = bf16[2,8,96,120]{3,2,1,0:T(8,128)(2,1)S(1)} collective-permute-done((bf16[2,8,96,120]{3,2,1,0:T(8,128)(2,1)S(1)}, bf16[2,8,96,120]{3,2,1,0:T(8,128)(2,1)S(1)}, u32[]{:S(2)}, u32[]{:S(2)}) %collective-permute-start.2) | collective-permute-done | bytes 368672 | tf_op jit(solution)/shard_map/ppermute | solution.py:382
  46.0 0.0 collective-permute-done.3.refs_0_.refs_3_
  46.0 0.0 collective-permute-done.4.refs_1_.refs_4_
  46.0 1.5 %collective-permute-done.5.refs_2_.refs_5_ = bf16[144,1280]{1,0:T(8,128)(2,1)S(1)} collective-permute-done((bf16[144,1280]{1,0:T(8,128)(2,1)S(1)}, bf16[144,1280]{1,0:T(8,128)(2,1)S(1)}, u32[]{:S(2)}, u32[]{:S(2)}) %collective-permute-start.5) | collective-permute-done | bytes 368672 | tf_op jit(solution)/shard_map/ppermute | solution.py:379
  47.6 1.1 %shard_map.85 = bf16[4,144,1024]{2,1,0:T(8,128)(2,1)} custom-call(bf16[144,1024]{1,0:T(8,128)(2,1)S(1)} %get-tuple-element.37.cross_ref, bf16[144,1280]{1,0:T(8,128)(2,1)S(1)} %collective-permute-done.3.refs_0_.refs_3_, bf16[144,1280]{1,0:T(8,128)(2,1)S(1)} %collective-permute-done.4.refs_1_.refs_4_, bf16[144,1280]{1,0:T(8,128)(2,1)S(1)} %collective-permute-done.5.refs_2_.refs_5_), custom_call_target="tpu_custom_call" | custom-call | tf_op jit(solution)/shard_map/pallas_call | solution.py:23
  48.7 0.0 collective-permute-start.6
  48.7 0.0 copy-done.4
  48.7 0.1 pad_add_fusion.refs_0_.place_ref
  48.8 3.0 %collective-permute-done.6.refs_2_ = bf16[4,144,1024]{2,1,0:T(8,128)(2,1)S(1)} collective-permute-done((bf16[4,144,1024]{2,1,0:T(8,128)(2,1)}, bf16[4,144,1024]{2,1,0:T(8,128)(2,1)S(1)}, u32[]{:S(2)}, u32[]{:S(2)}) %collective-permute-start.6) | collective-permute-done | bytes 1179680 | tf_op jit(solution)/shard_map/ppermute | solution.py:387
  51.7 2.2 %shard_map.86 = (bf16[4,512,768]{2,1,0:T(8,128)(2,1)S(1)}, bf16[4,512,128]{2,1,0:T(8,128)(2,1)S(1)}, bf16[3,4,16,768]{3,2,1,0:T(8,128)(2,1)S(1)}, bf16[3,4,16,128]{3,2,1,0:T(8,128)(2,1)S(1)}, f32[1,768]{1,0:T(1,128)S(1)}) custom-call(s32[1]{0:T(128)} %bitcast.refs_0_, bf16[144,1024]{1,0:T(8,128)(2,1)S(1)} %get-tuple-element.36.refs_1_, ...), custom_call_target="tpu_custom_call" | custom-call | tf_op jit(solution)/shard_map/pallas_call | solution.py:23
  54.0 7.9 %shard_map.87 = (bf16[4,512,480]{2,1,0:T(8,128)(2,1)}, bf16[480,768]{1,0:T(8,128)(2,1)}, bf16[4,512,128]{2,1,0:T(8,128)(2,1)}, bf16[32,112,120]{2,1,0:T(8,128)(2,1)}) custom-call(s32[2]{0:T(128)S(1)} %pad_add_fusion.refs_0_.place_ref, bf16[2,8,96,120]{3,2,1,0:T(8,128)(2,1)S(1)} %pad_maximum_fusion.refs_1_, ...), custom_call_target="tpu_custom_call" | custom-call | tf_op jit(solution)/shard_map/pallas_call | solution.py:23
  61.9 2.8 %all-to-all-start.1 = ((bf16[32,112,120]{2,1,0:T(8,128)(2,1)}), bf16[32,112,120]{2,1,0:T(8,128)(2,1)S(1)}, u32[]{:S(2)}, u32[]{:S(2)}) async-start(bf16[32,112,120]{2,1,0:T(8,128)(2,1)} %get-tuple-element.57), calls=%async_computation.1 | async-start | bytes 1835008 | tf_op jit(solution)/shard_map/all_to_all | solution.py:427
  64.7 0.0 copy-start.1
  64.8 0.0 copy-start.3
  64.8 5.0 %shard_map.88 = (bf16[4,128,1024]{2,1,0:T(8,128)(2,1)S(1)}, bf16[4,128,1024]{2,1,0:T(8,128)(2,1)S(1)}) custom-call(s32[2]{0:T(128)S(1)} %pad_add_fusion.refs_0_.place_ref, bf16[4,512,480]{2,1,0:T(8,128)(2,1)} %get-tuple-element.45.shifted_ref, bf16[480,768]{1,0:T(8,128)(2,1)} %get-tuple-element.46.kernel_ref, ...), custom_call_target="tpu_custom_call" | custom-call | tf_op jit(solution)/shard_map/pallas_call | solution.py:23
  69.8 0.1 collective-permute-start.7
  69.8 2.6 %collective-permute-done.7.refs_1_ = bf16[4,128,1024]{2,1,0:T(8,128)(2,1)S(1)} collective-permute-done((bf16[4,128,1024]{2,1,0:T(8,128)(2,1)S(1)}, bf16[4,128,1024]{2,1,0:T(8,128)(2,1)S(1)}, u32[]{:S(2)}, u32[]{:S(2)}) %collective-permute-start.7) | collective-permute-done | bytes 1048608 | tf_op jit(solution)/shard_map/ppermute | solution.py:440
  72.5 0.5 shard_map.89
  73.0 1.5 %collective-permute-start.8 = (bf16[128,1152]{1,0:T(8,128)(2,1)S(1)}, bf16[128,1152]{1,0:T(8,128)(2,1)S(1)}, u32[]{:S(2)}, u32[]{:S(2)}) collective-permute-start(bf16[128,1152]{1,0:T(8,128)(2,1)S(1)} %get-tuple-element.52), channel_id=1, source_target_pairs={{0,1},{1,0},{2,3},{3,2},{4,5},{5,4},{6,7},{7,6},{8,9},{9,8},{10,11... | collective-permute-start | bytes 884744 | tf_op jit(solution)/shard_map/ppermute | solution.py:448
  74.6 1.5 %collective-permute-start.9 = (bf16[128,1152]{1,0:T(8,128)(2,1)S(1)}, bf16[128,1152]{1,0:T(8,128)(2,1)S(1)}, u32[]{:S(2)}, u32[]{:S(2)}) collective-permute-start(bf16[128,1152]{1,0:T(8,128)(2,1)S(1)} %get-tuple-element.53), channel_id=1, source_target_pairs={{0,4},{1,5},{2,6},{3,7},{4,0},{5,1},{6,2},{7,3},{8,12},{9,13},{10,... | collective-permute-start | bytes 884744 | tf_op jit(solution)/shard_map/ppermute | solution.py:448
  76.0 0.5 collective-permute-start.10
  76.6 9.5 %collective-permute-done.8.refs_5_ = bf16[128,1152]{1,0:T(8,128)(2,1)S(1)} collective-permute-done((bf16[128,1152]{1,0:T(8,128)(2,1)S(1)}, bf16[128,1152]{1,0:T(8,128)(2,1)S(1)}, u32[]{:S(2)}, u32[]{:S(2)}) %collective-permute-start.8) | collective-permute-done | bytes 294944 | tf_op jit(solution)/shard_map/ppermute | solution.py:448
  86.1 0.8 collective-permute-done.9.refs_6_
  86.9 5.5 %collective-permute-done.10.refs_7_ = bf16[128,1152]{1,0:T(8,128)(2,1)S(1)} collective-permute-done((bf16[128,1152]{1,0:T(8,128)(2,1)S(1)}, bf16[128,1152]{1,0:T(8,128)(2,1)S(1)}, u32[]{:S(2)}, u32[]{:S(2)}) %collective-permute-start.10) | collective-permute-done | bytes 294944 | tf_op jit(solution)/shard_map/ppermute | solution.py:448
  92.4 0.0 copy-done.1
  92.4 0.0 copy-done.3
  92.4 1.8 %shard_map.90 = (bf16[128,768]{1,0:T(8,128)(2,1)}, bf16[128,768]{1,0:T(8,128)(2,1)}) custom-call(s32[1]{0:T(128)} %bitcast.refs_0_, bf16[128,768]{1,0:T(8,128)(2,1)S(1)} %bitcast.12, bf16[128,768]{1,0:T(8,128)(2,1)S(1)} %bitcast.15, s32[1,768]{1,0:T(1,128)S(1)} %reshape.24.refs_4_.refs_7_.pairing_ref.refs_3_, ...), custom_call_target="tpu_custom_call" | custom-call | tf_op jit(solution)/shard_map/pallas_call | solution.py:23
  94.2 0.0 all-to-all-done.1.refs_0_
  94.2 1.0 %shard_map.91 = (f32[120,768]{1,0:T(8,128)}, f32[1,24]{1,0:T(1,128)}) custom-call(bf16[32,112,120]{2,1,0:T(8,128)(2,1)S(1)} %all-to-all-done.1.refs_0_), custom_call_target="tpu_custom_call" | custom-call | tf_op jit(solution)/shard_map/pallas_call | solution.py:23
  (1 shorter events, 0.0 us)
Async XLA Ops:
  1.4 0.7 collective-permute-start
  3.2 45.5 %copy-start.4 = (f32[768]{0:T(1024)S(1)}, f32[768]{0:T(1024)}, u32[]{:S(2)}) copy-start(f32[768]{0:T(1024)} %param.8) | copy-start | bytes 9220
  18.6 7.3 %collective-permute-start.1 = (bf16[1,8,96,120]{3,2,1,0:T(8,128)(2,1)S(1)}, bf16[1,8,96,120]{3,2,1,0:T(8,128)(2,1)S(1)}, u32[]{:S(2)}, u32[]{:S(2)}) collective-permute-start(bf16[1,8,96,120]{3,2,1,0:T(8,128)(2,1)S(1)} %bitcast.17), channel_id=1, source_target_pairs={{0,8},{8,0},{16,24},{24,16},{1,9},{9,1},{17,25},{25,17},{2,10},{10... | collective-permute-start | bytes 552968 | tf_op jit(solution)/shard_map/ppermute | solution.py:362
  20.9 0.9 copy-start
  21.8 0.9 copy-start.2
  26.0 20.1 %collective-permute-start.2 = (bf16[2,8,96,120]{3,2,1,0:T(8,128)(2,1)S(1)}, bf16[2,8,96,120]{3,2,1,0:T(8,128)(2,1)S(1)}, u32[]{:S(2)}, u32[]{:S(2)}) collective-permute-start(bf16[2,8,96,120]{3,2,1,0:T(8,128)(2,1)S(1)} %pad_maximum_fusion.refs_1_), channel_id=1, source_target_pairs={{0,16},{8,24},{16,0},{24,8},{1,17},{9,25},{17,1},{25,9},{2,18},{10... | collective-permute-start | bytes 1105928 | tf_op jit(solution)/shard_map/ppermute | solution.py:382
  28.6 17.4 %collective-permute-start.3 = (bf16[144,1280]{1,0:T(8,128)(2,1)S(1)}, bf16[144,1280]{1,0:T(8,128)(2,1)S(1)}, u32[]{:S(2)}, u32[]{:S(2)}) collective-permute-start(bf16[144,1280]{1,0:T(8,128)(2,1)S(1)} %get-tuple-element.38), channel_id=1, source_target_pairs={{0,1},{1,0},{2,3},{3,2},{4,5},{5,4},{6,7},{7,6},{8,9},{9,8},{10,11... | collective-permute-start | bytes 1105928 | tf_op jit(solution)/shard_map/ppermute | solution.py:379
  29.3 16.8 %collective-permute-start.4 = (bf16[144,1280]{1,0:T(8,128)(2,1)S(1)}, bf16[144,1280]{1,0:T(8,128)(2,1)S(1)}, u32[]{:S(2)}, u32[]{:S(2)}) collective-permute-start(bf16[144,1280]{1,0:T(8,128)(2,1)S(1)} %get-tuple-element.39), channel_id=1, source_target_pairs={{0,4},{1,5},{2,6},{3,7},{4,0},{5,1},{6,2},{7,3},{8,12},{9,13},{10,... | collective-permute-start | bytes 1105928 | tf_op jit(solution)/shard_map/ppermute | solution.py:379
  29.9 17.7 %collective-permute-start.5 = (bf16[144,1280]{1,0:T(8,128)(2,1)S(1)}, bf16[144,1280]{1,0:T(8,128)(2,1)S(1)}, u32[]{:S(2)}, u32[]{:S(2)}) collective-permute-start(bf16[144,1280]{1,0:T(8,128)(2,1)S(1)} %get-tuple-element.40), channel_id=1, source_target_pairs={{0,5},{1,4},{2,7},{3,6},{4,1},{5,0},{6,3},{7,2},{8,13},{9,12},{10,... | collective-permute-start | bytes 1105928 | tf_op jit(solution)/shard_map/ppermute | solution.py:379
  48.7 3.1 %collective-permute-start.6 = (bf16[4,144,1024]{2,1,0:T(8,128)(2,1)}, bf16[4,144,1024]{2,1,0:T(8,128)(2,1)S(1)}, u32[]{:S(2)}, u32[]{:S(2)}) collective-permute-start(bf16[4,144,1024]{2,1,0:T(8,128)(2,1)} %shard_map.85), channel_id=1, source_target_pairs={{0,2},{1,3},{2,0},{3,1},{4,6},{5,7},{6,4},{7,5},{8,10},{9,11},{10,... | collective-permute-start | bytes 3538952 | tf_op jit(solution)/shard_map/ppermute | solution.py:387
  61.9 32.3 %all-to-all-start.1 = ((bf16[32,112,120]{2,1,0:T(8,128)(2,1)}), bf16[32,112,120]{2,1,0:T(8,128)(2,1)S(1)}, u32[]{:S(2)}, u32[]{:S(2)}) async-start(bf16[32,112,120]{2,1,0:T(8,128)(2,1)} %get-tuple-element.57), calls=%async_computation.1 | async-start | bytes 1835008 | tf_op jit(solution)/shard_map/all_to_all | solution.py:427
  64.7 27.7 %copy-start.1 = (bf16[1,128,768]{2,1,0:T(8,128)(2,1)S(1)}, bf16[1,128,768]{2,1,0:T(8,128)(2,1)}, u32[]{:S(2)}) copy-start(bf16[1,128,768]{2,1,0:T(8,128)(2,1)} %param.5) | copy-start | bytes 589828
  64.8 27.6 %copy-start.3 = (bf16[1,128,768]{2,1,0:T(8,128)(2,1)S(1)}, bf16[1,128,768]{2,1,0:T(8,128)(2,1)}, u32[]{:S(2)}) copy-start(bf16[1,128,768]{2,1,0:T(8,128)(2,1)} %param.6) | copy-start | bytes 589828
  69.8 2.7 %collective-permute-start.7 = (bf16[4,128,1024]{2,1,0:T(8,128)(2,1)S(1)}, bf16[4,128,1024]{2,1,0:T(8,128)(2,1)S(1)}, u32[]{:S(2)}, u32[]{:S(2)}) collective-permute-start(bf16[4,128,1024]{2,1,0:T(8,128)(2,1)S(1)} %get-tuple-element.50), channel_id=1, source_target_pairs={{0,2},{1,3},{2,0},{3,1},{4,6},{5,7},{6,4},{7,5},{8,10},{9,11},{10,... | collective-permute-start | bytes 3145736 | tf_op jit(solution)/shard_map/ppermute | solution.py:440
  73.0 13.1 %collective-permute-start.8 = (bf16[128,1152]{1,0:T(8,128)(2,1)S(1)}, bf16[128,1152]{1,0:T(8,128)(2,1)S(1)}, u32[]{:S(2)}, u32[]{:S(2)}) collective-permute-start(bf16[128,1152]{1,0:T(8,128)(2,1)S(1)} %get-tuple-element.52), channel_id=1, source_target_pairs={{0,1},{1,0},{2,3},{3,2},{4,5},{5,4},{6,7},{7,6},{8,9},{9,8},{10,11... | collective-permute-start | bytes 884744 | tf_op jit(solution)/shard_map/ppermute | solution.py:448
  74.6 12.3 %collective-permute-start.9 = (bf16[128,1152]{1,0:T(8,128)(2,1)S(1)}, bf16[128,1152]{1,0:T(8,128)(2,1)S(1)}, u32[]{:S(2)}, u32[]{:S(2)}) collective-permute-start(bf16[128,1152]{1,0:T(8,128)(2,1)S(1)} %get-tuple-element.53), channel_id=1, source_target_pairs={{0,4},{1,5},{2,6},{3,7},{4,0},{5,1},{6,2},{7,3},{8,12},{9,13},{10,... | collective-permute-start | bytes 884744 | tf_op jit(solution)/shard_map/ppermute | solution.py:448
  76.0 16.4 %collective-permute-start.10 = (bf16[128,1152]{1,0:T(8,128)(2,1)S(1)}, bf16[128,1152]{1,0:T(8,128)(2,1)S(1)}, u32[]{:S(2)}, u32[]{:S(2)}) collective-permute-start(bf16[128,1152]{1,0:T(8,128)(2,1)S(1)} %get-tuple-element.54), channel_id=1, source_target_pairs={{0,5},{1,4},{2,7},{3,6},{4,1},{5,0},{6,3},{7,2},{8,13},{9,12},{10,... | collective-permute-start | bytes 884744 | tf_op jit(solution)/shard_map/ppermute | solution.py:448

commit v9 on v8

--- a/solution.py
+++ b/solution.py
@@ -66,6 +66,34 @@
 
 def chip_masks(ranks, core):
     return [mask for mask in range(ranks) if not mask & core]
+
+
+class Moves:
+    def __init__(self, sems):
+        self.sems, self.copies = sems, []
+
+    def start(self, source, target):
+        copy = pltpu.make_async_copy(source, target, self.sems.at[len(self.copies)])
+        copy.start()
+        self.copies.append(copy)
+        return copy
+
+    def wait(self):
+        for copy in self.copies:
+            copy.wait()
+
+
+def spread(piece_of, weights_ref, out_ref, square, sent, sems):
+    rows, channels = weights_ref.shape
+    part = out_ref.shape[1]
+    square[...] = jnp.zeros_like(square)
+    square[:rows] = weights_ref[...].astype(f32)
+    turned = square[...].T.astype(bf16)
+    for owner, piece in enumerate(piece_of):
+        sent[owner] = turned[piece * part : (piece + 1) * part, :rows]
+    moves = Moves(sems)
+    moves.start(sent, out_ref)
+    moves.wait()
 
 
 def pack_messages(part, core, rank_ref, values_ref, cot_ref, edge_ref, pairing_ref, *refs):
@@ -105,9 +133,11 @@
     return [(t * rms * gain).astype(bf16) for t in (x, other)]
 
 
-def prepare(core, rank_ref, home_ref, crossed_ref, *refs):
-    arrived = refs[:-7]
-    gain_ref, pairing_ref, normed_ref, grads_ref, edge_normed_ref, edge_grads_ref, swapped_gain_ref = refs[-7:]
+def prepare(core, chips, rank_ref, home_ref, crossed_ref, *refs):
+    arrived, refs = refs[: chips - 1], refs[chips - 1 :]
+    gain_ref, pairing_ref, outs, refs = refs[0], refs[1], refs[2:7], refs[7:]
+    normed_ref, grads_ref, edge_normed_ref, edge_grads_ref, swapped_gain_ref, sems = refs
+    moves = Moves(sems)
     dp_ranks = normed_ref.shape[0] // 2
     channels = gain_ref.shape[1]
     masks = chip_masks(2 * (len(arrived) + 1), core)
@@ -132,6 +162,11 @@
             grads_ref[index, pl.ds(start, positions), :] = grads[:positions]
             edge_normed_ref[side, index] = normed[positions:]
             edge_grads_ref[side, index] = grads[positions:]
+            place = (index, pl.ds(start, positions))
+            moves.start(normed_ref.at[place], outs[0].at[place])
+    moves.start(grads_ref, outs[1])
+    moves.start(edge_normed_ref, outs[2])
+    moves.start(edge_grads_ref, outs[3])
     gain = gain_ref[...]
     first = gain.astype(bf16).astype(f32)
     second = (gain - first).astype(bf16).astype(f32)
@@ -140,21 +175,26 @@
     parts = jnp.where(row == 0, first, jnp.where(row == 1, second, jnp.where(row == 2, third, 0.0)))
     swapped = dot(parts.astype(bf16), swap, ((1,), (0,)))
     swapped_gain_ref[...] = swapped[0:1] + swapped[1:2] + swapped[2:3]
-
-
-def main_body(sizes, place_ref, near_ref, far_ref, normed_ref, grads_ref, edge_normed_ref, edge_grads_ref, *refs):
-    seq_blocks, dp_blocks, seq_ranks, dp_ranks = sizes
-    blocks = seq_blocks * dp_blocks
+    moves.start(swapped_gain_ref, outs[4])
+    moves.wait()
+
+
+def main_body(pieces_in, normed_in, grads_in, edge_normed_in, edge_grads_in, *refs):
     gain_ref, shifted_out, kernel_out, gelu_out, leaving_out = refs[:5]
-    pieces, padded, terms, halves, bent, slopes, total, shifted_ref, kernel_ref, gelu_ref, leaving, sems = refs[5:]
-    copies = []
-
-    def send(source, target):
-        copies.append(pltpu.make_async_copy(source, target, sems.at[len(copies)]))
-        copies[-1].start()
-
-    me = place_ref[1]
-    part, rows = near_ref.shape[2:]
+    pieces, normed_ref, grads_ref, edge_normed_ref, edge_grads_ref = refs[5:10]
+    padded, terms, halves, bent, slopes, total, shifted_ref, kernel_ref, gelu_ref, leaving, sems = refs[10:]
+    moves = Moves(sems)
+    owners, part, rows = pieces.shape
+    strands = normed_ref.shape[0]
+    dp_ranks = strands // 2
+    got_pieces = moves.start(pieces_in, pieces)
+    got_edges = [
+        moves.start(edge_normed_in, edge_normed_ref),
+        moves.start(edge_grads_in, edge_grads_ref),
+        moves.start(grads_in, grads_ref),
+    ]
+    got_normed = [moves.start(normed_in.at[n], normed_ref.at[n]) for n in range(strands)]
+    arrivals = len(moves.copies)
     strands, span, channels = normed_ref.shape
     taps = kernel_ref.shape[0] // part
     half = taps // 2
@@ -169,30 +209,24 @@
             yield tap, channel, count, first - owner * rows
             first += count
 
-    for ref, first in ((near_ref, 0), (far_ref, near_ref.shape[0])):
-        for j in range(ref.shape[0]):
-            pieces[lax.bitwise_xor(me, first + j)] = ref[j]
-    places = [
-        (sb * dp_blocks + db, sr * dp_ranks + dr)
-        for sb in range(seq_blocks)
-        for sr in range(seq_ranks)
-        for db in range(dp_blocks)
-        for dr in range(dp_ranks)
-    ]
-    for owner, (source, piece) in enumerate(places):
+    got_pieces.wait()
+    for owner in range(owners):
         for tap, channel, count, offset in runs(owner):
             kernel_ref[tap * part : (tap + 1) * part, channel : channel + count] = pieces[
-                source, piece, :, offset : offset + count
+                owner, :, offset : offset + count
             ]
-    send(kernel_ref, kernel_out)
+    moves.start(kernel_ref, kernel_out)
     padded[...] = jnp.zeros_like(padded)
     for k in range(taps):
         padded[k * LANES : k * LANES + part, :] = kernel_ref[k * part : (k + 1) * part, :]
     kernel = padded[...]
+    for copy in got_edges:
+        copy.wait()
     edge_normed = jnp.concatenate([edge_normed_ref[side, s] for side in range(2) for s in range(strands)], 0)
     edge_terms = dot(edge_normed, kernel, ((1,), (1,)))
     for strand in range(strands):
         forward = strand < dp_ranks
+        got_normed[strand].wait()
         terms[HALO : HALO + span, :] = dot(normed_ref[strand], kernel, ((1,), (1,)))
         halves[HALO : HALO + span, :] = grads_ref[strand].astype(f32)
         for side, start in enumerate((0, HALO + span)):
@@ -210,8 +244,8 @@
         for k in range(taps):
             start = reach - k if forward else k
             shifted_ref[strand, :, k * part : (k + 1) * part] = slopes[start : start + span, :part].astype(bf16)
-        send(shifted_ref.at[strand], shifted_out.at[strand])
-    send(gelu_ref, gelu_out)
+        moves.start(shifted_ref.at[strand], shifted_out.at[strand])
+    moves.start(gelu_ref, gelu_out)
     total[...] = dot(
         shifted_ref[...].reshape(strands * span, taps * part),
         normed_ref[...].reshape(strands * span, channels),
@@ -221,8 +255,8 @@
     gain_high = gain.astype(bf16).astype(f32)
     row = lax.broadcasted_iota(jnp.int32, (EXTRA, channels), 0)
     extra = jnp.where(row == 0, gain_high, jnp.where(row == 1, gain - gain_high, 0.0))
-    own_gain = channels // len(places)
-    for owner in range(len(places)):
+    own_gain = channels // owners
+    for owner in range(owners):
         for tap, channel, count, offset in runs(owner):
             leaving[owner, :part, offset : offset + count] = total[
                 tap * part : (tap + 1) * part, channel : channel + count
@@ -231,38 +265,37 @@
         leaving[owner, part:, :own_gain] = extra[
             :, owner * own_gain : (owner + 1) * own_gain
         ].astype(bf16)
-    send(leaving, leaving_out)
-    for copy in copies:
+    moves.start(leaving, leaving_out)
+    for copy in moves.copies[arrivals:]:
         copy.wait()
 
 
 def input_gradient(
-    place_ref, shifted_ref, kernel_ref, gelu_ref, gain_ref, swapped_gain_ref, pairing_ref, own_ref, cross_ref, *scratch
+    rank_ref, shifted_ref, kernel_ref, gelu_ref, gain_ref, swapped_gain_ref, pairing_ref, own_ref, cross_ref, *scratch
 ):
     scaled, shifted, kernel_in, gelus, sems = scratch
     strands = shifted_ref.shape[0]
-    moves = [(kernel_ref, kernel_in)]
-    moves += [(shifted_ref.at[n], shifted.at[n]) for n in range(strands)]
-    moves += [(gelu_ref, gelus)]
-    copies = [pltpu.make_async_copy(*move, sems.at[n]) for n, move in enumerate(moves)]
-    for copy in copies:
-        copy.start()
+    moves = Moves(sems)
+    got_kernel = moves.start(kernel_ref, kernel_in)
+    got_shifted = [moves.start(shifted_ref.at[n], shifted.at[n]) for n in range(strands)]
+    got_gelus = moves.start(gelu_ref, gelus)
     dp_ranks = strands // 2
     chips, positions, _ = own_ref.shape
     channels = gain_ref.shape[1]
-    copies[0].wait()
+    got_kernel.wait()
     kernel = kernel_in[...]
     swapped = dot(kernel, swap_map(pairing_ref[...]), ((1,), (0,))).astype(bf16)
-    for copy in copies[1:]:
-        copy.wait()
     for b in range(dp_ranks):
+        got_shifted[b].wait()
+        got_shifted[dp_ranks + b].wait()
         scaled[b] = (
             dot(shifted[b], kernel, ((1,), (0,))) * gain_ref[...]
             + dot(shifted[dp_ranks + b], swapped, ((1,), (0,))) * swapped_gain_ref[...]
         ).astype(bf16)
+    got_gelus.wait()
     for m, mask in enumerate(chip_masks(2 * chips, dp_ranks)):
         for out, flip in ((own_ref, mask), (cross_ref, mask | dp_ranks)):
-            target = lax.bitwise_xor(place_ref[0], flip)
+            target = lax.bitwise_xor(rank_ref[0], flip)
             b = lax.rem(target, dp_ranks)
             start = pl.multiple_of(lax.div(target, dp_ranks) * positions, positions)
             out[m, :, :channels] = scaled[b, pl.ds(start, positions), :]
@@ -345,22 +378,34 @@
     strands = 2 * dp_ranks
     width = channels + 2 * LANES
     rank = lax.axis_index(RANK).reshape(1)
-    place = jnp.concatenate([rank, lax.axis_index(BLOCK).reshape(1)])
     values, cot = activations[0], cotangent[0]
     along = ("seq_block", "seq_rank")
     ends = [(b * seq_ranks - 1, b * seq_ranks) for b in range(1, seq_blocks)]
     both = jnp.concatenate([values, cot], -1)
     edge = jnp.where(lax.axis_index("seq_rank") == 0, both[:HALO], both[-HALO:])
     edge = lax.ppermute(edge, along, ends + [(target, source) for source, target in ends])
-    edge, weights = lax.optimization_barrier((edge, weights))
-    blocks = seq_blocks * dp_blocks
-    slices = lax.all_to_all(weights.T.reshape(ranks, part, rows), RANK, 0, 0, tiled=True)
-    far = slices[None]
-    stages = [1 << bit for bit in range(blocks.bit_length() - 1)]
-    for mask in stages[:-1]:
-        near = far if mask == 1 else jnp.concatenate([near, far])
-        far = lax.ppermute(near, BLOCK, flipped_pairs(blocks, mask))
-    near = jnp.concatenate([near, far])
+    piece_of = [
+        sr * dp_ranks + dr
+        for _ in range(seq_blocks)
+        for sr in range(seq_ranks)
+        for _ in range(dp_blocks)
+        for dr in range(dp_ranks)
+    ]
+    square = -(-rows // LANES) * LANES
+    slices = called(
+        lambda *refs: spread(piece_of, *refs),
+        pltpu.HBM((owners, part, rows), bf16),
+        (weights,),
+        16,
+        scratch=[
+            pltpu.VMEM((square, channels), f32),
+            pltpu.VMEM((owners, part, rows), bf16),
+            pltpu.SemaphoreType.DMA((1,)),
+        ],
+        out_specs=HBM,
+    )
+    slices, packed = lax.optimization_barrier((slices, values))
+    pieces = lax.all_to_all(slices, EVERY, 0, 0, tiled=True)
     pairing = pairing.reshape(1, channels)
     gain = norm_gain.reshape(1, channels)
     core = dp_ranks
@@ -370,7 +415,7 @@
         lambda *refs: pack_messages(part, core, *refs),
         (shape_of((block, width), bf16),) * 2
         + tuple(shape_of((block, width + 2 * LANES), bf16) for _ in masks[1:]),
-        (rank, values, cot, edge, pairing),
+        (rank, packed, cot, edge, pairing),
         16,
         scratch=[pltpu.VMEM((ranks, block, 2 * LANES), bf16)],
         specs=[SMEM] + [VMEM] * 4,
@@ -379,26 +424,29 @@
         lax.ppermute(message, RANK, flipped_pairs(ranks, mask))
         for message, mask in zip(leaving, masks[1:])
     ]
-    far = lax.ppermute(near, BLOCK, flipped_pairs(blocks, stages[-1]))
-    far, cross = lax.optimization_barrier((far, cross))
     crossing = called(
         stack_crossing, shape_of((len(masks), block, width), bf16), (cross, *arrived), 8
     )
     crossed = lax.ppermute(crossing, RANK, flipped_pairs(ranks, core))
-    normed, grads, edge_normed, edge_grads, swapped_gain = called(
-        lambda *refs: prepare(core, *refs),
-        (
-            shape_of((strands, span, channels), bf16),
-            shape_of((strands, span, LANES), bf16),
-            shape_of((3, strands, HALO, channels), bf16),
-            shape_of((3, strands, HALO, LANES), bf16),
-            shape_of((1, channels), f32),
-        ),
+    ready_shapes = [
+        ((strands, span, channels), bf16),
+        ((strands, span, LANES), bf16),
+        ((3, strands, HALO, channels), bf16),
+        ((3, strands, HALO, LANES), bf16),
+        ((1, channels), f32),
+    ]
+    ready = called(
+        lambda *refs: prepare(core, len(masks), *refs),
+        tuple(pltpu.HBM(*shape) for shape in ready_shapes),
         (rank, home, crossed, *arrived, gain, pairing),
-        16,
+        24,
+        scratch=[pltpu.VMEM(*shape) for shape in ready_shapes]
+        + [pltpu.SemaphoreType.DMA((2 * ranks + 4,))],
         specs=[SMEM] + [VMEM] * (4 + len(arrived)),
-    )
-    sizes = (seq_blocks, dp_blocks, seq_ranks, dp_ranks)
+        out_specs=(HBM,) * 5,
+    )
+    ready = [pltpu.with_memory_space_constraint(x, pltpu.HBM) for x in ready]
+    pieces = pltpu.with_memory_space_constraint(pieces, pltpu.HBM)
     shapes = (
         (strands, span, taps * part),
         (taps * part, channels),
@@ -406,12 +454,13 @@
         (owners, part + EXTRA, rows),
     )
     shifted, kernel, gelus, outgoing = called(
-        lambda *refs: main_body(sizes, *refs),
+        main_body,
         tuple(pltpu.HBM(shape, bf16) for shape in shapes),
-        (place, near, far, normed, grads, edge_normed, edge_grads, gain),
+        (pieces, *ready[:4], gain),
         40,
-        scratch=[
-            pltpu.VMEM((blocks, ranks, part, rows), bf16),
+        scratch=[pltpu.VMEM(pieces.shape, bf16)]
+        + [pltpu.VMEM(*shape) for shape in ready_shapes[:4]]
+        + [
             pltpu.VMEM((taps * LANES, channels), bf16),
             pltpu.VMEM((long, taps * LANES), f32),
             pltpu.VMEM((long, LANES), f32),
@@ -420,8 +469,8 @@
             pltpu.VMEM((taps * part, channels), f32),
         ]
         + [pltpu.VMEM(shape, bf16) for shape in shapes]
-        + [pltpu.SemaphoreType.DMA((strands + 3,))],
-        specs=[SMEM] + [VMEM] * 7,
+        + [pltpu.SemaphoreType.DMA((2 * strands + 7,))],
+        specs=[HBM] * 5 + [VMEM],
         out_specs=(HBM,) * 4,
     )
     terms = lax.all_to_all(outgoing, EVERY, 0, 0, tiled=True)
@@ -430,7 +479,7 @@
     own, cross = called(
         input_gradient,
         (halves, halves),
-        (place, *kept, gain, swapped_gain, pairing),
+        (rank, *kept, gain, ready[4], pairing),
         24,
         scratch=[pltpu.VMEM((dp_ranks, span, channels), bf16)]
         + [pltpu.VMEM(shape, bf16) for shape in shapes[:3]]

time: 95.6 us -> 92 us (0.962)
  blocking collectives: 15.4 us -> 0 us
  starting transfers between devices: 14.8 us -> 29.1 us
  waiting for transfers between devices: 38.1 us -> 31.6 us
  Pallas kernels: 21.5 us -> 25.7 us
    all_to_all x1 -> x0, blocking collectives: 15.4 us -> none  [per_device(): lax.all_to_all(weights.T.reshape(ranks, part, rows), RANK, 0, 0, tiled=True)]
    ppermute x2 -> x0, waiting for transfers between devices: 15.1 us -> none  [the longest x1 13.9 us: per_device(): far = lax.ppermute(near, BLOCK, flipped_pairs(blocks, stages[-1]))]
    ppermute x6, waiting for transfers between devices: 17.4 us -> 26.6 us  [per_device(): lax.ppermute(message, RANK, flipped_pairs(ranks, mask))]
    all_to_all x0 -> x1, starting transfers between devices: none -> 8.38 us  [per_device(): pieces = lax.all_to_all(slices, EVERY, 0, 0, tiled=True)]
    all_to_all x1, starting transfers between devices: 2.83 us -> 7.33 us  [per_device(): terms = lax.all_to_all(outgoing, EVERY, 0, 0, tiled=True)]
    ppermute x1, starting transfers between devices: 0.01 us -> 4.48 us  [per_device(): crossed = lax.ppermute(crossing, RANK, flipped_pairs(ranks, core))]
    pallas_call x8 -> x9, Pallas kernels: 21.5 us -> 25.7 us  [called(): pl.pallas_call(body, out_shape=outs, in_specs=specs or [VMEM] * len(args)...]
    ppermute x2 -> x0, starting transfers between devices: 4.23 us -> none  [the longest x1 2.65 us: per_device(): far = lax.ppermute(near, BLOCK, flipped_pairs(blocks, stages[-1]))]
  transfers between devices with their start and end apart: 12 -> 11, of which waited for: 8 -> 7; matrix products, arithmetic and copies ran while one was open for 1% -> 1% of each run, Pallas kernels for 10% -> 13%
where the time goes in v9:
time: 92 us; the launch traced here: 91.6 us
  waiting for transfers between devices  31.6 us (34%)
  starting transfers between devices  29.1 us (32%)
  Pallas kernels  25.7 us (28%)
  local copies, waits for them, and re-layouts  3.48 us (4%)
    ppermute x6, waiting for transfers between devices, per_device(): lax.ppermute(message, RANK, flipped_pairs(ranks, mask))  26.6 us
    pallas_call x9, Pallas kernels, called(): pl.pallas_call(body, out_shape=outs, in_specs=specs or [VMEM] * len(args)...  25.7 us
    all_to_all x1, starting transfers between devices, per_device(): pieces = lax.all_to_all(slices, EVERY, 0, 0, tiled=True)  8.38 us
    ppermute x6, starting transfers between devices, per_device(): lax.ppermute(message, RANK, flipped_pairs(ranks, mask))  8.13 us
    all_to_all x1, starting transfers between devices, per_device(): terms = lax.all_to_all(outgoing, EVERY, 0, 0, tiled=True)  7.33 us
    ppermute x1, starting transfers between devices, per_device(): crossed = lax.ppermute(crossing, RANK, flipped_pairs(ranks, core))  4.48 us
    unnamed x12, local copies, waits for them, and re-layouts  2.79 us
    ppermute x1, waiting for transfers between devices, per_device(): crossed = lax.ppermute(cross, RANK, flipped_pairs(ranks, core))  2.58 us
  transfers between devices with their start and end apart: 11, of which 7 were waited for; matrix products, arithmetic and copies ran while one was open for 1% of the time, Pallas kernels for 13%

profile of v9, /device:TPU:0, one launch (start us, length us, event | category | flops | bytes accessed | tf_op | source)
XLA Modules:
  0.0 91.6 jit_solution(14830768189962968542)
XLA Ops:
  0.6 0.8 fusion
  1.4 0.7 collective-permute-start
  2.1 0.7 reshape.18.refs_4_.refs_7_.pairing_ref.refs_3_
  2.8 0.0 copy-start.4
  2.8 0.9 %copy-done.4 = bf16[120,768]{1,0:T(8,128)(2,1)S(1)} copy-done((bf16[120,768]{1,0:T(8,128)(2,1)S(1)}, bf16[120,768]{1,0:T(8,128)(2,1)}, u32[]{:S(2)}) %copy-start.4) | copy-done | bytes 184344
  3.7 1.1 %shard_map.84 = bf16[32,96,120]{2,1,0:T(8,128)(2,1)} custom-call(bf16[120,768]{1,0:T(8,128)(2,1)S(1)} %copy-done.4), custom_call_target="tpu_custom_call" | custom-call | tf_op jit(solution)/shard_map/pallas_call | solution.py:23
  4.8 0.0 collective-permute-done.refs_3_
  4.8 0.0 copy-start
  4.8 0.9 %copy-done = bf16[1,128,768]{2,1,0:T(8,128)(2,1)S(1)} copy-done((bf16[1,128,768]{2,1,0:T(8,128)(2,1)S(1)}, bf16[1,128,768]{2,1,0:T(8,128)(2,1)}, u32[]{:S(2)}) %copy-start) | copy-done | bytes 196632
  5.8 0.0 copy-start.2
  5.8 0.9 %copy-done.2 = bf16[1,128,768]{2,1,0:T(8,128)(2,1)S(1)} copy-done((bf16[1,128,768]{2,1,0:T(8,128)(2,1)S(1)}, bf16[1,128,768]{2,1,0:T(8,128)(2,1)}, u32[]{:S(2)}) %copy-start.2) | copy-done | bytes 196632
  6.7 1.9 %shard_map.85 = (bf16[144,1024]{1,0:T(8,128)(2,1)S(1)}, bf16[144,1024]{1,0:T(8,128)(2,1)S(1)}, bf16[144,1280]{1,0:T(8,128)(2,1)S(1)}, bf16[144,1280]{1,0:T(8,128)(2,1)S(1)}, bf16[144,1280]{1,0:T(8,128)(2,1)S(1)}) custom-call(s32[1]{0:T(128)} %bitcast.refs_0_.rank_ref, bf16[128,768]{1,0:T(8,128)(2,1)S(1)} %bitcast.7, bf16[128,768]{1,0:T(8,128)(2,1)S(1)} %bitcast.10, ...), custom_call_target="tpu_custom_call" | custom-call | tf_op jit(solution)/shard_map/pallas_call | solution.py:23
  8.6 0.0 copy-start.5
  8.7 3.0 %collective-permute-start.1 = (bf16[144,1280]{1,0:T(8,128)(2,1)S(1)}, bf16[144,1280]{1,0:T(8,128)(2,1)S(1)}, u32[]{:S(2)}, u32[]{:S(2)}) collective-permute-start(bf16[144,1280]{1,0:T(8,128)(2,1)S(1)} %get-tuple-element.34), channel_id=1, source_target_pairs={{0,1},{1,0},{2,3},{3,2},{4,5},{5,4},{6,7},{7,6},{8,9},{9,8},{10,11... | collective-permute-start | bytes 1105928 | tf_op jit(solution)/shard_map/ppermute | solution.py:424
  11.7 1.5 %collective-permute-start.2 = (bf16[144,1280]{1,0:T(8,128)(2,1)S(1)}, bf16[144,1280]{1,0:T(8,128)(2,1)S(1)}, u32[]{:S(2)}, u32[]{:S(2)}) collective-permute-start(bf16[144,1280]{1,0:T(8,128)(2,1)S(1)} %get-tuple-element.35), channel_id=1, source_target_pairs={{0,4},{1,5},{2,6},{3,7},{4,0},{5,1},{6,2},{7,3},{8,12},{9,13},{10,... | collective-permute-start | bytes 1105928 | tf_op jit(solution)/shard_map/ppermute | solution.py:424
  13.2 0.1 collective-permute-start.3
  13.2 8.4 %all-to-all-start = ((bf16[32,96,120]{2,1,0:T(8,128)(2,1)}), bf16[32,96,120]{2,1,0:T(8,128)(2,1)}, u32[]{:S(2)}, u32[]{:S(2)}) async-start(bf16[32,96,120]{2,1,0:T(8,128)(2,1)} %shard_map.84), calls=%async_computation | async-start | bytes 1572864 | tf_op jit(solution)/shard_map/all_to_all | solution.py:408
  21.6 0.0 collective-permute-done.1.refs_0_.refs_3_
  21.6 0.1 collective-permute-done.2.refs_1_.refs_4_
  21.7 10.9 %collective-permute-done.3.refs_2_.refs_5_ = bf16[144,1280]{1,0:T(8,128)(2,1)S(1)} collective-permute-done((bf16[144,1280]{1,0:T(8,128)(2,1)S(1)}, bf16[144,1280]{1,0:T(8,128)(2,1)S(1)}, u32[]{:S(2)}, u32[]{:S(2)}) %collective-permute-start.3) | collective-permute-done | bytes 368672 | tf_op jit(solution)/shard_map/ppermute | solution.py:424
  32.6 0.1 shard_map.86
  32.6 4.5 %collective-permute-start.4 = (bf16[4,144,1024]{2,1,0:T(8,128)(2,1)S(1)}, bf16[4,144,1024]{2,1,0:T(8,128)(2,1)S(1)}, u32[]{:S(2)}, u32[]{:S(2)}) collective-permute-start(bf16[4,144,1024]{2,1,0:T(8,128)(2,1)S(1)} %shard_map.86), channel_id=1, source_target_pairs={{0,2},{1,3},{2,0},{3,1},{4,6},{5,7},{6,4},{7,5},{8,10},{9,11},{10,... | collective-permute-start | bytes 3538952 | tf_op jit(solution)/shard_map/ppermute | solution.py:430
  37.1 0.0 copy-done.5
  37.1 2.5 %collective-permute-done.4.refs_2_ = bf16[4,144,1024]{2,1,0:T(8,128)(2,1)S(1)} collective-permute-done((bf16[4,144,1024]{2,1,0:T(8,128)(2,1)S(1)}, bf16[4,144,1024]{2,1,0:T(8,128)(2,1)S(1)}, u32[]{:S(2)}, u32[]{:S(2)}) %collective-permute-start.4) | collective-permute-done | bytes 1179680 | tf_op jit(solution)/shard_map/ppermute | solution.py:430
  39.6 3.3 %shard_map.87 = (bf16[4,512,768]{2,1,0:T(8,128)(2,1)}, bf16[4,512,128]{2,1,0:T(8,128)(2,1)}, bf16[3,4,16,768]{3,2,1,0:T(8,128)(2,1)}, bf16[3,4,16,128]{3,2,1,0:T(8,128)(2,1)}, f32[1,768]{1,0:T(1,128)}) custom-call(s32[1]{0:T(128)} %bitcast.refs_0_.rank_ref, bf16[144,1024]{1,0:T(8,128)(2,1)S(1)} %get-tuple-element.32.refs_1_, ...), custom_call_target="tpu_custom_call" | custom-call | tf_op jit(solution)/shard_map/pallas_call | solution.py:23
  42.9 0.0 all-to-all-done.pieces_in
  42.9 10.6 %shard_map.88 = (bf16[4,512,480]{2,1,0:T(8,128)(2,1)}, bf16[480,768]{1,0:T(8,128)(2,1)}, bf16[4,512,128]{2,1,0:T(8,128)(2,1)}, bf16[32,112,120]{2,1,0:T(8,128)(2,1)}) custom-call(bf16[32,96,120]{2,1,0:T(8,128)(2,1)} %all-to-all-done.pieces_in, bf16[4,512,768]{2,1,0:T(8,128)(2,1)} %get-tuple-element.37.normed_in, ...), custom_call_target="tpu_custom_call" | custom-call | tf_op jit(solution)/shard_map/pallas_call | solution.py:23
  53.6 7.3 %all-to-all-start.1 = ((bf16[32,112,120]{2,1,0:T(8,128)(2,1)}), bf16[32,112,120]{2,1,0:T(8,128)(2,1)S(1)}, u32[]{:S(2)}, u32[]{:S(2)}) async-start(bf16[32,112,120]{2,1,0:T(8,128)(2,1)} %get-tuple-element.53), calls=%async_computation.1 | async-start | bytes 1835008 | tf_op jit(solution)/shard_map/all_to_all | solution.py:476
  60.9 0.0 copy-start.1
  60.9 0.0 copy-start.3
  60.9 5.4 %shard_map.89 = (bf16[4,128,1024]{2,1,0:T(8,128)(2,1)S(1)}, bf16[4,128,1024]{2,1,0:T(8,128)(2,1)S(1)}) custom-call(s32[1]{0:T(128)} %bitcast.refs_0_.rank_ref, bf16[4,512,480]{2,1,0:T(8,128)(2,1)} %get-tuple-element.41.shifted_ref, bf16[480,768]{1,0:T(8,128)(2,1)} %get-tuple-element.42.kernel_ref, bf16[4,512,128]{2,1,0:T(8,128)(2,1)} %get-tuple-element.43.gelu_ref, ...), custom_call_target="tpu_custom_call" | custom-call | tf_op jit(solution)/shard_map/pallas_call | solution.py:23
  66.3 0.1 collective-permute-start.5
  66.5 2.6 %collective-permute-done.5.refs_1_ = bf16[4,128,1024]{2,1,0:T(8,128)(2,1)S(1)} collective-permute-done((bf16[4,128,1024]{2,1,0:T(8,128)(2,1)S(1)}, bf16[4,128,1024]{2,1,0:T(8,128)(2,1)S(1)}, u32[]{:S(2)}, u32[]{:S(2)}) %collective-permute-start.5) | collective-permute-done | bytes 1048608 | tf_op jit(solution)/shard_map/ppermute | solution.py:489
  69.0 0.5 shard_map.90
  69.6 1.7 %collective-permute-start.6 = (bf16[128,1152]{1,0:T(8,128)(2,1)S(1)}, bf16[128,1152]{1,0:T(8,128)(2,1)S(1)}, u32[]{:S(2)}, u32[]{:S(2)}) collective-permute-start(bf16[128,1152]{1,0:T(8,128)(2,1)S(1)} %get-tuple-element.48), channel_id=1, source_target_pairs={{0,1},{1,0},{2,3},{3,2},{4,5},{5,4},{6,7},{7,6},{8,9},{9,8},{10,11... | collective-permute-start | bytes 884744 | tf_op jit(solution)/shard_map/ppermute | solution.py:497
  71.2 1.5 %collective-permute-start.7 = (bf16[128,1152]{1,0:T(8,128)(2,1)S(1)}, bf16[128,1152]{1,0:T(8,128)(2,1)S(1)}, u32[]{:S(2)}, u32[]{:S(2)}) collective-permute-start(bf16[128,1152]{1,0:T(8,128)(2,1)S(1)} %get-tuple-element.49), channel_id=1, source_target_pairs={{0,4},{1,5},{2,6},{3,7},{4,0},{5,1},{6,2},{7,3},{8,12},{9,13},{10,... | collective-permute-start | bytes 884744 | tf_op jit(solution)/shard_map/ppermute | solution.py:497
  72.7 0.4 collective-permute-start.8
  73.1 9.9 %collective-permute-done.6.refs_5_ = bf16[128,1152]{1,0:T(8,128)(2,1)S(1)} collective-permute-done((bf16[128,1152]{1,0:T(8,128)(2,1)S(1)}, bf16[128,1152]{1,0:T(8,128)(2,1)S(1)}, u32[]{:S(2)}, u32[]{:S(2)}) %collective-permute-start.6) | collective-permute-done | bytes 294944 | tf_op jit(solution)/shard_map/ppermute | solution.py:497
  83.0 0.6 collective-permute-done.7.refs_6_
  83.6 5.2 %collective-permute-done.8.refs_7_ = bf16[128,1152]{1,0:T(8,128)(2,1)S(1)} collective-permute-done((bf16[128,1152]{1,0:T(8,128)(2,1)S(1)}, bf16[128,1152]{1,0:T(8,128)(2,1)S(1)}, u32[]{:S(2)}, u32[]{:S(2)}) %collective-permute-start.8) | collective-permute-done | bytes 294944 | tf_op jit(solution)/shard_map/ppermute | solution.py:497
  88.8 0.0 copy-done.1
  88.8 0.0 copy-done.3
  88.8 1.8 %shard_map.91 = (bf16[128,768]{1,0:T(8,128)(2,1)}, bf16[128,768]{1,0:T(8,128)(2,1)}) custom-call(s32[1]{0:T(128)} %bitcast.refs_0_.rank_ref, bf16[128,768]{1,0:T(8,128)(2,1)S(1)} %bitcast.8, bf16[128,768]{1,0:T(8,128)(2,1)S(1)} %bitcast.11, s32[1,768]{1,0:T(1,128)S(1)} %reshape.18.refs_4_.refs_7_.pairing_ref.refs_3_, ...), custom_call_target="tpu_custom_call" | custom-call | tf_op jit(solution)/shard_map/pallas_call | solution.py:23
  90.6 0.0 all-to-all-done.1.refs_0_
  90.6 1.0 %shard_map.92 = (f32[120,768]{1,0:T(8,128)}, f32[1,24]{1,0:T(1,128)}) custom-call(bf16[32,112,120]{2,1,0:T(8,128)(2,1)S(1)} %all-to-all-done.1.refs_0_), custom_call_target="tpu_custom_call" | custom-call | tf_op jit(solution)/shard_map/pallas_call | solution.py:23
  (1 shorter events, 0.0 us)
Async XLA Ops:
  1.4 3.4 %collective-permute-start = (bf16[16,1536]{1,0:T(8,128)(2,1)S(1)}, bf16[16,1536]{1,0:T(8,128)(2,1)S(1)}, u32[]{:S(2)}, u32[]{:S(2)}) collective-permute-start(bf16[16,1536]{1,0:T(8,128)(2,1)S(1)} %fusion), channel_id=1, source_target_pairs={{6,8},{14,16},{22,24},{8,6},{16,14},{24,22},{7,9},{15,17},{23,25},... | collective-permute-start | bytes 147464 | tf_op jit(solution)/shard_map/ppermute | solution.py:386
  2.8 0.9 %copy-start.4 = (bf16[120,768]{1,0:T(8,128)(2,1)S(1)}, bf16[120,768]{1,0:T(8,128)(2,1)}, u32[]{:S(2)}) copy-start(bf16[120,768]{1,0:T(8,128)(2,1)} %refs_0_.1) | copy-start | bytes 552964
  4.8 0.9 %copy-start = (bf16[1,128,768]{2,1,0:T(8,128)(2,1)S(1)}, bf16[1,128,768]{2,1,0:T(8,128)(2,1)}, u32[]{:S(2)}) copy-start(bf16[1,128,768]{2,1,0:T(8,128)(2,1)} %param.5) | copy-start | bytes 589828
  5.8 0.9 %copy-start.2 = (bf16[1,128,768]{2,1,0:T(8,128)(2,1)S(1)}, bf16[1,128,768]{2,1,0:T(8,128)(2,1)}, u32[]{:S(2)}) copy-start(bf16[1,128,768]{2,1,0:T(8,128)(2,1)} %param.6) | copy-start | bytes 589828
  8.6 28.5 %copy-start.5 = (f32[768]{0:T(1024)S(1)}, f32[768]{0:T(1024)}, u32[]{:S(2)}) copy-start(f32[768]{0:T(1024)} %param.8) | copy-start | bytes 9220
  8.7 13.0 %collective-permute-start.1 = (bf16[144,1280]{1,0:T(8,128)(2,1)S(1)}, bf16[144,1280]{1,0:T(8,128)(2,1)S(1)}, u32[]{:S(2)}, u32[]{:S(2)}) collective-permute-start(bf16[144,1280]{1,0:T(8,128)(2,1)S(1)} %get-tuple-element.34), channel_id=1, source_target_pairs={{0,1},{1,0},{2,3},{3,2},{4,5},{5,4},{6,7},{7,6},{8,9},{9,8},{10,11... | collective-permute-start | bytes 1105928 | tf_op jit(solution)/shard_map/ppermute | solution.py:424
  11.7 10.0 %collective-permute-start.2 = (bf16[144,1280]{1,0:T(8,128)(2,1)S(1)}, bf16[144,1280]{1,0:T(8,128)(2,1)S(1)}, u32[]{:S(2)}, u32[]{:S(2)}) collective-permute-start(bf16[144,1280]{1,0:T(8,128)(2,1)S(1)} %get-tuple-element.35), channel_id=1, source_target_pairs={{0,4},{1,5},{2,6},{3,7},{4,0},{5,1},{6,2},{7,3},{8,12},{9,13},{10,... | collective-permute-start | bytes 1105928 | tf_op jit(solution)/shard_map/ppermute | solution.py:424
  13.2 19.4 %collective-permute-start.3 = (bf16[144,1280]{1,0:T(8,128)(2,1)S(1)}, bf16[144,1280]{1,0:T(8,128)(2,1)S(1)}, u32[]{:S(2)}, u32[]{:S(2)}) collective-permute-start(bf16[144,1280]{1,0:T(8,128)(2,1)S(1)} %get-tuple-element.36), channel_id=1, source_target_pairs={{0,5},{1,4},{2,7},{3,6},{4,1},{5,0},{6,3},{7,2},{8,13},{9,12},{10,... | collective-permute-start | bytes 1105928 | tf_op jit(solution)/shard_map/ppermute | solution.py:424
  13.2 29.7 %all-to-all-start = ((bf16[32,96,120]{2,1,0:T(8,128)(2,1)}), bf16[32,96,120]{2,1,0:T(8,128)(2,1)}, u32[]{:S(2)}, u32[]{:S(2)}) async-start(bf16[32,96,120]{2,1,0:T(8,128)(2,1)} %shard_map.84), calls=%async_computation | async-start | bytes 1572864 | tf_op jit(solution)/shard_map/all_to_all | solution.py:408
  32.6 7.0 %collective-permute-start.4 = (bf16[4,144,1024]{2,1,0:T(8,128)(2,1)S(1)}, bf16[4,144,1024]{2,1,0:T(8,128)(2,1)S(1)}, u32[]{:S(2)}, u32[]{:S(2)}) collective-permute-start(bf16[4,144,1024]{2,1,0:T(8,128)(2,1)S(1)} %shard_map.86), channel_id=1, source_target_pairs={{0,2},{1,3},{2,0},{3,1},{4,6},{5,7},{6,4},{7,5},{8,10},{9,11},{10,... | collective-permute-start | bytes 3538952 | tf_op jit(solution)/shard_map/ppermute | solution.py:430
  53.6 37.0 %all-to-all-start.1 = ((bf16[32,112,120]{2,1,0:T(8,128)(2,1)}), bf16[32,112,120]{2,1,0:T(8,128)(2,1)S(1)}, u32[]{:S(2)}, u32[]{:S(2)}) async-start(bf16[32,112,120]{2,1,0:T(8,128)(2,1)} %get-tuple-element.53), calls=%async_computation.1 | async-start | bytes 1835008 | tf_op jit(solution)/shard_map/all_to_all | solution.py:476
  60.9 27.9 %copy-start.1 = (bf16[1,128,768]{2,1,0:T(8,128)(2,1)S(1)}, bf16[1,128,768]{2,1,0:T(8,128)(2,1)}, u32[]{:S(2)}) copy-start(bf16[1,128,768]{2,1,0:T(8,128)(2,1)} %param.5) | copy-start | bytes 589828
  60.9 27.9 %copy-start.3 = (bf16[1,128,768]{2,1,0:T(8,128)(2,1)S(1)}, bf16[1,128,768]{2,1,0:T(8,128)(2,1)}, u32[]{:S(2)}) copy-start(bf16[1,128,768]{2,1,0:T(8,128)(2,1)} %param.6) | copy-start | bytes 589828
  66.3 2.7 %collective-permute-start.5 = (bf16[4,128,1024]{2,1,0:T(8,128)(2,1)S(1)}, bf16[4,128,1024]{2,1,0:T(8,128)(2,1)S(1)}, u32[]{:S(2)}, u32[]{:S(2)}) collective-permute-start(bf16[4,128,1024]{2,1,0:T(8,128)(2,1)S(1)} %get-tuple-element.46), channel_id=1, source_target_pairs={{0,2},{1,3},{2,0},{3,1},{4,6},{5,7},{6,4},{7,5},{8,10},{9,11},{10,... | collective-permute-start | bytes 3145736 | tf_op jit(solution)/shard_map/ppermute | solution.py:489
  69.6 13.4 %collective-permute-start.6 = (bf16[128,1152]{1,0:T(8,128)(2,1)S(1)}, bf16[128,1152]{1,0:T(8,128)(2,1)S(1)}, u32[]{:S(2)}, u32[]{:S(2)}) collective-permute-start(bf16[128,1152]{1,0:T(8,128)(2,1)S(1)} %get-tuple-element.48), channel_id=1, source_target_pairs={{0,1},{1,0},{2,3},{3,2},{4,5},{5,4},{6,7},{7,6},{8,9},{9,8},{10,11... | collective-permute-start | bytes 884744 | tf_op jit(solution)/shard_map/ppermute | solution.py:497
  71.2 12.3 %collective-permute-start.7 = (bf16[128,1152]{1,0:T(8,128)(2,1)S(1)}, bf16[128,1152]{1,0:T(8,128)(2,1)S(1)}, u32[]{:S(2)}, u32[]{:S(2)}) collective-permute-start(bf16[128,1152]{1,0:T(8,128)(2,1)S(1)} %get-tuple-element.49), channel_id=1, source_target_pairs={{0,4},{1,5},{2,6},{3,7},{4,0},{5,1},{6,2},{7,3},{8,12},{9,13},{10,... | collective-permute-start | bytes 884744 | tf_op jit(solution)/shard_map/ppermute | solution.py:497
  72.7 16.1 %collective-permute-start.8 = (bf16[128,1152]{1,0:T(8,128)(2,1)S(1)}, bf16[128,1152]{1,0:T(8,128)(2,1)S(1)}, u32[]{:S(2)}, u32[]{:S(2)}) collective-permute-start(bf16[128,1152]{1,0:T(8,128)(2,1)S(1)} %get-tuple-element.50), channel_id=1, source_target_pairs={{0,5},{1,4},{2,7},{3,6},{4,1},{5,0},{6,3},{7,2},{8,13},{9,12},{10,... | collective-permute-start | bytes 884744 | tf_op jit(solution)/shard_map/ppermute | solution.py:497

commit v10 on v9

--- a/solution.py
+++ b/solution.py
@@ -7,7 +7,6 @@
 
 epsilon = 1e-06
 RANK = ("seq_rank", "dp_rank")
-BLOCK = ("seq_block", "dp_block")
 EVERY = ("seq_block", "seq_rank", "dp_block", "dp_rank")
 LANES = 128
 HALO = 16
@@ -105,18 +104,17 @@
         for rows, source in ((here, cot_ref[...]), (edge, edge_ref[:, channels:])):
             piece = dot(source, map_of, ((1,), (1,))).astype(bf16)
             for j in range(ranks):
-                slices[j, rows, n * LANES : (n + 1) * LANES] = piece[:, j * LANES : (j + 1) * LANES]
+                slices[j, rows, n * part : (n + 1) * part] = piece[:, j * LANES : j * LANES + part]
     rank = rank_ref[0]
-    two = 2 * LANES
-    starts = [(home_ref, 0), (cross_ref, two)] + [(out, two) for out in leaving]
-    for out, start in starts:
-        out[here, start : start + channels] = values_ref[...]
-        out[edge, start : start + channels] = edge_ref[:, :channels]
+    width = home_ref.shape[1]
+    for out in refs[:-1]:
+        out[here, :channels] = values_ref[...]
+        out[edge, :channels] = edge_ref[:, :channels]
     home_ref[:, channels:] = slices[rank]
-    cross_ref[:, :two] = slices[lax.bitwise_xor(rank, core)]
+    cross_ref[:, channels:] = slices[lax.bitwise_xor(rank, core)]
     for mask, out in zip(chip_masks(ranks, core)[1:], leaving):
-        out[:, :two] = slices[lax.bitwise_xor(rank, mask | core)]
-        out[:, two + channels :] = slices[lax.bitwise_xor(rank, mask)]
+        out[:, channels:width] = slices[lax.bitwise_xor(rank, mask | core)]
+        out[:, width:] = slices[lax.bitwise_xor(rank, mask)]
 
 
 def stack_crossing(cross_ref, *refs):
@@ -133,69 +131,44 @@
     return [(t * rms * gain).astype(bf16) for t in (x, other)]
 
 
-def prepare(core, chips, rank_ref, home_ref, crossed_ref, *refs):
-    arrived, refs = refs[: chips - 1], refs[chips - 1 :]
-    gain_ref, pairing_ref, outs, refs = refs[0], refs[1], refs[2:7], refs[7:]
-    normed_ref, grads_ref, edge_normed_ref, edge_grads_ref, swapped_gain_ref, sems = refs
+def main_body(core, chips, rank_ref, pieces_in, home_in, crossed_in, *refs):
+    arrived_in, refs = refs[: chips - 1], refs[chips - 1 :]
+    gain_ref, pairing_ref, shifted_out, kernel_out, gelu_out, leaving_out = refs[:6]
+    pieces, home, crossed, arrived, normed_ref, grads_ref, edge_normed_ref, edge_grads_ref = refs[6:14]
+    padded, terms, halves, bent, slopes, total, shifted_ref, kernel_ref, gelu_ref, leaving, sems = refs[14:]
+    owners, part, rows = pieces.shape
+    strands = normed_ref.shape[0]
+    dp_ranks = strands // 2
     moves = Moves(sems)
-    dp_ranks = normed_ref.shape[0] // 2
-    channels = gain_ref.shape[1]
-    masks = chip_masks(2 * (len(arrived) + 1), core)
-    seq_ranks = 2 * len(masks) // dp_ranks
-    positions = home_ref.shape[0] - HALO
-    two = 2 * LANES
+    got_blocks = [moves.start(home_in, home)]
+    got_blocks += [moves.start(block, arrived.at[m]) for m, block in enumerate(arrived_in)]
+    got_blocks += [moves.start(crossed_in.at[m], crossed.at[m]) for m in range(chips)]
+    got_pieces = moves.start(pieces_in, pieces)
+    arrivals = len(moves.copies)
+    masks = chip_masks(2 * chips, core)
+    seq_ranks = 2 * chips // dp_ranks
+    positions = home.shape[0] - HALO
+    channels, width = gain_ref.shape[1], home.shape[1]
     swap = swap_map(pairing_ref[...])
-    blocks = [(0, home_ref, 0, channels)]
-    blocks += [(mask, ref, two, two + channels) for mask, ref in zip(masks[1:], arrived)]
-    blocks += [(mask | core, crossed_ref.at[m], two, 0) for m, mask in enumerate(masks)]
-    for flip, ref, lane, grad_lane in blocks:
+    blocks = [(0, home, channels)]
+    blocks += [(mask, arrived.at[m], width) for m, mask in enumerate(masks[1:])]
+    blocks += [(mask | core, crossed.at[m], channels) for m, mask in enumerate(masks)]
+    for got, (flip, ref, lane) in zip(got_blocks, blocks):
+        got.wait()
         source = lax.bitwise_xor(rank_ref[0], flip)
         b, i = lax.rem(source, dp_ranks), lax.div(source, dp_ranks)
         start = pl.multiple_of(i * positions, positions)
         side = jnp.where(i == 0, 0, jnp.where(i == seq_ranks - 1, 1, 2))
-        both = normalize(ref[:, lane : lane + channels], gain_ref[...], swap)
+        both = normalize(ref[:, :channels], gain_ref[...], swap)
         for n, normed in enumerate(both):
-            first = grad_lane + n * LANES
-            grads = (0.5 * ref[:, first : first + LANES].astype(f32)).astype(bf16)
+            first = lane + n * part
+            grads = 0.5 * ref[:, first : first + part].astype(f32)
             index = n * dp_ranks + b
             normed_ref[index, pl.ds(start, positions), :] = normed[:positions]
-            grads_ref[index, pl.ds(start, positions), :] = grads[:positions]
+            grads_ref[index, pl.ds(start, positions), :part] = grads[:positions]
             edge_normed_ref[side, index] = normed[positions:]
-            edge_grads_ref[side, index] = grads[positions:]
-            place = (index, pl.ds(start, positions))
-            moves.start(normed_ref.at[place], outs[0].at[place])
-    moves.start(grads_ref, outs[1])
-    moves.start(edge_normed_ref, outs[2])
-    moves.start(edge_grads_ref, outs[3])
-    gain = gain_ref[...]
-    first = gain.astype(bf16).astype(f32)
-    second = (gain - first).astype(bf16).astype(f32)
-    third = gain - first - second
-    row = lax.broadcasted_iota(jnp.int32, (HALO, channels), 0)
-    parts = jnp.where(row == 0, first, jnp.where(row == 1, second, jnp.where(row == 2, third, 0.0)))
-    swapped = dot(parts.astype(bf16), swap, ((1,), (0,)))
-    swapped_gain_ref[...] = swapped[0:1] + swapped[1:2] + swapped[2:3]
-    moves.start(swapped_gain_ref, outs[4])
-    moves.wait()
-
-
-def main_body(pieces_in, normed_in, grads_in, edge_normed_in, edge_grads_in, *refs):
-    gain_ref, shifted_out, kernel_out, gelu_out, leaving_out = refs[:5]
-    pieces, normed_ref, grads_ref, edge_normed_ref, edge_grads_ref = refs[5:10]
-    padded, terms, halves, bent, slopes, total, shifted_ref, kernel_ref, gelu_ref, leaving, sems = refs[10:]
-    moves = Moves(sems)
-    owners, part, rows = pieces.shape
-    strands = normed_ref.shape[0]
-    dp_ranks = strands // 2
-    got_pieces = moves.start(pieces_in, pieces)
-    got_edges = [
-        moves.start(edge_normed_in, edge_normed_ref),
-        moves.start(edge_grads_in, edge_grads_ref),
-        moves.start(grads_in, grads_ref),
-    ]
-    got_normed = [moves.start(normed_in.at[n], normed_ref.at[n]) for n in range(strands)]
-    arrivals = len(moves.copies)
-    strands, span, channels = normed_ref.shape
+            edge_grads_ref[side, index, :, :part] = grads[positions:]
+    span = normed_ref.shape[1]
     taps = kernel_ref.shape[0] // part
     half = taps // 2
     reach = 2 * half
@@ -220,19 +193,16 @@
     for k in range(taps):
         padded[k * LANES : k * LANES + part, :] = kernel_ref[k * part : (k + 1) * part, :]
     kernel = padded[...]
-    for copy in got_edges:
-        copy.wait()
     edge_normed = jnp.concatenate([edge_normed_ref[side, s] for side in range(2) for s in range(strands)], 0)
     edge_terms = dot(edge_normed, kernel, ((1,), (1,)))
     for strand in range(strands):
         forward = strand < dp_ranks
-        got_normed[strand].wait()
         terms[HALO : HALO + span, :] = dot(normed_ref[strand], kernel, ((1,), (1,)))
-        halves[HALO : HALO + span, :] = grads_ref[strand].astype(f32)
+        halves[HALO : HALO + span, :] = grads_ref[strand]
         for side, start in enumerate((0, HALO + span)):
             first = (side * strands + strand) * HALO
             terms[start : start + HALO, :] = edge_terms[first : first + HALO]
-            halves[start : start + HALO, :] = edge_grads_ref[side, strand].astype(f32)
+            halves[start : start + HALO, :] = edge_grads_ref[side, strand]
         preact = jnp.zeros((wide, LANES), f32)
         for k in range(taps):
             start = HALO - reach + k if forward else HALO - k
@@ -271,7 +241,7 @@
 
 
 def input_gradient(
-    rank_ref, shifted_ref, kernel_ref, gelu_ref, gain_ref, swapped_gain_ref, pairing_ref, own_ref, cross_ref, *scratch
+    rank_ref, shifted_ref, kernel_ref, gelu_ref, gain_ref, pairing_ref, own_ref, cross_ref, *scratch
 ):
     scaled, shifted, kernel_in, gelus, sems = scratch
     strands = shifted_ref.shape[0]
@@ -284,13 +254,22 @@
     channels = gain_ref.shape[1]
     got_kernel.wait()
     kernel = kernel_in[...]
-    swapped = dot(kernel, swap_map(pairing_ref[...]), ((1,), (0,))).astype(bf16)
+    swap = swap_map(pairing_ref[...])
+    swapped = dot(kernel, swap, ((1,), (0,))).astype(bf16)
+    gain = gain_ref[...]
+    first = gain.astype(bf16).astype(f32)
+    second = (gain - first).astype(bf16).astype(f32)
+    third = gain - first - second
+    row = lax.broadcasted_iota(jnp.int32, (HALO, channels), 0)
+    parts = jnp.where(row == 0, first, jnp.where(row == 1, second, jnp.where(row == 2, third, 0.0)))
+    swapped_gain = dot(parts.astype(bf16), swap, ((1,), (0,)))
+    swapped_gain = swapped_gain[0:1] + swapped_gain[1:2] + swapped_gain[2:3]
     for b in range(dp_ranks):
         got_shifted[b].wait()
         got_shifted[dp_ranks + b].wait()
         scaled[b] = (
             dot(shifted[b], kernel, ((1,), (0,))) * gain_ref[...]
-            + dot(shifted[dp_ranks + b], swapped, ((1,), (0,))) * swapped_gain_ref[...]
+            + dot(shifted[dp_ranks + b], swapped, ((1,), (0,))) * swapped_gain
         ).astype(bf16)
     got_gelus.wait()
     for m, mask in enumerate(chip_masks(2 * chips, dp_ranks)):
@@ -377,6 +356,7 @@
     wide = -(-(span + reach) // 8) * 8
     strands = 2 * dp_ranks
     width = channels + 2 * LANES
+    slim = channels + 2 * part
     rank = lax.axis_index(RANK).reshape(1)
     values, cot = activations[0], cotangent[0]
     along = ("seq_block", "seq_rank")
@@ -413,11 +393,11 @@
     block = positions + HALO
     home, cross, *leaving = called(
         lambda *refs: pack_messages(part, core, *refs),
-        (shape_of((block, width), bf16),) * 2
-        + tuple(shape_of((block, width + 2 * LANES), bf16) for _ in masks[1:]),
+        (pltpu.HBM((block, slim), bf16), shape_of((block, slim), bf16))
+        + tuple(shape_of((block, slim + 2 * part), bf16) for _ in masks[1:]),
         (rank, packed, cot, edge, pairing),
         16,
-        scratch=[pltpu.VMEM((ranks, block, 2 * LANES), bf16)],
+        scratch=[pltpu.VMEM((ranks, block, 2 * part), bf16)],
         specs=[SMEM] + [VMEM] * 4,
     )
     arrived = [
@@ -425,28 +405,10 @@
         for message, mask in zip(leaving, masks[1:])
     ]
     crossing = called(
-        stack_crossing, shape_of((len(masks), block, width), bf16), (cross, *arrived), 8
+        stack_crossing, shape_of((len(masks), block, slim), bf16), (cross, *arrived), 8
     )
     crossed = lax.ppermute(crossing, RANK, flipped_pairs(ranks, core))
-    ready_shapes = [
-        ((strands, span, channels), bf16),
-        ((strands, span, LANES), bf16),
-        ((3, strands, HALO, channels), bf16),
-        ((3, strands, HALO, LANES), bf16),
-        ((1, channels), f32),
-    ]
-    ready = called(
-        lambda *refs: prepare(core, len(masks), *refs),
-        tuple(pltpu.HBM(*shape) for shape in ready_shapes),
-        (rank, home, crossed, *arrived, gain, pairing),
-        24,
-        scratch=[pltpu.VMEM(*shape) for shape in ready_shapes]
-        + [pltpu.SemaphoreType.DMA((2 * ranks + 4,))],
-        specs=[SMEM] + [VMEM] * (4 + len(arrived)),
-        out_specs=(HBM,) * 5,
-    )
-    ready = [pltpu.with_memory_space_constraint(x, pltpu.HBM) for x in ready]
-    pieces = pltpu.with_memory_space_constraint(pieces, pltpu.HBM)
+    held = (pieces, home, crossed, *arrived)
     shapes = (
         (strands, span, taps * part),
         (taps * part, channels),
@@ -454,13 +416,19 @@
         (owners, part + EXTRA, rows),
     )
     shifted, kernel, gelus, outgoing = called(
-        main_body,
+        lambda *refs: main_body(core, len(masks), *refs),
         tuple(pltpu.HBM(shape, bf16) for shape in shapes),
-        (pieces, *ready[:4], gain),
+        (rank, *held, gain, pairing),
         40,
-        scratch=[pltpu.VMEM(pieces.shape, bf16)]
-        + [pltpu.VMEM(*shape) for shape in ready_shapes[:4]]
-        + [
+        scratch=[
+            pltpu.VMEM(pieces.shape, bf16),
+            pltpu.VMEM(home.shape, bf16),
+            pltpu.VMEM(crossed.shape, bf16),
+            pltpu.VMEM((len(arrived), *arrived[0].shape), bf16),
+            pltpu.VMEM((strands, span, channels), bf16),
+            pltpu.VMEM((strands, span, LANES), f32),
+            pltpu.VMEM((3, strands, HALO, channels), bf16),
+            pltpu.VMEM((3, strands, HALO, LANES), f32),
             pltpu.VMEM((taps * LANES, channels), bf16),
             pltpu.VMEM((long, taps * LANES), f32),
             pltpu.VMEM((long, LANES), f32),
@@ -469,8 +437,8 @@
             pltpu.VMEM((taps * part, channels), f32),
         ]
         + [pltpu.VMEM(shape, bf16) for shape in shapes]
-        + [pltpu.SemaphoreType.DMA((2 * strands + 7,))],
-        specs=[HBM] * 5 + [VMEM],
+        + [pltpu.SemaphoreType.DMA((ranks + strands + 4,))],
+        specs=[SMEM] + [pl.BlockSpec(memory_space=pl.ANY)] * len(held) + [VMEM] * 2,
         out_specs=(HBM,) * 4,
     )
     terms = lax.all_to_all(outgoing, EVERY, 0, 0, tiled=True)
@@ -479,12 +447,12 @@
     own, cross = called(
         input_gradient,
         (halves, halves),
-        (rank, *kept, gain, ready[4], pairing),
+        (rank, *kept, gain, pairing),
         24,
         scratch=[pltpu.VMEM((dp_ranks, span, channels), bf16)]
         + [pltpu.VMEM(shape, bf16) for shape in shapes[:3]]
         + [pltpu.SemaphoreType.DMA((strands + 2,))],
-        specs=[SMEM] + [HBM] * 3 + [VMEM] * 3,
+        specs=[SMEM] + [HBM] * 3 + [VMEM] * 2,
     )
     crossed = lax.ppermute(cross, RANK, flipped_pairs(ranks, core))
     leaving = called(

time: 92 us -> 88.4 us (0.961)
  starting transfers between devices: 29.1 us -> 25.7 us
  waiting for transfers between devices: 31.6 us -> 33.9 us
  Pallas kernels: 25.7 us -> 24.2 us
    all_to_all x1, waiting for transfers between devices: 0.01 us -> 6.27 us  [per_device(): pieces = lax.all_to_all(slices, EVERY, 0, 0, tiled=True)]
    all_to_all x1, starting transfers between devices: 7.33 us -> 4.05 us  [per_device(): terms = lax.all_to_all(outgoing, EVERY, 0, 0, tiled=True)]
    ppermute x1, waiting for transfers between devices: 2.47 us -> 0.01 us  [per_device(): crossed = lax.ppermute(crossing, RANK, flipped_pairs(ranks, core))]
    ppermute x6, waiting for transfers between devices: 26.6 us -> 25 us  [per_device(): lax.ppermute(message, RANK, flipped_pairs(ranks, mask))]
    pallas_call x9 -> x8, Pallas kernels: 25.7 us -> 24.2 us  [called(): pl.pallas_call(body, out_shape=outs, in_specs=specs or [VMEM] * len(args)...]
    unnamed x12 -> x10, local copies, waits for them, and re-layouts: 2.79 us -> 1.9 us
  transfers between devices with their start and end apart: 11 -> 11, of which waited for: 7 -> 4; matrix products, arithmetic and copies ran while one was open for 1% -> 1% of each run, Pallas kernels for 13% -> 10%
where the time goes in v10:
time: 88.4 us; the launch traced here: 88 us
  waiting for transfers between devices  33.9 us (38%)
  starting transfers between devices  25.7 us (29%)
  Pallas kernels  24.2 us (27%)
  local copies, waits for them, and re-layouts  2.59 us (3%)
    ppermute x6, waiting for transfers between devices, per_device(): lax.ppermute(message, RANK, flipped_pairs(ranks, mask))  25 us
    pallas_call x8, Pallas kernels, called(): pl.pallas_call(body, out_shape=outs, in_specs=specs or [VMEM] * len(args)...  24.2 us
    all_to_all x1, starting transfers between devices, per_device(): pieces = lax.all_to_all(slices, EVERY, 0, 0, tiled=True)  8.31 us
    ppermute x6, starting transfers between devices, per_device(): lax.ppermute(message, RANK, flipped_pairs(ranks, mask))  8.02 us
    all_to_all x1, waiting for transfers between devices, per_device(): pieces = lax.all_to_all(slices, EVERY, 0, 0, tiled=True)  6.27 us
    ppermute x1, starting transfers between devices, per_device(): crossed = lax.ppermute(crossing, RANK, flipped_pairs(ranks, core))  4.49 us
    all_to_all x1, starting transfers between devices, per_device(): terms = lax.all_to_all(outgoing, EVERY, 0, 0, tiled=True)  4.05 us
    ppermute x1, waiting for transfers between devices, per_device(): crossed = lax.ppermute(cross, RANK, flipped_pairs(ranks, core))  2.58 us
  transfers between devices with their start and end apart: 11, of which 4 were waited for; matrix products, arithmetic and copies ran while one was open for 1% of the time, Pallas kernels for 10%

profile of v10, /device:TPU:0, one launch (start us, length us, event | category | flops | bytes accessed | tf_op | source)
XLA Modules:
  0.0 88.0 jit_solution(11798985874272387477)
XLA Ops:
  0.6 0.0 copy-start.1
  0.6 0.0 copy-start
  0.7 0.9 fusion
  1.5 0.7 collective-permute-start
  2.2 0.7 reshape.18.refs_4_.refs_8_.pairing_ref.refs_3_
  2.9 0.0 copy-start.3
  2.9 0.9 %copy-done.3 = bf16[120,768]{1,0:T(8,128)(2,1)S(1)} copy-done((bf16[120,768]{1,0:T(8,128)(2,1)S(1)}, bf16[120,768]{1,0:T(8,128)(2,1)}, u32[]{:S(2)}) %copy-start.3) | copy-done | bytes 184344
  3.8 1.1 %shard_map.84 = bf16[32,96,120]{2,1,0:T(8,128)(2,1)} custom-call(bf16[120,768]{1,0:T(8,128)(2,1)S(1)} %copy-done.3), custom_call_target="tpu_custom_call" | custom-call | tf_op jit(solution)/shard_map/pallas_call | solution.py:22
  4.9 0.0 collective-permute-done.refs_3_
  4.9 0.0 copy-done.1
  4.9 0.0 copy-done
  4.9 2.9 %shard_map.85 = (bf16[144,960]{1,0:T(8,128)(2,1)}, bf16[144,960]{1,0:T(8,128)(2,1)S(1)}, bf16[144,1152]{1,0:T(8,128)(2,1)}, bf16[144,1152]{1,0:T(8,128)(2,1)S(1)}, bf16[144,1152]{1,0:T(8,128)(2,1)S(1)}) custom-call(s32[1]{0:T(128)} %bitcast.refs_0_.rank_ref, bf16[128,768]{1,0:T(8,128)(2,1)S(1)} %bitcast.7, bf16[128,768]{1,0:T(8,128)(2,1)S(1)} %bitcast.10, ...), custom_call_target="tpu_custom_call" | custom-call | tf_op jit(solution)/shard_map/pallas_call | solution.py:22
  7.8 3.0 %collective-permute-start.1 = (bf16[144,1152]{1,0:T(8,128)(2,1)}, bf16[144,1152]{1,0:T(8,128)(2,1)S(1)}, u32[]{:S(2)}, u32[]{:S(2)}) collective-permute-start(bf16[144,1152]{1,0:T(8,128)(2,1)} %get-tuple-element.29), channel_id=1, source_target_pairs={{0,1},{1,0},{2,3},{3,2},{4,5},{5,4},{6,7},{7,6},{8,9},{9,8},{10,11... | collective-permute-start | bytes 995336 | tf_op jit(solution)/shard_map/ppermute | solution.py:404
  10.8 1.5 %collective-permute-start.2 = (bf16[144,1152]{1,0:T(8,128)(2,1)S(1)}, bf16[144,1152]{1,0:T(8,128)(2,1)S(1)}, u32[]{:S(2)}, u32[]{:S(2)}) collective-permute-start(bf16[144,1152]{1,0:T(8,128)(2,1)S(1)} %get-tuple-element.30), channel_id=1, source_target_pairs={{0,4},{1,5},{2,6},{3,7},{4,0},{5,1},{6,2},{7,3},{8,12},{9,13},{10,... | collective-permute-start | bytes 995336 | tf_op jit(solution)/shard_map/ppermute | solution.py:404
  12.3 0.0 collective-permute-start.3
  12.3 8.3 %all-to-all-start = ((bf16[32,96,120]{2,1,0:T(8,128)(2,1)}), bf16[32,96,120]{2,1,0:T(8,128)(2,1)S(1)}, u32[]{:S(2)}, u32[]{:S(2)}) async-start(bf16[32,96,120]{2,1,0:T(8,128)(2,1)} %shard_map.84), calls=%async_computation | async-start | bytes 1572864 | tf_op jit(solution)/shard_map/all_to_all | solution.py:388
  20.6 0.0 collective-permute-done.1.refs_0_.refs_4_
  20.6 0.0 collective-permute-done.2.refs_1_.refs_5_
  20.6 8.7 %collective-permute-done.3.refs_2_.refs_6_ = bf16[144,1152]{1,0:T(8,128)(2,1)S(1)} collective-permute-done((bf16[144,1152]{1,0:T(8,128)(2,1)S(1)}, bf16[144,1152]{1,0:T(8,128)(2,1)S(1)}, u32[]{:S(2)}, u32[]{:S(2)}) %collective-permute-start.3) | collective-permute-done | bytes 331808 | tf_op jit(solution)/shard_map/ppermute | solution.py:404
  29.3 0.0 copy-start.4
  29.3 1.1 %shard_map.86 = bf16[4,144,960]{2,1,0:T(8,128)(2,1)} custom-call(bf16[144,960]{1,0:T(8,128)(2,1)S(1)} %get-tuple-element.28.cross_ref, bf16[144,1152]{1,0:T(8,128)(2,1)S(1)} %collective-permute-done.1.refs_0_.refs_4_, bf16[144,1152]{1,0:T(8,128)(2,1)S(1)} %collective-permute-done.2.refs_1_.refs_5_, bf16[144,1152]{1,0:T(8,128)(2,1)S(1)} %collective-permute-done.3.refs_2_.refs_6_), custom_call_target="tpu_custom_call" | custom-call | tf_op jit(solution)/shard_map/pallas_call | solution.py:22
  30.5 4.5 %collective-permute-start.4 = (bf16[4,144,960]{2,1,0:T(8,128)(2,1)}, bf16[4,144,960]{2,1,0:T(8,128)(2,1)S(1)}, u32[]{:S(2)}, u32[]{:S(2)}) collective-permute-start(bf16[4,144,960]{2,1,0:T(8,128)(2,1)} %shard_map.86), channel_id=1, source_target_pairs={{0,2},{1,3},{2,0},{3,1},{4,6},{5,7},{6,4},{7,5},{8,10},{9,11},{10,... | collective-permute-start | bytes 3317768 | tf_op jit(solution)/shard_map/ppermute | solution.py:410
  35.0 0.0 copy-done.4
  35.0 6.3 %all-to-all-done.refs_1_ = bf16[32,96,120]{2,1,0:T(8,128)(2,1)S(1)} async-done(((bf16[32,96,120]{2,1,0:T(8,128)(2,1)}), bf16[32,96,120]{2,1,0:T(8,128)(2,1)S(1)}, u32[]{:S(2)}, u32[]{:S(2)}) %all-to-all-start) | async-done | bytes 737312 | tf_op jit(solution)/shard_map/all_to_all | solution.py:388
  41.2 0.0 collective-permute-done.4.refs_3_
  41.2 0.0 copy-start.2
  41.2 1.0 %copy-done.2 = bf16[144,960]{1,0:T(8,128)(2,1)S(1)} copy-done((bf16[144,960]{1,0:T(8,128)(2,1)S(1)}, bf16[144,960]{1,0:T(8,128)(2,1)}, u32[]{:S(2)}) %copy-start.2) | copy-done | bytes 276504
  42.2 11.5 %shard_map.87 = (bf16[4,512,480]{2,1,0:T(8,128)(2,1)}, bf16[480,768]{1,0:T(8,128)(2,1)}, bf16[4,512,128]{2,1,0:T(8,128)(2,1)}, bf16[32,112,120]{2,1,0:T(8,128)(2,1)}) custom-call(s32[1]{0:T(128)} %bitcast.refs_0_.rank_ref, bf16[32,96,120]{2,1,0:T(8,128)(2,1)S(1)} %all-to-all-done.refs_1_, bf16[144,960]{1,0:T(8,128)(2,1)S(1)} %copy-done.2, ...), custom_call_target="tpu_custom_call" | custom-call | tf_op jit(solution)/shard_map/pallas_call | solution.py:22
  53.7 4.1 %all-to-all-start.1 = ((bf16[32,112,120]{2,1,0:T(8,128)(2,1)}), bf16[32,112,120]{2,1,0:T(8,128)(2,1)S(1)}, u32[]{:S(2)}, u32[]{:S(2)}) async-start(bf16[32,112,120]{2,1,0:T(8,128)(2,1)} %get-tuple-element.43), calls=%async_computation.1 | async-start | bytes 1835008 | tf_op jit(solution)/shard_map/all_to_all | solution.py:444
  57.8 4.3 %shard_map.88 = (bf16[4,128,1024]{2,1,0:T(8,128)(2,1)S(1)}, bf16[4,128,1024]{2,1,0:T(8,128)(2,1)S(1)}) custom-call(s32[1]{0:T(128)} %bitcast.refs_0_.rank_ref, bf16[4,512,480]{2,1,0:T(8,128)(2,1)} %get-tuple-element.32.shifted_ref, bf16[480,768]{1,0:T(8,128)(2,1)} %get-tuple-element.33.kernel_ref, bf16[4,512,128]{2,1,0:T(8,128)(2,1)} %get-tuple-element.34.gelu_ref, ...), custom_call_target="tpu_custom_call" | custom-call | tf_op jit(solution)/shard_map/pallas_call | solution.py:22
  62.1 0.1 collective-permute-start.5
  62.2 2.6 %collective-permute-done.5.refs_1_ = bf16[4,128,1024]{2,1,0:T(8,128)(2,1)S(1)} collective-permute-done((bf16[4,128,1024]{2,1,0:T(8,128)(2,1)S(1)}, bf16[4,128,1024]{2,1,0:T(8,128)(2,1)S(1)}, u32[]{:S(2)}, u32[]{:S(2)}) %collective-permute-start.5) | collective-permute-done | bytes 1048608 | tf_op jit(solution)/shard_map/ppermute | solution.py:457
  64.8 0.5 shard_map.89
  65.3 1.7 %collective-permute-start.6 = (bf16[128,1152]{1,0:T(8,128)(2,1)S(1)}, bf16[128,1152]{1,0:T(8,128)(2,1)S(1)}, u32[]{:S(2)}, u32[]{:S(2)}) collective-permute-start(bf16[128,1152]{1,0:T(8,128)(2,1)S(1)} %get-tuple-element.38), channel_id=1, source_target_pairs={{0,1},{1,0},{2,3},{3,2},{4,5},{5,4},{6,7},{7,6},{8,9},{9,8},{10,11... | collective-permute-start | bytes 884744 | tf_op jit(solution)/shard_map/ppermute | solution.py:465
  67.0 1.5 %collective-permute-start.7 = (bf16[128,1152]{1,0:T(8,128)(2,1)S(1)}, bf16[128,1152]{1,0:T(8,128)(2,1)S(1)}, u32[]{:S(2)}, u32[]{:S(2)}) collective-permute-start(bf16[128,1152]{1,0:T(8,128)(2,1)S(1)} %get-tuple-element.39), channel_id=1, source_target_pairs={{0,4},{1,5},{2,6},{3,7},{4,0},{5,1},{6,2},{7,3},{8,12},{9,13},{10,... | collective-permute-start | bytes 884744 | tf_op jit(solution)/shard_map/ppermute | solution.py:465
  68.5 0.4 collective-permute-start.8
  68.9 16.3 %collective-permute-done.6.refs_5_ = bf16[128,1152]{1,0:T(8,128)(2,1)S(1)} collective-permute-done((bf16[128,1152]{1,0:T(8,128)(2,1)S(1)}, bf16[128,1152]{1,0:T(8,128)(2,1)S(1)}, u32[]{:S(2)}, u32[]{:S(2)}) %collective-permute-start.6) | collective-permute-done | bytes 294944 | tf_op jit(solution)/shard_map/ppermute | solution.py:465
  85.2 0.0 collective-permute-done.7.refs_6_
  85.2 0.0 collective-permute-done.8.refs_7_
  85.2 1.8 %shard_map.90 = (bf16[128,768]{1,0:T(8,128)(2,1)}, bf16[128,768]{1,0:T(8,128)(2,1)}) custom-call(s32[1]{0:T(128)} %bitcast.refs_0_.rank_ref, bf16[128,768]{1,0:T(8,128)(2,1)S(1)} %bitcast.8, bf16[128,768]{1,0:T(8,128)(2,1)S(1)} %bitcast.11, s32[1,768]{1,0:T(1,128)S(1)} %reshape.18.refs_4_.refs_8_.pairing_ref.refs_3_, ...), custom_call_target="tpu_custom_call" | custom-call | tf_op jit(solution)/shard_map/pallas_call | solution.py:22
  87.0 0.0 all-to-all-done.1.refs_0_
  87.0 1.0 %shard_map.91 = (f32[120,768]{1,0:T(8,128)}, f32[1,24]{1,0:T(1,128)}) custom-call(bf16[32,112,120]{2,1,0:T(8,128)(2,1)S(1)} %all-to-all-done.1.refs_0_), custom_call_target="tpu_custom_call" | custom-call | tf_op jit(solution)/shard_map/pallas_call | solution.py:22
  (1 shorter events, 0.0 us)
Async XLA Ops:
  0.6 4.3 %copy-start.1 = (bf16[1,128,768]{2,1,0:T(8,128)(2,1)S(1)}, bf16[1,128,768]{2,1,0:T(8,128)(2,1)}, u32[]{:S(2)}) copy-start(bf16[1,128,768]{2,1,0:T(8,128)(2,1)} %param.6) | copy-start | bytes 589828
  0.6 4.3 %copy-start = (bf16[1,128,768]{2,1,0:T(8,128)(2,1)S(1)}, bf16[1,128,768]{2,1,0:T(8,128)(2,1)}, u32[]{:S(2)}) copy-start(bf16[1,128,768]{2,1,0:T(8,128)(2,1)} %param.5) | copy-start | bytes 589828
  1.5 3.4 %collective-permute-start = (bf16[16,1536]{1,0:T(8,128)(2,1)S(1)}, bf16[16,1536]{1,0:T(8,128)(2,1)S(1)}, u32[]{:S(2)}, u32[]{:S(2)}) collective-permute-start(bf16[16,1536]{1,0:T(8,128)(2,1)S(1)} %fusion), channel_id=1, source_target_pairs={{6,8},{14,16},{22,24},{8,6},{16,14},{24,22},{7,9},{15,17},{23,25},... | collective-permute-start | bytes 147464 | tf_op jit(solution)/shard_map/ppermute | solution.py:366
  2.9 0.9 %copy-start.3 = (bf16[120,768]{1,0:T(8,128)(2,1)S(1)}, bf16[120,768]{1,0:T(8,128)(2,1)}, u32[]{:S(2)}) copy-start(bf16[120,768]{1,0:T(8,128)(2,1)} %refs_0_.1) | copy-start | bytes 552964
  7.8 12.8 %collective-permute-start.1 = (bf16[144,1152]{1,0:T(8,128)(2,1)}, bf16[144,1152]{1,0:T(8,128)(2,1)S(1)}, u32[]{:S(2)}, u32[]{:S(2)}) collective-permute-start(bf16[144,1152]{1,0:T(8,128)(2,1)} %get-tuple-element.29), channel_id=1, source_target_pairs={{0,1},{1,0},{2,3},{3,2},{4,5},{5,4},{6,7},{7,6},{8,9},{9,8},{10,11... | collective-permute-start | bytes 995336 | tf_op jit(solution)/shard_map/ppermute | solution.py:404
  10.8 9.8 %collective-permute-start.2 = (bf16[144,1152]{1,0:T(8,128)(2,1)S(1)}, bf16[144,1152]{1,0:T(8,128)(2,1)S(1)}, u32[]{:S(2)}, u32[]{:S(2)}) collective-permute-start(bf16[144,1152]{1,0:T(8,128)(2,1)S(1)} %get-tuple-element.30), channel_id=1, source_target_pairs={{0,4},{1,5},{2,6},{3,7},{4,0},{5,1},{6,2},{7,3},{8,12},{9,13},{10,... | collective-permute-start | bytes 995336 | tf_op jit(solution)/shard_map/ppermute | solution.py:404
  12.3 17.1 %collective-permute-start.3 = (bf16[144,1152]{1,0:T(8,128)(2,1)S(1)}, bf16[144,1152]{1,0:T(8,128)(2,1)S(1)}, u32[]{:S(2)}, u32[]{:S(2)}) collective-permute-start(bf16[144,1152]{1,0:T(8,128)(2,1)S(1)} %get-tuple-element.31), channel_id=1, source_target_pairs={{0,5},{1,4},{2,7},{3,6},{4,1},{5,0},{6,3},{7,2},{8,13},{9,12},{10,... | collective-permute-start | bytes 995336 | tf_op jit(solution)/shard_map/ppermute | solution.py:404
  12.3 28.9 %all-to-all-start = ((bf16[32,96,120]{2,1,0:T(8,128)(2,1)}), bf16[32,96,120]{2,1,0:T(8,128)(2,1)S(1)}, u32[]{:S(2)}, u32[]{:S(2)}) async-start(bf16[32,96,120]{2,1,0:T(8,128)(2,1)} %shard_map.84), calls=%async_computation | async-start | bytes 1572864 | tf_op jit(solution)/shard_map/all_to_all | solution.py:388
  29.3 5.6 %copy-start.4 = (f32[768]{0:T(1024)S(1)}, f32[768]{0:T(1024)}, u32[]{:S(2)}) copy-start(f32[768]{0:T(1024)} %param.8) | copy-start | bytes 9220
  30.5 10.8 %collective-permute-start.4 = (bf16[4,144,960]{2,1,0:T(8,128)(2,1)}, bf16[4,144,960]{2,1,0:T(8,128)(2,1)S(1)}, u32[]{:S(2)}, u32[]{:S(2)}) collective-permute-start(bf16[4,144,960]{2,1,0:T(8,128)(2,1)} %shard_map.86), channel_id=1, source_target_pairs={{0,2},{1,3},{2,0},{3,1},{4,6},{5,7},{6,4},{7,5},{8,10},{9,11},{10,... | collective-permute-start | bytes 3317768 | tf_op jit(solution)/shard_map/ppermute | solution.py:410
  41.2 1.0 %copy-start.2 = (bf16[144,960]{1,0:T(8,128)(2,1)S(1)}, bf16[144,960]{1,0:T(8,128)(2,1)}, u32[]{:S(2)}) copy-start(bf16[144,960]{1,0:T(8,128)(2,1)} %get-tuple-element.27.refs_2_) | copy-start | bytes 829444
  53.7 33.3 %all-to-all-start.1 = ((bf16[32,112,120]{2,1,0:T(8,128)(2,1)}), bf16[32,112,120]{2,1,0:T(8,128)(2,1)S(1)}, u32[]{:S(2)}, u32[]{:S(2)}) async-start(bf16[32,112,120]{2,1,0:T(8,128)(2,1)} %get-tuple-element.43), calls=%async_computation.1 | async-start | bytes 1835008 | tf_op jit(solution)/shard_map/all_to_all | solution.py:444
  62.1 2.7 %collective-permute-start.5 = (bf16[4,128,1024]{2,1,0:T(8,128)(2,1)S(1)}, bf16[4,128,1024]{2,1,0:T(8,128)(2,1)S(1)}, u32[]{:S(2)}, u32[]{:S(2)}) collective-permute-start(bf16[4,128,1024]{2,1,0:T(8,128)(2,1)S(1)} %get-tuple-element.36), channel_id=1, source_target_pairs={{0,2},{1,3},{2,0},{3,1},{4,6},{5,7},{6,4},{7,5},{8,10},{9,11},{10,... | collective-permute-start | bytes 3145736 | tf_op jit(solution)/shard_map/ppermute | solution.py:457
  65.3 19.9 %collective-permute-start.6 = (bf16[128,1152]{1,0:T(8,128)(2,1)S(1)}, bf16[128,1152]{1,0:T(8,128)(2,1)S(1)}, u32[]{:S(2)}, u32[]{:S(2)}) collective-permute-start(bf16[128,1152]{1,0:T(8,128)(2,1)S(1)} %get-tuple-element.38), channel_id=1, source_target_pairs={{0,1},{1,0},{2,3},{3,2},{4,5},{5,4},{6,7},{7,6},{8,9},{9,8},{10,11... | collective-permute-start | bytes 884744 | tf_op jit(solution)/shard_map/ppermute | solution.py:465
  67.0 18.2 %collective-permute-start.7 = (bf16[128,1152]{1,0:T(8,128)(2,1)S(1)}, bf16[128,1152]{1,0:T(8,128)(2,1)S(1)}, u32[]{:S(2)}, u32[]{:S(2)}) collective-permute-start(bf16[128,1152]{1,0:T(8,128)(2,1)S(1)} %get-tuple-element.39), channel_id=1, source_target_pairs={{0,4},{1,5},{2,6},{3,7},{4,0},{5,1},{6,2},{7,3},{8,12},{9,13},{10,... | collective-permute-start | bytes 884744 | tf_op jit(solution)/shard_map/ppermute | solution.py:465
  68.5 16.8 %collective-permute-start.8 = (bf16[128,1152]{1,0:T(8,128)(2,1)S(1)}, bf16[128,1152]{1,0:T(8,128)(2,1)S(1)}, u32[]{:S(2)}, u32[]{:S(2)}) collective-permute-start(bf16[128,1152]{1,0:T(8,128)(2,1)S(1)} %get-tuple-element.40), channel_id=1, source_target_pairs={{0,5},{1,4},{2,7},{3,6},{4,1},{5,0},{6,3},{7,2},{8,13},{9,12},{10,... | collective-permute-start | bytes 884744 | tf_op jit(solution)/shard_map/ppermute | solution.py:465

commit v11 on v10

--- a/solution.py
+++ b/solution.py
@@ -95,32 +95,38 @@
     moves.wait()
 
 
-def pack_messages(part, core, rank_ref, values_ref, cot_ref, edge_ref, pairing_ref, *refs):
-    home_ref, cross_ref, leaving, slices = refs[0], refs[1], refs[2:-1], refs[-1]
+def pack_messages(part, core, rank_ref, values_ref, cot_ref, edge_ref, pairing_ref, *outs):
     positions, channels = values_ref.shape
-    ranks = slices.shape[0]
-    here, edge = slice(0, positions), slice(positions, None)
-    for n, map_of in enumerate(slot_maps(part, ranks * LANES, pairing_ref[...])):
-        for rows, source in ((here, cot_ref[...]), (edge, edge_ref[:, channels:])):
-            piece = dot(source, map_of, ((1,), (1,))).astype(bf16)
-            for j in range(ranks):
-                slices[j, rows, n * part : (n + 1) * part] = piece[:, j * LANES : j * LANES + part]
-    rank = rank_ref[0]
-    width = home_ref.shape[1]
-    for out in refs[:-1]:
-        out[here, :channels] = values_ref[...]
-        out[edge, :channels] = edge_ref[:, :channels]
-    home_ref[:, channels:] = slices[rank]
-    cross_ref[:, channels:] = slices[lax.bitwise_xor(rank, core)]
-    for mask, out in zip(chip_masks(ranks, core)[1:], leaving):
-        out[:, channels:width] = slices[lax.bitwise_xor(rank, mask | core)]
-        out[:, width:] = slices[lax.bitwise_xor(rank, mask)]
-
-
-def stack_crossing(cross_ref, *refs):
+    home_ref, cross_ref, leaving = outs[0], outs[1], outs[2:]
+    masks = chip_masks(2 * (len(leaving) + 1), core)
+    flips = [mask | c for mask in masks[1:] for c in (core, 0)] + [0, core]
+    shape = (part, channels)
+    row = lax.broadcasted_iota(jnp.int32, shape, 0)
+    column = lax.broadcasted_iota(jnp.int32, shape, 1)
+    offsets = [column - row, pairing_ref[...] - row]
+    maps = [
+        jnp.where(offset == lax.bitwise_xor(rank_ref[0], flip) * part, 1.0, 0.0).astype(bf16)
+        for flip in flips
+        for offset in offsets
+    ]
+    maps = jnp.concatenate(maps, 0)
+    for rows, kept, cot in (
+        (slice(0, positions), values_ref[...], cot_ref[...]),
+        (slice(positions, None), edge_ref[:, :channels], edge_ref[:, channels:]),
+    ):
+        slices = dot(cot, maps, ((1,), (1,))).astype(bf16)
+        lane = 0
+        for out in (*leaving, home_ref, cross_ref):
+            count = out.shape[1] - channels
+            out[rows, :channels] = kept
+            out[rows, channels:] = slices[:, lane : lane + count]
+            lane += count
+
+
+def stack_crossing(*refs):
     out_ref = refs[-1]
     width = out_ref.shape[2]
-    for m, ref in enumerate((cross_ref,) + refs[:-1]):
+    for m, ref in enumerate(refs[:-1]):
         out_ref[m] = ref[:, :width]
 
 
@@ -131,18 +137,21 @@
     return [(t * rms * gain).astype(bf16) for t in (x, other)]
 
 
-def main_body(core, chips, rank_ref, pieces_in, home_in, crossed_in, *refs):
+def main_body(core, chips, groups, rank_ref, pieces_in, home_in, *refs):
     arrived_in, refs = refs[: chips - 1], refs[chips - 1 :]
-    gain_ref, pairing_ref, shifted_out, kernel_out, gelu_out, leaving_out = refs[:6]
-    pieces, home, crossed, arrived, normed_ref, grads_ref, edge_normed_ref, edge_grads_ref = refs[6:14]
-    padded, terms, halves, bent, slopes, total, shifted_ref, kernel_ref, gelu_ref, leaving, sems = refs[14:]
+    crossed_in, refs = refs[:groups], refs[groups:]
+    gain_ref, pairing_ref, leaving_out, cross_out, own_out = refs[:5]
+    pieces, home, crossed, arrived, normed_ref, grads_ref, edge_normed_ref, edge_grads_ref = refs[5:13]
+    padded, terms, halves, bent, slopes, total, shifted_ref, kernel_ref, gelu_ref = refs[13:22]
+    scaled, leaving, cross, own, sems = refs[22:]
     owners, part, rows = pieces.shape
     strands = normed_ref.shape[0]
     dp_ranks = strands // 2
     moves = Moves(sems)
     got_blocks = [moves.start(home_in, home)]
     got_blocks += [moves.start(block, arrived.at[m]) for m, block in enumerate(arrived_in)]
-    got_blocks += [moves.start(crossed_in.at[m], crossed.at[m]) for m in range(chips)]
+    per = chips // groups
+    got_blocks += [moves.start(crossed_in[m // per].at[m % per], crossed.at[m]) for m in range(chips)]
     got_pieces = moves.start(pieces_in, pieces)
     arrivals = len(moves.copies)
     masks = chip_masks(2 * chips, core)
@@ -188,7 +197,6 @@
             kernel_ref[tap * part : (tap + 1) * part, channel : channel + count] = pieces[
                 owner, :, offset : offset + count
             ]
-    moves.start(kernel_ref, kernel_out)
     padded[...] = jnp.zeros_like(padded)
     for k in range(taps):
         padded[k * LANES : k * LANES + part, :] = kernel_ref[k * part : (k + 1) * part, :]
@@ -214,8 +222,6 @@
         for k in range(taps):
             start = reach - k if forward else k
             shifted_ref[strand, :, k * part : (k + 1) * part] = slopes[start : start + span, :part].astype(bf16)
-        moves.start(shifted_ref.at[strand], shifted_out.at[strand])
-    moves.start(gelu_ref, gelu_out)
     total[...] = dot(
         shifted_ref[...].reshape(strands * span, taps * part),
         normed_ref[...].reshape(strands * span, channels),
@@ -236,51 +242,32 @@
             :, owner * own_gain : (owner + 1) * own_gain
         ].astype(bf16)
     moves.start(leaving, leaving_out)
-    for copy in moves.copies[arrivals:]:
-        copy.wait()
-
-
-def input_gradient(
-    rank_ref, shifted_ref, kernel_ref, gelu_ref, gain_ref, pairing_ref, own_ref, cross_ref, *scratch
-):
-    scaled, shifted, kernel_in, gelus, sems = scratch
-    strands = shifted_ref.shape[0]
-    moves = Moves(sems)
-    got_kernel = moves.start(kernel_ref, kernel_in)
-    got_shifted = [moves.start(shifted_ref.at[n], shifted.at[n]) for n in range(strands)]
-    got_gelus = moves.start(gelu_ref, gelus)
-    dp_ranks = strands // 2
-    chips, positions, _ = own_ref.shape
-    channels = gain_ref.shape[1]
-    got_kernel.wait()
-    kernel = kernel_in[...]
-    swap = swap_map(pairing_ref[...])
+    kernel = kernel_ref[...]
     swapped = dot(kernel, swap, ((1,), (0,))).astype(bf16)
     gain = gain_ref[...]
     first = gain.astype(bf16).astype(f32)
     second = (gain - first).astype(bf16).astype(f32)
     third = gain - first - second
-    row = lax.broadcasted_iota(jnp.int32, (HALO, channels), 0)
     parts = jnp.where(row == 0, first, jnp.where(row == 1, second, jnp.where(row == 2, third, 0.0)))
     swapped_gain = dot(parts.astype(bf16), swap, ((1,), (0,)))
     swapped_gain = swapped_gain[0:1] + swapped_gain[1:2] + swapped_gain[2:3]
     for b in range(dp_ranks):
-        got_shifted[b].wait()
-        got_shifted[dp_ranks + b].wait()
         scaled[b] = (
-            dot(shifted[b], kernel, ((1,), (0,))) * gain_ref[...]
-            + dot(shifted[dp_ranks + b], swapped, ((1,), (0,))) * swapped_gain
+            dot(shifted_ref[b], kernel, ((1,), (0,))) * gain
+            + dot(shifted_ref[dp_ranks + b], swapped, ((1,), (0,))) * swapped_gain
         ).astype(bf16)
-    got_gelus.wait()
-    for m, mask in enumerate(chip_masks(2 * chips, dp_ranks)):
-        for out, flip in ((own_ref, mask), (cross_ref, mask | dp_ranks)):
-            target = lax.bitwise_xor(rank_ref[0], flip)
+    for out, target_out, flip in ((cross, cross_out, core), (own, own_out, 0)):
+        for m, mask in enumerate(masks):
+            target = lax.bitwise_xor(rank_ref[0], mask | flip)
             b = lax.rem(target, dp_ranks)
             start = pl.multiple_of(lax.div(target, dp_ranks) * positions, positions)
             out[m, :, :channels] = scaled[b, pl.ds(start, positions), :]
             for n in range(2):
                 lane = channels + n * LANES
-                out[m, :, lane : lane + LANES] = gelus[n * dp_ranks + b, pl.ds(start, positions), :]
+                out[m, :, lane : lane + LANES] = gelu_ref[n * dp_ranks + b, pl.ds(start, positions), :]
+        moves.start(out, target_out)
+    for copy in moves.copies[arrivals:]:
+        copy.wait()
 
 
 def chip_sum(part, own_ref, crossed_ref, *outs):
@@ -397,33 +384,30 @@
         + tuple(shape_of((block, slim + 2 * part), bf16) for _ in masks[1:]),
         (rank, packed, cot, edge, pairing),
         16,
-        scratch=[pltpu.VMEM((ranks, block, 2 * part), bf16)],
         specs=[SMEM] + [VMEM] * 4,
     )
     arrived = [
         lax.ppermute(message, RANK, flipped_pairs(ranks, mask))
         for message, mask in zip(leaving, masks[1:])
     ]
-    crossing = called(
-        stack_crossing, shape_of((len(masks), block, slim), bf16), (cross, *arrived), 8
-    )
-    crossed = lax.ppermute(crossing, RANK, flipped_pairs(ranks, core))
-    held = (pieces, home, crossed, *arrived)
-    shapes = (
-        (strands, span, taps * part),
-        (taps * part, channels),
-        (strands, span, LANES),
-        (owners, part + EXTRA, rows),
-    )
-    shifted, kernel, gelus, outgoing = called(
-        lambda *refs: main_body(core, len(masks), *refs),
+    both_cores = []
+    for first in range(0, len(masks), 2):
+        group = (cross, *arrived)[first : first + 2]
+        crossing = called(stack_crossing, shape_of((len(group), block, slim), bf16), group, 8)
+        both_cores.append(lax.ppermute(crossing, RANK, flipped_pairs(ranks, core)))
+    held = (pieces, home, *arrived, *both_cores)
+    halves = (len(masks), positions, width)
+    shapes = ((owners, part + EXTRA, rows), halves, halves)
+    groups = len(both_cores)
+    outgoing, cross, own = called(
+        lambda *refs: main_body(core, len(masks), groups, *refs),
         tuple(pltpu.HBM(shape, bf16) for shape in shapes),
         (rank, *held, gain, pairing),
-        40,
+        44,
         scratch=[
             pltpu.VMEM(pieces.shape, bf16),
             pltpu.VMEM(home.shape, bf16),
-            pltpu.VMEM(crossed.shape, bf16),
+            pltpu.VMEM((len(masks), block, slim), bf16),
             pltpu.VMEM((len(arrived), *arrived[0].shape), bf16),
             pltpu.VMEM((strands, span, channels), bf16),
             pltpu.VMEM((strands, span, LANES), f32),
@@ -435,25 +419,17 @@
             pltpu.VMEM((wide, LANES), f32),
             pltpu.VMEM((wide, LANES), f32),
             pltpu.VMEM((taps * part, channels), f32),
+            pltpu.VMEM((strands, span, taps * part), bf16),
+            pltpu.VMEM((taps * part, channels), bf16),
+            pltpu.VMEM((strands, span, LANES), bf16),
+            pltpu.VMEM((dp_ranks, span, channels), bf16),
         ]
         + [pltpu.VMEM(shape, bf16) for shape in shapes]
-        + [pltpu.SemaphoreType.DMA((ranks + strands + 4,))],
+        + [pltpu.SemaphoreType.DMA((ranks + 4,))],
         specs=[SMEM] + [pl.BlockSpec(memory_space=pl.ANY)] * len(held) + [VMEM] * 2,
-        out_specs=(HBM,) * 4,
+        out_specs=(HBM,) * 3,
     )
     terms = lax.all_to_all(outgoing, EVERY, 0, 0, tiled=True)
-    halves = shape_of((len(masks), positions, width), bf16)
-    kept = [pltpu.with_memory_space_constraint(x, pltpu.HBM) for x in (shifted, kernel, gelus)]
-    own, cross = called(
-        input_gradient,
-        (halves, halves),
-        (rank, *kept, gain, pairing),
-        24,
-        scratch=[pltpu.VMEM((dp_ranks, span, channels), bf16)]
-        + [pltpu.VMEM(shape, bf16) for shape in shapes[:3]]
-        + [pltpu.SemaphoreType.DMA((strands + 2,))],
-        specs=[SMEM] + [HBM] * 3 + [VMEM] * 2,
-    )
     crossed = lax.ppermute(cross, RANK, flipped_pairs(ranks, core))
     leaving = called(
         lambda *refs: chip_sum(part, *refs),
@@ -464,14 +440,6 @@
     arrived = leaving[:1] + tuple(
         lax.ppermute(message, RANK, flipped_pairs(ranks, mask))
         for message, mask in zip(leaving[1:], masks[1:])
-    )
-    combined, grad_input = called(
-        lambda *refs: finish(part, core, *refs),
-        (shape_of((positions, channels), bf16), shape_of((positions, channels), bf16)),
-        (rank, values, cot, pairing, *arrived),
-        16,
-        scratch=[pltpu.VMEM((2, ranks, positions, LANES), bf16)],
-        specs=[SMEM] + [VMEM] * (3 + len(arrived)),
     )
     order = [
         [
@@ -489,6 +457,15 @@
         16,
         scratch=[pltpu.VMEM((channels, -(-rows // LANES) * LANES), f32)],
     )
+    grad_kernel, home, *arrived = lax.optimization_barrier((grad_kernel, *arrived))
+    combined, grad_input = called(
+        lambda *refs: finish(part, core, *refs),
+        (shape_of((positions, channels), bf16), shape_of((positions, channels), bf16)),
+        (rank, values, cot, pairing, home, *arrived),
+        16,
+        scratch=[pltpu.VMEM((2, ranks, positions, LANES), bf16)],
+        specs=[SMEM] + [VMEM] * (4 + len(arrived)),
+    )
     return combined[None], grad_input[None], grad_kernel, grad_gain[0]
 
 

time: 88.4 us -> 96.7 us (1.094)
  starting transfers between devices: 25.7 us -> 37.3 us
  Pallas kernels: 24.2 us -> 21 us
  waiting for transfers between devices: 33.9 us -> 35.4 us
    all_to_all x1, waiting for transfers between devices: 0.01 us -> 15.9 us  [per_device(): terms = lax.all_to_all(outgoing, EVERY, 0, 0, tiled=True)]
    ppermute x6, waiting for transfers between devices: 25 us -> 15.2 us  [per_device(): lax.ppermute(message, RANK, flipped_pairs(ranks, mask))]
    all_to_all x1, starting transfers between devices: 4.05 us -> 13.3 us  [per_device(): terms = lax.all_to_all(outgoing, EVERY, 0, 0, tiled=True)]
    all_to_all x1, waiting for transfers between devices: 6.27 us -> 0.01 us  [per_device(): pieces = lax.all_to_all(slices, EVERY, 0, 0, tiled=True)]
    ppermute x1 -> x2, starting transfers between devices: 4.49 us -> 8.75 us  [per_device(): both_cores.append(lax.ppermute(crossing, RANK, flipped_pairs(ranks, core)))]
    pallas_call x8, Pallas kernels: 24.2 us -> 21 us  [called(): pl.pallas_call(body, out_shape=outs, in_specs=specs or [VMEM] * len(args)...]
    ppermute x1 -> x2, waiting for transfers between devices: 0.01 us -> 1.62 us  [per_device(): both_cores.append(lax.ppermute(crossing, RANK, flipped_pairs(ranks, core)))]
    ppermute x6, starting transfers between devices: 8.02 us -> 6.98 us  [per_device(): lax.ppermute(message, RANK, flipped_pairs(ranks, mask))]
  transfers between devices with their start and end apart: 11 -> 12, of which waited for: 4 -> 7; matrix products, arithmetic and copies ran while one was open for 1% -> 0% of each run, Pallas kernels for 10% -> 5%
where the time goes in v11:
time: 96.7 us; the launch traced here: 96.4 us
  starting transfers between devices  37.3 us (39%)
  waiting for transfers between devices  35.4 us (37%)
  Pallas kernels  21 us (22%)
  local copies, waits for them, and re-layouts  1.92 us (2%)
    pallas_call x8, Pallas kernels, called(): pl.pallas_call(body, out_shape=outs, in_specs=specs or [VMEM] * len(args)...  21 us
    all_to_all x1, waiting for transfers between devices, per_device(): terms = lax.all_to_all(outgoing, EVERY, 0, 0, tiled=True)  15.9 us
    ppermute x6, waiting for transfers between devices, per_device(): lax.ppermute(message, RANK, flipped_pairs(ranks, mask))  15.2 us
    all_to_all x1, starting transfers between devices, per_device(): terms = lax.all_to_all(outgoing, EVERY, 0, 0, tiled=True)  13.3 us
    ppermute x2, starting transfers between devices, per_device(): both_cores.append(lax.ppermute(crossing, RANK, flipped_pairs(ranks, core)))  8.75 us
    all_to_all x1, starting transfers between devices, per_device(): pieces = lax.all_to_all(slices, EVERY, 0, 0, tiled=True)  7.3 us
    ppermute x6, starting transfers between devices, per_device(): lax.ppermute(message, RANK, flipped_pairs(ranks, mask))  6.98 us
    ppermute x1, waiting for transfers between devices, per_device(): crossed = lax.ppermute(cross, RANK, flipped_pairs(ranks, core))  2.62 us
  transfers between devices with their start and end apart: 12, of which 7 were waited for; matrix products, arithmetic and copies ran while one was open for 0% of the time, Pallas kernels for 5%

profile of v11, /device:TPU:0, one launch (start us, length us, event | category | flops | bytes accessed | tf_op | source)
XLA Modules:
  0.0 96.4 jit_solution(8886927680418112581)
XLA Ops:
  0.6 0.0 copy-start.4
  0.6 0.9 copy-done.4
  1.6 1.1 %shard_map.84 = bf16[32,96,120]{2,1,0:T(8,128)(2,1)} custom-call(bf16[120,768]{1,0:T(8,128)(2,1)S(1)} %copy-done.4), custom_call_target="tpu_custom_call" | custom-call | tf_op jit(solution)/shard_map/pallas_call | solution.py:22
  2.6 0.0 copy-start
  2.6 0.0 copy-start.1
  2.6 7.3 %all-to-all-start = ((bf16[32,96,120]{2,1,0:T(8,128)(2,1)}), bf16[32,96,120]{2,1,0:T(8,128)(2,1)S(1)}, u32[]{:S(2)}, u32[]{:S(2)}) async-start(bf16[32,96,120]{2,1,0:T(8,128)(2,1)} %shard_map.84), calls=%async_computation | async-start | bytes 1572864 | tf_op jit(solution)/shard_map/all_to_all | solution.py:375
  10.0 0.0 copy-done
  10.0 0.0 copy-done.1
  10.0 0.0 copy-start.5
  10.0 0.7 collective-permute-start
  10.7 0.0 copy-done.5
  10.7 0.0 collective-permute-done.refs_3_
  10.7 2.2 %shard_map.85 = (bf16[144,960]{1,0:T(8,128)(2,1)}, bf16[144,960]{1,0:T(8,128)(2,1)S(1)}, bf16[144,1152]{1,0:T(8,128)(2,1)S(1)}, bf16[144,1152]{1,0:T(8,128)(2,1)S(1)}, bf16[144,1152]{1,0:T(8,128)(2,1)S(1)}) custom-call(s32[1]{0:T(128)} %bitcast.refs_0_, bf16[128,768]{1,0:T(8,128)(2,1)S(1)} %bitcast.7, bf16[128,768]{1,0:T(8,128)(2,1)S(1)} %bitcast.10, ...), custom_call_target="tpu_custom_call" | custom-call | tf_op jit(solution)/shard_map/pallas_call | solution.py:22
  13.0 1.8 %collective-permute-start.2 = (bf16[144,1152]{1,0:T(8,128)(2,1)S(1)}, bf16[144,1152]{1,0:T(8,128)(2,1)S(1)}, u32[]{:S(2)}, u32[]{:S(2)}) collective-permute-start(bf16[144,1152]{1,0:T(8,128)(2,1)S(1)} %get-tuple-element.31), channel_id=1, source_target_pairs={{0,4},{1,5},{2,6},{3,7},{4,0},{5,1},{6,2},{7,3},{8,12},{9,13},{10,... | collective-permute-start | bytes 995336 | tf_op jit(solution)/shard_map/ppermute | solution.py:390
  14.7 1.5 %collective-permute-start.3 = (bf16[144,1152]{1,0:T(8,128)(2,1)S(1)}, bf16[144,1152]{1,0:T(8,128)(2,1)S(1)}, u32[]{:S(2)}, u32[]{:S(2)}) collective-permute-start(bf16[144,1152]{1,0:T(8,128)(2,1)S(1)} %get-tuple-element.32), channel_id=1, source_target_pairs={{0,5},{1,4},{2,7},{3,6},{4,1},{5,0},{6,3},{7,2},{8,13},{9,12},{10,... | collective-permute-start | bytes 995336 | tf_op jit(solution)/shard_map/ppermute | solution.py:390
  16.2 0.3 collective-permute-start.1
  16.4 6.8 %collective-permute-done.2.refs_0_.refs_4_ = bf16[144,1152]{1,0:T(8,128)(2,1)S(1)} collective-permute-done((bf16[144,1152]{1,0:T(8,128)(2,1)S(1)}, bf16[144,1152]{1,0:T(8,128)(2,1)S(1)}, u32[]{:S(2)}, u32[]{:S(2)}) %collective-permute-start.2) | collective-permute-done | bytes 331808 | tf_op jit(solution)/shard_map/ppermute | solution.py:390
  23.3 6.1 %collective-permute-done.3.refs_1_.refs_5_ = bf16[144,1152]{1,0:T(8,128)(2,1)S(1)} collective-permute-done((bf16[144,1152]{1,0:T(8,128)(2,1)S(1)}, bf16[144,1152]{1,0:T(8,128)(2,1)S(1)}, u32[]{:S(2)}, u32[]{:S(2)}) %collective-permute-start.3) | collective-permute-done | bytes 331808 | tf_op jit(solution)/shard_map/ppermute | solution.py:390
  29.5 7.6 %collective-permute-start.5 = (bf16[2,144,960]{2,1,0:T(8,128)(2,1)S(1)}, bf16[2,144,960]{2,1,0:T(8,128)(2,1)S(1)}, u32[]{:S(2)}, u32[]{:S(2)}) collective-permute-start(bf16[2,144,960]{2,1,0:T(8,128)(2,1)S(1)} %shard_map.87), channel_id=1, source_target_pairs={{0,2},{1,3},{2,0},{3,1},{4,6},{5,7},{6,4},{7,5},{8,10},{9,11},{10,... | collective-permute-start | bytes 1658888 | tf_op jit(solution)/shard_map/ppermute | solution.py:397
  37.1 0.0 collective-permute-done.1.refs_1_.refs_3_
  37.1 0.0 copy-start.6
  37.1 1.1 %collective-permute-start.4 = (bf16[2,144,960]{2,1,0:T(8,128)(2,1)S(1)}, bf16[2,144,960]{2,1,0:T(8,128)(2,1)S(1)}, u32[]{:S(2)}, u32[]{:S(2)}) collective-permute-start(bf16[2,144,960]{2,1,0:T(8,128)(2,1)S(1)} %shard_map.86), channel_id=1, source_target_pairs={{0,2},{1,3},{2,0},{3,1},{4,6},{5,7},{6,4},{7,5},{8,10},{9,11},{10,... | collective-permute-start | bytes 1658888 | tf_op jit(solution)/shard_map/ppermute | solution.py:397
  38.3 0.0 copy-done.6
  38.3 0.4 collective-permute-done.5.refs_7_
  38.7 1.2 %collective-permute-done.4.refs_6_ = bf16[2,144,960]{2,1,0:T(8,128)(2,1)S(1)} collective-permute-done((bf16[2,144,960]{2,1,0:T(8,128)(2,1)S(1)}, bf16[2,144,960]{2,1,0:T(8,128)(2,1)S(1)}, u32[]{:S(2)}, u32[]{:S(2)}) %collective-permute-start.4) | collective-permute-done | bytes 552992 | tf_op jit(solution)/shard_map/ppermute | solution.py:397
  39.9 0.0 all-to-all-done.refs_1_
  39.9 0.0 copy-start.3
  39.9 1.0 copy-done.3
  40.9 13.8 %shard_map.88 = (bf16[32,112,120]{2,1,0:T(8,128)(2,1)}, bf16[4,128,1024]{2,1,0:T(8,128)(2,1)}, bf16[4,128,1024]{2,1,0:T(8,128)(2,1)}) custom-call(s32[1]{0:T(128)} %bitcast.refs_0_, bf16[32,96,120]{2,1,0:T(8,128)(2,1)S(1)} %all-to-all-done.refs_1_, bf16[144,960]{1,0:T(8,128)(2,1)S(1)} %copy-done.3, ...), custom_call_target="tpu_custom_call" | custom-call | tf_op jit(solution)/shard_map/pallas_call | solution.py:22
  54.6 0.0 copy-start.2
  54.6 13.3 %all-to-all-start.1 = ((bf16[32,112,120]{2,1,0:T(8,128)(2,1)}), bf16[32,112,120]{2,1,0:T(8,128)(2,1)S(1)}, u32[]{:S(2)}, u32[]{:S(2)}) async-start(bf16[32,112,120]{2,1,0:T(8,128)(2,1)} %get-tuple-element.34), calls=%async_computation.1 | async-start | bytes 1835008 | tf_op jit(solution)/shard_map/all_to_all | solution.py:432
  68.0 0.3 collective-permute-start.6
  68.3 2.6 %collective-permute-done.6.refs_1_ = bf16[4,128,1024]{2,1,0:T(8,128)(2,1)S(1)} collective-permute-done((bf16[4,128,1024]{2,1,0:T(8,128)(2,1)}, bf16[4,128,1024]{2,1,0:T(8,128)(2,1)S(1)}, u32[]{:S(2)}, u32[]{:S(2)}) %collective-permute-start.6) | collective-permute-done | bytes 1048608 | tf_op jit(solution)/shard_map/ppermute | solution.py:433
  70.9 0.0 copy-done.2
  70.9 1.1 %shard_map.90 = (bf16[128,1152]{1,0:T(8,128)(2,1)S(1)}, bf16[128,1152]{1,0:T(8,128)(2,1)}, bf16[128,1152]{1,0:T(8,128)(2,1)S(1)}, bf16[128,1152]{1,0:T(8,128)(2,1)S(1)}) custom-call(bf16[4,128,1024]{2,1,0:T(8,128)(2,1)S(1)} %copy-done.2, bf16[4,128,1024]{2,1,0:T(8,128)(2,1)S(1)} %collective-permute-done.6.refs_1_), custom_call_target="tpu_custom_call" | custom-call | tf_op jit(solution)/shard_map/pallas_call | solution.py:22
  72.0 1.8 %collective-permute-start.7 = (bf16[128,1152]{1,0:T(8,128)(2,1)}, bf16[128,1152]{1,0:T(8,128)(2,1)S(1)}, u32[]{:S(2)}, u32[]{:S(2)}) collective-permute-start(bf16[128,1152]{1,0:T(8,128)(2,1)} %get-tuple-element.39), channel_id=1, source_target_pairs={{0,1},{1,0},{2,3},{3,2},{4,5},{5,4},{6,7},{7,6},{8,9},{9,8},{10,11... | collective-permute-start | bytes 884744 | tf_op jit(solution)/shard_map/ppermute | solution.py:441
  73.8 1.5 %collective-permute-start.8 = (bf16[128,1152]{1,0:T(8,128)(2,1)S(1)}, bf16[128,1152]{1,0:T(8,128)(2,1)S(1)}, u32[]{:S(2)}, u32[]{:S(2)}) collective-permute-start(bf16[128,1152]{1,0:T(8,128)(2,1)S(1)} %get-tuple-element.40), channel_id=1, source_target_pairs={{0,4},{1,5},{2,6},{3,7},{4,0},{5,1},{6,2},{7,3},{8,12},{9,13},{10,... | collective-permute-start | bytes 884744 | tf_op jit(solution)/shard_map/ppermute | solution.py:441
  75.2 0.3 collective-permute-start.9
  75.5 15.9 %all-to-all-done.1.refs_0_ = bf16[32,112,120]{2,1,0:T(8,128)(2,1)S(1)} async-done(((bf16[32,112,120]{2,1,0:T(8,128)(2,1)}), bf16[32,112,120]{2,1,0:T(8,128)(2,1)S(1)}, u32[]{:S(2)}, u32[]{:S(2)}) %all-to-all-start.1) | async-done | bytes 860192 | tf_op jit(solution)/shard_map/all_to_all | solution.py:432
  91.4 0.9 shard_map.89
  92.3 0.0 collective-permute-done.7.refs_5_
  92.3 0.0 collective-permute-done.8.refs_6_
  92.3 2.3 %collective-permute-done.9.refs_7_ = bf16[128,1152]{1,0:T(8,128)(2,1)S(1)} collective-permute-done((bf16[128,1152]{1,0:T(8,128)(2,1)S(1)}, bf16[128,1152]{1,0:T(8,128)(2,1)S(1)}, u32[]{:S(2)}, u32[]{:S(2)}) %collective-permute-start.9) | collective-permute-done | bytes 294944 | tf_op jit(solution)/shard_map/ppermute | solution.py:441
  94.6 1.8 %shard_map.91 = (bf16[128,768]{1,0:T(8,128)(2,1)}, bf16[128,768]{1,0:T(8,128)(2,1)}) custom-call(s32[1]{0:T(128)} %bitcast.refs_0_, bf16[128,768]{1,0:T(8,128)(2,1)S(1)} %bitcast.8, bf16[128,768]{1,0:T(8,128)(2,1)S(1)} %bitcast.11, s32[1,768]{1,0:T(1,128)S(1)} %reshape.18.refs_4_.refs_9_.refs_3_, bf16[128,1152]{1,0:T(8,128)(2,1)S(1)} %get-tuple-element.42.refs_4_, ...), custom_call_target="tpu_custom_call" | custom-call | tf_op jit(solution)/shard_map/pallas_call | solution.py:22
  (5 shorter events, 0.1 us)
Async XLA Ops:
  0.6 0.9 copy-start.4
  2.6 7.3 %copy-start = (bf16[1,128,768]{2,1,0:T(8,128)(2,1)S(1)}, bf16[1,128,768]{2,1,0:T(8,128)(2,1)}, u32[]{:S(2)}) copy-start(bf16[1,128,768]{2,1,0:T(8,128)(2,1)} %param.5) | copy-start | bytes 589828
  2.6 7.3 %copy-start.1 = (bf16[1,128,768]{2,1,0:T(8,128)(2,1)S(1)}, bf16[1,128,768]{2,1,0:T(8,128)(2,1)}, u32[]{:S(2)}) copy-start(bf16[1,128,768]{2,1,0:T(8,128)(2,1)} %param.6) | copy-start | bytes 589828
  2.6 37.2 %all-to-all-start = ((bf16[32,96,120]{2,1,0:T(8,128)(2,1)}), bf16[32,96,120]{2,1,0:T(8,128)(2,1)S(1)}, u32[]{:S(2)}, u32[]{:S(2)}) async-start(bf16[32,96,120]{2,1,0:T(8,128)(2,1)} %shard_map.84), calls=%async_computation | async-start | bytes 1572864 | tf_op jit(solution)/shard_map/all_to_all | solution.py:375
  10.0 0.7 copy-start.5
  10.0 0.7 collective-permute-start
  13.0 10.3 %collective-permute-start.2 = (bf16[144,1152]{1,0:T(8,128)(2,1)S(1)}, bf16[144,1152]{1,0:T(8,128)(2,1)S(1)}, u32[]{:S(2)}, u32[]{:S(2)}) collective-permute-start(bf16[144,1152]{1,0:T(8,128)(2,1)S(1)} %get-tuple-element.31), channel_id=1, source_target_pairs={{0,4},{1,5},{2,6},{3,7},{4,0},{5,1},{6,2},{7,3},{8,12},{9,13},{10,... | collective-permute-start | bytes 995336 | tf_op jit(solution)/shard_map/ppermute | solution.py:390
  14.7 14.7 %collective-permute-start.3 = (bf16[144,1152]{1,0:T(8,128)(2,1)S(1)}, bf16[144,1152]{1,0:T(8,128)(2,1)S(1)}, u32[]{:S(2)}, u32[]{:S(2)}) collective-permute-start(bf16[144,1152]{1,0:T(8,128)(2,1)S(1)} %get-tuple-element.32), channel_id=1, source_target_pairs={{0,5},{1,4},{2,7},{3,6},{4,1},{5,0},{6,3},{7,2},{8,13},{9,12},{10,... | collective-permute-start | bytes 995336 | tf_op jit(solution)/shard_map/ppermute | solution.py:390
  16.2 20.9 %collective-permute-start.1 = (bf16[144,1152]{1,0:T(8,128)(2,1)S(1)}, bf16[144,1152]{1,0:T(8,128)(2,1)S(1)}, u32[]{:S(2)}, u32[]{:S(2)}) collective-permute-start(bf16[144,1152]{1,0:T(8,128)(2,1)S(1)} %get-tuple-element.30), channel_id=1, source_target_pairs={{0,1},{1,0},{2,3},{3,2},{4,5},{5,4},{6,7},{7,6},{8,9},{9,8},{10,11... | collective-permute-start | bytes 995336 | tf_op jit(solution)/shard_map/ppermute | solution.py:390
  29.5 9.3 %collective-permute-start.5 = (bf16[2,144,960]{2,1,0:T(8,128)(2,1)S(1)}, bf16[2,144,960]{2,1,0:T(8,128)(2,1)S(1)}, u32[]{:S(2)}, u32[]{:S(2)}) collective-permute-start(bf16[2,144,960]{2,1,0:T(8,128)(2,1)S(1)} %shard_map.87), channel_id=1, source_target_pairs={{0,2},{1,3},{2,0},{3,1},{4,6},{5,7},{6,4},{7,5},{8,10},{9,11},{10,... | collective-permute-start | bytes 1658888 | tf_op jit(solution)/shard_map/ppermute | solution.py:397
  37.1 1.2 %copy-start.6 = (f32[768]{0:T(1024)S(1)}, f32[768]{0:T(1024)}, u32[]{:S(2)}) copy-start(f32[768]{0:T(1024)} %param.8) | copy-start | bytes 9220
  37.1 2.8 %collective-permute-start.4 = (bf16[2,144,960]{2,1,0:T(8,128)(2,1)S(1)}, bf16[2,144,960]{2,1,0:T(8,128)(2,1)S(1)}, u32[]{:S(2)}, u32[]{:S(2)}) collective-permute-start(bf16[2,144,960]{2,1,0:T(8,128)(2,1)S(1)} %shard_map.86), channel_id=1, source_target_pairs={{0,2},{1,3},{2,0},{3,1},{4,6},{5,7},{6,4},{7,5},{8,10},{9,11},{10,... | collective-permute-start | bytes 1658888 | tf_op jit(solution)/shard_map/ppermute | solution.py:397
  39.9 1.0 copy-start.3
  54.6 16.3 %copy-start.2 = (bf16[4,128,1024]{2,1,0:T(8,128)(2,1)S(1)}, bf16[4,128,1024]{2,1,0:T(8,128)(2,1)}, u32[]{:S(2)}) copy-start(bf16[4,128,1024]{2,1,0:T(8,128)(2,1)} %get-tuple-element.36.refs_0_) | copy-start | bytes 3145732
  54.6 36.8 %all-to-all-start.1 = ((bf16[32,112,120]{2,1,0:T(8,128)(2,1)}), bf16[32,112,120]{2,1,0:T(8,128)(2,1)S(1)}, u32[]{:S(2)}, u32[]{:S(2)}) async-start(bf16[32,112,120]{2,1,0:T(8,128)(2,1)} %get-tuple-element.34), calls=%async_computation.1 | async-start | bytes 1835008 | tf_op jit(solution)/shard_map/all_to_all | solution.py:432
  68.0 2.9 %collective-permute-start.6 = (bf16[4,128,1024]{2,1,0:T(8,128)(2,1)}, bf16[4,128,1024]{2,1,0:T(8,128)(2,1)S(1)}, u32[]{:S(2)}, u32[]{:S(2)}) collective-permute-start(bf16[4,128,1024]{2,1,0:T(8,128)(2,1)} %get-tuple-element.37), channel_id=1, source_target_pairs={{0,2},{1,3},{2,0},{3,1},{4,6},{5,7},{6,4},{7,5},{8,10},{9,11},{10,... | collective-permute-start | bytes 3145736 | tf_op jit(solution)/shard_map/ppermute | solution.py:433
  72.0 20.4 %collective-permute-start.7 = (bf16[128,1152]{1,0:T(8,128)(2,1)}, bf16[128,1152]{1,0:T(8,128)(2,1)S(1)}, u32[]{:S(2)}, u32[]{:S(2)}) collective-permute-start(bf16[128,1152]{1,0:T(8,128)(2,1)} %get-tuple-element.39), channel_id=1, source_target_pairs={{0,1},{1,0},{2,3},{3,2},{4,5},{5,4},{6,7},{7,6},{8,9},{9,8},{10,11... | collective-permute-start | bytes 884744 | tf_op jit(solution)/shard_map/ppermute | solution.py:441
  73.8 18.6 %collective-permute-start.8 = (bf16[128,1152]{1,0:T(8,128)(2,1)S(1)}, bf16[128,1152]{1,0:T(8,128)(2,1)S(1)}, u32[]{:S(2)}, u32[]{:S(2)}) collective-permute-start(bf16[128,1152]{1,0:T(8,128)(2,1)S(1)} %get-tuple-element.40), channel_id=1, source_target_pairs={{0,4},{1,5},{2,6},{3,7},{4,0},{5,1},{6,2},{7,3},{8,12},{9,13},{10,... | collective-permute-start | bytes 884744 | tf_op jit(solution)/shard_map/ppermute | solution.py:441
  75.2 19.4 %collective-permute-start.9 = (bf16[128,1152]{1,0:T(8,128)(2,1)S(1)}, bf16[128,1152]{1,0:T(8,128)(2,1)S(1)}, u32[]{:S(2)}, u32[]{:S(2)}) collective-permute-start(bf16[128,1152]{1,0:T(8,128)(2,1)S(1)} %get-tuple-element.41), channel_id=1, source_target_pairs={{0,5},{1,4},{2,7},{3,6},{4,1},{5,0},{6,3},{7,2},{8,13},{9,12},{10,... | collective-permute-start | bytes 884744 | tf_op jit(solution)/shard_map/ppermute | solution.py:441

commit v12 on v11

--- a/solution.py
+++ b/solution.py
@@ -371,7 +371,7 @@
         ],
         out_specs=HBM,
     )
-    slices, packed = lax.optimization_barrier((slices, values))
+    slices, edge, packed = lax.optimization_barrier((slices, edge, values))
     pieces = lax.all_to_all(slices, EVERY, 0, 0, tiled=True)
     pairing = pairing.reshape(1, channels)
     gain = norm_gain.reshape(1, channels)

time: 96.7 us -> 90.9 us (0.940)
  starting transfers between devices: 37.3 us -> 22.8 us
  waiting for transfers between devices: 35.4 us -> 43.1 us
    all_to_all x1, starting transfers between devices: 13.3 us -> 3.63 us  [per_device(): terms = lax.all_to_all(outgoing, EVERY, 0, 0, tiled=True)]
    ppermute x2, starting transfers between devices: 8.75 us -> 0.34 us  [per_device(): both_cores.append(lax.ppermute(crossing, RANK, flipped_pairs(ranks, core)))]
    ppermute x6, waiting for transfers between devices: 15.2 us -> 22.7 us  [per_device(): lax.ppermute(message, RANK, flipped_pairs(ranks, mask))]
    all_to_all x1, starting transfers between devices: 7.3 us -> 10.9 us  [per_device(): pieces = lax.all_to_all(slices, EVERY, 0, 0, tiled=True)]
  transfers between devices with their start and end apart: 12 -> 12, of which waited for: 7 -> 8; matrix products, arithmetic and copies ran while one was open for 0% -> 0% of each run, Pallas kernels for 5% -> 6%
where the time goes in v12:
time: 90.9 us; the launch traced here: 90.5 us
  waiting for transfers between devices  43.1 us (47%)
  starting transfers between devices  22.8 us (25%)
  Pallas kernels  21 us (23%)
  local copies, waits for them, and re-layouts  2.04 us (2%)
    ppermute x6, waiting for transfers between devices, per_device(): lax.ppermute(message, RANK, flipped_pairs(ranks, mask))  22.7 us
    pallas_call x8, Pallas kernels, called(): pl.pallas_call(body, out_shape=outs, in_specs=specs or [VMEM] * len(args)...  21 us
    all_to_all x1, waiting for transfers between devices, per_device(): terms = lax.all_to_all(outgoing, EVERY, 0, 0, tiled=True)  15.9 us
    all_to_all x1, starting transfers between devices, per_device(): pieces = lax.all_to_all(slices, EVERY, 0, 0, tiled=True)  10.9 us
    ppermute x6, starting transfers between devices, per_device(): lax.ppermute(message, RANK, flipped_pairs(ranks, mask))  6.98 us
    all_to_all x1, starting transfers between devices, per_device(): terms = lax.all_to_all(outgoing, EVERY, 0, 0, tiled=True)  3.63 us
    ppermute x1, waiting for transfers between devices, per_device(): crossed = lax.ppermute(cross, RANK, flipped_pairs(ranks, core))  2.62 us
    unnamed x14, local copies, waits for them, and re-layouts  2.04 us
  transfers between devices with their start and end apart: 12, of which 8 were waited for; matrix products, arithmetic and copies ran while one was open for 0% of the time, Pallas kernels for 6%

profile of v12, /device:TPU:0, one launch (start us, length us, event | category | flops | bytes accessed | tf_op | source)
XLA Modules:
  0.0 90.5 jit_solution(9676390315212508756)
XLA Ops:
  0.6 0.0 copy-start.4
  0.6 0.8 fusion
  1.5 0.7 collective-permute-start
  2.2 0.0 copy-done.4
  2.2 1.1 %shard_map.84 = bf16[32,96,120]{2,1,0:T(8,128)(2,1)} custom-call(bf16[120,768]{1,0:T(8,128)(2,1)S(1)} %copy-done.4), custom_call_target="tpu_custom_call" | custom-call | tf_op jit(solution)/shard_map/pallas_call | solution.py:22
  3.2 0.0 copy-start
  3.3 0.0 copy-start.1
  3.3 0.0 collective-permute-done.refs_3_
  3.3 10.9 %all-to-all-start = ((bf16[32,96,120]{2,1,0:T(8,128)(2,1)}), bf16[32,96,120]{2,1,0:T(8,128)(2,1)S(1)}, u32[]{:S(2)}, u32[]{:S(2)}) async-start(bf16[32,96,120]{2,1,0:T(8,128)(2,1)} %shard_map.84), calls=%async_computation | async-start | bytes 1572864 | tf_op jit(solution)/shard_map/all_to_all | solution.py:375
  14.2 0.0 copy-start.5
  14.2 0.7 copy-done.5
  14.9 0.0 copy-done
  14.9 0.0 copy-done.1
  14.9 2.2 %shard_map.85 = (bf16[144,960]{1,0:T(8,128)(2,1)}, bf16[144,960]{1,0:T(8,128)(2,1)S(1)}, bf16[144,1152]{1,0:T(8,128)(2,1)S(1)}, bf16[144,1152]{1,0:T(8,128)(2,1)S(1)}, bf16[144,1152]{1,0:T(8,128)(2,1)S(1)}) custom-call(s32[1]{0:T(128)} %bitcast.refs_0_, bf16[128,768]{1,0:T(8,128)(2,1)S(1)} %bitcast.7, bf16[128,768]{1,0:T(8,128)(2,1)S(1)} %bitcast.10, ...), custom_call_target="tpu_custom_call" | custom-call | tf_op jit(solution)/shard_map/pallas_call | solution.py:22
  17.1 1.8 %collective-permute-start.2 = (bf16[144,1152]{1,0:T(8,128)(2,1)S(1)}, bf16[144,1152]{1,0:T(8,128)(2,1)S(1)}, u32[]{:S(2)}, u32[]{:S(2)}) collective-permute-start(bf16[144,1152]{1,0:T(8,128)(2,1)S(1)} %get-tuple-element.33), channel_id=1, source_target_pairs={{0,4},{1,5},{2,6},{3,7},{4,0},{5,1},{6,2},{7,3},{8,12},{9,13},{10,... | collective-permute-start | bytes 995336 | tf_op jit(solution)/shard_map/ppermute | solution.py:390
  18.9 1.5 %collective-permute-start.3 = (bf16[144,1152]{1,0:T(8,128)(2,1)S(1)}, bf16[144,1152]{1,0:T(8,128)(2,1)S(1)}, u32[]{:S(2)}, u32[]{:S(2)}) collective-permute-start(bf16[144,1152]{1,0:T(8,128)(2,1)S(1)} %get-tuple-element.34), channel_id=1, source_target_pairs={{0,5},{1,4},{2,7},{3,6},{4,1},{5,0},{6,3},{7,2},{8,13},{9,12},{10,... | collective-permute-start | bytes 995336 | tf_op jit(solution)/shard_map/ppermute | solution.py:390
  20.3 0.3 collective-permute-start.1
  20.6 11.5 %collective-permute-done.2.refs_0_.refs_4_ = bf16[144,1152]{1,0:T(8,128)(2,1)S(1)} collective-permute-done((bf16[144,1152]{1,0:T(8,128)(2,1)S(1)}, bf16[144,1152]{1,0:T(8,128)(2,1)S(1)}, u32[]{:S(2)}, u32[]{:S(2)}) %collective-permute-start.2) | collective-permute-done | bytes 331808 | tf_op jit(solution)/shard_map/ppermute | solution.py:390
  32.1 8.6 %collective-permute-done.3.refs_1_.refs_5_ = bf16[144,1152]{1,0:T(8,128)(2,1)S(1)} collective-permute-done((bf16[144,1152]{1,0:T(8,128)(2,1)S(1)}, bf16[144,1152]{1,0:T(8,128)(2,1)S(1)}, u32[]{:S(2)}, u32[]{:S(2)}) %collective-permute-start.3) | collective-permute-done | bytes 331808 | tf_op jit(solution)/shard_map/ppermute | solution.py:390
  40.8 0.1 collective-permute-start.5
  40.9 0.3 collective-permute-done.1.refs_1_.refs_3_
  41.2 0.0 copy-start.6
  41.2 0.3 collective-permute-start.4
  41.5 0.4 copy-done.6
  41.9 1.0 %collective-permute-done.5.refs_7_ = bf16[2,144,960]{2,1,0:T(8,128)(2,1)S(1)} collective-permute-done((bf16[2,144,960]{2,1,0:T(8,128)(2,1)S(1)}, bf16[2,144,960]{2,1,0:T(8,128)(2,1)S(1)}, u32[]{:S(2)}, u32[]{:S(2)}) %collective-permute-start.5) | collective-permute-done | bytes 552992 | tf_op jit(solution)/shard_map/ppermute | solution.py:397
  42.9 0.8 collective-permute-done.4.refs_6_
  43.7 0.0 all-to-all-done.refs_1_
  43.7 0.0 copy-start.3
  43.7 1.0 %copy-done.3 = bf16[144,960]{1,0:T(8,128)(2,1)S(1)} copy-done((bf16[144,960]{1,0:T(8,128)(2,1)S(1)}, bf16[144,960]{1,0:T(8,128)(2,1)}, u32[]{:S(2)}) %copy-start.3) | copy-done | bytes 276504
  44.7 13.8 %shard_map.88 = (bf16[32,112,120]{2,1,0:T(8,128)(2,1)}, bf16[4,128,1024]{2,1,0:T(8,128)(2,1)}, bf16[4,128,1024]{2,1,0:T(8,128)(2,1)}) custom-call(s32[1]{0:T(128)} %bitcast.refs_0_, bf16[32,96,120]{2,1,0:T(8,128)(2,1)S(1)} %all-to-all-done.refs_1_, bf16[144,960]{1,0:T(8,128)(2,1)S(1)} %copy-done.3, ...), custom_call_target="tpu_custom_call" | custom-call | tf_op jit(solution)/shard_map/pallas_call | solution.py:22
  58.4 0.0 copy-start.2
  58.5 3.6 %all-to-all-start.1 = ((bf16[32,112,120]{2,1,0:T(8,128)(2,1)}), bf16[32,112,120]{2,1,0:T(8,128)(2,1)S(1)}, u32[]{:S(2)}, u32[]{:S(2)}) async-start(bf16[32,112,120]{2,1,0:T(8,128)(2,1)} %get-tuple-element.36), calls=%async_computation.1 | async-start | bytes 1835008 | tf_op jit(solution)/shard_map/all_to_all | solution.py:432
  62.1 0.3 collective-permute-start.6
  62.4 2.6 %collective-permute-done.6.refs_1_ = bf16[4,128,1024]{2,1,0:T(8,128)(2,1)S(1)} collective-permute-done((bf16[4,128,1024]{2,1,0:T(8,128)(2,1)}, bf16[4,128,1024]{2,1,0:T(8,128)(2,1)S(1)}, u32[]{:S(2)}, u32[]{:S(2)}) %collective-permute-start.6) | collective-permute-done | bytes 1048608 | tf_op jit(solution)/shard_map/ppermute | solution.py:433
  65.0 0.0 copy-done.2
  65.0 1.1 %shard_map.90 = (bf16[128,1152]{1,0:T(8,128)(2,1)S(1)}, bf16[128,1152]{1,0:T(8,128)(2,1)}, bf16[128,1152]{1,0:T(8,128)(2,1)S(1)}, bf16[128,1152]{1,0:T(8,128)(2,1)S(1)}) custom-call(bf16[4,128,1024]{2,1,0:T(8,128)(2,1)S(1)} %copy-done.2, bf16[4,128,1024]{2,1,0:T(8,128)(2,1)S(1)} %collective-permute-done.6.refs_1_), custom_call_target="tpu_custom_call" | custom-call | tf_op jit(solution)/shard_map/pallas_call | solution.py:22
  66.1 1.8 %collective-permute-start.7 = (bf16[128,1152]{1,0:T(8,128)(2,1)}, bf16[128,1152]{1,0:T(8,128)(2,1)S(1)}, u32[]{:S(2)}, u32[]{:S(2)}) collective-permute-start(bf16[128,1152]{1,0:T(8,128)(2,1)} %get-tuple-element.41), channel_id=1, source_target_pairs={{0,1},{1,0},{2,3},{3,2},{4,5},{5,4},{6,7},{7,6},{8,9},{9,8},{10,11... | collective-permute-start | bytes 884744 | tf_op jit(solution)/shard_map/ppermute | solution.py:441
  67.9 1.5 %collective-permute-start.8 = (bf16[128,1152]{1,0:T(8,128)(2,1)S(1)}, bf16[128,1152]{1,0:T(8,128)(2,1)S(1)}, u32[]{:S(2)}, u32[]{:S(2)}) collective-permute-start(bf16[128,1152]{1,0:T(8,128)(2,1)S(1)} %get-tuple-element.42), channel_id=1, source_target_pairs={{0,4},{1,5},{2,6},{3,7},{4,0},{5,1},{6,2},{7,3},{8,12},{9,13},{10,... | collective-permute-start | bytes 884744 | tf_op jit(solution)/shard_map/ppermute | solution.py:441
  69.3 0.3 collective-permute-start.9
  69.6 15.9 %all-to-all-done.1.refs_0_ = bf16[32,112,120]{2,1,0:T(8,128)(2,1)S(1)} async-done(((bf16[32,112,120]{2,1,0:T(8,128)(2,1)}), bf16[32,112,120]{2,1,0:T(8,128)(2,1)S(1)}, u32[]{:S(2)}, u32[]{:S(2)}) %all-to-all-start.1) | async-done | bytes 860192 | tf_op jit(solution)/shard_map/all_to_all | solution.py:432
  85.5 0.9 %shard_map.89 = (f32[120,768]{1,0:T(8,128)}, f32[1,24]{1,0:T(1,128)}) custom-call(bf16[32,112,120]{2,1,0:T(8,128)(2,1)S(1)} %all-to-all-done.1.refs_0_), custom_call_target="tpu_custom_call" | custom-call | tf_op jit(solution)/shard_map/pallas_call | solution.py:22
  86.5 0.0 collective-permute-done.7.refs_5_
  86.5 0.0 collective-permute-done.8.refs_6_
  86.5 2.3 %collective-permute-done.9.refs_7_ = bf16[128,1152]{1,0:T(8,128)(2,1)S(1)} collective-permute-done((bf16[128,1152]{1,0:T(8,128)(2,1)S(1)}, bf16[128,1152]{1,0:T(8,128)(2,1)S(1)}, u32[]{:S(2)}, u32[]{:S(2)}) %collective-permute-start.9) | collective-permute-done | bytes 294944 | tf_op jit(solution)/shard_map/ppermute | solution.py:441
  88.7 1.8 %shard_map.91 = (bf16[128,768]{1,0:T(8,128)(2,1)}, bf16[128,768]{1,0:T(8,128)(2,1)}) custom-call(s32[1]{0:T(128)} %bitcast.refs_0_, bf16[128,768]{1,0:T(8,128)(2,1)S(1)} %bitcast.8, bf16[128,768]{1,0:T(8,128)(2,1)S(1)} %bitcast.11, s32[1,768]{1,0:T(1,128)S(1)} %reshape.18.refs_4_.refs_9_.refs_3_, bf16[128,1152]{1,0:T(8,128)(2,1)S(1)} %get-tuple-element.44.refs_4_, ...), custom_call_target="tpu_custom_call" | custom-call | tf_op jit(solution)/shard_map/pallas_call | solution.py:22
  (4 shorter events, 0.1 us)
Async XLA Ops:
  0.6 1.5 %copy-start.4 = (bf16[120,768]{1,0:T(8,128)(2,1)S(1)}, bf16[120,768]{1,0:T(8,128)(2,1)}, u32[]{:S(2)}) copy-start(bf16[120,768]{1,0:T(8,128)(2,1)} %refs_0_.1) | copy-start | bytes 552964
  1.5 1.8 %collective-permute-start = (bf16[16,1536]{1,0:T(8,128)(2,1)S(1)}, bf16[16,1536]{1,0:T(8,128)(2,1)S(1)}, u32[]{:S(2)}, u32[]{:S(2)}) collective-permute-start(bf16[16,1536]{1,0:T(8,128)(2,1)S(1)} %fusion), channel_id=1, source_target_pairs={{6,8},{14,16},{22,24},{8,6},{16,14},{24,22},{7,9},{15,17},{23,25},... | collective-permute-start | bytes 147464 | tf_op jit(solution)/shard_map/ppermute | solution.py:353
  3.2 11.6 %copy-start = (bf16[1,128,768]{2,1,0:T(8,128)(2,1)S(1)}, bf16[1,128,768]{2,1,0:T(8,128)(2,1)}, u32[]{:S(2)}) copy-start(bf16[1,128,768]{2,1,0:T(8,128)(2,1)} %param.5) | copy-start | bytes 589828
  3.3 11.6 %copy-start.1 = (bf16[1,128,768]{2,1,0:T(8,128)(2,1)S(1)}, bf16[1,128,768]{2,1,0:T(8,128)(2,1)}, u32[]{:S(2)}) copy-start(bf16[1,128,768]{2,1,0:T(8,128)(2,1)} %param.6) | copy-start | bytes 589828
  3.3 40.4 %all-to-all-start = ((bf16[32,96,120]{2,1,0:T(8,128)(2,1)}), bf16[32,96,120]{2,1,0:T(8,128)(2,1)S(1)}, u32[]{:S(2)}, u32[]{:S(2)}) async-start(bf16[32,96,120]{2,1,0:T(8,128)(2,1)} %shard_map.84), calls=%async_computation | async-start | bytes 1572864 | tf_op jit(solution)/shard_map/all_to_all | solution.py:375
  14.2 0.7 copy-start.5
  17.1 15.0 %collective-permute-start.2 = (bf16[144,1152]{1,0:T(8,128)(2,1)S(1)}, bf16[144,1152]{1,0:T(8,128)(2,1)S(1)}, u32[]{:S(2)}, u32[]{:S(2)}) collective-permute-start(bf16[144,1152]{1,0:T(8,128)(2,1)S(1)} %get-tuple-element.33), channel_id=1, source_target_pairs={{0,4},{1,5},{2,6},{3,7},{4,0},{5,1},{6,2},{7,3},{8,12},{9,13},{10,... | collective-permute-start | bytes 995336 | tf_op jit(solution)/shard_map/ppermute | solution.py:390
  18.9 21.9 %collective-permute-start.3 = (bf16[144,1152]{1,0:T(8,128)(2,1)S(1)}, bf16[144,1152]{1,0:T(8,128)(2,1)S(1)}, u32[]{:S(2)}, u32[]{:S(2)}) collective-permute-start(bf16[144,1152]{1,0:T(8,128)(2,1)S(1)} %get-tuple-element.34), channel_id=1, source_target_pairs={{0,5},{1,4},{2,7},{3,6},{4,1},{5,0},{6,3},{7,2},{8,13},{9,12},{10,... | collective-permute-start | bytes 995336 | tf_op jit(solution)/shard_map/ppermute | solution.py:390
  20.3 20.8 %collective-permute-start.1 = (bf16[144,1152]{1,0:T(8,128)(2,1)S(1)}, bf16[144,1152]{1,0:T(8,128)(2,1)S(1)}, u32[]{:S(2)}, u32[]{:S(2)}) collective-permute-start(bf16[144,1152]{1,0:T(8,128)(2,1)S(1)} %get-tuple-element.32), channel_id=1, source_target_pairs={{0,1},{1,0},{2,3},{3,2},{4,5},{5,4},{6,7},{7,6},{8,9},{9,8},{10,11... | collective-permute-start | bytes 995336 | tf_op jit(solution)/shard_map/ppermute | solution.py:390
  40.8 2.1 %collective-permute-start.5 = (bf16[2,144,960]{2,1,0:T(8,128)(2,1)S(1)}, bf16[2,144,960]{2,1,0:T(8,128)(2,1)S(1)}, u32[]{:S(2)}, u32[]{:S(2)}) collective-permute-start(bf16[2,144,960]{2,1,0:T(8,128)(2,1)S(1)} %shard_map.87), channel_id=1, source_target_pairs={{0,2},{1,3},{2,0},{3,1},{4,6},{5,7},{6,4},{7,5},{8,10},{9,11},{10,... | collective-permute-start | bytes 1658888 | tf_op jit(solution)/shard_map/ppermute | solution.py:397
  41.2 0.7 copy-start.6
  41.2 2.5 %collective-permute-start.4 = (bf16[2,144,960]{2,1,0:T(8,128)(2,1)S(1)}, bf16[2,144,960]{2,1,0:T(8,128)(2,1)S(1)}, u32[]{:S(2)}, u32[]{:S(2)}) collective-permute-start(bf16[2,144,960]{2,1,0:T(8,128)(2,1)S(1)} %shard_map.86), channel_id=1, source_target_pairs={{0,2},{1,3},{2,0},{3,1},{4,6},{5,7},{6,4},{7,5},{8,10},{9,11},{10,... | collective-permute-start | bytes 1658888 | tf_op jit(solution)/shard_map/ppermute | solution.py:397
  43.7 1.0 %copy-start.3 = (bf16[144,960]{1,0:T(8,128)(2,1)S(1)}, bf16[144,960]{1,0:T(8,128)(2,1)}, u32[]{:S(2)}) copy-start(bf16[144,960]{1,0:T(8,128)(2,1)} %get-tuple-element.31.refs_2_) | copy-start | bytes 829444
  58.4 6.6 %copy-start.2 = (bf16[4,128,1024]{2,1,0:T(8,128)(2,1)S(1)}, bf16[4,128,1024]{2,1,0:T(8,128)(2,1)}, u32[]{:S(2)}) copy-start(bf16[4,128,1024]{2,1,0:T(8,128)(2,1)} %get-tuple-element.38.refs_0_) | copy-start | bytes 3145732
  58.5 27.1 %all-to-all-start.1 = ((bf16[32,112,120]{2,1,0:T(8,128)(2,1)}), bf16[32,112,120]{2,1,0:T(8,128)(2,1)S(1)}, u32[]{:S(2)}, u32[]{:S(2)}) async-start(bf16[32,112,120]{2,1,0:T(8,128)(2,1)} %get-tuple-element.36), calls=%async_computation.1 | async-start | bytes 1835008 | tf_op jit(solution)/shard_map/all_to_all | solution.py:432
  62.1 2.9 %collective-permute-start.6 = (bf16[4,128,1024]{2,1,0:T(8,128)(2,1)}, bf16[4,128,1024]{2,1,0:T(8,128)(2,1)S(1)}, u32[]{:S(2)}, u32[]{:S(2)}) collective-permute-start(bf16[4,128,1024]{2,1,0:T(8,128)(2,1)} %get-tuple-element.39), channel_id=1, source_target_pairs={{0,2},{1,3},{2,0},{3,1},{4,6},{5,7},{6,4},{7,5},{8,10},{9,11},{10,... | collective-permute-start | bytes 3145736 | tf_op jit(solution)/shard_map/ppermute | solution.py:433
  66.1 20.4 %collective-permute-start.7 = (bf16[128,1152]{1,0:T(8,128)(2,1)}, bf16[128,1152]{1,0:T(8,128)(2,1)S(1)}, u32[]{:S(2)}, u32[]{:S(2)}) collective-permute-start(bf16[128,1152]{1,0:T(8,128)(2,1)} %get-tuple-element.41), channel_id=1, source_target_pairs={{0,1},{1,0},{2,3},{3,2},{4,5},{5,4},{6,7},{7,6},{8,9},{9,8},{10,11... | collective-permute-start | bytes 884744 | tf_op jit(solution)/shard_map/ppermute | solution.py:441
  67.9 18.6 %collective-permute-start.8 = (bf16[128,1152]{1,0:T(8,128)(2,1)S(1)}, bf16[128,1152]{1,0:T(8,128)(2,1)S(1)}, u32[]{:S(2)}, u32[]{:S(2)}) collective-permute-start(bf16[128,1152]{1,0:T(8,128)(2,1)S(1)} %get-tuple-element.42), channel_id=1, source_target_pairs={{0,4},{1,5},{2,6},{3,7},{4,0},{5,1},{6,2},{7,3},{8,12},{9,13},{10,... | collective-permute-start | bytes 884744 | tf_op jit(solution)/shard_map/ppermute | solution.py:441
  69.3 19.4 %collective-permute-start.9 = (bf16[128,1152]{1,0:T(8,128)(2,1)S(1)}, bf16[128,1152]{1,0:T(8,128)(2,1)S(1)}, u32[]{:S(2)}, u32[]{:S(2)}) collective-permute-start(bf16[128,1152]{1,0:T(8,128)(2,1)S(1)} %get-tuple-element.43), channel_id=1, source_target_pairs={{0,5},{1,4},{2,7},{3,6},{4,1},{5,0},{6,3},{7,2},{8,13},{9,12},{10,... | collective-permute-start | bytes 884744 | tf_op jit(solution)/shard_map/ppermute | solution.py:441

commit v13 on v11

--- a/solution.py
+++ b/solution.py
@@ -10,10 +10,11 @@
 EVERY = ("seq_block", "seq_rank", "dp_block", "dp_rank")
 LANES = 128
 HALO = 16
-EXTRA = 16
+EXTRA = 2
 VMEM = pl.BlockSpec(memory_space=pltpu.VMEM)
 SMEM = pl.BlockSpec(memory_space=pltpu.SMEM)
 HBM = pl.BlockSpec(memory_space=pltpu.HBM)
+ANY = pl.BlockSpec(memory_space=pl.ANY)
 bf16 = jnp.bfloat16
 f32 = jnp.float32
 
@@ -229,17 +230,17 @@
     )
     gain = jnp.sum(total[...] * kernel_ref[...].astype(f32), 0, keepdims=True) / gain_ref[...]
     gain_high = gain.astype(bf16).astype(f32)
-    row = lax.broadcasted_iota(jnp.int32, (EXTRA, channels), 0)
-    extra = jnp.where(row == 0, gain_high, jnp.where(row == 1, gain - gain_high, 0.0))
+    row = lax.broadcasted_iota(jnp.int32, (HALO, channels), 0)
+    extra = jnp.where(row == 0, gain_high, jnp.where(row == 1, gain - gain_high, 0.0)).T
     own_gain = channels // owners
     for owner in range(owners):
         for tap, channel, count, offset in runs(owner):
-            leaving[owner, :part, offset : offset + count] = total[
+            leaving[owner, :, offset : offset + count] = total[
                 tap * part : (tap + 1) * part, channel : channel + count
             ].astype(bf16)
-        leaving[owner, part:, :] = jnp.zeros((EXTRA, rows), bf16)
-        leaving[owner, part:, :own_gain] = extra[
-            :, owner * own_gain : (owner + 1) * own_gain
+        leaving[owner, :, rows:] = jnp.zeros((part, EXTRA), bf16)
+        leaving[owner, :own_gain, rows:] = extra[
+            owner * own_gain : (owner + 1) * own_gain, :EXTRA
         ].astype(bf16)
     moves.start(leaving, leaving_out)
     kernel = kernel_ref[...]
@@ -308,18 +309,19 @@
 
 
 def collect(owner_of, terms_ref, kernel_ref, gain_ref, joined):
-    _, height, rows = terms_ref.shape
-    part = height - EXTRA
+    part = terms_ref.shape[1]
+    rows = kernel_ref.shape[0]
+    own_gain = gain_ref.shape[0]
     joined[...] = jnp.zeros_like(joined)
-    gain = jnp.zeros((1, rows), f32)
+    gain = jnp.zeros((own_gain, EXTRA), f32)
     for rank, owners in enumerate(owner_of):
         total = terms_ref[owners[0]].astype(f32)
         for owner in owners[1:]:
             total += terms_ref[owner].astype(f32)
-        joined[rank * part : (rank + 1) * part, :rows] = total[:part]
-        gain += total[part : part + 1] + total[part + 1 : part + 2]
+        joined[rank * part : (rank + 1) * part, :rows] = total[:, :rows]
+        gain += total[:own_gain, rows:]
     kernel_ref[...] = joined[...].T[:rows]
-    gain_ref[...] = gain[:, : gain_ref.shape[1]]
+    gain_ref[...] = jnp.sum(gain, -1, keepdims=True)
 
 
 def flipped_pairs(count, mask):
@@ -391,13 +393,13 @@
         for message, mask in zip(leaving, masks[1:])
     ]
     both_cores = []
-    for first in range(0, len(masks), 2):
-        group = (cross, *arrived)[first : first + 2]
+    for group in ((cross, *arrived),):
         crossing = called(stack_crossing, shape_of((len(group), block, slim), bf16), group, 8)
         both_cores.append(lax.ppermute(crossing, RANK, flipped_pairs(ranks, core)))
+    home = pltpu.with_memory_space_constraint(home, pltpu.HBM)
     held = (pieces, home, *arrived, *both_cores)
     halves = (len(masks), positions, width)
-    shapes = ((owners, part + EXTRA, rows), halves, halves)
+    shapes = ((owners, part, rows + EXTRA), halves, halves)
     groups = len(both_cores)
     outgoing, cross, own = called(
         lambda *refs: main_body(core, len(masks), groups, *refs),
@@ -426,7 +428,7 @@
         ]
         + [pltpu.VMEM(shape, bf16) for shape in shapes]
         + [pltpu.SemaphoreType.DMA((ranks + 4,))],
-        specs=[SMEM] + [pl.BlockSpec(memory_space=pl.ANY)] * len(held) + [VMEM] * 2,
+        specs=[SMEM, ANY, HBM] + [ANY] * (len(held) - 2) + [VMEM] * 2,
         out_specs=(HBM,) * 3,
     )
     terms = lax.all_to_all(outgoing, EVERY, 0, 0, tiled=True)
@@ -452,7 +454,7 @@
     ]
     grad_kernel, grad_gain = called(
         lambda *refs: collect(order, *refs),
-        (shape_of((rows, channels), f32), shape_of((1, channels // owners), f32)),
+        (shape_of((rows, channels), f32), shape_of((channels // owners, 1), f32)),
         (terms,),
         16,
         scratch=[pltpu.VMEM((channels, -(-rows // LANES) * LANES), f32)],
@@ -466,7 +468,7 @@
         scratch=[pltpu.VMEM((2, ranks, positions, LANES), bf16)],
         specs=[SMEM] + [VMEM] * (4 + len(arrived)),
     )
-    return combined[None], grad_input[None], grad_kernel, grad_gain[0]
+    return combined[None], grad_input[None], grad_kernel, grad_gain[:, 0]
 
 
 def solution(mesh):

time: 96.7 us -> 86.6 us (0.90)
  starting transfers between devices: 37.3 us -> 25.6 us
  other arithmetic: 0.02 us -> 1.48 us
  Pallas kernels: 21 us -> 22.2 us
    all_to_all x1, starting transfers between devices: 13.3 us -> 3.88 us  [per_device(): terms = lax.all_to_all(outgoing, EVERY, 0, 0, tiled=True)]
    all_to_all x1, waiting for transfers between devices: 0.01 us -> 6.25 us  [per_device(): pieces = lax.all_to_all(slices, EVERY, 0, 0, tiled=True)]
    ppermute x2 -> x1, starting transfers between devices: 8.75 us -> 4.5 us  [per_device(): both_cores.append(lax.ppermute(crossing, RANK, flipped_pairs(ranks, core)))]
    all_to_all x1, waiting for transfers between devices: 15.9 us -> 13.1 us  [per_device(): terms = lax.all_to_all(outgoing, EVERY, 0, 0, tiled=True)]
    ppermute x6, waiting for transfers between devices: 15.2 us -> 12.5 us  [per_device(): lax.ppermute(message, RANK, flipped_pairs(ranks, mask))]
    ppermute x2 -> x1, waiting for transfers between devices: 1.62 us -> 0.01 us  [per_device(): both_cores.append(lax.ppermute(crossing, RANK, flipped_pairs(ranks, core)))]
    pallas_call x8 -> x7, Pallas kernels: 21 us -> 22.2 us  [called(): pl.pallas_call(body, out_shape=outs, in_specs=specs or [VMEM] * len(args)...]
    all_to_all x1, starting transfers between devices: 7.3 us -> 8.31 us  [per_device(): pieces = lax.all_to_all(slices, EVERY, 0, 0, tiled=True)]
  transfers between devices with their start and end apart: 12 -> 11, of which waited for: 7 -> 5; matrix products, arithmetic and copies ran while one was open for 0% -> 1% of each run, Pallas kernels for 5% -> 5%
where the time goes in v13:
time: 86.6 us; the launch traced here: 86.2 us
  waiting for transfers between devices  34.5 us (40%)
  starting transfers between devices  25.6 us (30%)
  Pallas kernels  22.2 us (26%)
  local copies, waits for them, and re-layouts  1.63 us (2%)
  other arithmetic  1.48 us (2%)
    pallas_call x7, Pallas kernels, called(): pl.pallas_call(body, out_shape=outs, in_specs=specs or [VMEM] * len(args)...  22.2 us
    all_to_all x1, waiting for transfers between devices, per_device(): terms = lax.all_to_all(outgoing, EVERY, 0, 0, tiled=True)  13.1 us
    ppermute x6, waiting for transfers between devices, per_device(): lax.ppermute(message, RANK, flipped_pairs(ranks, mask))  12.5 us
    all_to_all x1, starting transfers between devices, per_device(): pieces = lax.all_to_all(slices, EVERY, 0, 0, tiled=True)  8.31 us
    ppermute x6, starting transfers between devices, per_device(): lax.ppermute(message, RANK, flipped_pairs(ranks, mask))  7.95 us
    all_to_all x1, waiting for transfers between devices, per_device(): pieces = lax.all_to_all(slices, EVERY, 0, 0, tiled=True)  6.25 us
    ppermute x1, starting transfers between devices, per_device(): both_cores.append(lax.ppermute(crossing, RANK, flipped_pairs(ranks, core)))  4.5 us
    all_to_all x1, starting transfers between devices, per_device(): terms = lax.all_to_all(outgoing, EVERY, 0, 0, tiled=True)  3.88 us
  transfers between devices with their start and end apart: 11, of which 5 were waited for; matrix products, arithmetic and copies ran while one was open for 1% of the time, Pallas kernels for 5%

profile of v13, /device:TPU:0, one launch (start us, length us, event | category | flops | bytes accessed | tf_op | source)
XLA Modules:
  0.0 86.2 jit_solution(6460611680844473691)
XLA Ops:
  0.6 0.0 copy-start.1
  0.6 0.0 copy-start
  0.7 0.9 fusion
  1.5 0.7 collective-permute-start
  2.2 0.7 reshape.18.refs_4_.refs_8_.refs_3_
  2.9 0.0 copy-start.3
  2.9 0.9 %copy-done.3 = bf16[120,768]{1,0:T(8,128)(2,1)S(1)} copy-done((bf16[120,768]{1,0:T(8,128)(2,1)S(1)}, bf16[120,768]{1,0:T(8,128)(2,1)}, u32[]{:S(2)}) %copy-start.3) | copy-done | bytes 184344
  3.8 1.1 %shard_map.84 = bf16[32,96,120]{2,1,0:T(8,128)(2,1)} custom-call(bf16[120,768]{1,0:T(8,128)(2,1)S(1)} %copy-done.3), custom_call_target="tpu_custom_call" | custom-call | tf_op jit(solution)/shard_map/pallas_call | solution.py:23
  4.9 0.0 collective-permute-done.refs_3_
  4.9 0.0 copy-done.1
  4.9 0.0 copy-done
  4.9 2.3 %shard_map.85 = (bf16[144,960]{1,0:T(8,128)(2,1)}, bf16[144,960]{1,0:T(8,128)(2,1)S(1)}, bf16[144,1152]{1,0:T(8,128)(2,1)}, bf16[144,1152]{1,0:T(8,128)(2,1)S(1)}, bf16[144,1152]{1,0:T(8,128)(2,1)S(1)}) custom-call(s32[1]{0:T(128)} %bitcast.refs_0_, bf16[128,768]{1,0:T(8,128)(2,1)S(1)} %bitcast.6, bf16[128,768]{1,0:T(8,128)(2,1)S(1)} %bitcast.9, ...), custom_call_target="tpu_custom_call" | custom-call | tf_op jit(solution)/shard_map/pallas_call | solution.py:23
  7.2 3.0 %collective-permute-start.1 = (bf16[144,1152]{1,0:T(8,128)(2,1)}, bf16[144,1152]{1,0:T(8,128)(2,1)S(1)}, u32[]{:S(2)}, u32[]{:S(2)}) collective-permute-start(bf16[144,1152]{1,0:T(8,128)(2,1)} %get-tuple-element.30), channel_id=1, source_target_pairs={{0,1},{1,0},{2,3},{3,2},{4,5},{5,4},{6,7},{7,6},{8,9},{9,8},{10,11... | collective-permute-start | bytes 995336 | tf_op jit(solution)/shard_map/ppermute | solution.py:392
  10.2 1.5 %collective-permute-start.2 = (bf16[144,1152]{1,0:T(8,128)(2,1)S(1)}, bf16[144,1152]{1,0:T(8,128)(2,1)S(1)}, u32[]{:S(2)}, u32[]{:S(2)}) collective-permute-start(bf16[144,1152]{1,0:T(8,128)(2,1)S(1)} %get-tuple-element.31), channel_id=1, source_target_pairs={{0,4},{1,5},{2,6},{3,7},{4,0},{5,1},{6,2},{7,3},{8,12},{9,13},{10,... | collective-permute-start | bytes 995336 | tf_op jit(solution)/shard_map/ppermute | solution.py:392
  11.7 0.0 collective-permute-start.3
  11.7 8.3 %all-to-all-start = ((bf16[32,96,120]{2,1,0:T(8,128)(2,1)}), bf16[32,96,120]{2,1,0:T(8,128)(2,1)S(1)}, u32[]{:S(2)}, u32[]{:S(2)}) async-start(bf16[32,96,120]{2,1,0:T(8,128)(2,1)} %shard_map.84), calls=%async_computation | async-start | bytes 1572864 | tf_op jit(solution)/shard_map/all_to_all | solution.py:377
  20.0 0.0 collective-permute-done.1.refs_1_.refs_3_
  20.0 0.0 collective-permute-done.2.refs_2_.refs_4_
  20.0 8.7 %collective-permute-done.3.refs_3_.refs_5_ = bf16[144,1152]{1,0:T(8,128)(2,1)S(1)} collective-permute-done((bf16[144,1152]{1,0:T(8,128)(2,1)S(1)}, bf16[144,1152]{1,0:T(8,128)(2,1)S(1)}, u32[]{:S(2)}, u32[]{:S(2)}) %collective-permute-start.3) | collective-permute-done | bytes 331808 | tf_op jit(solution)/shard_map/ppermute | solution.py:392
  28.8 0.0 copy-start.4
  28.8 1.1 %shard_map.86 = bf16[4,144,960]{2,1,0:T(8,128)(2,1)} custom-call(bf16[144,960]{1,0:T(8,128)(2,1)S(1)} %get-tuple-element.33.refs_0_, bf16[144,1152]{1,0:T(8,128)(2,1)S(1)} %collective-permute-done.1.refs_1_.refs_3_, bf16[144,1152]{1,0:T(8,128)(2,1)S(1)} %collective-permute-done.2.refs_2_.refs_4_, bf16[144,1152]{1,0:T(8,128)(2,1)S(1)} %collective-permute-done.3.refs_3_.refs_5_), custom_call_target="tpu_custom_call" | custom-call | tf_op jit(solution)/shard_map/pallas_call | solution.py:23
  29.9 4.5 %collective-permute-start.4 = (bf16[4,144,960]{2,1,0:T(8,128)(2,1)}, bf16[4,144,960]{2,1,0:T(8,128)(2,1)S(1)}, u32[]{:S(2)}, u32[]{:S(2)}) collective-permute-start(bf16[4,144,960]{2,1,0:T(8,128)(2,1)} %shard_map.86), channel_id=1, source_target_pairs={{0,2},{1,3},{2,0},{3,1},{4,6},{5,7},{6,4},{7,5},{8,10},{9,11},{10,... | collective-permute-start | bytes 3317768 | tf_op jit(solution)/shard_map/ppermute | solution.py:398
  34.4 0.0 copy-done.4
  34.4 6.3 %all-to-all-done.refs_1_ = bf16[32,96,120]{2,1,0:T(8,128)(2,1)S(1)} async-done(((bf16[32,96,120]{2,1,0:T(8,128)(2,1)}), bf16[32,96,120]{2,1,0:T(8,128)(2,1)S(1)}, u32[]{:S(2)}, u32[]{:S(2)}) %all-to-all-start) | async-done | bytes 737312 | tf_op jit(solution)/shard_map/all_to_all | solution.py:377
  40.6 0.0 collective-permute-done.4.refs_6_
  40.6 13.7 %shard_map.87 = (bf16[32,96,122]{2,1,0:T(8,128)(2,1)}, bf16[4,128,1024]{2,1,0:T(8,128)(2,1)}, bf16[4,128,1024]{2,1,0:T(8,128)(2,1)}) custom-call(s32[1]{0:T(128)} %bitcast.refs_0_, bf16[32,96,120]{2,1,0:T(8,128)(2,1)S(1)} %all-to-all-done.refs_1_, bf16[144,960]{1,0:T(8,128)(2,1)} %get-tuple-element.29.refs_2_, ...), custom_call_target="tpu_custom_call" | custom-call | tf_op jit(solution)/shard_map/pallas_call | solution.py:23
  54.4 0.0 copy-start.2
  54.4 3.9 %all-to-all-start.1 = ((bf16[32,96,122]{2,1,0:T(8,128)(2,1)}), bf16[32,96,122]{2,1,0:T(8,128)(2,1)S(1)}, u32[]{:S(2)}, u32[]{:S(2)}) async-start(bf16[32,96,122]{2,1,0:T(8,128)(2,1)} %get-tuple-element.34), calls=%async_computation.1 | async-start | bytes 1572864 | tf_op jit(solution)/shard_map/all_to_all | solution.py:434
  58.3 0.3 collective-permute-start.5
  58.6 2.6 %collective-permute-done.5.refs_1_ = bf16[4,128,1024]{2,1,0:T(8,128)(2,1)S(1)} collective-permute-done((bf16[4,128,1024]{2,1,0:T(8,128)(2,1)}, bf16[4,128,1024]{2,1,0:T(8,128)(2,1)S(1)}, u32[]{:S(2)}, u32[]{:S(2)}) %collective-permute-start.5) | collective-permute-done | bytes 1048608 | tf_op jit(solution)/shard_map/ppermute | solution.py:435
  61.2 0.0 copy-done.2
  61.2 1.1 %shard_map.89 = (bf16[128,1152]{1,0:T(8,128)(2,1)S(1)}, bf16[128,1152]{1,0:T(8,128)(2,1)}, bf16[128,1152]{1,0:T(8,128)(2,1)S(1)}, bf16[128,1152]{1,0:T(8,128)(2,1)S(1)}) custom-call(bf16[4,128,1024]{2,1,0:T(8,128)(2,1)S(1)} %copy-done.2, bf16[4,128,1024]{2,1,0:T(8,128)(2,1)S(1)} %collective-permute-done.5.refs_1_), custom_call_target="tpu_custom_call" | custom-call | tf_op jit(solution)/shard_map/pallas_call | solution.py:23
  62.3 1.8 %collective-permute-start.6 = (bf16[128,1152]{1,0:T(8,128)(2,1)}, bf16[128,1152]{1,0:T(8,128)(2,1)S(1)}, u32[]{:S(2)}, u32[]{:S(2)}) collective-permute-start(bf16[128,1152]{1,0:T(8,128)(2,1)} %get-tuple-element.39), channel_id=1, source_target_pairs={{0,1},{1,0},{2,3},{3,2},{4,5},{5,4},{6,7},{7,6},{8,9},{9,8},{10,11... | collective-permute-start | bytes 884744 | tf_op jit(solution)/shard_map/ppermute | solution.py:443
  64.1 1.5 %collective-permute-start.7 = (bf16[128,1152]{1,0:T(8,128)(2,1)S(1)}, bf16[128,1152]{1,0:T(8,128)(2,1)S(1)}, u32[]{:S(2)}, u32[]{:S(2)}) collective-permute-start(bf16[128,1152]{1,0:T(8,128)(2,1)S(1)} %get-tuple-element.40), channel_id=1, source_target_pairs={{0,4},{1,5},{2,6},{3,7},{4,0},{5,1},{6,2},{7,3},{8,12},{9,13},{10,... | collective-permute-start | bytes 884744 | tf_op jit(solution)/shard_map/ppermute | solution.py:443
  65.5 0.3 collective-permute-start.8
  65.8 13.1 %all-to-all-done.1.refs_0_ = bf16[32,96,122]{2,1,0:T(8,128)(2,1)S(1)} async-done(((bf16[32,96,122]{2,1,0:T(8,128)(2,1)}), bf16[32,96,122]{2,1,0:T(8,128)(2,1)S(1)}, u32[]{:S(2)}, u32[]{:S(2)}) %all-to-all-start.1) | async-done | bytes 749600 | tf_op jit(solution)/shard_map/all_to_all | solution.py:434
  78.9 1.1 %shard_map.88 = (f32[120,768]{1,0:T(8,128)}, f32[24,1]{1,0:T(8,128)S(1)}) custom-call(bf16[32,96,122]{2,1,0:T(8,128)(2,1)S(1)} %all-to-all-done.1.refs_0_), custom_call_target="tpu_custom_call" | custom-call | tf_op jit(solution)/shard_map/pallas_call | solution.py:23
  80.0 0.0 collective-permute-done.6.refs_5_
  80.0 0.0 collective-permute-done.7.refs_6_
  80.0 3.8 %collective-permute-done.8.refs_7_ = bf16[128,1152]{1,0:T(8,128)(2,1)S(1)} collective-permute-done((bf16[128,1152]{1,0:T(8,128)(2,1)S(1)}, bf16[128,1152]{1,0:T(8,128)(2,1)S(1)}, u32[]{:S(2)}, u32[]{:S(2)}) %collective-permute-start.8) | collective-permute-done | bytes 294944 | tf_op jit(solution)/shard_map/ppermute | solution.py:443
  83.8 0.6 reduce
  84.4 1.8 %shard_map.90 = (bf16[128,768]{1,0:T(8,128)(2,1)}, bf16[128,768]{1,0:T(8,128)(2,1)}) custom-call(s32[1]{0:T(128)} %bitcast.refs_0_, bf16[128,768]{1,0:T(8,128)(2,1)S(1)} %bitcast.7, bf16[128,768]{1,0:T(8,128)(2,1)S(1)} %bitcast.10, s32[1,768]{1,0:T(1,128)S(1)} %reshape.18.refs_4_.refs_8_.refs_3_, bf16[128,1152]{1,0:T(8,128)(2,1)S(1)} %get-tuple-element.42.refs_4_, ...), custom_call_target="tpu_custom_call" | custom-call | tf_op jit(solution)/shard_map/pallas_call | solution.py:23
  (1 shorter events, 0.0 us)
Async XLA Ops:
  0.6 4.3 %copy-start.1 = (bf16[1,128,768]{2,1,0:T(8,128)(2,1)S(1)}, bf16[1,128,768]{2,1,0:T(8,128)(2,1)}, u32[]{:S(2)}) copy-start(bf16[1,128,768]{2,1,0:T(8,128)(2,1)} %param.6) | copy-start | bytes 589828
  0.6 4.3 %copy-start = (bf16[1,128,768]{2,1,0:T(8,128)(2,1)S(1)}, bf16[1,128,768]{2,1,0:T(8,128)(2,1)}, u32[]{:S(2)}) copy-start(bf16[1,128,768]{2,1,0:T(8,128)(2,1)} %param.5) | copy-start | bytes 589828
  1.5 3.4 %collective-permute-start = (bf16[16,1536]{1,0:T(8,128)(2,1)S(1)}, bf16[16,1536]{1,0:T(8,128)(2,1)S(1)}, u32[]{:S(2)}, u32[]{:S(2)}) collective-permute-start(bf16[16,1536]{1,0:T(8,128)(2,1)S(1)} %fusion), channel_id=1, source_target_pairs={{6,8},{14,16},{22,24},{8,6},{16,14},{24,22},{7,9},{15,17},{23,25},... | collective-permute-start | bytes 147464 | tf_op jit(solution)/shard_map/ppermute | solution.py:355
  2.9 0.9 %copy-start.3 = (bf16[120,768]{1,0:T(8,128)(2,1)S(1)}, bf16[120,768]{1,0:T(8,128)(2,1)}, u32[]{:S(2)}) copy-start(bf16[120,768]{1,0:T(8,128)(2,1)} %refs_0_.1) | copy-start | bytes 552964
  7.2 12.8 %collective-permute-start.1 = (bf16[144,1152]{1,0:T(8,128)(2,1)}, bf16[144,1152]{1,0:T(8,128)(2,1)S(1)}, u32[]{:S(2)}, u32[]{:S(2)}) collective-permute-start(bf16[144,1152]{1,0:T(8,128)(2,1)} %get-tuple-element.30), channel_id=1, source_target_pairs={{0,1},{1,0},{2,3},{3,2},{4,5},{5,4},{6,7},{7,6},{8,9},{9,8},{10,11... | collective-permute-start | bytes 995336 | tf_op jit(solution)/shard_map/ppermute | solution.py:392
  10.2 9.8 %collective-permute-start.2 = (bf16[144,1152]{1,0:T(8,128)(2,1)S(1)}, bf16[144,1152]{1,0:T(8,128)(2,1)S(1)}, u32[]{:S(2)}, u32[]{:S(2)}) collective-permute-start(bf16[144,1152]{1,0:T(8,128)(2,1)S(1)} %get-tuple-element.31), channel_id=1, source_target_pairs={{0,4},{1,5},{2,6},{3,7},{4,0},{5,1},{6,2},{7,3},{8,12},{9,13},{10,... | collective-permute-start | bytes 995336 | tf_op jit(solution)/shard_map/ppermute | solution.py:392
  11.7 17.1 %collective-permute-start.3 = (bf16[144,1152]{1,0:T(8,128)(2,1)S(1)}, bf16[144,1152]{1,0:T(8,128)(2,1)S(1)}, u32[]{:S(2)}, u32[]{:S(2)}) collective-permute-start(bf16[144,1152]{1,0:T(8,128)(2,1)S(1)} %get-tuple-element.32), channel_id=1, source_target_pairs={{0,5},{1,4},{2,7},{3,6},{4,1},{5,0},{6,3},{7,2},{8,13},{9,12},{10,... | collective-permute-start | bytes 995336 | tf_op jit(solution)/shard_map/ppermute | solution.py:392
  11.7 28.9 %all-to-all-start = ((bf16[32,96,120]{2,1,0:T(8,128)(2,1)}), bf16[32,96,120]{2,1,0:T(8,128)(2,1)S(1)}, u32[]{:S(2)}, u32[]{:S(2)}) async-start(bf16[32,96,120]{2,1,0:T(8,128)(2,1)} %shard_map.84), calls=%async_computation | async-start | bytes 1572864 | tf_op jit(solution)/shard_map/all_to_all | solution.py:377
  28.8 5.6 %copy-start.4 = (f32[768]{0:T(1024)S(1)}, f32[768]{0:T(1024)}, u32[]{:S(2)}) copy-start(f32[768]{0:T(1024)} %param.8) | copy-start | bytes 9220
  29.9 10.8 %collective-permute-start.4 = (bf16[4,144,960]{2,1,0:T(8,128)(2,1)}, bf16[4,144,960]{2,1,0:T(8,128)(2,1)S(1)}, u32[]{:S(2)}, u32[]{:S(2)}) collective-permute-start(bf16[4,144,960]{2,1,0:T(8,128)(2,1)} %shard_map.86), channel_id=1, source_target_pairs={{0,2},{1,3},{2,0},{3,1},{4,6},{5,7},{6,4},{7,5},{8,10},{9,11},{10,... | collective-permute-start | bytes 3317768 | tf_op jit(solution)/shard_map/ppermute | solution.py:398
  54.4 6.8 %copy-start.2 = (bf16[4,128,1024]{2,1,0:T(8,128)(2,1)S(1)}, bf16[4,128,1024]{2,1,0:T(8,128)(2,1)}, u32[]{:S(2)}) copy-start(bf16[4,128,1024]{2,1,0:T(8,128)(2,1)} %get-tuple-element.36.refs_0_) | copy-start | bytes 3145732
  54.4 24.5 %all-to-all-start.1 = ((bf16[32,96,122]{2,1,0:T(8,128)(2,1)}), bf16[32,96,122]{2,1,0:T(8,128)(2,1)S(1)}, u32[]{:S(2)}, u32[]{:S(2)}) async-start(bf16[32,96,122]{2,1,0:T(8,128)(2,1)} %get-tuple-element.34), calls=%async_computation.1 | async-start | bytes 1572864 | tf_op jit(solution)/shard_map/all_to_all | solution.py:434
  58.3 2.9 %collective-permute-start.5 = (bf16[4,128,1024]{2,1,0:T(8,128)(2,1)}, bf16[4,128,1024]{2,1,0:T(8,128)(2,1)S(1)}, u32[]{:S(2)}, u32[]{:S(2)}) collective-permute-start(bf16[4,128,1024]{2,1,0:T(8,128)(2,1)} %get-tuple-element.37), channel_id=1, source_target_pairs={{0,2},{1,3},{2,0},{3,1},{4,6},{5,7},{6,4},{7,5},{8,10},{9,11},{10,... | collective-permute-start | bytes 3145736 | tf_op jit(solution)/shard_map/ppermute | solution.py:435
  62.3 17.7 %collective-permute-start.6 = (bf16[128,1152]{1,0:T(8,128)(2,1)}, bf16[128,1152]{1,0:T(8,128)(2,1)S(1)}, u32[]{:S(2)}, u32[]{:S(2)}) collective-permute-start(bf16[128,1152]{1,0:T(8,128)(2,1)} %get-tuple-element.39), channel_id=1, source_target_pairs={{0,1},{1,0},{2,3},{3,2},{4,5},{5,4},{6,7},{7,6},{8,9},{9,8},{10,11... | collective-permute-start | bytes 884744 | tf_op jit(solution)/shard_map/ppermute | solution.py:443
  64.1 15.9 %collective-permute-start.7 = (bf16[128,1152]{1,0:T(8,128)(2,1)S(1)}, bf16[128,1152]{1,0:T(8,128)(2,1)S(1)}, u32[]{:S(2)}, u32[]{:S(2)}) collective-permute-start(bf16[128,1152]{1,0:T(8,128)(2,1)S(1)} %get-tuple-element.40), channel_id=1, source_target_pairs={{0,4},{1,5},{2,6},{3,7},{4,0},{5,1},{6,2},{7,3},{8,12},{9,13},{10,... | collective-permute-start | bytes 884744 | tf_op jit(solution)/shard_map/ppermute | solution.py:443
  65.5 18.2 %collective-permute-start.8 = (bf16[128,1152]{1,0:T(8,128)(2,1)S(1)}, bf16[128,1152]{1,0:T(8,128)(2,1)S(1)}, u32[]{:S(2)}, u32[]{:S(2)}) collective-permute-start(bf16[128,1152]{1,0:T(8,128)(2,1)S(1)} %get-tuple-element.41), channel_id=1, source_target_pairs={{0,5},{1,4},{2,7},{3,6},{4,1},{5,0},{6,3},{7,2},{8,13},{9,12},{10,... | collective-permute-start | bytes 884744 | tf_op jit(solution)/shard_map/ppermute | solution.py:443

commit v14 on v13

--- a/solution.py
+++ b/solution.py
@@ -104,7 +104,7 @@
     shape = (part, channels)
     row = lax.broadcasted_iota(jnp.int32, shape, 0)
     column = lax.broadcasted_iota(jnp.int32, shape, 1)
-    offsets = [column - row, pairing_ref[...] - row]
+    offsets = [column - row, pairing_ref[...].reshape(1, -1) - row]
     maps = [
         jnp.where(offset == lax.bitwise_xor(rank_ref[0], flip) * part, 1.0, 0.0).astype(bf16)
         for flip in flips
@@ -131,11 +131,20 @@
         out_ref[m] = ref[:, :width]
 
 
-def normalize(x, gain, swap):
-    other = dot(x, swap, ((1,), (0,)))
+def normalize(x, gains):
     x = x.astype(f32)
-    rms = lax.rsqrt(jnp.mean(x * x, -1, keepdims=True) + epsilon)
-    return [(t * rms * gain).astype(bf16) for t in (x, other)]
+    x = x * lax.rsqrt(jnp.mean(x * x, -1, keepdims=True) + epsilon)
+    return [(x * gain).astype(bf16) for gain in gains]
+
+
+def swapped_row(row, swap):
+    first = row.astype(bf16).astype(f32)
+    second = (row - first).astype(bf16).astype(f32)
+    third = row - first - second
+    index = lax.broadcasted_iota(jnp.int32, (HALO, row.shape[1]), 0)
+    parts = jnp.where(index == 0, first, jnp.where(index == 1, second, jnp.where(index == 2, third, 0.0)))
+    result = dot(parts.astype(bf16), swap, ((1,), (0,)))
+    return result[0:1] + result[1:2] + result[2:3]
 
 
 def main_body(core, chips, groups, rank_ref, pieces_in, home_in, *refs):
@@ -159,7 +168,8 @@
     seq_ranks = 2 * chips // dp_ranks
     positions = home.shape[0] - HALO
     channels, width = gain_ref.shape[1], home.shape[1]
-    swap = swap_map(pairing_ref[...])
+    swap = swap_map(pairing_ref[...].reshape(1, -1))
+    gains = [gain_ref[...], swapped_row(gain_ref[...], swap)]
     blocks = [(0, home, channels)]
     blocks += [(mask, arrived.at[m], width) for m, mask in enumerate(masks[1:])]
     blocks += [(mask | core, crossed.at[m], channels) for m, mask in enumerate(masks)]
@@ -169,7 +179,7 @@
         b, i = lax.rem(source, dp_ranks), lax.div(source, dp_ranks)
         start = pl.multiple_of(i * positions, positions)
         side = jnp.where(i == 0, 0, jnp.where(i == seq_ranks - 1, 1, 2))
-        both = normalize(ref[:, :channels], gain_ref[...], swap)
+        both = normalize(ref[:, :channels], gains)
         for n, normed in enumerate(both):
             first = lane + n * part
             grads = 0.5 * ref[:, first : first + part].astype(f32)
@@ -198,19 +208,26 @@
             kernel_ref[tap * part : (tap + 1) * part, channel : channel + count] = pieces[
                 owner, :, offset : offset + count
             ]
+    kernel = kernel_ref[...]
+    kernels = [kernel, dot(kernel, swap, ((1,), (0,))).astype(bf16)]
     padded[...] = jnp.zeros_like(padded)
-    for k in range(taps):
-        padded[k * LANES : k * LANES + part, :] = kernel_ref[k * part : (k + 1) * part, :]
-    kernel = padded[...]
-    edge_normed = jnp.concatenate([edge_normed_ref[side, s] for side in range(2) for s in range(strands)], 0)
-    edge_terms = dot(edge_normed, kernel, ((1,), (1,)))
+    for n in range(2):
+        for k in range(taps):
+            padded[n, k * LANES : k * LANES + part, :] = kernels[n][k * part : (k + 1) * part, :]
+    edge_terms = []
+    for n in range(2):
+        edges = [
+            edge_normed_ref[side, n * dp_ranks + b] for side in range(2) for b in range(dp_ranks)
+        ]
+        edge_terms.append(dot(jnp.concatenate(edges, 0), padded[n], ((1,), (1,))))
     for strand in range(strands):
         forward = strand < dp_ranks
-        terms[HALO : HALO + span, :] = dot(normed_ref[strand], kernel, ((1,), (1,)))
+        n, b = divmod(strand, dp_ranks)
+        terms[HALO : HALO + span, :] = dot(normed_ref[strand], padded[n], ((1,), (1,)))
         halves[HALO : HALO + span, :] = grads_ref[strand]
         for side, start in enumerate((0, HALO + span)):
-            first = (side * strands + strand) * HALO
-            terms[start : start + HALO, :] = edge_terms[first : first + HALO]
+            first = (side * dp_ranks + b) * HALO
+            terms[start : start + HALO, :] = edge_terms[n][first : first + HALO]
             halves[start : start + HALO, :] = edge_grads_ref[side, strand]
         preact = jnp.zeros((wide, LANES), f32)
         for k in range(taps):
@@ -223,12 +240,16 @@
         for k in range(taps):
             start = reach - k if forward else k
             shifted_ref[strand, :, k * part : (k + 1) * part] = slopes[start : start + span, :part].astype(bf16)
-    total[...] = dot(
-        shifted_ref[...].reshape(strands * span, taps * part),
-        normed_ref[...].reshape(strands * span, channels),
-        ((0,), (0,)),
-    )
-    gain = jnp.sum(total[...] * kernel_ref[...].astype(f32), 0, keepdims=True) / gain_ref[...]
+    plain, other = [
+        dot(
+            shifted_ref[n * dp_ranks : (n + 1) * dp_ranks].reshape(dp_ranks * span, taps * part),
+            normed_ref[n * dp_ranks : (n + 1) * dp_ranks].reshape(dp_ranks * span, channels),
+            ((0,), (0,)),
+        )
+        for n in range(2)
+    ]
+    total[...] = plain + dot(other.astype(bf16), swap, ((1,), (0,)))
+    gain = jnp.sum(total[...] * kernel.astype(f32), 0, keepdims=True) / gain_ref[...]
     gain_high = gain.astype(bf16).astype(f32)
     row = lax.broadcasted_iota(jnp.int32, (HALO, channels), 0)
     extra = jnp.where(row == 0, gain_high, jnp.where(row == 1, gain - gain_high, 0.0)).T
@@ -243,19 +264,10 @@
             owner * own_gain : (owner + 1) * own_gain, :EXTRA
         ].astype(bf16)
     moves.start(leaving, leaving_out)
-    kernel = kernel_ref[...]
-    swapped = dot(kernel, swap, ((1,), (0,))).astype(bf16)
-    gain = gain_ref[...]
-    first = gain.astype(bf16).astype(f32)
-    second = (gain - first).astype(bf16).astype(f32)
-    third = gain - first - second
-    parts = jnp.where(row == 0, first, jnp.where(row == 1, second, jnp.where(row == 2, third, 0.0)))
-    swapped_gain = dot(parts.astype(bf16), swap, ((1,), (0,)))
-    swapped_gain = swapped_gain[0:1] + swapped_gain[1:2] + swapped_gain[2:3]
     for b in range(dp_ranks):
         scaled[b] = (
-            dot(shifted_ref[b], kernel, ((1,), (0,))) * gain
-            + dot(shifted_ref[dp_ranks + b], swapped, ((1,), (0,))) * swapped_gain
+            dot(shifted_ref[b], kernels[0], ((1,), (0,))) * gains[0]
+            + dot(shifted_ref[dp_ranks + b], kernels[1], ((1,), (0,))) * gains[1]
         ).astype(bf16)
     for out, target_out, flip in ((cross, cross_out, core), (own, own_out, 0)):
         for m, mask in enumerate(masks):
@@ -298,7 +310,7 @@
                 start = channels + (2 * c + n) * part
                 gelus[n, source, :, :part] = block[:, start : start + part]
     joined = [jnp.concatenate([gelus[n, j] for j in range(ranks)], -1) for n in range(2)]
-    maps = slot_maps(part, ranks * LANES, pairing_ref[...])
+    maps = slot_maps(part, ranks * LANES, pairing_ref[...].reshape(1, -1))
     plain, other = [dot(j, m, ((1,), (0,))) for j, m in zip(joined, maps)]
     values = values_ref[...].astype(f32)
     rms = lax.rsqrt(jnp.mean(values * values, -1, keepdims=True) + epsilon)
@@ -311,7 +323,7 @@
 def collect(owner_of, terms_ref, kernel_ref, gain_ref, joined):
     part = terms_ref.shape[1]
     rows = kernel_ref.shape[0]
-    own_gain = gain_ref.shape[0]
+    own_gain = gain_ref.shape[1]
     joined[...] = jnp.zeros_like(joined)
     gain = jnp.zeros((own_gain, EXTRA), f32)
     for rank, owners in enumerate(owner_of):
@@ -320,8 +332,11 @@
             total += terms_ref[owner].astype(f32)
         joined[rank * part : (rank + 1) * part, :rows] = total[:, :rows]
         gain += total[:own_gain, rows:]
-    kernel_ref[...] = joined[...].T[:rows]
-    gain_ref[...] = jnp.sum(gain, -1, keepdims=True)
+    channels = kernel_ref.shape[1]
+    joined[channels : channels + own_gain, :EXTRA] = gain
+    turned = joined[...].T
+    kernel_ref[...] = turned[:rows, :channels]
+    gain_ref[...] = sum(turned[n : n + 1, channels : channels + own_gain] for n in range(EXTRA))
 
 
 def flipped_pairs(count, mask):
@@ -375,7 +390,6 @@
     )
     slices, packed = lax.optimization_barrier((slices, values))
     pieces = lax.all_to_all(slices, EVERY, 0, 0, tiled=True)
-    pairing = pairing.reshape(1, channels)
     gain = norm_gain.reshape(1, channels)
     core = dp_ranks
     masks = chip_masks(ranks, core)
@@ -415,7 +429,7 @@
             pltpu.VMEM((strands, span, LANES), f32),
             pltpu.VMEM((3, strands, HALO, channels), bf16),
             pltpu.VMEM((3, strands, HALO, LANES), f32),
-            pltpu.VMEM((taps * LANES, channels), bf16),
+            pltpu.VMEM((2, taps * LANES, channels), bf16),
             pltpu.VMEM((long, taps * LANES), f32),
             pltpu.VMEM((long, LANES), f32),
             pltpu.VMEM((wide, LANES), f32),
@@ -454,10 +468,10 @@
     ]
     grad_kernel, grad_gain = called(
         lambda *refs: collect(order, *refs),
-        (shape_of((rows, channels), f32), shape_of((channels // owners, 1), f32)),
+        (shape_of((rows, channels), f32), shape_of((1, channels // owners), f32)),
         (terms,),
         16,
-        scratch=[pltpu.VMEM((channels, -(-rows // LANES) * LANES), f32)],
+        scratch=[pltpu.VMEM((channels + LANES, -(-rows // LANES) * LANES), f32)],
     )
     grad_kernel, home, *arrived = lax.optimization_barrier((grad_kernel, *arrived))
     combined, grad_input = called(
@@ -468,7 +482,7 @@
         scratch=[pltpu.VMEM((2, ranks, positions, LANES), bf16)],
         specs=[SMEM] + [VMEM] * (4 + len(arrived)),
     )
-    return combined[None], grad_input[None], grad_kernel, grad_gain[:, 0]
+    return combined[None], grad_input[None], grad_kernel, grad_gain[0]
 
 
 def solution(mesh):

time: 86.6 us -> 84.9 us (0.980)
  starting transfers between devices: 25.6 us -> 28.2 us
  waiting for transfers between devices: 34.5 us -> 32.9 us
  Pallas kernels: 22.2 us -> 20.9 us
    ppermute x6, waiting for transfers between devices: 12.5 us -> 10.2 us  [per_device(): lax.ppermute(message, RANK, flipped_pairs(ranks, mask))]
    ppermute x1, starting transfers between devices: 4.5 us -> 6.22 us  [per_device(): both_cores.append(lax.ppermute(crossing, RANK, flipped_pairs(ranks, core)))]
    pallas_call x7, Pallas kernels: 22.2 us -> 20.9 us  [called(): pl.pallas_call(body, out_shape=outs, in_specs=specs or [VMEM] * len(args)...]
  transfers between devices with their start and end apart: 11 -> 11, of which waited for: 5 -> 5; matrix products, arithmetic and copies ran while one was open for 1% -> 0% of each run, Pallas kernels for 5% -> 5%
where the time goes in v14:
time: 84.9 us; the launch traced here: 84.6 us
  waiting for transfers between devices  32.9 us (39%)
  starting transfers between devices  28.2 us (33%)
  Pallas kernels  20.9 us (25%)
  local copies, waits for them, and re-layouts  0.94 us (1%)
  other arithmetic  0.86 us (1%)
    pallas_call x7, Pallas kernels, called(): pl.pallas_call(body, out_shape=outs, in_specs=specs or [VMEM] * len(args)...  20.9 us
    all_to_all x1, waiting for transfers between devices, per_device(): terms = lax.all_to_all(outgoing, EVERY, 0, 0, tiled=True)  13.1 us
    ppermute x6, waiting for transfers between devices, per_device(): lax.ppermute(message, RANK, flipped_pairs(ranks, mask))  10.2 us
    all_to_all x1, starting transfers between devices, per_device(): pieces = lax.all_to_all(slices, EVERY, 0, 0, tiled=True)  8.99 us
    ppermute x6, starting transfers between devices, per_device(): lax.ppermute(message, RANK, flipped_pairs(ranks, mask))  7.95 us
    all_to_all x1, waiting for transfers between devices, per_device(): pieces = lax.all_to_all(slices, EVERY, 0, 0, tiled=True)  6.93 us
    ppermute x1, starting transfers between devices, per_device(): both_cores.append(lax.ppermute(crossing, RANK, flipped_pairs(ranks, core)))  6.22 us
    all_to_all x1, starting transfers between devices, per_device(): terms = lax.all_to_all(outgoing, EVERY, 0, 0, tiled=True)  4.06 us
  transfers between devices with their start and end apart: 11, of which 5 were waited for; matrix products, arithmetic and copies ran while one was open for 0% of the time, Pallas kernels for 5%

profile of v14, /device:TPU:0, one launch (start us, length us, event | category | flops | bytes accessed | tf_op | source)
XLA Modules:
  0.0 84.6 jit_solution(6829053891962011417)
XLA Ops:
  0.6 0.0 copy-start.1
  0.6 0.0 copy-start
  0.7 0.0 copy-start.4
  0.7 0.9 %fusion = bf16[16,1536]{1,0:T(8,128)(2,1)S(1)} fusion(bf16[128,768]{1,0:T(8,128)(2,1)} %bitcast.9, bf16[128,768]{1,0:T(8,128)(2,1)} %bitcast.6, pred[]{:T(512)S(6)} %eq.3), kind=kLoop, calls=%fused_computation.1 | loop fusion | flops 221184 | bytes 442369 | tf_op jit(solution)/shard_map/jit(_where)/select_n | solution.py:369
  1.5 0.7 collective-permute-start
  2.2 0.0 copy-start.3
  2.2 0.9 %copy-done.3 = bf16[120,768]{1,0:T(8,128)(2,1)S(1)} copy-done((bf16[120,768]{1,0:T(8,128)(2,1)S(1)}, bf16[120,768]{1,0:T(8,128)(2,1)}, u32[]{:S(2)}) %copy-start.3) | copy-done | bytes 184344
  3.1 1.1 %shard_map.84 = bf16[32,96,120]{2,1,0:T(8,128)(2,1)} custom-call(bf16[120,768]{1,0:T(8,128)(2,1)S(1)} %copy-done.3), custom_call_target="tpu_custom_call" | custom-call | tf_op jit(solution)/shard_map/pallas_call | solution.py:23
  4.2 0.0 collective-permute-done.refs_3_
  4.2 0.0 copy-done.1
  4.2 0.0 copy-done
  4.2 0.0 copy-done.4
  4.3 2.3 %shard_map.85 = (bf16[144,960]{1,0:T(8,128)(2,1)}, bf16[144,960]{1,0:T(8,128)(2,1)S(1)}, bf16[144,1152]{1,0:T(8,128)(2,1)}, bf16[144,1152]{1,0:T(8,128)(2,1)S(1)}, bf16[144,1152]{1,0:T(8,128)(2,1)S(1)}) custom-call(s32[1]{0:T(128)} %bitcast.refs_0_, bf16[128,768]{1,0:T(8,128)(2,1)S(1)} %bitcast.7, bf16[128,768]{1,0:T(8,128)(2,1)S(1)} %bitcast.10, ...), custom_call_target="tpu_custom_call" | custom-call | tf_op jit(solution)/shard_map/pallas_call | solution.py:23
  6.6 3.0 %collective-permute-start.1 = (bf16[144,1152]{1,0:T(8,128)(2,1)}, bf16[144,1152]{1,0:T(8,128)(2,1)S(1)}, u32[]{:S(2)}, u32[]{:S(2)}) collective-permute-start(bf16[144,1152]{1,0:T(8,128)(2,1)} %get-tuple-element.30), channel_id=1, source_target_pairs={{0,1},{1,0},{2,3},{3,2},{4,5},{5,4},{6,7},{7,6},{8,9},{9,8},{10,11... | collective-permute-start | bytes 995336 | tf_op jit(solution)/shard_map/ppermute | solution.py:406
  9.6 1.5 %collective-permute-start.2 = (bf16[144,1152]{1,0:T(8,128)(2,1)S(1)}, bf16[144,1152]{1,0:T(8,128)(2,1)S(1)}, u32[]{:S(2)}, u32[]{:S(2)}) collective-permute-start(bf16[144,1152]{1,0:T(8,128)(2,1)S(1)} %get-tuple-element.31), channel_id=1, source_target_pairs={{0,4},{1,5},{2,6},{3,7},{4,0},{5,1},{6,2},{7,3},{8,12},{9,13},{10,... | collective-permute-start | bytes 995336 | tf_op jit(solution)/shard_map/ppermute | solution.py:406
  11.1 0.0 collective-permute-start.3
  11.1 9.0 %all-to-all-start = ((bf16[32,96,120]{2,1,0:T(8,128)(2,1)}), bf16[32,96,120]{2,1,0:T(8,128)(2,1)S(1)}, u32[]{:S(2)}, u32[]{:S(2)}) async-start(bf16[32,96,120]{2,1,0:T(8,128)(2,1)} %shard_map.84), calls=%async_computation | async-start | bytes 1572864 | tf_op jit(solution)/shard_map/all_to_all | solution.py:392
  20.1 0.0 collective-permute-done.1.refs_1_.refs_3_
  20.1 0.0 collective-permute-done.2.refs_2_.refs_4_
  20.1 6.3 %collective-permute-done.3.refs_3_.refs_5_ = bf16[144,1152]{1,0:T(8,128)(2,1)S(1)} collective-permute-done((bf16[144,1152]{1,0:T(8,128)(2,1)S(1)}, bf16[144,1152]{1,0:T(8,128)(2,1)S(1)}, u32[]{:S(2)}, u32[]{:S(2)}) %collective-permute-start.3) | collective-permute-done | bytes 331808 | tf_op jit(solution)/shard_map/ppermute | solution.py:406
  26.4 0.0 copy-start.5
  26.4 1.1 %shard_map.86 = bf16[4,144,960]{2,1,0:T(8,128)(2,1)} custom-call(bf16[144,960]{1,0:T(8,128)(2,1)S(1)} %get-tuple-element.33.refs_0_, bf16[144,1152]{1,0:T(8,128)(2,1)S(1)} %collective-permute-done.1.refs_1_.refs_3_, bf16[144,1152]{1,0:T(8,128)(2,1)S(1)} %collective-permute-done.2.refs_2_.refs_4_, bf16[144,1152]{1,0:T(8,128)(2,1)S(1)} %collective-permute-done.3.refs_3_.refs_5_), custom_call_target="tpu_custom_call" | custom-call | tf_op jit(solution)/shard_map/pallas_call | solution.py:23
  27.5 6.2 %collective-permute-start.4 = (bf16[4,144,960]{2,1,0:T(8,128)(2,1)}, bf16[4,144,960]{2,1,0:T(8,128)(2,1)S(1)}, u32[]{:S(2)}, u32[]{:S(2)}) collective-permute-start(bf16[4,144,960]{2,1,0:T(8,128)(2,1)} %shard_map.86), channel_id=1, source_target_pairs={{0,2},{1,3},{2,0},{3,1},{4,6},{5,7},{6,4},{7,5},{8,10},{9,11},{10,... | collective-permute-start | bytes 3317768 | tf_op jit(solution)/shard_map/ppermute | solution.py:412
  33.7 0.0 copy-done.5
  33.8 6.9 %all-to-all-done.refs_1_ = bf16[32,96,120]{2,1,0:T(8,128)(2,1)S(1)} async-done(((bf16[32,96,120]{2,1,0:T(8,128)(2,1)}), bf16[32,96,120]{2,1,0:T(8,128)(2,1)S(1)}, u32[]{:S(2)}, u32[]{:S(2)}) %all-to-all-start) | async-done | bytes 737312 | tf_op jit(solution)/shard_map/all_to_all | solution.py:392
  40.7 0.0 collective-permute-done.4.refs_6_
  40.7 12.5 %shard_map.87 = (bf16[32,96,122]{2,1,0:T(8,128)(2,1)}, bf16[4,128,1024]{2,1,0:T(8,128)(2,1)}, bf16[4,128,1024]{2,1,0:T(8,128)(2,1)}) custom-call(s32[1]{0:T(128)} %bitcast.refs_0_, bf16[32,96,120]{2,1,0:T(8,128)(2,1)S(1)} %all-to-all-done.refs_1_, bf16[144,960]{1,0:T(8,128)(2,1)} %get-tuple-element.29.refs_2_, ...), custom_call_target="tpu_custom_call" | custom-call | tf_op jit(solution)/shard_map/pallas_call | solution.py:23
  53.2 0.0 copy-start.2
  53.2 4.1 %all-to-all-start.1 = ((bf16[32,96,122]{2,1,0:T(8,128)(2,1)}), bf16[32,96,122]{2,1,0:T(8,128)(2,1)S(1)}, u32[]{:S(2)}, u32[]{:S(2)}) async-start(bf16[32,96,122]{2,1,0:T(8,128)(2,1)} %get-tuple-element.34), calls=%async_computation.1 | async-start | bytes 1572864 | tf_op jit(solution)/shard_map/all_to_all | solution.py:448
  57.3 0.3 collective-permute-start.5
  57.6 2.6 %collective-permute-done.5.refs_1_ = bf16[4,128,1024]{2,1,0:T(8,128)(2,1)S(1)} collective-permute-done((bf16[4,128,1024]{2,1,0:T(8,128)(2,1)}, bf16[4,128,1024]{2,1,0:T(8,128)(2,1)S(1)}, u32[]{:S(2)}, u32[]{:S(2)}) %collective-permute-start.5) | collective-permute-done | bytes 1048608 | tf_op jit(solution)/shard_map/ppermute | solution.py:449
  60.2 0.0 copy-done.2
  60.2 1.1 %shard_map.89 = (bf16[128,1152]{1,0:T(8,128)(2,1)S(1)}, bf16[128,1152]{1,0:T(8,128)(2,1)}, bf16[128,1152]{1,0:T(8,128)(2,1)S(1)}, bf16[128,1152]{1,0:T(8,128)(2,1)S(1)}) custom-call(bf16[4,128,1024]{2,1,0:T(8,128)(2,1)S(1)} %copy-done.2, bf16[4,128,1024]{2,1,0:T(8,128)(2,1)S(1)} %collective-permute-done.5.refs_1_), custom_call_target="tpu_custom_call" | custom-call | tf_op jit(solution)/shard_map/pallas_call | solution.py:23
  61.3 1.8 %collective-permute-start.6 = (bf16[128,1152]{1,0:T(8,128)(2,1)}, bf16[128,1152]{1,0:T(8,128)(2,1)S(1)}, u32[]{:S(2)}, u32[]{:S(2)}) collective-permute-start(bf16[128,1152]{1,0:T(8,128)(2,1)} %get-tuple-element.39), channel_id=1, source_target_pairs={{0,1},{1,0},{2,3},{3,2},{4,5},{5,4},{6,7},{7,6},{8,9},{9,8},{10,11... | collective-permute-start | bytes 884744 | tf_op jit(solution)/shard_map/ppermute | solution.py:457
  63.1 1.5 %collective-permute-start.7 = (bf16[128,1152]{1,0:T(8,128)(2,1)S(1)}, bf16[128,1152]{1,0:T(8,128)(2,1)S(1)}, u32[]{:S(2)}, u32[]{:S(2)}) collective-permute-start(bf16[128,1152]{1,0:T(8,128)(2,1)S(1)} %get-tuple-element.40), channel_id=1, source_target_pairs={{0,4},{1,5},{2,6},{3,7},{4,0},{5,1},{6,2},{7,3},{8,12},{9,13},{10,... | collective-permute-start | bytes 884744 | tf_op jit(solution)/shard_map/ppermute | solution.py:457
  64.6 0.3 collective-permute-start.8
  64.8 13.1 %all-to-all-done.1.refs_0_ = bf16[32,96,122]{2,1,0:T(8,128)(2,1)S(1)} async-done(((bf16[32,96,122]{2,1,0:T(8,128)(2,1)}), bf16[32,96,122]{2,1,0:T(8,128)(2,1)S(1)}, u32[]{:S(2)}, u32[]{:S(2)}) %all-to-all-start.1) | async-done | bytes 749600 | tf_op jit(solution)/shard_map/all_to_all | solution.py:448
  77.9 1.0 %shard_map.88 = (f32[120,768]{1,0:T(8,128)}, f32[1,24]{1,0:T(1,128)}) custom-call(bf16[32,96,122]{2,1,0:T(8,128)(2,1)S(1)} %all-to-all-done.1.refs_0_), custom_call_target="tpu_custom_call" | custom-call | tf_op jit(solution)/shard_map/pallas_call | solution.py:23
  78.9 0.0 collective-permute-done.6.refs_5_
  78.9 0.0 collective-permute-done.7.refs_6_
  78.9 3.9 %collective-permute-done.8.refs_7_ = bf16[128,1152]{1,0:T(8,128)(2,1)S(1)} collective-permute-done((bf16[128,1152]{1,0:T(8,128)(2,1)S(1)}, bf16[128,1152]{1,0:T(8,128)(2,1)S(1)}, u32[]{:S(2)}, u32[]{:S(2)}) %collective-permute-start.8) | collective-permute-done | bytes 294944 | tf_op jit(solution)/shard_map/ppermute | solution.py:457
  82.8 1.8 %shard_map.90 = (bf16[128,768]{1,0:T(8,128)(2,1)}, bf16[128,768]{1,0:T(8,128)(2,1)}) custom-call(s32[1]{0:T(128)} %bitcast.refs_0_, bf16[128,768]{1,0:T(8,128)(2,1)S(1)} %bitcast.8, bf16[128,768]{1,0:T(8,128)(2,1)S(1)} %bitcast.11, s32[768]{0:T(1024)S(1)} %copy-done.4, bf16[128,1152]{1,0:T(8,128)(2,1)S(1)} %get-tuple-element.42.refs_4_, ...), custom_call_target="tpu_custom_call" | custom-call | tf_op jit(solution)/shard_map/pallas_call | solution.py:23
  (1 shorter events, 0.0 us)
Async XLA Ops:
  0.6 3.6 %copy-start.1 = (bf16[1,128,768]{2,1,0:T(8,128)(2,1)S(1)}, bf16[1,128,768]{2,1,0:T(8,128)(2,1)}, u32[]{:S(2)}) copy-start(bf16[1,128,768]{2,1,0:T(8,128)(2,1)} %param.6) | copy-start | bytes 589828
  0.6 3.6 %copy-start = (bf16[1,128,768]{2,1,0:T(8,128)(2,1)S(1)}, bf16[1,128,768]{2,1,0:T(8,128)(2,1)}, u32[]{:S(2)}) copy-start(bf16[1,128,768]{2,1,0:T(8,128)(2,1)} %param.5) | copy-start | bytes 589828
  0.7 3.6 %copy-start.4 = (s32[768]{0:T(1024)S(1)}, s32[768]{0:T(1024)}, u32[]{:S(2)}) copy-start(s32[768]{0:T(1024)} %refs_3_.1) | copy-start | bytes 9220
  1.5 2.7 %collective-permute-start = (bf16[16,1536]{1,0:T(8,128)(2,1)S(1)}, bf16[16,1536]{1,0:T(8,128)(2,1)S(1)}, u32[]{:S(2)}, u32[]{:S(2)}) collective-permute-start(bf16[16,1536]{1,0:T(8,128)(2,1)S(1)} %fusion), channel_id=1, source_target_pairs={{6,8},{14,16},{22,24},{8,6},{16,14},{24,22},{7,9},{15,17},{23,25},... | collective-permute-start | bytes 147464 | tf_op jit(solution)/shard_map/ppermute | solution.py:370
  2.2 0.9 %copy-start.3 = (bf16[120,768]{1,0:T(8,128)(2,1)S(1)}, bf16[120,768]{1,0:T(8,128)(2,1)}, u32[]{:S(2)}) copy-start(bf16[120,768]{1,0:T(8,128)(2,1)} %refs_0_.1) | copy-start | bytes 552964
  6.6 13.5 %collective-permute-start.1 = (bf16[144,1152]{1,0:T(8,128)(2,1)}, bf16[144,1152]{1,0:T(8,128)(2,1)S(1)}, u32[]{:S(2)}, u32[]{:S(2)}) collective-permute-start(bf16[144,1152]{1,0:T(8,128)(2,1)} %get-tuple-element.30), channel_id=1, source_target_pairs={{0,1},{1,0},{2,3},{3,2},{4,5},{5,4},{6,7},{7,6},{8,9},{9,8},{10,11... | collective-permute-start | bytes 995336 | tf_op jit(solution)/shard_map/ppermute | solution.py:406
  9.6 10.5 %collective-permute-start.2 = (bf16[144,1152]{1,0:T(8,128)(2,1)S(1)}, bf16[144,1152]{1,0:T(8,128)(2,1)S(1)}, u32[]{:S(2)}, u32[]{:S(2)}) collective-permute-start(bf16[144,1152]{1,0:T(8,128)(2,1)S(1)} %get-tuple-element.31), channel_id=1, source_target_pairs={{0,4},{1,5},{2,6},{3,7},{4,0},{5,1},{6,2},{7,3},{8,12},{9,13},{10,... | collective-permute-start | bytes 995336 | tf_op jit(solution)/shard_map/ppermute | solution.py:406
  11.1 15.4 %collective-permute-start.3 = (bf16[144,1152]{1,0:T(8,128)(2,1)S(1)}, bf16[144,1152]{1,0:T(8,128)(2,1)S(1)}, u32[]{:S(2)}, u32[]{:S(2)}) collective-permute-start(bf16[144,1152]{1,0:T(8,128)(2,1)S(1)} %get-tuple-element.32), channel_id=1, source_target_pairs={{0,5},{1,4},{2,7},{3,6},{4,1},{5,0},{6,3},{7,2},{8,13},{9,12},{10,... | collective-permute-start | bytes 995336 | tf_op jit(solution)/shard_map/ppermute | solution.py:406
  11.1 29.6 %all-to-all-start = ((bf16[32,96,120]{2,1,0:T(8,128)(2,1)}), bf16[32,96,120]{2,1,0:T(8,128)(2,1)S(1)}, u32[]{:S(2)}, u32[]{:S(2)}) async-start(bf16[32,96,120]{2,1,0:T(8,128)(2,1)} %shard_map.84), calls=%async_computation | async-start | bytes 1572864 | tf_op jit(solution)/shard_map/all_to_all | solution.py:392
  26.4 7.3 %copy-start.5 = (f32[768]{0:T(1024)S(1)}, f32[768]{0:T(1024)}, u32[]{:S(2)}) copy-start(f32[768]{0:T(1024)} %param.8) | copy-start | bytes 9220
  27.5 13.2 %collective-permute-start.4 = (bf16[4,144,960]{2,1,0:T(8,128)(2,1)}, bf16[4,144,960]{2,1,0:T(8,128)(2,1)S(1)}, u32[]{:S(2)}, u32[]{:S(2)}) collective-permute-start(bf16[4,144,960]{2,1,0:T(8,128)(2,1)} %shard_map.86), channel_id=1, source_target_pairs={{0,2},{1,3},{2,0},{3,1},{4,6},{5,7},{6,4},{7,5},{8,10},{9,11},{10,... | collective-permute-start | bytes 3317768 | tf_op jit(solution)/shard_map/ppermute | solution.py:412
  53.2 7.0 %copy-start.2 = (bf16[4,128,1024]{2,1,0:T(8,128)(2,1)S(1)}, bf16[4,128,1024]{2,1,0:T(8,128)(2,1)}, u32[]{:S(2)}) copy-start(bf16[4,128,1024]{2,1,0:T(8,128)(2,1)} %get-tuple-element.36.refs_0_) | copy-start | bytes 3145732
  53.2 24.7 %all-to-all-start.1 = ((bf16[32,96,122]{2,1,0:T(8,128)(2,1)}), bf16[32,96,122]{2,1,0:T(8,128)(2,1)S(1)}, u32[]{:S(2)}, u32[]{:S(2)}) async-start(bf16[32,96,122]{2,1,0:T(8,128)(2,1)} %get-tuple-element.34), calls=%async_computation.1 | async-start | bytes 1572864 | tf_op jit(solution)/shard_map/all_to_all | solution.py:448
  57.3 2.9 %collective-permute-start.5 = (bf16[4,128,1024]{2,1,0:T(8,128)(2,1)}, bf16[4,128,1024]{2,1,0:T(8,128)(2,1)S(1)}, u32[]{:S(2)}, u32[]{:S(2)}) collective-permute-start(bf16[4,128,1024]{2,1,0:T(8,128)(2,1)} %get-tuple-element.37), channel_id=1, source_target_pairs={{0,2},{1,3},{2,0},{3,1},{4,6},{5,7},{6,4},{7,5},{8,10},{9,11},{10,... | collective-permute-start | bytes 3145736 | tf_op jit(solution)/shard_map/ppermute | solution.py:449
  61.3 17.6 %collective-permute-start.6 = (bf16[128,1152]{1,0:T(8,128)(2,1)}, bf16[128,1152]{1,0:T(8,128)(2,1)S(1)}, u32[]{:S(2)}, u32[]{:S(2)}) collective-permute-start(bf16[128,1152]{1,0:T(8,128)(2,1)} %get-tuple-element.39), channel_id=1, source_target_pairs={{0,1},{1,0},{2,3},{3,2},{4,5},{5,4},{6,7},{7,6},{8,9},{9,8},{10,11... | collective-permute-start | bytes 884744 | tf_op jit(solution)/shard_map/ppermute | solution.py:457
  63.1 15.8 %collective-permute-start.7 = (bf16[128,1152]{1,0:T(8,128)(2,1)S(1)}, bf16[128,1152]{1,0:T(8,128)(2,1)S(1)}, u32[]{:S(2)}, u32[]{:S(2)}) collective-permute-start(bf16[128,1152]{1,0:T(8,128)(2,1)S(1)} %get-tuple-element.40), channel_id=1, source_target_pairs={{0,4},{1,5},{2,6},{3,7},{4,0},{5,1},{6,2},{7,3},{8,12},{9,13},{10,... | collective-permute-start | bytes 884744 | tf_op jit(solution)/shard_map/ppermute | solution.py:457
  64.6 18.2 %collective-permute-start.8 = (bf16[128,1152]{1,0:T(8,128)(2,1)S(1)}, bf16[128,1152]{1,0:T(8,128)(2,1)S(1)}, u32[]{:S(2)}, u32[]{:S(2)}) collective-permute-start(bf16[128,1152]{1,0:T(8,128)(2,1)S(1)} %get-tuple-element.41), channel_id=1, source_target_pairs={{0,5},{1,4},{2,7},{3,6},{4,1},{5,0},{6,3},{7,2},{8,13},{9,12},{10,... | collective-permute-start | bytes 884744 | tf_op jit(solution)/shard_map/ppermute | solution.py:457

commit v15 on v14

--- a/solution.py
+++ b/solution.py
@@ -49,15 +49,6 @@
     return x * half_sum, slope
 
 
-def slot_maps(part, slots, pairing):
-    shape = (slots, pairing.shape[1])
-    slot = lax.broadcasted_iota(jnp.int32, shape, 0)
-    lane = lax.bitwise_and(slot, LANES - 1)
-    channel_of = jnp.where(lane < part, lax.div(slot, LANES) * part + lane, -1)
-    channel = lax.broadcasted_iota(jnp.int32, shape, 1)
-    return [jnp.where(channel_of == c, 1.0, 0.0).astype(bf16) for c in (channel, pairing)]
-
-
 def swap_map(pairing):
     channels = pairing.shape[1]
     row = lax.broadcasted_iota(jnp.int32, (channels, channels), 0)
@@ -65,7 +56,8 @@
 
 
 def chip_masks(ranks, core):
-    return [mask for mask in range(ranks) if not mask & core]
+    masks = [mask for mask in range(ranks) if not mask & core]
+    return masks[:1] + sorted(masks[1:], key=lambda mask: -mask.bit_count())
 
 
 class Moves:
@@ -111,17 +103,15 @@
         for offset in offsets
     ]
     maps = jnp.concatenate(maps, 0)
-    for rows, kept, cot in (
-        (slice(0, positions), values_ref[...], cot_ref[...]),
-        (slice(positions, None), edge_ref[:, :channels], edge_ref[:, channels:]),
-    ):
-        slices = dot(cot, maps, ((1,), (1,))).astype(bf16)
-        lane = 0
-        for out in (*leaving, home_ref, cross_ref):
-            count = out.shape[1] - channels
-            out[rows, :channels] = kept
-            out[rows, channels:] = slices[:, lane : lane + count]
-            lane += count
+    cot = jnp.concatenate([cot_ref[...], edge_ref[:, channels:]], 0)
+    slices = dot(cot, maps, ((1,), (1,))).astype(bf16)
+    lane = 0
+    for out in (*leaving, home_ref, cross_ref):
+        count = out.shape[1] - channels
+        out[:positions, :channels] = values_ref[...]
+        out[positions:, :channels] = edge_ref[:, :channels]
+        out[:, channels:] = slices[:, lane : lane + count]
+        lane += count
 
 
 def stack_crossing(*refs):
@@ -300,7 +290,6 @@
     arrived, (combined_ref, grad_ref, gelus) = refs[:-3], refs[-3:]
     channels = values_ref.shape[1]
     ranks = gelus.shape[1]
-    gelus[...] = jnp.zeros_like(gelus)
     scaled = jnp.zeros(values_ref.shape, f32)
     for mask, block in zip(chip_masks(ranks, core), arrived):
         scaled += block[:, :channels].astype(f32)
@@ -308,10 +297,10 @@
             source = lax.bitwise_xor(rank_ref[0], mask | c * core)
             for n in range(2):
                 start = channels + (2 * c + n) * part
-                gelus[n, source, :, :part] = block[:, start : start + part]
-    joined = [jnp.concatenate([gelus[n, j] for j in range(ranks)], -1) for n in range(2)]
-    maps = slot_maps(part, ranks * LANES, pairing_ref[...].reshape(1, -1))
-    plain, other = [dot(j, m, ((1,), (0,))) for j, m in zip(joined, maps)]
+                gelus[n, source] = block[:, start : start + part]
+    plain, other = [jnp.concatenate([gelus[n, j] for j in range(ranks)], -1) for n in range(2)]
+    plain = plain.astype(f32)
+    other = dot(other, swap_map(pairing_ref[...].reshape(1, -1)), ((1,), (0,)))
     values = values_ref[...].astype(f32)
     rms = lax.rsqrt(jnp.mean(values * values, -1, keepdims=True) + epsilon)
     reverse_out = (values + other).astype(bf16).astype(f32)
@@ -479,7 +468,7 @@
         (shape_of((positions, channels), bf16), shape_of((positions, channels), bf16)),
         (rank, values, cot, pairing, home, *arrived),
         16,
-        scratch=[pltpu.VMEM((2, ranks, positions, LANES), bf16)],
+        scratch=[pltpu.VMEM((2, ranks, positions, part), bf16)],
         specs=[SMEM] + [VMEM] * (4 + len(arrived)),
     )
     return combined[None], grad_input[None], grad_kernel, grad_gain[0]

time: 84.9 us -> 84.1 us (level)
  starting transfers between devices: 28.2 us -> 24 us
  waiting for transfers between devices: 32.9 us -> 37 us
    ppermute x1, starting transfers between devices: 6.22 us -> 2.47 us  [per_device(): both_cores.append(lax.ppermute(crossing, RANK, flipped_pairs(ranks, core)))]
    ppermute x6, waiting for transfers between devices: 10.2 us -> 13.4 us  [per_device(): lax.ppermute(message, RANK, flipped_pairs(ranks, mask))]
    all_to_all x1, waiting for transfers between devices: 6.93 us -> 7.9 us  [per_device(): pieces = lax.all_to_all(slices, EVERY, 0, 0, tiled=True)]
  transfers between devices with their start and end apart: 11 -> 11, of which waited for: 5 -> 6; matrix products, arithmetic and copies ran while one was open for 0% -> 0% of each run, Pallas kernels for 5% -> 5%
where the time goes in v15:
time: 84.1 us; the launch traced here: 83.7 us
  waiting for transfers between devices  37 us (44%)
  starting transfers between devices  24 us (29%)
  Pallas kernels  20.2 us (24%)
  local copies, waits for them, and re-layouts  0.94 us (1%)
  other arithmetic  0.86 us (1%)
    pallas_call x7, Pallas kernels, called(): pl.pallas_call(body, out_shape=outs, in_specs=specs or [VMEM] * len(args)...  20.2 us
    ppermute x6, waiting for transfers between devices, per_device(): lax.ppermute(message, RANK, flipped_pairs(ranks, mask))  13.4 us
    all_to_all x1, waiting for transfers between devices, per_device(): terms = lax.all_to_all(outgoing, EVERY, 0, 0, tiled=True)  13.1 us
    all_to_all x1, starting transfers between devices, per_device(): pieces = lax.all_to_all(slices, EVERY, 0, 0, tiled=True)  8.99 us
    ppermute x6, starting transfers between devices, per_device(): lax.ppermute(message, RANK, flipped_pairs(ranks, mask))  7.96 us
    all_to_all x1, waiting for transfers between devices, per_device(): pieces = lax.all_to_all(slices, EVERY, 0, 0, tiled=True)  7.9 us
    all_to_all x1, starting transfers between devices, per_device(): terms = lax.all_to_all(outgoing, EVERY, 0, 0, tiled=True)  3.62 us
    ppermute x1, waiting for transfers between devices, per_device(): crossed = lax.ppermute(cross, RANK, flipped_pairs(ranks, core))  2.62 us
  transfers between devices with their start and end apart: 11, of which 6 were waited for; matrix products, arithmetic and copies ran while one was open for 0% of the time, Pallas kernels for 5%

profile of v15, /device:TPU:0, one launch (start us, length us, event | category | flops | bytes accessed | tf_op | source)
XLA Modules:
  0.0 83.7 jit_solution(10858022537276980801)
XLA Ops:
  0.6 0.0 copy-start.1
  0.6 0.0 copy-start
  0.7 0.0 copy-start.4
  0.7 0.9 %fusion = bf16[16,1536]{1,0:T(8,128)(2,1)S(1)} fusion(bf16[128,768]{1,0:T(8,128)(2,1)} %bitcast.9, bf16[128,768]{1,0:T(8,128)(2,1)} %bitcast.6, pred[]{:T(512)S(6)} %eq.3), kind=kLoop, calls=%fused_computation.1 | loop fusion | flops 221184 | bytes 442369 | tf_op jit(solution)/shard_map/jit(_where)/select_n | solution.py:358
  1.5 0.7 collective-permute-start
  2.2 0.0 copy-start.3
  2.2 0.9 %copy-done.3 = bf16[120,768]{1,0:T(8,128)(2,1)S(1)} copy-done((bf16[120,768]{1,0:T(8,128)(2,1)S(1)}, bf16[120,768]{1,0:T(8,128)(2,1)}, u32[]{:S(2)}) %copy-start.3) | copy-done | bytes 184344
  3.1 1.1 %shard_map.84 = bf16[32,96,120]{2,1,0:T(8,128)(2,1)} custom-call(bf16[120,768]{1,0:T(8,128)(2,1)S(1)} %copy-done.3), custom_call_target="tpu_custom_call" | custom-call | tf_op jit(solution)/shard_map/pallas_call | solution.py:23
  4.2 0.0 collective-permute-done.refs_3_
  4.2 0.0 copy-done.1
  4.2 0.0 copy-done
  4.2 0.0 copy-done.4
  4.3 1.8 %shard_map.85 = (bf16[144,960]{1,0:T(8,128)(2,1)}, bf16[144,960]{1,0:T(8,128)(2,1)S(1)}, bf16[144,1152]{1,0:T(8,128)(2,1)}, bf16[144,1152]{1,0:T(8,128)(2,1)S(1)}, bf16[144,1152]{1,0:T(8,128)(2,1)S(1)}) custom-call(s32[1]{0:T(128)} %bitcast.refs_0_, bf16[128,768]{1,0:T(8,128)(2,1)S(1)} %bitcast.7, bf16[128,768]{1,0:T(8,128)(2,1)S(1)} %bitcast.10, ...), custom_call_target="tpu_custom_call" | custom-call | tf_op jit(solution)/shard_map/pallas_call | solution.py:23
  6.1 3.9 %collective-permute-start.1 = (bf16[144,1152]{1,0:T(8,128)(2,1)}, bf16[144,1152]{1,0:T(8,128)(2,1)S(1)}, u32[]{:S(2)}, u32[]{:S(2)}) collective-permute-start(bf16[144,1152]{1,0:T(8,128)(2,1)} %get-tuple-element.30), channel_id=1, source_target_pairs={{0,5},{1,4},{2,7},{3,6},{4,1},{5,0},{6,3},{7,2},{8,13},{9,12},{10,... | collective-permute-start | bytes 995336 | tf_op jit(solution)/shard_map/ppermute | solution.py:395
  10.0 0.5 collective-permute-start.2
  10.5 0.1 collective-permute-start.3
  10.5 9.0 %all-to-all-start = ((bf16[32,96,120]{2,1,0:T(8,128)(2,1)}), bf16[32,96,120]{2,1,0:T(8,128)(2,1)S(1)}, u32[]{:S(2)}, u32[]{:S(2)}) async-start(bf16[32,96,120]{2,1,0:T(8,128)(2,1)} %shard_map.84), calls=%async_computation | async-start | bytes 1572864 | tf_op jit(solution)/shard_map/all_to_all | solution.py:381
  19.5 0.0 collective-permute-done.1.refs_1_.refs_3_
  19.5 9.1 %collective-permute-done.2.refs_2_.refs_4_ = bf16[144,1152]{1,0:T(8,128)(2,1)S(1)} collective-permute-done((bf16[144,1152]{1,0:T(8,128)(2,1)S(1)}, bf16[144,1152]{1,0:T(8,128)(2,1)S(1)}, u32[]{:S(2)}, u32[]{:S(2)}) %collective-permute-start.2) | collective-permute-done | bytes 331808 | tf_op jit(solution)/shard_map/ppermute | solution.py:395
  28.7 0.0 collective-permute-done.3.refs_3_.refs_5_
  28.7 0.0 copy-start.5
  28.7 1.1 %shard_map.86 = bf16[4,144,960]{2,1,0:T(8,128)(2,1)} custom-call(bf16[144,960]{1,0:T(8,128)(2,1)S(1)} %get-tuple-element.33.refs_0_, bf16[144,1152]{1,0:T(8,128)(2,1)S(1)} %collective-permute-done.1.refs_1_.refs_3_, bf16[144,1152]{1,0:T(8,128)(2,1)S(1)} %collective-permute-done.2.refs_2_.refs_4_, bf16[144,1152]{1,0:T(8,128)(2,1)S(1)} %collective-permute-done.3.refs_3_.refs_5_), custom_call_target="tpu_custom_call" | custom-call | tf_op jit(solution)/shard_map/pallas_call | solution.py:23
  29.8 2.5 %collective-permute-start.4 = (bf16[4,144,960]{2,1,0:T(8,128)(2,1)}, bf16[4,144,960]{2,1,0:T(8,128)(2,1)S(1)}, u32[]{:S(2)}, u32[]{:S(2)}) collective-permute-start(bf16[4,144,960]{2,1,0:T(8,128)(2,1)} %shard_map.86), channel_id=1, source_target_pairs={{0,2},{1,3},{2,0},{3,1},{4,6},{5,7},{6,4},{7,5},{8,10},{9,11},{10,... | collective-permute-start | bytes 3317768 | tf_op jit(solution)/shard_map/ppermute | solution.py:401
  32.2 0.0 copy-done.5
  32.2 7.9 %all-to-all-done.refs_1_ = bf16[32,96,120]{2,1,0:T(8,128)(2,1)S(1)} async-done(((bf16[32,96,120]{2,1,0:T(8,128)(2,1)}), bf16[32,96,120]{2,1,0:T(8,128)(2,1)S(1)}, u32[]{:S(2)}, u32[]{:S(2)}) %all-to-all-start) | async-done | bytes 737312 | tf_op jit(solution)/shard_map/all_to_all | solution.py:381
  40.1 0.0 collective-permute-done.4.refs_6_
  40.1 12.5 %shard_map.87 = (bf16[32,96,122]{2,1,0:T(8,128)(2,1)}, bf16[4,128,1024]{2,1,0:T(8,128)(2,1)}, bf16[4,128,1024]{2,1,0:T(8,128)(2,1)}) custom-call(s32[1]{0:T(128)} %bitcast.refs_0_, bf16[32,96,120]{2,1,0:T(8,128)(2,1)S(1)} %all-to-all-done.refs_1_, bf16[144,960]{1,0:T(8,128)(2,1)} %get-tuple-element.29.refs_2_, ...), custom_call_target="tpu_custom_call" | custom-call | tf_op jit(solution)/shard_map/pallas_call | solution.py:23
  52.7 0.0 copy-start.2
  52.7 3.6 %all-to-all-start.1 = ((bf16[32,96,122]{2,1,0:T(8,128)(2,1)}), bf16[32,96,122]{2,1,0:T(8,128)(2,1)S(1)}, u32[]{:S(2)}, u32[]{:S(2)}) async-start(bf16[32,96,122]{2,1,0:T(8,128)(2,1)} %get-tuple-element.34), calls=%async_computation.1 | async-start | bytes 1572864 | tf_op jit(solution)/shard_map/all_to_all | solution.py:437
  56.3 0.3 collective-permute-start.5
  56.7 2.6 %collective-permute-done.5.refs_1_ = bf16[4,128,1024]{2,1,0:T(8,128)(2,1)S(1)} collective-permute-done((bf16[4,128,1024]{2,1,0:T(8,128)(2,1)}, bf16[4,128,1024]{2,1,0:T(8,128)(2,1)S(1)}, u32[]{:S(2)}, u32[]{:S(2)}) %collective-permute-start.5) | collective-permute-done | bytes 1048608 | tf_op jit(solution)/shard_map/ppermute | solution.py:438
  59.3 0.0 copy-done.2
  59.3 1.1 %shard_map.89 = (bf16[128,1152]{1,0:T(8,128)(2,1)S(1)}, bf16[128,1152]{1,0:T(8,128)(2,1)}, bf16[128,1152]{1,0:T(8,128)(2,1)S(1)}, bf16[128,1152]{1,0:T(8,128)(2,1)S(1)}) custom-call(bf16[4,128,1024]{2,1,0:T(8,128)(2,1)S(1)} %copy-done.2, bf16[4,128,1024]{2,1,0:T(8,128)(2,1)S(1)} %collective-permute-done.5.refs_1_), custom_call_target="tpu_custom_call" | custom-call | tf_op jit(solution)/shard_map/pallas_call | solution.py:23
  60.4 2.7 %collective-permute-start.6 = (bf16[128,1152]{1,0:T(8,128)(2,1)}, bf16[128,1152]{1,0:T(8,128)(2,1)S(1)}, u32[]{:S(2)}, u32[]{:S(2)}) collective-permute-start(bf16[128,1152]{1,0:T(8,128)(2,1)} %get-tuple-element.39), channel_id=1, source_target_pairs={{0,5},{1,4},{2,7},{3,6},{4,1},{5,0},{6,3},{7,2},{8,13},{9,12},{10,... | collective-permute-start | bytes 884744 | tf_op jit(solution)/shard_map/ppermute | solution.py:446
  63.0 0.6 collective-permute-start.7
  63.6 0.3 collective-permute-start.8
  63.9 13.1 %all-to-all-done.1.refs_0_ = bf16[32,96,122]{2,1,0:T(8,128)(2,1)S(1)} async-done(((bf16[32,96,122]{2,1,0:T(8,128)(2,1)}), bf16[32,96,122]{2,1,0:T(8,128)(2,1)S(1)}, u32[]{:S(2)}, u32[]{:S(2)}) %all-to-all-start.1) | async-done | bytes 749600 | tf_op jit(solution)/shard_map/all_to_all | solution.py:437
  77.0 1.0 %shard_map.88 = (f32[120,768]{1,0:T(8,128)}, f32[1,24]{1,0:T(1,128)}) custom-call(bf16[32,96,122]{2,1,0:T(8,128)(2,1)S(1)} %all-to-all-done.1.refs_0_), custom_call_target="tpu_custom_call" | custom-call | tf_op jit(solution)/shard_map/pallas_call | solution.py:23
  77.9 0.0 collective-permute-done.6.refs_5_
  77.9 3.9 %collective-permute-done.7.refs_6_ = bf16[128,1152]{1,0:T(8,128)(2,1)S(1)} collective-permute-done((bf16[128,1152]{1,0:T(8,128)(2,1)S(1)}, bf16[128,1152]{1,0:T(8,128)(2,1)S(1)}, u32[]{:S(2)}, u32[]{:S(2)}) %collective-permute-start.7) | collective-permute-done | bytes 294944 | tf_op jit(solution)/shard_map/ppermute | solution.py:446
  81.8 0.4 collective-permute-done.8.refs_7_
  82.2 1.6 %shard_map.90 = (bf16[128,768]{1,0:T(8,128)(2,1)}, bf16[128,768]{1,0:T(8,128)(2,1)}) custom-call(s32[1]{0:T(128)} %bitcast.refs_0_, bf16[128,768]{1,0:T(8,128)(2,1)S(1)} %bitcast.8, bf16[128,768]{1,0:T(8,128)(2,1)S(1)} %bitcast.11, s32[768]{0:T(1024)S(1)} %copy-done.4, bf16[128,1152]{1,0:T(8,128)(2,1)S(1)} %get-tuple-element.42.refs_4_, ...), custom_call_target="tpu_custom_call" | custom-call | tf_op jit(solution)/shard_map/pallas_call | solution.py:23
  (1 shorter events, 0.0 us)
Async XLA Ops:
  0.6 3.6 %copy-start.1 = (bf16[1,128,768]{2,1,0:T(8,128)(2,1)S(1)}, bf16[1,128,768]{2,1,0:T(8,128)(2,1)}, u32[]{:S(2)}) copy-start(bf16[1,128,768]{2,1,0:T(8,128)(2,1)} %param.6) | copy-start | bytes 589828
  0.6 3.6 %copy-start = (bf16[1,128,768]{2,1,0:T(8,128)(2,1)S(1)}, bf16[1,128,768]{2,1,0:T(8,128)(2,1)}, u32[]{:S(2)}) copy-start(bf16[1,128,768]{2,1,0:T(8,128)(2,1)} %param.5) | copy-start | bytes 589828
  0.7 3.6 %copy-start.4 = (s32[768]{0:T(1024)S(1)}, s32[768]{0:T(1024)}, u32[]{:S(2)}) copy-start(s32[768]{0:T(1024)} %refs_3_.1) | copy-start | bytes 9220
  1.5 2.7 %collective-permute-start = (bf16[16,1536]{1,0:T(8,128)(2,1)S(1)}, bf16[16,1536]{1,0:T(8,128)(2,1)S(1)}, u32[]{:S(2)}, u32[]{:S(2)}) collective-permute-start(bf16[16,1536]{1,0:T(8,128)(2,1)S(1)} %fusion), channel_id=1, source_target_pairs={{6,8},{14,16},{22,24},{8,6},{16,14},{24,22},{7,9},{15,17},{23,25},... | collective-permute-start | bytes 147464 | tf_op jit(solution)/shard_map/ppermute | solution.py:359
  2.2 0.9 %copy-start.3 = (bf16[120,768]{1,0:T(8,128)(2,1)S(1)}, bf16[120,768]{1,0:T(8,128)(2,1)}, u32[]{:S(2)}) copy-start(bf16[120,768]{1,0:T(8,128)(2,1)} %refs_0_.1) | copy-start | bytes 552964
  6.1 13.5 %collective-permute-start.1 = (bf16[144,1152]{1,0:T(8,128)(2,1)}, bf16[144,1152]{1,0:T(8,128)(2,1)S(1)}, u32[]{:S(2)}, u32[]{:S(2)}) collective-permute-start(bf16[144,1152]{1,0:T(8,128)(2,1)} %get-tuple-element.30), channel_id=1, source_target_pairs={{0,5},{1,4},{2,7},{3,6},{4,1},{5,0},{6,3},{7,2},{8,13},{9,12},{10,... | collective-permute-start | bytes 995336 | tf_op jit(solution)/shard_map/ppermute | solution.py:395
  10.0 18.7 %collective-permute-start.2 = (bf16[144,1152]{1,0:T(8,128)(2,1)S(1)}, bf16[144,1152]{1,0:T(8,128)(2,1)S(1)}, u32[]{:S(2)}, u32[]{:S(2)}) collective-permute-start(bf16[144,1152]{1,0:T(8,128)(2,1)S(1)} %get-tuple-element.31), channel_id=1, source_target_pairs={{0,1},{1,0},{2,3},{3,2},{4,5},{5,4},{6,7},{7,6},{8,9},{9,8},{10,11... | collective-permute-start | bytes 995336 | tf_op jit(solution)/shard_map/ppermute | solution.py:395
  10.5 18.2 %collective-permute-start.3 = (bf16[144,1152]{1,0:T(8,128)(2,1)S(1)}, bf16[144,1152]{1,0:T(8,128)(2,1)S(1)}, u32[]{:S(2)}, u32[]{:S(2)}) collective-permute-start(bf16[144,1152]{1,0:T(8,128)(2,1)S(1)} %get-tuple-element.32), channel_id=1, source_target_pairs={{0,4},{1,5},{2,6},{3,7},{4,0},{5,1},{6,2},{7,3},{8,12},{9,13},{10,... | collective-permute-start | bytes 995336 | tf_op jit(solution)/shard_map/ppermute | solution.py:395
  10.5 29.6 %all-to-all-start = ((bf16[32,96,120]{2,1,0:T(8,128)(2,1)}), bf16[32,96,120]{2,1,0:T(8,128)(2,1)S(1)}, u32[]{:S(2)}, u32[]{:S(2)}) async-start(bf16[32,96,120]{2,1,0:T(8,128)(2,1)} %shard_map.84), calls=%async_computation | async-start | bytes 1572864 | tf_op jit(solution)/shard_map/all_to_all | solution.py:381
  28.7 3.6 %copy-start.5 = (f32[768]{0:T(1024)S(1)}, f32[768]{0:T(1024)}, u32[]{:S(2)}) copy-start(f32[768]{0:T(1024)} %param.8) | copy-start | bytes 9220
  29.8 10.4 %collective-permute-start.4 = (bf16[4,144,960]{2,1,0:T(8,128)(2,1)}, bf16[4,144,960]{2,1,0:T(8,128)(2,1)S(1)}, u32[]{:S(2)}, u32[]{:S(2)}) collective-permute-start(bf16[4,144,960]{2,1,0:T(8,128)(2,1)} %shard_map.86), channel_id=1, source_target_pairs={{0,2},{1,3},{2,0},{3,1},{4,6},{5,7},{6,4},{7,5},{8,10},{9,11},{10,... | collective-permute-start | bytes 3317768 | tf_op jit(solution)/shard_map/ppermute | solution.py:401
  52.7 6.6 %copy-start.2 = (bf16[4,128,1024]{2,1,0:T(8,128)(2,1)S(1)}, bf16[4,128,1024]{2,1,0:T(8,128)(2,1)}, u32[]{:S(2)}) copy-start(bf16[4,128,1024]{2,1,0:T(8,128)(2,1)} %get-tuple-element.36.refs_0_) | copy-start | bytes 3145732
  52.7 24.3 %all-to-all-start.1 = ((bf16[32,96,122]{2,1,0:T(8,128)(2,1)}), bf16[32,96,122]{2,1,0:T(8,128)(2,1)S(1)}, u32[]{:S(2)}, u32[]{:S(2)}) async-start(bf16[32,96,122]{2,1,0:T(8,128)(2,1)} %get-tuple-element.34), calls=%async_computation.1 | async-start | bytes 1572864 | tf_op jit(solution)/shard_map/all_to_all | solution.py:437
  56.3 2.9 %collective-permute-start.5 = (bf16[4,128,1024]{2,1,0:T(8,128)(2,1)}, bf16[4,128,1024]{2,1,0:T(8,128)(2,1)S(1)}, u32[]{:S(2)}, u32[]{:S(2)}) collective-permute-start(bf16[4,128,1024]{2,1,0:T(8,128)(2,1)} %get-tuple-element.37), channel_id=1, source_target_pairs={{0,2},{1,3},{2,0},{3,1},{4,6},{5,7},{6,4},{7,5},{8,10},{9,11},{10,... | collective-permute-start | bytes 3145736 | tf_op jit(solution)/shard_map/ppermute | solution.py:438
  60.4 17.6 %collective-permute-start.6 = (bf16[128,1152]{1,0:T(8,128)(2,1)}, bf16[128,1152]{1,0:T(8,128)(2,1)S(1)}, u32[]{:S(2)}, u32[]{:S(2)}) collective-permute-start(bf16[128,1152]{1,0:T(8,128)(2,1)} %get-tuple-element.39), channel_id=1, source_target_pairs={{0,5},{1,4},{2,7},{3,6},{4,1},{5,0},{6,3},{7,2},{8,13},{9,12},{10,... | collective-permute-start | bytes 884744 | tf_op jit(solution)/shard_map/ppermute | solution.py:446
  63.0 18.8 %collective-permute-start.7 = (bf16[128,1152]{1,0:T(8,128)(2,1)S(1)}, bf16[128,1152]{1,0:T(8,128)(2,1)S(1)}, u32[]{:S(2)}, u32[]{:S(2)}) collective-permute-start(bf16[128,1152]{1,0:T(8,128)(2,1)S(1)} %get-tuple-element.40), channel_id=1, source_target_pairs={{0,1},{1,0},{2,3},{3,2},{4,5},{5,4},{6,7},{7,6},{8,9},{9,8},{10,11... | collective-permute-start | bytes 884744 | tf_op jit(solution)/shard_map/ppermute | solution.py:446
  63.6 18.6 %collective-permute-start.8 = (bf16[128,1152]{1,0:T(8,128)(2,1)S(1)}, bf16[128,1152]{1,0:T(8,128)(2,1)S(1)}, u32[]{:S(2)}, u32[]{:S(2)}) collective-permute-start(bf16[128,1152]{1,0:T(8,128)(2,1)S(1)} %get-tuple-element.41), channel_id=1, source_target_pairs={{0,4},{1,5},{2,6},{3,7},{4,0},{5,1},{6,2},{7,3},{8,12},{9,13},{10,... | collective-permute-start | bytes 884744 | tf_op jit(solution)/shard_map/ppermute | solution.py:446

commit v16 on v15

--- a/solution.py
+++ b/solution.py
@@ -152,8 +152,7 @@
     got_blocks += [moves.start(block, arrived.at[m]) for m, block in enumerate(arrived_in)]
     per = chips // groups
     got_blocks += [moves.start(crossed_in[m // per].at[m % per], crossed.at[m]) for m in range(chips)]
-    got_pieces = moves.start(pieces_in, pieces)
-    arrivals = len(moves.copies)
+    got_pieces = None
     masks = chip_masks(2 * chips, core)
     seq_ranks = 2 * chips // dp_ranks
     positions = home.shape[0] - HALO
@@ -165,6 +164,8 @@
     blocks += [(mask | core, crossed.at[m], channels) for m, mask in enumerate(masks)]
     for got, (flip, ref, lane) in zip(got_blocks, blocks):
         got.wait()
+        if got is got_blocks[1]:
+            got_pieces = moves.start(pieces_in, pieces)
         source = lax.bitwise_xor(rank_ref[0], flip)
         b, i = lax.rem(source, dp_ranks), lax.div(source, dp_ranks)
         start = pl.multiple_of(i * positions, positions)
@@ -193,6 +194,7 @@
             first += count
 
     got_pieces.wait()
+    arrivals = len(moves.copies)
     for owner in range(owners):
         for tap, channel, count, offset in runs(owner):
             kernel_ref[tap * part : (tap + 1) * part, channel : channel + count] = pieces[
@@ -259,8 +261,9 @@
             dot(shifted_ref[b], kernels[0], ((1,), (0,))) * gains[0]
             + dot(shifted_ref[dp_ranks + b], kernels[1], ((1,), (0,))) * gains[1]
         ).astype(bf16)
+    order = [*range(1, chips), 0]
     for out, target_out, flip in ((cross, cross_out, core), (own, own_out, 0)):
-        for m, mask in enumerate(masks):
+        for m, mask in [(m, masks[m]) for m in order]:
             target = lax.bitwise_xor(rank_ref[0], mask | flip)
             b = lax.rem(target, dp_ranks)
             start = pl.multiple_of(lax.div(target, dp_ranks) * positions, positions)
@@ -268,18 +271,23 @@
             for n in range(2):
                 lane = channels + n * LANES
                 out[m, :, lane : lane + LANES] = gelu_ref[n * dp_ranks + b, pl.ds(start, positions), :]
-        moves.start(out, target_out)
+            moves.start(out.at[m], target_out.at[m])
     for copy in moves.copies[arrivals:]:
         copy.wait()
 
 
-def chip_sum(part, own_ref, crossed_ref, *outs):
-    channels = own_ref.shape[2] - 2 * LANES
-    for m, out in enumerate(outs):
-        out[:, :channels] = (
-            own_ref[m, :, :channels].astype(f32) + crossed_ref[m, :, :channels].astype(f32)
-        ).astype(bf16)
-        for c, ref in enumerate((own_ref, crossed_ref)):
+def chip_sum(part, own_in, crossed_in, *refs):
+    outs, (own, crossed, sems) = refs[:-3], refs[-3:]
+    channels = own.shape[2] - 2 * LANES
+    moves = Moves(sems)
+    order = [*range(1, len(outs)), 0]
+    got = {m: (moves.start(own_in.at[m], own.at[m]), moves.start(crossed_in.at[m], crossed.at[m])) for m in order}
+    for m in order:
+        for copy in got[m]:
+            copy.wait()
+        out = outs[m]
+        out[:, :channels] = (own[m, :, :channels].astype(f32) + crossed[m, :, :channels].astype(f32)).astype(bf16)
+        for c, ref in enumerate((own, crossed)):
             for n in range(2):
                 lane = channels + n * LANES
                 start = channels + (2 * c + n) * part
@@ -430,17 +438,20 @@
             pltpu.VMEM((dp_ranks, span, channels), bf16),
         ]
         + [pltpu.VMEM(shape, bf16) for shape in shapes]
-        + [pltpu.SemaphoreType.DMA((ranks + 4,))],
+        + [pltpu.SemaphoreType.DMA((2 * ranks + 4,))],
         specs=[SMEM, ANY, HBM] + [ANY] * (len(held) - 2) + [VMEM] * 2,
         out_specs=(HBM,) * 3,
     )
     terms = lax.all_to_all(outgoing, EVERY, 0, 0, tiled=True)
     crossed = lax.ppermute(cross, RANK, flipped_pairs(ranks, core))
+    own = pltpu.with_memory_space_constraint(own, pltpu.HBM)
     leaving = called(
         lambda *refs: chip_sum(part, *refs),
         tuple(shape_of((positions, channels + 4 * part), bf16) for _ in masks),
         (own, crossed),
-        8,
+        16,
+        scratch=[pltpu.VMEM(halves, bf16)] * 2 + [pltpu.SemaphoreType.DMA((2 * len(masks),))],
+        specs=[HBM, ANY],
     )
     arrived = leaving[:1] + tuple(
         lax.ppermute(message, RANK, flipped_pairs(ranks, mask))

time: 84.1 us -> 84.2 us (level)
  transfers between devices with their start and end apart: 11 -> 11, of which waited for: 6 -> 6; matrix products, arithmetic and copies ran while one was open for 0% -> 0% of each run, Pallas kernels for 5% -> 6%
where the time goes in v16:
time: 84.2 us; the launch traced here: 83.8 us
  waiting for transfers between devices  36.4 us (43%)
  starting transfers between devices  24.1 us (29%)
  Pallas kernels  20.8 us (25%)
  local copies, waits for them, and re-layouts  0.94 us (1%)
  other arithmetic  0.86 us (1%)
    pallas_call x7, Pallas kernels, called(): pl.pallas_call(body, out_shape=outs, in_specs=specs or [VMEM] * len(args)...  20.8 us
    ppermute x6, waiting for transfers between devices, per_device(): lax.ppermute(message, RANK, flipped_pairs(ranks, mask))  13.5 us
    all_to_all x1, waiting for transfers between devices, per_device(): terms = lax.all_to_all(outgoing, EVERY, 0, 0, tiled=True)  12.6 us
    all_to_all x1, starting transfers between devices, per_device(): pieces = lax.all_to_all(slices, EVERY, 0, 0, tiled=True)  8.99 us
    ppermute x6, starting transfers between devices, per_device(): lax.ppermute(message, RANK, flipped_pairs(ranks, mask))  8.02 us
    all_to_all x1, waiting for transfers between devices, per_device(): pieces = lax.all_to_all(slices, EVERY, 0, 0, tiled=True)  7.9 us
    all_to_all x1, starting transfers between devices, per_device(): terms = lax.all_to_all(outgoing, EVERY, 0, 0, tiled=True)  3.62 us
    ppermute x1, starting transfers between devices, per_device(): both_cores.append(lax.ppermute(crossing, RANK, flipped_pairs(ranks, core)))  2.47 us
  transfers between devices with their start and end apart: 11, of which 6 were waited for; matrix products, arithmetic and copies ran while one was open for 0% of the time, Pallas kernels for 6%

profile of v16, /device:TPU:0, one launch (start us, length us, event | category | flops | bytes accessed | tf_op | source)
XLA Modules:
  0.0 83.8 jit_solution(13809807763761526776)
XLA Ops:
  0.6 0.0 copy-start.1
  0.6 0.0 copy-start
  0.7 0.0 copy-start.3
  0.7 0.9 %fusion = bf16[16,1536]{1,0:T(8,128)(2,1)S(1)} fusion(bf16[128,768]{1,0:T(8,128)(2,1)} %bitcast.9, bf16[128,768]{1,0:T(8,128)(2,1)} %bitcast.6, pred[]{:T(512)S(6)} %eq.3), kind=kLoop, calls=%fused_computation.1 | loop fusion | flops 221184 | bytes 442369 | tf_op jit(solution)/shard_map/jit(_where)/select_n | solution.py:366
  1.5 0.7 collective-permute-start
  2.2 0.0 copy-start.2
  2.2 0.9 %copy-done.2 = bf16[120,768]{1,0:T(8,128)(2,1)S(1)} copy-done((bf16[120,768]{1,0:T(8,128)(2,1)S(1)}, bf16[120,768]{1,0:T(8,128)(2,1)}, u32[]{:S(2)}) %copy-start.2) | copy-done | bytes 184344
  3.1 1.1 %shard_map.84 = bf16[32,96,120]{2,1,0:T(8,128)(2,1)} custom-call(bf16[120,768]{1,0:T(8,128)(2,1)S(1)} %copy-done.2), custom_call_target="tpu_custom_call" | custom-call | tf_op jit(solution)/shard_map/pallas_call | solution.py:23
  4.2 0.0 collective-permute-done.refs_3_
  4.2 0.0 copy-done.1
  4.2 0.0 copy-done
  4.2 0.0 copy-done.3
  4.3 1.8 %shard_map.85 = (bf16[144,960]{1,0:T(8,128)(2,1)}, bf16[144,960]{1,0:T(8,128)(2,1)S(1)}, bf16[144,1152]{1,0:T(8,128)(2,1)}, bf16[144,1152]{1,0:T(8,128)(2,1)S(1)}, bf16[144,1152]{1,0:T(8,128)(2,1)S(1)}) custom-call(s32[1]{0:T(128)} %bitcast.refs_0_, bf16[128,768]{1,0:T(8,128)(2,1)S(1)} %bitcast.7, bf16[128,768]{1,0:T(8,128)(2,1)S(1)} %bitcast.10, ...), custom_call_target="tpu_custom_call" | custom-call | tf_op jit(solution)/shard_map/pallas_call | solution.py:23
  6.1 3.9 %collective-permute-start.1 = (bf16[144,1152]{1,0:T(8,128)(2,1)}, bf16[144,1152]{1,0:T(8,128)(2,1)S(1)}, u32[]{:S(2)}, u32[]{:S(2)}) collective-permute-start(bf16[144,1152]{1,0:T(8,128)(2,1)} %get-tuple-element.30), channel_id=1, source_target_pairs={{0,5},{1,4},{2,7},{3,6},{4,1},{5,0},{6,3},{7,2},{8,13},{9,12},{10,... | collective-permute-start | bytes 995336 | tf_op jit(solution)/shard_map/ppermute | solution.py:403
  10.0 0.5 collective-permute-start.2
  10.5 0.1 collective-permute-start.3
  10.5 9.0 %all-to-all-start = ((bf16[32,96,120]{2,1,0:T(8,128)(2,1)}), bf16[32,96,120]{2,1,0:T(8,128)(2,1)S(1)}, u32[]{:S(2)}, u32[]{:S(2)}) async-start(bf16[32,96,120]{2,1,0:T(8,128)(2,1)} %shard_map.84), calls=%async_computation | async-start | bytes 1572864 | tf_op jit(solution)/shard_map/all_to_all | solution.py:389
  19.5 0.0 collective-permute-done.1.refs_1_.refs_3_
  19.5 9.1 %collective-permute-done.2.refs_2_.refs_4_ = bf16[144,1152]{1,0:T(8,128)(2,1)S(1)} collective-permute-done((bf16[144,1152]{1,0:T(8,128)(2,1)S(1)}, bf16[144,1152]{1,0:T(8,128)(2,1)S(1)}, u32[]{:S(2)}, u32[]{:S(2)}) %collective-permute-start.2) | collective-permute-done | bytes 331808 | tf_op jit(solution)/shard_map/ppermute | solution.py:403
  28.7 0.0 collective-permute-done.3.refs_3_.refs_5_
  28.7 0.0 copy-start.4
  28.7 1.1 %shard_map.86 = bf16[4,144,960]{2,1,0:T(8,128)(2,1)} custom-call(bf16[144,960]{1,0:T(8,128)(2,1)S(1)} %get-tuple-element.33.refs_0_, bf16[144,1152]{1,0:T(8,128)(2,1)S(1)} %collective-permute-done.1.refs_1_.refs_3_, bf16[144,1152]{1,0:T(8,128)(2,1)S(1)} %collective-permute-done.2.refs_2_.refs_4_, bf16[144,1152]{1,0:T(8,128)(2,1)S(1)} %collective-permute-done.3.refs_3_.refs_5_), custom_call_target="tpu_custom_call" | custom-call | tf_op jit(solution)/shard_map/pallas_call | solution.py:23
  29.8 2.5 %collective-permute-start.4 = (bf16[4,144,960]{2,1,0:T(8,128)(2,1)}, bf16[4,144,960]{2,1,0:T(8,128)(2,1)S(1)}, u32[]{:S(2)}, u32[]{:S(2)}) collective-permute-start(bf16[4,144,960]{2,1,0:T(8,128)(2,1)} %shard_map.86), channel_id=1, source_target_pairs={{0,2},{1,3},{2,0},{3,1},{4,6},{5,7},{6,4},{7,5},{8,10},{9,11},{10,... | collective-permute-start | bytes 3317768 | tf_op jit(solution)/shard_map/ppermute | solution.py:409
  32.2 0.0 copy-done.4
  32.2 7.9 %all-to-all-done.refs_1_ = bf16[32,96,120]{2,1,0:T(8,128)(2,1)S(1)} async-done(((bf16[32,96,120]{2,1,0:T(8,128)(2,1)}), bf16[32,96,120]{2,1,0:T(8,128)(2,1)S(1)}, u32[]{:S(2)}, u32[]{:S(2)}) %all-to-all-start) | async-done | bytes 737312 | tf_op jit(solution)/shard_map/all_to_all | solution.py:389
  40.1 0.0 collective-permute-done.4.refs_6_
  40.1 12.5 %shard_map.87 = (bf16[32,96,122]{2,1,0:T(8,128)(2,1)}, bf16[4,128,1024]{2,1,0:T(8,128)(2,1)}, bf16[4,128,1024]{2,1,0:T(8,128)(2,1)}) custom-call(s32[1]{0:T(128)} %bitcast.refs_0_, bf16[32,96,120]{2,1,0:T(8,128)(2,1)S(1)} %all-to-all-done.refs_1_, bf16[144,960]{1,0:T(8,128)(2,1)} %get-tuple-element.29.refs_2_, ...), custom_call_target="tpu_custom_call" | custom-call | tf_op jit(solution)/shard_map/pallas_call | solution.py:23
  52.7 0.0 copy-start.5
  52.7 3.6 %all-to-all-start.1 = ((bf16[32,96,122]{2,1,0:T(8,128)(2,1)}), bf16[32,96,122]{2,1,0:T(8,128)(2,1)S(1)}, u32[]{:S(2)}, u32[]{:S(2)}) async-start(bf16[32,96,122]{2,1,0:T(8,128)(2,1)} %get-tuple-element.34), calls=%async_computation.1 | async-start | bytes 1572864 | tf_op jit(solution)/shard_map/all_to_all | solution.py:445
  56.3 0.0 copy-done.5
  56.3 0.3 collective-permute-start.5
  56.6 2.4 %collective-permute-done.5.refs_1_ = bf16[4,128,1024]{2,1,0:T(8,128)(2,1)S(1)} collective-permute-done((bf16[4,128,1024]{2,1,0:T(8,128)(2,1)S(1)}, bf16[4,128,1024]{2,1,0:T(8,128)(2,1)S(1)}, u32[]{:S(2)}, u32[]{:S(2)}) %collective-permute-start.5) | collective-permute-done | bytes 1048608 | tf_op jit(solution)/shard_map/ppermute | solution.py:446
  59.0 1.7 %shard_map.89 = (bf16[128,1152]{1,0:T(8,128)(2,1)S(1)}, bf16[128,1152]{1,0:T(8,128)(2,1)S(1)}, bf16[128,1152]{1,0:T(8,128)(2,1)S(1)}, bf16[128,1152]{1,0:T(8,128)(2,1)S(1)}) custom-call(bf16[4,128,1024]{2,1,0:T(8,128)(2,1)} %get-tuple-element.36.refs_0_, bf16[4,128,1024]{2,1,0:T(8,128)(2,1)S(1)} %collective-permute-done.5.refs_1_), custom_call_target="tpu_custom_call" | custom-call | tf_op jit(solution)/shard_map/pallas_call | solution.py:23
  60.8 2.7 %collective-permute-start.6 = (bf16[128,1152]{1,0:T(8,128)(2,1)S(1)}, bf16[128,1152]{1,0:T(8,128)(2,1)S(1)}, u32[]{:S(2)}, u32[]{:S(2)}) collective-permute-start(bf16[128,1152]{1,0:T(8,128)(2,1)S(1)} %get-tuple-element.39), channel_id=1, source_target_pairs={{0,5},{1,4},{2,7},{3,6},{4,1},{5,0},{6,3},{7,2},{8,13},{9,12},{10,... | collective-permute-start | bytes 884744 | tf_op jit(solution)/shard_map/ppermute | solution.py:457
  63.5 0.6 collective-permute-start.7
  64.1 0.3 collective-permute-start.8
  64.3 12.6 %all-to-all-done.1.refs_0_ = bf16[32,96,122]{2,1,0:T(8,128)(2,1)S(1)} async-done(((bf16[32,96,122]{2,1,0:T(8,128)(2,1)}), bf16[32,96,122]{2,1,0:T(8,128)(2,1)S(1)}, u32[]{:S(2)}, u32[]{:S(2)}) %all-to-all-start.1) | async-done | bytes 749600 | tf_op jit(solution)/shard_map/all_to_all | solution.py:445
  76.9 1.0 %shard_map.88 = (f32[120,768]{1,0:T(8,128)}, f32[1,24]{1,0:T(1,128)}) custom-call(bf16[32,96,122]{2,1,0:T(8,128)(2,1)S(1)} %all-to-all-done.1.refs_0_), custom_call_target="tpu_custom_call" | custom-call | tf_op jit(solution)/shard_map/pallas_call | solution.py:23
  77.9 0.0 collective-permute-done.6.refs_5_
  77.9 4.1 %collective-permute-done.7.refs_6_ = bf16[128,1152]{1,0:T(8,128)(2,1)S(1)} collective-permute-done((bf16[128,1152]{1,0:T(8,128)(2,1)S(1)}, bf16[128,1152]{1,0:T(8,128)(2,1)S(1)}, u32[]{:S(2)}, u32[]{:S(2)}) %collective-permute-start.7) | collective-permute-done | bytes 294944 | tf_op jit(solution)/shard_map/ppermute | solution.py:457
  82.0 0.2 collective-permute-done.8.refs_7_
  82.3 1.6 %shard_map.90 = (bf16[128,768]{1,0:T(8,128)(2,1)}, bf16[128,768]{1,0:T(8,128)(2,1)}) custom-call(s32[1]{0:T(128)} %bitcast.refs_0_, bf16[128,768]{1,0:T(8,128)(2,1)S(1)} %bitcast.8, bf16[128,768]{1,0:T(8,128)(2,1)S(1)} %bitcast.11, s32[768]{0:T(1024)S(1)} %copy-done.3, bf16[128,1152]{1,0:T(8,128)(2,1)S(1)} %get-tuple-element.42.refs_4_, ...), custom_call_target="tpu_custom_call" | custom-call | tf_op jit(solution)/shard_map/pallas_call | solution.py:23
  (1 shorter events, 0.0 us)
Async XLA Ops:
  0.6 3.6 %copy-start.1 = (bf16[1,128,768]{2,1,0:T(8,128)(2,1)S(1)}, bf16[1,128,768]{2,1,0:T(8,128)(2,1)}, u32[]{:S(2)}) copy-start(bf16[1,128,768]{2,1,0:T(8,128)(2,1)} %param.6) | copy-start | bytes 589828
  0.6 3.6 %copy-start = (bf16[1,128,768]{2,1,0:T(8,128)(2,1)S(1)}, bf16[1,128,768]{2,1,0:T(8,128)(2,1)}, u32[]{:S(2)}) copy-start(bf16[1,128,768]{2,1,0:T(8,128)(2,1)} %param.5) | copy-start | bytes 589828
  0.7 3.6 %copy-start.3 = (s32[768]{0:T(1024)S(1)}, s32[768]{0:T(1024)}, u32[]{:S(2)}) copy-start(s32[768]{0:T(1024)} %refs_3_.1) | copy-start | bytes 9220
  1.5 2.7 %collective-permute-start = (bf16[16,1536]{1,0:T(8,128)(2,1)S(1)}, bf16[16,1536]{1,0:T(8,128)(2,1)S(1)}, u32[]{:S(2)}, u32[]{:S(2)}) collective-permute-start(bf16[16,1536]{1,0:T(8,128)(2,1)S(1)} %fusion), channel_id=1, source_target_pairs={{6,8},{14,16},{22,24},{8,6},{16,14},{24,22},{7,9},{15,17},{23,25},... | collective-permute-start | bytes 147464 | tf_op jit(solution)/shard_map/ppermute | solution.py:367
  2.2 0.9 %copy-start.2 = (bf16[120,768]{1,0:T(8,128)(2,1)S(1)}, bf16[120,768]{1,0:T(8,128)(2,1)}, u32[]{:S(2)}) copy-start(bf16[120,768]{1,0:T(8,128)(2,1)} %refs_0_.1) | copy-start | bytes 552964
  6.1 13.5 %collective-permute-start.1 = (bf16[144,1152]{1,0:T(8,128)(2,1)}, bf16[144,1152]{1,0:T(8,128)(2,1)S(1)}, u32[]{:S(2)}, u32[]{:S(2)}) collective-permute-start(bf16[144,1152]{1,0:T(8,128)(2,1)} %get-tuple-element.30), channel_id=1, source_target_pairs={{0,5},{1,4},{2,7},{3,6},{4,1},{5,0},{6,3},{7,2},{8,13},{9,12},{10,... | collective-permute-start | bytes 995336 | tf_op jit(solution)/shard_map/ppermute | solution.py:403
  10.0 18.7 %collective-permute-start.2 = (bf16[144,1152]{1,0:T(8,128)(2,1)S(1)}, bf16[144,1152]{1,0:T(8,128)(2,1)S(1)}, u32[]{:S(2)}, u32[]{:S(2)}) collective-permute-start(bf16[144,1152]{1,0:T(8,128)(2,1)S(1)} %get-tuple-element.31), channel_id=1, source_target_pairs={{0,1},{1,0},{2,3},{3,2},{4,5},{5,4},{6,7},{7,6},{8,9},{9,8},{10,11... | collective-permute-start | bytes 995336 | tf_op jit(solution)/shard_map/ppermute | solution.py:403
  10.5 18.2 %collective-permute-start.3 = (bf16[144,1152]{1,0:T(8,128)(2,1)S(1)}, bf16[144,1152]{1,0:T(8,128)(2,1)S(1)}, u32[]{:S(2)}, u32[]{:S(2)}) collective-permute-start(bf16[144,1152]{1,0:T(8,128)(2,1)S(1)} %get-tuple-element.32), channel_id=1, source_target_pairs={{0,4},{1,5},{2,6},{3,7},{4,0},{5,1},{6,2},{7,3},{8,12},{9,13},{10,... | collective-permute-start | bytes 995336 | tf_op jit(solution)/shard_map/ppermute | solution.py:403
  10.5 29.6 %all-to-all-start = ((bf16[32,96,120]{2,1,0:T(8,128)(2,1)}), bf16[32,96,120]{2,1,0:T(8,128)(2,1)S(1)}, u32[]{:S(2)}, u32[]{:S(2)}) async-start(bf16[32,96,120]{2,1,0:T(8,128)(2,1)} %shard_map.84), calls=%async_computation | async-start | bytes 1572864 | tf_op jit(solution)/shard_map/all_to_all | solution.py:389
  28.7 3.6 %copy-start.4 = (f32[768]{0:T(1024)S(1)}, f32[768]{0:T(1024)}, u32[]{:S(2)}) copy-start(f32[768]{0:T(1024)} %param.8) | copy-start | bytes 9220
  29.8 10.4 %collective-permute-start.4 = (bf16[4,144,960]{2,1,0:T(8,128)(2,1)}, bf16[4,144,960]{2,1,0:T(8,128)(2,1)S(1)}, u32[]{:S(2)}, u32[]{:S(2)}) collective-permute-start(bf16[4,144,960]{2,1,0:T(8,128)(2,1)} %shard_map.86), channel_id=1, source_target_pairs={{0,2},{1,3},{2,0},{3,1},{4,6},{5,7},{6,4},{7,5},{8,10},{9,11},{10,... | collective-permute-start | bytes 3317768 | tf_op jit(solution)/shard_map/ppermute | solution.py:409
  52.7 3.6 %copy-start.5 = (bf16[4,128,1024]{2,1,0:T(8,128)(2,1)S(1)}, bf16[4,128,1024]{2,1,0:T(8,128)(2,1)}, u32[]{:S(2)}) copy-start(bf16[4,128,1024]{2,1,0:T(8,128)(2,1)} %get-tuple-element.37) | copy-start | bytes 3145732
  52.7 24.2 %all-to-all-start.1 = ((bf16[32,96,122]{2,1,0:T(8,128)(2,1)}), bf16[32,96,122]{2,1,0:T(8,128)(2,1)S(1)}, u32[]{:S(2)}, u32[]{:S(2)}) async-start(bf16[32,96,122]{2,1,0:T(8,128)(2,1)} %get-tuple-element.34), calls=%async_computation.1 | async-start | bytes 1572864 | tf_op jit(solution)/shard_map/all_to_all | solution.py:445
  56.3 2.7 %collective-permute-start.5 = (bf16[4,128,1024]{2,1,0:T(8,128)(2,1)S(1)}, bf16[4,128,1024]{2,1,0:T(8,128)(2,1)S(1)}, u32[]{:S(2)}, u32[]{:S(2)}) collective-permute-start(bf16[4,128,1024]{2,1,0:T(8,128)(2,1)S(1)} %copy-done.5), channel_id=1, source_target_pairs={{0,2},{1,3},{2,0},{3,1},{4,6},{5,7},{6,4},{7,5},{8,10},{9,11},{10,... | collective-permute-start | bytes 3145736 | tf_op jit(solution)/shard_map/ppermute | solution.py:446
  60.8 17.1 %collective-permute-start.6 = (bf16[128,1152]{1,0:T(8,128)(2,1)S(1)}, bf16[128,1152]{1,0:T(8,128)(2,1)S(1)}, u32[]{:S(2)}, u32[]{:S(2)}) collective-permute-start(bf16[128,1152]{1,0:T(8,128)(2,1)S(1)} %get-tuple-element.39), channel_id=1, source_target_pairs={{0,5},{1,4},{2,7},{3,6},{4,1},{5,0},{6,3},{7,2},{8,13},{9,12},{10,... | collective-permute-start | bytes 884744 | tf_op jit(solution)/shard_map/ppermute | solution.py:457
  63.5 18.5 %collective-permute-start.7 = (bf16[128,1152]{1,0:T(8,128)(2,1)S(1)}, bf16[128,1152]{1,0:T(8,128)(2,1)S(1)}, u32[]{:S(2)}, u32[]{:S(2)}) collective-permute-start(bf16[128,1152]{1,0:T(8,128)(2,1)S(1)} %get-tuple-element.40), channel_id=1, source_target_pairs={{0,1},{1,0},{2,3},{3,2},{4,5},{5,4},{6,7},{7,6},{8,9},{9,8},{10,11... | collective-permute-start | bytes 884744 | tf_op jit(solution)/shard_map/ppermute | solution.py:457
  64.1 18.2 %collective-permute-start.8 = (bf16[128,1152]{1,0:T(8,128)(2,1)S(1)}, bf16[128,1152]{1,0:T(8,128)(2,1)S(1)}, u32[]{:S(2)}, u32[]{:S(2)}) collective-permute-start(bf16[128,1152]{1,0:T(8,128)(2,1)S(1)} %get-tuple-element.41), channel_id=1, source_target_pairs={{0,4},{1,5},{2,6},{3,7},{4,0},{5,1},{6,2},{7,3},{8,12},{9,13},{10,... | collective-permute-start | bytes 884744 | tf_op jit(solution)/shard_map/ppermute | solution.py:457

commit v17 on v15

--- a/solution.py
+++ b/solution.py
@@ -10,6 +10,7 @@
 EVERY = ("seq_block", "seq_rank", "dp_block", "dp_rank")
 LANES = 128
 HALO = 16
+EDGE = 8
 EXTRA = 2
 VMEM = pl.BlockSpec(memory_space=pltpu.VMEM)
 SMEM = pl.BlockSpec(memory_space=pltpu.SMEM)
@@ -152,11 +153,10 @@
     got_blocks += [moves.start(block, arrived.at[m]) for m, block in enumerate(arrived_in)]
     per = chips // groups
     got_blocks += [moves.start(crossed_in[m // per].at[m % per], crossed.at[m]) for m in range(chips)]
-    got_pieces = moves.start(pieces_in, pieces)
-    arrivals = len(moves.copies)
+    got_pieces = None
     masks = chip_masks(2 * chips, core)
     seq_ranks = 2 * chips // dp_ranks
-    positions = home.shape[0] - HALO
+    positions = home.shape[0] - EDGE
     channels, width = gain_ref.shape[1], home.shape[1]
     swap = swap_map(pairing_ref[...].reshape(1, -1))
     gains = [gain_ref[...], swapped_row(gain_ref[...], swap)]
@@ -165,6 +165,8 @@
     blocks += [(mask | core, crossed.at[m], channels) for m, mask in enumerate(masks)]
     for got, (flip, ref, lane) in zip(got_blocks, blocks):
         got.wait()
+        if got is got_blocks[1]:
+            got_pieces = moves.start(pieces_in, pieces)
         source = lax.bitwise_xor(rank_ref[0], flip)
         b, i = lax.rem(source, dp_ranks), lax.div(source, dp_ranks)
         start = pl.multiple_of(i * positions, positions)
@@ -176,7 +178,7 @@
             index = n * dp_ranks + b
             normed_ref[index, pl.ds(start, positions), :] = normed[:positions]
             grads_ref[index, pl.ds(start, positions), :part] = grads[:positions]
-            edge_normed_ref[side, index] = normed[positions:]
+            edge_normed_ref[side, index] = normed[positions:].astype(f32)
             edge_grads_ref[side, index, :, :part] = grads[positions:]
     span = normed_ref.shape[1]
     taps = kernel_ref.shape[0] // part
@@ -193,6 +195,7 @@
             first += count
 
     got_pieces.wait()
+    arrivals = len(moves.copies)
     for owner in range(owners):
         for tap, channel, count, offset in runs(owner):
             kernel_ref[tap * part : (tap + 1) * part, channel : channel + count] = pieces[
@@ -209,16 +212,16 @@
         edges = [
             edge_normed_ref[side, n * dp_ranks + b] for side in range(2) for b in range(dp_ranks)
         ]
-        edge_terms.append(dot(jnp.concatenate(edges, 0), padded[n], ((1,), (1,))))
+        edge_terms.append(dot(jnp.concatenate(edges, 0).astype(bf16), padded[n], ((1,), (1,))))
     for strand in range(strands):
         forward = strand < dp_ranks
         n, b = divmod(strand, dp_ranks)
         terms[HALO : HALO + span, :] = dot(normed_ref[strand], padded[n], ((1,), (1,)))
         halves[HALO : HALO + span, :] = grads_ref[strand]
-        for side, start in enumerate((0, HALO + span)):
-            first = (side * dp_ranks + b) * HALO
-            terms[start : start + HALO, :] = edge_terms[n][first : first + HALO]
-            halves[start : start + HALO, :] = edge_grads_ref[side, strand]
+        for side, start in enumerate((HALO - EDGE, HALO + span)):
+            first = (side * dp_ranks + b) * EDGE
+            terms[start : start + EDGE, :] = edge_terms[n][first : first + EDGE]
+            halves[start : start + EDGE, :] = edge_grads_ref[side, strand]
         preact = jnp.zeros((wide, LANES), f32)
         for k in range(taps):
             start = HALO - reach + k if forward else HALO - k
@@ -259,8 +262,9 @@
             dot(shifted_ref[b], kernels[0], ((1,), (0,))) * gains[0]
             + dot(shifted_ref[dp_ranks + b], kernels[1], ((1,), (0,))) * gains[1]
         ).astype(bf16)
+    order = [*range(1, chips), 0]
     for out, target_out, flip in ((cross, cross_out, core), (own, own_out, 0)):
-        for m, mask in enumerate(masks):
+        for m, mask in [(m, masks[m]) for m in order]:
             target = lax.bitwise_xor(rank_ref[0], mask | flip)
             b = lax.rem(target, dp_ranks)
             start = pl.multiple_of(lax.div(target, dp_ranks) * positions, positions)
@@ -268,7 +272,7 @@
             for n in range(2):
                 lane = channels + n * LANES
                 out[m, :, lane : lane + LANES] = gelu_ref[n * dp_ranks + b, pl.ds(start, positions), :]
-        moves.start(out, target_out)
+            moves.start(out.at[m], target_out.at[m])
     for copy in moves.copies[arrivals:]:
         copy.wait()
 
@@ -355,7 +359,7 @@
     along = ("seq_block", "seq_rank")
     ends = [(b * seq_ranks - 1, b * seq_ranks) for b in range(1, seq_blocks)]
     both = jnp.concatenate([values, cot], -1)
-    edge = jnp.where(lax.axis_index("seq_rank") == 0, both[:HALO], both[-HALO:])
+    edge = jnp.where(lax.axis_index("seq_rank") == 0, both[:EDGE], both[-EDGE:])
     edge = lax.ppermute(edge, along, ends + [(target, source) for source, target in ends])
     piece_of = [
         sr * dp_ranks + dr
@@ -382,7 +386,7 @@
     gain = norm_gain.reshape(1, channels)
     core = dp_ranks
     masks = chip_masks(ranks, core)
-    block = positions + HALO
+    block = positions + EDGE
     home, cross, *leaving = called(
         lambda *refs: pack_messages(part, core, *refs),
         (pltpu.HBM((block, slim), bf16), shape_of((block, slim), bf16))
@@ -416,8 +420,8 @@
             pltpu.VMEM((len(arrived), *arrived[0].shape), bf16),
             pltpu.VMEM((strands, span, channels), bf16),
             pltpu.VMEM((strands, span, LANES), f32),
-            pltpu.VMEM((3, strands, HALO, channels), bf16),
-            pltpu.VMEM((3, strands, HALO, LANES), f32),
+            pltpu.VMEM((3, strands, EDGE, channels), f32),
+            pltpu.VMEM((3, strands, EDGE, LANES), f32),
             pltpu.VMEM((2, taps * LANES, channels), bf16),
             pltpu.VMEM((long, taps * LANES), f32),
             pltpu.VMEM((long, LANES), f32),
@@ -430,7 +434,7 @@
             pltpu.VMEM((dp_ranks, span, channels), bf16),
         ]
         + [pltpu.VMEM(shape, bf16) for shape in shapes]
-        + [pltpu.SemaphoreType.DMA((ranks + 4,))],
+        + [pltpu.SemaphoreType.DMA((2 * ranks + 4,))],
         specs=[SMEM, ANY, HBM] + [ANY] * (len(held) - 2) + [VMEM] * 2,
         out_specs=(HBM,) * 3,
     )

time: 84.1 us -> 90.8 us (1.080)
  starting transfers between devices: 24 us -> 35 us
  Pallas kernels: 20.2 us -> 18.4 us
  waiting for transfers between devices: 37 us -> 35.3 us
    all_to_all x1, starting transfers between devices: 3.62 us -> 12.6 us  [per_device(): terms = lax.all_to_all(outgoing, EVERY, 0, 0, tiled=True)]
    all_to_all x1, waiting for transfers between devices: 7.9 us -> 0.01 us  [per_device(): pieces = lax.all_to_all(slices, EVERY, 0, 0, tiled=True)]
    ppermute x1, starting transfers between devices: 2.47 us -> 7.14 us  [per_device(): both_cores.append(lax.ppermute(crossing, RANK, flipped_pairs(ranks, core)))]
    ppermute x6, waiting for transfers between devices: 13.4 us -> 16.7 us  [per_device(): lax.ppermute(message, RANK, flipped_pairs(ranks, mask))]
    ppermute x1, waiting for transfers between devices: 0.01 us -> 2.37 us  [per_device(): both_cores.append(lax.ppermute(crossing, RANK, flipped_pairs(ranks, core)))]
    pallas_call x7, Pallas kernels: 20.2 us -> 18.4 us  [called(): pl.pallas_call(body, out_shape=outs, in_specs=specs or [VMEM] * len(args)...]
    all_to_all x1, starting transfers between devices: 8.99 us -> 7.3 us  [per_device(): pieces = lax.all_to_all(slices, EVERY, 0, 0, tiled=True)]
    ppermute x6, starting transfers between devices: 7.96 us -> 7.04 us  [per_device(): lax.ppermute(message, RANK, flipped_pairs(ranks, mask))]
  transfers between devices with their start and end apart: 11 -> 11, of which waited for: 6 -> 7; matrix products, arithmetic and copies ran while one was open for 0% -> 0% of each run, Pallas kernels for 5% -> 4%
where the time goes in v17:
time: 90.8 us; the launch traced here: 90.4 us
  waiting for transfers between devices  35.3 us (39%)
  starting transfers between devices  35 us (39%)
  Pallas kernels  18.4 us (20%)
  local copies, waits for them, and re-layouts  0.99 us (1%)
    pallas_call x7, Pallas kernels, called(): pl.pallas_call(body, out_shape=outs, in_specs=specs or [VMEM] * len(args)...  18.4 us
    ppermute x6, waiting for transfers between devices, per_device(): lax.ppermute(message, RANK, flipped_pairs(ranks, mask))  16.7 us
    all_to_all x1, waiting for transfers between devices, per_device(): terms = lax.all_to_all(outgoing, EVERY, 0, 0, tiled=True)  13.6 us
    all_to_all x1, starting transfers between devices, per_device(): terms = lax.all_to_all(outgoing, EVERY, 0, 0, tiled=True)  12.6 us
    all_to_all x1, starting transfers between devices, per_device(): pieces = lax.all_to_all(slices, EVERY, 0, 0, tiled=True)  7.3 us
    ppermute x1, starting transfers between devices, per_device(): both_cores.append(lax.ppermute(crossing, RANK, flipped_pairs(ranks, core)))  7.14 us
    ppermute x6, starting transfers between devices, per_device(): lax.ppermute(message, RANK, flipped_pairs(ranks, mask))  7.04 us
    ppermute x1, waiting for transfers between devices, per_device(): crossed = lax.ppermute(cross, RANK, flipped_pairs(ranks, core))  2.62 us
  transfers between devices with their start and end apart: 11, of which 7 were waited for; matrix products, arithmetic and copies ran while one was open for 0% of the time, Pallas kernels for 4%

profile of v17, /device:TPU:0, one launch (start us, length us, event | category | flops | bytes accessed | tf_op | source)
XLA Modules:
  0.0 90.4 jit_solution(5093654416520520847)
XLA Ops:
  0.6 0.0 copy-start
  0.6 0.0 copy-start.1
  0.7 0.0 copy-start.3
  0.7 1.0 %copy-done.3 = bf16[120,768]{1,0:T(8,128)(2,1)S(1)} copy-done((bf16[120,768]{1,0:T(8,128)(2,1)S(1)}, bf16[120,768]{1,0:T(8,128)(2,1)}, u32[]{:S(2)}) %copy-start.3) | copy-done | bytes 184344
  1.6 1.1 %shard_map.84 = bf16[32,96,120]{2,1,0:T(8,128)(2,1)} custom-call(bf16[120,768]{1,0:T(8,128)(2,1)S(1)} %copy-done.3), custom_call_target="tpu_custom_call" | custom-call | tf_op jit(solution)/shard_map/pallas_call | solution.py:24
  2.7 0.0 copy-start.4
  2.7 7.3 %all-to-all-start = ((bf16[32,96,120]{2,1,0:T(8,128)(2,1)}), bf16[32,96,120]{2,1,0:T(8,128)(2,1)S(1)}, u32[]{:S(2)}, u32[]{:S(2)}) async-start(bf16[32,96,120]{2,1,0:T(8,128)(2,1)} %shard_map.84), calls=%async_computation | async-start | bytes 1572864 | tf_op jit(solution)/shard_map/all_to_all | solution.py:385
  10.0 0.0 copy-done
  10.0 0.0 copy-done.1
  10.1 0.7 collective-permute-start
  10.7 0.0 collective-permute-done.refs_3_
  10.8 0.0 copy-done.4
  10.8 1.7 %shard_map.85 = (bf16[136,960]{1,0:T(8,128)(2,1)}, bf16[136,960]{1,0:T(8,128)(2,1)S(1)}, bf16[136,1152]{1,0:T(8,128)(2,1)S(1)}, bf16[136,1152]{1,0:T(8,128)(2,1)S(1)}, bf16[136,1152]{1,0:T(8,128)(2,1)S(1)}) custom-call(s32[1]{0:T(128)} %bitcast.refs_0_, bf16[128,768]{1,0:T(8,128)(2,1)S(1)} %bitcast.7, bf16[128,768]{1,0:T(8,128)(2,1)S(1)} %bitcast.10, ...), custom_call_target="tpu_custom_call" | custom-call | tf_op jit(solution)/shard_map/pallas_call | solution.py:24
  12.5 2.7 %collective-permute-start.1 = (bf16[136,1152]{1,0:T(8,128)(2,1)S(1)}, bf16[136,1152]{1,0:T(8,128)(2,1)S(1)}, u32[]{:S(2)}, u32[]{:S(2)}) collective-permute-start(bf16[136,1152]{1,0:T(8,128)(2,1)S(1)} %get-tuple-element.30), channel_id=1, source_target_pairs={{0,5},{1,4},{2,7},{3,6},{4,1},{5,0},{6,3},{7,2},{8,13},{9,12},{10,... | collective-permute-start | bytes 940040 | tf_op jit(solution)/shard_map/ppermute | solution.py:399
  15.1 0.6 collective-permute-start.2
  15.7 0.3 collective-permute-start.3
  15.9 8.2 %collective-permute-done.1.refs_1_.refs_3_ = bf16[136,1152]{1,0:T(8,128)(2,1)S(1)} collective-permute-done((bf16[136,1152]{1,0:T(8,128)(2,1)S(1)}, bf16[136,1152]{1,0:T(8,128)(2,1)S(1)}, u32[]{:S(2)}, u32[]{:S(2)}) %collective-permute-start.1) | collective-permute-done | bytes 313376 | tf_op jit(solution)/shard_map/ppermute | solution.py:399
  24.2 4.0 %collective-permute-done.2.refs_2_.refs_4_ = bf16[136,1152]{1,0:T(8,128)(2,1)S(1)} collective-permute-done((bf16[136,1152]{1,0:T(8,128)(2,1)S(1)}, bf16[136,1152]{1,0:T(8,128)(2,1)S(1)}, u32[]{:S(2)}, u32[]{:S(2)}) %collective-permute-start.2) | collective-permute-done | bytes 313376 | tf_op jit(solution)/shard_map/ppermute | solution.py:399
  28.2 0.8 collective-permute-done.3.refs_3_.refs_5_
  29.0 0.0 copy-start.5
  29.0 0.1 shard_map.86
  29.1 7.1 %collective-permute-start.4 = (bf16[4,136,960]{2,1,0:T(8,128)(2,1)S(1)}, bf16[4,136,960]{2,1,0:T(8,128)(2,1)S(1)}, u32[]{:S(2)}, u32[]{:S(2)}) collective-permute-start(bf16[4,136,960]{2,1,0:T(8,128)(2,1)S(1)} %shard_map.86), channel_id=1, source_target_pairs={{0,2},{1,3},{2,0},{3,1},{4,6},{5,7},{6,4},{7,5},{8,10},{9,11},{10,... | collective-permute-start | bytes 3133448 | tf_op jit(solution)/shard_map/ppermute | solution.py:405
  36.2 0.0 copy-done.5
  36.2 2.4 %collective-permute-done.4.refs_6_ = bf16[4,136,960]{2,1,0:T(8,128)(2,1)S(1)} collective-permute-done((bf16[4,136,960]{2,1,0:T(8,128)(2,1)S(1)}, bf16[4,136,960]{2,1,0:T(8,128)(2,1)S(1)}, u32[]{:S(2)}, u32[]{:S(2)}) %collective-permute-start.4) | collective-permute-done | bytes 1044512 | tf_op jit(solution)/shard_map/ppermute | solution.py:405
  38.6 0.0 all-to-all-done.refs_1_
  38.6 12.5 %shard_map.87 = (bf16[32,96,122]{2,1,0:T(8,128)(2,1)}, bf16[4,128,1024]{2,1,0:T(8,128)(2,1)}, bf16[4,128,1024]{2,1,0:T(8,128)(2,1)}) custom-call(s32[1]{0:T(128)} %bitcast.refs_0_, bf16[32,96,120]{2,1,0:T(8,128)(2,1)S(1)} %all-to-all-done.refs_1_, bf16[136,960]{1,0:T(8,128)(2,1)} %get-tuple-element.29.refs_2_, ...), custom_call_target="tpu_custom_call" | custom-call | tf_op jit(solution)/shard_map/pallas_call | solution.py:24
  51.1 0.0 copy-start.2
  51.1 12.6 %all-to-all-start.1 = ((bf16[32,96,122]{2,1,0:T(8,128)(2,1)}), bf16[32,96,122]{2,1,0:T(8,128)(2,1)S(1)}, u32[]{:S(2)}, u32[]{:S(2)}) async-start(bf16[32,96,122]{2,1,0:T(8,128)(2,1)} %get-tuple-element.34), calls=%async_computation.1 | async-start | bytes 1572864 | tf_op jit(solution)/shard_map/all_to_all | solution.py:441
  63.7 0.3 collective-permute-start.5
  64.0 2.6 %collective-permute-done.5.refs_1_ = bf16[4,128,1024]{2,1,0:T(8,128)(2,1)S(1)} collective-permute-done((bf16[4,128,1024]{2,1,0:T(8,128)(2,1)}, bf16[4,128,1024]{2,1,0:T(8,128)(2,1)S(1)}, u32[]{:S(2)}, u32[]{:S(2)}) %collective-permute-start.5) | collective-permute-done | bytes 1048608 | tf_op jit(solution)/shard_map/ppermute | solution.py:442
  66.6 0.0 copy-done.2
  66.6 0.5 shard_map.89
  67.1 2.7 %collective-permute-start.6 = (bf16[128,1152]{1,0:T(8,128)(2,1)S(1)}, bf16[128,1152]{1,0:T(8,128)(2,1)S(1)}, u32[]{:S(2)}, u32[]{:S(2)}) collective-permute-start(bf16[128,1152]{1,0:T(8,128)(2,1)S(1)} %get-tuple-element.39), channel_id=1, source_target_pairs={{0,5},{1,4},{2,7},{3,6},{4,1},{5,0},{6,3},{7,2},{8,13},{9,12},{10,... | collective-permute-start | bytes 884744 | tf_op jit(solution)/shard_map/ppermute | solution.py:450
  69.8 0.6 collective-permute-start.7
  70.4 0.3 collective-permute-start.8
  70.7 13.6 %all-to-all-done.1.refs_0_ = bf16[32,96,122]{2,1,0:T(8,128)(2,1)S(1)} async-done(((bf16[32,96,122]{2,1,0:T(8,128)(2,1)}), bf16[32,96,122]{2,1,0:T(8,128)(2,1)S(1)}, u32[]{:S(2)}, u32[]{:S(2)}) %all-to-all-start.1) | async-done | bytes 749600 | tf_op jit(solution)/shard_map/all_to_all | solution.py:441
  84.3 1.0 %shard_map.88 = (f32[120,768]{1,0:T(8,128)}, f32[1,24]{1,0:T(1,128)}) custom-call(bf16[32,96,122]{2,1,0:T(8,128)(2,1)S(1)} %all-to-all-done.1.refs_0_), custom_call_target="tpu_custom_call" | custom-call | tf_op jit(solution)/shard_map/pallas_call | solution.py:24
  85.3 0.0 collective-permute-done.6.refs_5_
  85.3 3.6 %collective-permute-done.7.refs_6_ = bf16[128,1152]{1,0:T(8,128)(2,1)S(1)} collective-permute-done((bf16[128,1152]{1,0:T(8,128)(2,1)S(1)}, bf16[128,1152]{1,0:T(8,128)(2,1)S(1)}, u32[]{:S(2)}, u32[]{:S(2)}) %collective-permute-start.7) | collective-permute-done | bytes 294944 | tf_op jit(solution)/shard_map/ppermute | solution.py:450
  88.8 0.0 collective-permute-done.8.refs_7_
  88.9 1.6 %shard_map.90 = (bf16[128,768]{1,0:T(8,128)(2,1)}, bf16[128,768]{1,0:T(8,128)(2,1)}) custom-call(s32[1]{0:T(128)} %bitcast.refs_0_, bf16[128,768]{1,0:T(8,128)(2,1)S(1)} %bitcast.8, bf16[128,768]{1,0:T(8,128)(2,1)S(1)} %bitcast.11, s32[768]{0:T(1024)S(1)} %copy-done.4, bf16[128,1152]{1,0:T(8,128)(2,1)S(1)} %get-tuple-element.42.refs_4_, ...), custom_call_target="tpu_custom_call" | custom-call | tf_op jit(solution)/shard_map/pallas_call | solution.py:24
  (2 shorter events, 0.0 us)
Async XLA Ops:
  0.6 9.4 %copy-start = (bf16[1,128,768]{2,1,0:T(8,128)(2,1)S(1)}, bf16[1,128,768]{2,1,0:T(8,128)(2,1)}, u32[]{:S(2)}) copy-start(bf16[1,128,768]{2,1,0:T(8,128)(2,1)} %param.5) | copy-start | bytes 589828
  0.6 9.4 %copy-start.1 = (bf16[1,128,768]{2,1,0:T(8,128)(2,1)S(1)}, bf16[1,128,768]{2,1,0:T(8,128)(2,1)}, u32[]{:S(2)}) copy-start(bf16[1,128,768]{2,1,0:T(8,128)(2,1)} %param.6) | copy-start | bytes 589828
  0.7 1.0 %copy-start.3 = (bf16[120,768]{1,0:T(8,128)(2,1)S(1)}, bf16[120,768]{1,0:T(8,128)(2,1)}, u32[]{:S(2)}) copy-start(bf16[120,768]{1,0:T(8,128)(2,1)} %refs_0_.1) | copy-start | bytes 552964
  2.7 8.1 %copy-start.4 = (s32[768]{0:T(1024)S(1)}, s32[768]{0:T(1024)}, u32[]{:S(2)}) copy-start(s32[768]{0:T(1024)} %refs_3_.1) | copy-start | bytes 9220
  2.7 35.9 %all-to-all-start = ((bf16[32,96,120]{2,1,0:T(8,128)(2,1)}), bf16[32,96,120]{2,1,0:T(8,128)(2,1)S(1)}, u32[]{:S(2)}, u32[]{:S(2)}) async-start(bf16[32,96,120]{2,1,0:T(8,128)(2,1)} %shard_map.84), calls=%async_computation | async-start | bytes 1572864 | tf_op jit(solution)/shard_map/all_to_all | solution.py:385
  10.1 0.7 collective-permute-start
  12.5 11.7 %collective-permute-start.1 = (bf16[136,1152]{1,0:T(8,128)(2,1)S(1)}, bf16[136,1152]{1,0:T(8,128)(2,1)S(1)}, u32[]{:S(2)}, u32[]{:S(2)}) collective-permute-start(bf16[136,1152]{1,0:T(8,128)(2,1)S(1)} %get-tuple-element.30), channel_id=1, source_target_pairs={{0,5},{1,4},{2,7},{3,6},{4,1},{5,0},{6,3},{7,2},{8,13},{9,12},{10,... | collective-permute-start | bytes 940040 | tf_op jit(solution)/shard_map/ppermute | solution.py:399
  15.1 13.1 %collective-permute-start.2 = (bf16[136,1152]{1,0:T(8,128)(2,1)S(1)}, bf16[136,1152]{1,0:T(8,128)(2,1)S(1)}, u32[]{:S(2)}, u32[]{:S(2)}) collective-permute-start(bf16[136,1152]{1,0:T(8,128)(2,1)S(1)} %get-tuple-element.31), channel_id=1, source_target_pairs={{0,1},{1,0},{2,3},{3,2},{4,5},{5,4},{6,7},{7,6},{8,9},{9,8},{10,11... | collective-permute-start | bytes 940040 | tf_op jit(solution)/shard_map/ppermute | solution.py:399
  15.7 13.3 %collective-permute-start.3 = (bf16[136,1152]{1,0:T(8,128)(2,1)S(1)}, bf16[136,1152]{1,0:T(8,128)(2,1)S(1)}, u32[]{:S(2)}, u32[]{:S(2)}) collective-permute-start(bf16[136,1152]{1,0:T(8,128)(2,1)S(1)} %get-tuple-element.32), channel_id=1, source_target_pairs={{0,4},{1,5},{2,6},{3,7},{4,0},{5,1},{6,2},{7,3},{8,12},{9,13},{10,... | collective-permute-start | bytes 940040 | tf_op jit(solution)/shard_map/ppermute | solution.py:399
  29.0 7.2 %copy-start.5 = (f32[768]{0:T(1024)S(1)}, f32[768]{0:T(1024)}, u32[]{:S(2)}) copy-start(f32[768]{0:T(1024)} %param.8) | copy-start | bytes 9220
  29.1 9.5 %collective-permute-start.4 = (bf16[4,136,960]{2,1,0:T(8,128)(2,1)S(1)}, bf16[4,136,960]{2,1,0:T(8,128)(2,1)S(1)}, u32[]{:S(2)}, u32[]{:S(2)}) collective-permute-start(bf16[4,136,960]{2,1,0:T(8,128)(2,1)S(1)} %shard_map.86), channel_id=1, source_target_pairs={{0,2},{1,3},{2,0},{3,1},{4,6},{5,7},{6,4},{7,5},{8,10},{9,11},{10,... | collective-permute-start | bytes 3133448 | tf_op jit(solution)/shard_map/ppermute | solution.py:405
  51.1 15.5 %copy-start.2 = (bf16[4,128,1024]{2,1,0:T(8,128)(2,1)S(1)}, bf16[4,128,1024]{2,1,0:T(8,128)(2,1)}, u32[]{:S(2)}) copy-start(bf16[4,128,1024]{2,1,0:T(8,128)(2,1)} %get-tuple-element.36.refs_0_) | copy-start | bytes 3145732
  51.1 33.2 %all-to-all-start.1 = ((bf16[32,96,122]{2,1,0:T(8,128)(2,1)}), bf16[32,96,122]{2,1,0:T(8,128)(2,1)S(1)}, u32[]{:S(2)}, u32[]{:S(2)}) async-start(bf16[32,96,122]{2,1,0:T(8,128)(2,1)} %get-tuple-element.34), calls=%async_computation.1 | async-start | bytes 1572864 | tf_op jit(solution)/shard_map/all_to_all | solution.py:441
  63.7 2.9 %collective-permute-start.5 = (bf16[4,128,1024]{2,1,0:T(8,128)(2,1)}, bf16[4,128,1024]{2,1,0:T(8,128)(2,1)S(1)}, u32[]{:S(2)}, u32[]{:S(2)}) collective-permute-start(bf16[4,128,1024]{2,1,0:T(8,128)(2,1)} %get-tuple-element.37), channel_id=1, source_target_pairs={{0,2},{1,3},{2,0},{3,1},{4,6},{5,7},{6,4},{7,5},{8,10},{9,11},{10,... | collective-permute-start | bytes 3145736 | tf_op jit(solution)/shard_map/ppermute | solution.py:442
  67.1 18.1 %collective-permute-start.6 = (bf16[128,1152]{1,0:T(8,128)(2,1)S(1)}, bf16[128,1152]{1,0:T(8,128)(2,1)S(1)}, u32[]{:S(2)}, u32[]{:S(2)}) collective-permute-start(bf16[128,1152]{1,0:T(8,128)(2,1)S(1)} %get-tuple-element.39), channel_id=1, source_target_pairs={{0,5},{1,4},{2,7},{3,6},{4,1},{5,0},{6,3},{7,2},{8,13},{9,12},{10,... | collective-permute-start | bytes 884744 | tf_op jit(solution)/shard_map/ppermute | solution.py:450
  69.8 19.0 %collective-permute-start.7 = (bf16[128,1152]{1,0:T(8,128)(2,1)S(1)}, bf16[128,1152]{1,0:T(8,128)(2,1)S(1)}, u32[]{:S(2)}, u32[]{:S(2)}) collective-permute-start(bf16[128,1152]{1,0:T(8,128)(2,1)S(1)} %get-tuple-element.40), channel_id=1, source_target_pairs={{0,1},{1,0},{2,3},{3,2},{4,5},{5,4},{6,7},{7,6},{8,9},{9,8},{10,11... | collective-permute-start | bytes 884744 | tf_op jit(solution)/shard_map/ppermute | solution.py:450
  70.4 18.5 %collective-permute-start.8 = (bf16[128,1152]{1,0:T(8,128)(2,1)S(1)}, bf16[128,1152]{1,0:T(8,128)(2,1)S(1)}, u32[]{:S(2)}, u32[]{:S(2)}) collective-permute-start(bf16[128,1152]{1,0:T(8,128)(2,1)S(1)} %get-tuple-element.41), channel_id=1, source_target_pairs={{0,4},{1,5},{2,6},{3,7},{4,0},{5,1},{6,2},{7,3},{8,12},{9,13},{10,... | collective-permute-start | bytes 884744 | tf_op jit(solution)/shard_map/ppermute | solution.py:450

commit v18 on v17

--- a/solution.py
+++ b/solution.py
@@ -117,9 +117,8 @@
 
 def stack_crossing(*refs):
     out_ref = refs[-1]
-    width = out_ref.shape[2]
     for m, ref in enumerate(refs[:-1]):
-        out_ref[m] = ref[:, :width]
+        out_ref[m, :, : ref.shape[1]] = ref[...]
 
 
 def normalize(x, gains):
@@ -401,7 +400,7 @@
     ]
     both_cores = []
     for group in ((cross, *arrived),):
-        crossing = called(stack_crossing, shape_of((len(group), block, slim), bf16), group, 8)
+        crossing = called(stack_crossing, shape_of((len(group), block, slim + 2 * part), bf16), group, 8)
         both_cores.append(lax.ppermute(crossing, RANK, flipped_pairs(ranks, core)))
     home = pltpu.with_memory_space_constraint(home, pltpu.HBM)
     held = (pieces, home, *arrived, *both_cores)
@@ -416,7 +415,7 @@
         scratch=[
             pltpu.VMEM(pieces.shape, bf16),
             pltpu.VMEM(home.shape, bf16),
-            pltpu.VMEM((len(masks), block, slim), bf16),
+            pltpu.VMEM((len(masks), block, slim + 2 * part), bf16),
             pltpu.VMEM((len(arrived), *arrived[0].shape), bf16),
             pltpu.VMEM((strands, span, channels), bf16),
             pltpu.VMEM((strands, span, LANES), f32),

time: 90.8 us -> 83.6 us (0.921)
  starting transfers between devices: 35 us -> 23.6 us
  waiting for transfers between devices: 35.3 us -> 37.1 us
  Pallas kernels: 18.4 us -> 20 us
    all_to_all x1, waiting for transfers between devices: 0.01 us -> 9.45 us  [per_device(): pieces = lax.all_to_all(slices, EVERY, 0, 0, tiled=True)]
    all_to_all x1, starting transfers between devices: 12.6 us -> 3.62 us  [per_device(): terms = lax.all_to_all(outgoing, EVERY, 0, 0, tiled=True)]
    ppermute x1, starting transfers between devices: 7.14 us -> 2.3 us  [per_device(): both_cores.append(lax.ppermute(crossing, RANK, flipped_pairs(ranks, core)))]
    ppermute x6, waiting for transfers between devices: 16.7 us -> 11.9 us  [per_device(): lax.ppermute(message, RANK, flipped_pairs(ranks, mask))]
    ppermute x1, waiting for transfers between devices: 2.37 us -> 0.01 us  [per_device(): both_cores.append(lax.ppermute(crossing, RANK, flipped_pairs(ranks, core)))]
    pallas_call x7, Pallas kernels: 18.4 us -> 20 us  [called(): pl.pallas_call(body, out_shape=outs, in_specs=specs or [VMEM] * len(args)...]
    all_to_all x1, starting transfers between devices: 7.3 us -> 8.72 us  [per_device(): pieces = lax.all_to_all(slices, EVERY, 0, 0, tiled=True)]
  transfers between devices with their start and end apart: 11 -> 11, of which waited for: 7 -> 6; matrix products, arithmetic and copies ran while one was open for 0% -> 0% of each run, Pallas kernels for 4% -> 5%
where the time goes in v18:
time: 83.6 us; the launch traced here: 83.2 us
  waiting for transfers between devices  37.1 us (44%)
  starting transfers between devices  23.6 us (28%)
  Pallas kernels  20 us (24%)
  local copies, waits for them, and re-layouts  0.94 us (1%)
    pallas_call x7, Pallas kernels, called(): pl.pallas_call(body, out_shape=outs, in_specs=specs or [VMEM] * len(args)...  20 us
    all_to_all x1, waiting for transfers between devices, per_device(): terms = lax.all_to_all(outgoing, EVERY, 0, 0, tiled=True)  13.1 us
    ppermute x6, waiting for transfers between devices, per_device(): lax.ppermute(message, RANK, flipped_pairs(ranks, mask))  11.9 us
    all_to_all x1, waiting for transfers between devices, per_device(): pieces = lax.all_to_all(slices, EVERY, 0, 0, tiled=True)  9.45 us
    all_to_all x1, starting transfers between devices, per_device(): pieces = lax.all_to_all(slices, EVERY, 0, 0, tiled=True)  8.72 us
    ppermute x6, starting transfers between devices, per_device(): lax.ppermute(message, RANK, flipped_pairs(ranks, mask))  7.95 us
    all_to_all x1, starting transfers between devices, per_device(): terms = lax.all_to_all(outgoing, EVERY, 0, 0, tiled=True)  3.62 us
    ppermute x1, waiting for transfers between devices, per_device(): crossed = lax.ppermute(cross, RANK, flipped_pairs(ranks, core))  2.62 us
  transfers between devices with their start and end apart: 11, of which 6 were waited for; matrix products, arithmetic and copies ran while one was open for 0% of the time, Pallas kernels for 5%

profile of v18, /device:TPU:0, one launch (start us, length us, event | category | flops | bytes accessed | tf_op | source)
XLA Modules:
  0.0 83.2 jit_solution(16536176833425864315)
XLA Ops:
  0.6 0.0 copy-start.1
  0.6 0.0 copy-start
  0.7 0.0 copy-start.4
  0.7 0.8 fusion
  1.5 0.7 collective-permute-start
  2.2 0.0 copy-start.3
  2.2 0.9 %copy-done.3 = bf16[120,768]{1,0:T(8,128)(2,1)S(1)} copy-done((bf16[120,768]{1,0:T(8,128)(2,1)S(1)}, bf16[120,768]{1,0:T(8,128)(2,1)}, u32[]{:S(2)}) %copy-start.3) | copy-done | bytes 184344
  3.1 1.1 %shard_map.84 = bf16[32,96,120]{2,1,0:T(8,128)(2,1)} custom-call(bf16[120,768]{1,0:T(8,128)(2,1)S(1)} %copy-done.3), custom_call_target="tpu_custom_call" | custom-call | tf_op jit(solution)/shard_map/pallas_call | solution.py:24
  4.2 0.0 collective-permute-done.refs_3_
  4.2 0.0 copy-done.1
  4.2 0.0 copy-done
  4.2 0.0 copy-done.4
  4.2 1.7 %shard_map.85 = (bf16[136,960]{1,0:T(8,128)(2,1)}, bf16[136,960]{1,0:T(8,128)(2,1)S(1)}, bf16[136,1152]{1,0:T(8,128)(2,1)S(1)}, bf16[136,1152]{1,0:T(8,128)(2,1)S(1)}, bf16[136,1152]{1,0:T(8,128)(2,1)S(1)}) custom-call(s32[1]{0:T(128)} %bitcast.refs_0_, bf16[128,768]{1,0:T(8,128)(2,1)S(1)} %bitcast.7, bf16[128,768]{1,0:T(8,128)(2,1)S(1)} %bitcast.10, ...), custom_call_target="tpu_custom_call" | custom-call | tf_op jit(solution)/shard_map/pallas_call | solution.py:24
  5.9 3.9 %collective-permute-start.1 = (bf16[136,1152]{1,0:T(8,128)(2,1)S(1)}, bf16[136,1152]{1,0:T(8,128)(2,1)S(1)}, u32[]{:S(2)}, u32[]{:S(2)}) collective-permute-start(bf16[136,1152]{1,0:T(8,128)(2,1)S(1)} %get-tuple-element.30), channel_id=1, source_target_pairs={{0,5},{1,4},{2,7},{3,6},{4,1},{5,0},{6,3},{7,2},{8,13},{9,12},{10,... | collective-permute-start | bytes 940040 | tf_op jit(solution)/shard_map/ppermute | solution.py:398
  9.8 0.5 collective-permute-start.2
  10.3 0.1 collective-permute-start.3
  10.4 8.7 %all-to-all-start = ((bf16[32,96,120]{2,1,0:T(8,128)(2,1)}), bf16[32,96,120]{2,1,0:T(8,128)(2,1)S(1)}, u32[]{:S(2)}, u32[]{:S(2)}) async-start(bf16[32,96,120]{2,1,0:T(8,128)(2,1)} %shard_map.84), calls=%async_computation | async-start | bytes 1572864 | tf_op jit(solution)/shard_map/all_to_all | solution.py:384
  19.1 0.0 copy-start.5
  19.1 0.0 collective-permute-done.1.refs_1_.refs_3_
  19.1 7.7 %collective-permute-done.2.refs_2_.refs_4_ = bf16[136,1152]{1,0:T(8,128)(2,1)S(1)} collective-permute-done((bf16[136,1152]{1,0:T(8,128)(2,1)S(1)}, bf16[136,1152]{1,0:T(8,128)(2,1)S(1)}, u32[]{:S(2)}, u32[]{:S(2)}) %collective-permute-start.2) | collective-permute-done | bytes 313376 | tf_op jit(solution)/shard_map/ppermute | solution.py:398
  26.8 0.0 collective-permute-done.3.refs_3_.refs_5_
  26.8 1.2 %shard_map.86 = bf16[4,136,1152]{2,1,0:T(8,128)(2,1)} custom-call(bf16[136,960]{1,0:T(8,128)(2,1)S(1)} %get-tuple-element.33.refs_0_, bf16[136,1152]{1,0:T(8,128)(2,1)S(1)} %collective-permute-done.1.refs_1_.refs_3_, bf16[136,1152]{1,0:T(8,128)(2,1)S(1)} %collective-permute-done.2.refs_2_.refs_4_, bf16[136,1152]{1,0:T(8,128)(2,1)S(1)} %collective-permute-done.3.refs_3_.refs_5_), custom_call_target="tpu_custom_call" | custom-call | tf_op jit(solution)/shard_map/pallas_call | solution.py:24
  28.0 2.3 %collective-permute-start.4 = (bf16[4,136,1152]{2,1,0:T(8,128)(2,1)}, bf16[4,136,1152]{2,1,0:T(8,128)(2,1)S(1)}, u32[]{:S(2)}, u32[]{:S(2)}) collective-permute-start(bf16[4,136,1152]{2,1,0:T(8,128)(2,1)} %shard_map.86), channel_id=1, source_target_pairs={{0,2},{1,3},{2,0},{3,1},{4,6},{5,7},{6,4},{7,5},{8,10},{9,11},{10,... | collective-permute-start | bytes 3760136 | tf_op jit(solution)/shard_map/ppermute | solution.py:404
  30.3 0.0 copy-done.5
  30.3 9.4 %all-to-all-done.refs_1_ = bf16[32,96,120]{2,1,0:T(8,128)(2,1)S(1)} async-done(((bf16[32,96,120]{2,1,0:T(8,128)(2,1)}), bf16[32,96,120]{2,1,0:T(8,128)(2,1)S(1)}, u32[]{:S(2)}, u32[]{:S(2)}) %all-to-all-start) | async-done | bytes 737312 | tf_op jit(solution)/shard_map/all_to_all | solution.py:384
  39.7 0.0 collective-permute-done.4.refs_6_
  39.7 12.5 %shard_map.87 = (bf16[32,96,122]{2,1,0:T(8,128)(2,1)}, bf16[4,128,1024]{2,1,0:T(8,128)(2,1)}, bf16[4,128,1024]{2,1,0:T(8,128)(2,1)}) custom-call(s32[1]{0:T(128)} %bitcast.refs_0_, bf16[32,96,120]{2,1,0:T(8,128)(2,1)S(1)} %all-to-all-done.refs_1_, bf16[136,960]{1,0:T(8,128)(2,1)} %get-tuple-element.29.refs_2_, ...), custom_call_target="tpu_custom_call" | custom-call | tf_op jit(solution)/shard_map/pallas_call | solution.py:24
  52.2 0.0 copy-start.2
  52.2 3.6 %all-to-all-start.1 = ((bf16[32,96,122]{2,1,0:T(8,128)(2,1)}), bf16[32,96,122]{2,1,0:T(8,128)(2,1)S(1)}, u32[]{:S(2)}, u32[]{:S(2)}) async-start(bf16[32,96,122]{2,1,0:T(8,128)(2,1)} %get-tuple-element.34), calls=%async_computation.1 | async-start | bytes 1572864 | tf_op jit(solution)/shard_map/all_to_all | solution.py:440
  55.8 0.3 collective-permute-start.5
  56.1 2.6 %collective-permute-done.5.refs_1_ = bf16[4,128,1024]{2,1,0:T(8,128)(2,1)S(1)} collective-permute-done((bf16[4,128,1024]{2,1,0:T(8,128)(2,1)}, bf16[4,128,1024]{2,1,0:T(8,128)(2,1)S(1)}, u32[]{:S(2)}, u32[]{:S(2)}) %collective-permute-start.5) | collective-permute-done | bytes 1048608 | tf_op jit(solution)/shard_map/ppermute | solution.py:441
  58.8 0.0 copy-done.2
  58.8 1.1 %shard_map.89 = (bf16[128,1152]{1,0:T(8,128)(2,1)S(1)}, bf16[128,1152]{1,0:T(8,128)(2,1)}, bf16[128,1152]{1,0:T(8,128)(2,1)S(1)}, bf16[128,1152]{1,0:T(8,128)(2,1)S(1)}) custom-call(bf16[4,128,1024]{2,1,0:T(8,128)(2,1)S(1)} %copy-done.2, bf16[4,128,1024]{2,1,0:T(8,128)(2,1)S(1)} %collective-permute-done.5.refs_1_), custom_call_target="tpu_custom_call" | custom-call | tf_op jit(solution)/shard_map/pallas_call | solution.py:24
  59.9 2.7 %collective-permute-start.6 = (bf16[128,1152]{1,0:T(8,128)(2,1)}, bf16[128,1152]{1,0:T(8,128)(2,1)S(1)}, u32[]{:S(2)}, u32[]{:S(2)}) collective-permute-start(bf16[128,1152]{1,0:T(8,128)(2,1)} %get-tuple-element.39), channel_id=1, source_target_pairs={{0,5},{1,4},{2,7},{3,6},{4,1},{5,0},{6,3},{7,2},{8,13},{9,12},{10,... | collective-permute-start | bytes 884744 | tf_op jit(solution)/shard_map/ppermute | solution.py:449
  62.5 0.6 collective-permute-start.7
  63.1 0.3 collective-permute-start.8
  63.4 13.1 %all-to-all-done.1.refs_0_ = bf16[32,96,122]{2,1,0:T(8,128)(2,1)S(1)} async-done(((bf16[32,96,122]{2,1,0:T(8,128)(2,1)}), bf16[32,96,122]{2,1,0:T(8,128)(2,1)S(1)}, u32[]{:S(2)}, u32[]{:S(2)}) %all-to-all-start.1) | async-done | bytes 749600 | tf_op jit(solution)/shard_map/all_to_all | solution.py:440
  76.5 1.0 %shard_map.88 = (f32[120,768]{1,0:T(8,128)}, f32[1,24]{1,0:T(1,128)}) custom-call(bf16[32,96,122]{2,1,0:T(8,128)(2,1)S(1)} %all-to-all-done.1.refs_0_), custom_call_target="tpu_custom_call" | custom-call | tf_op jit(solution)/shard_map/pallas_call | solution.py:24
  77.4 0.0 collective-permute-done.6.refs_5_
  77.4 3.9 %collective-permute-done.7.refs_6_ = bf16[128,1152]{1,0:T(8,128)(2,1)S(1)} collective-permute-done((bf16[128,1152]{1,0:T(8,128)(2,1)S(1)}, bf16[128,1152]{1,0:T(8,128)(2,1)S(1)}, u32[]{:S(2)}, u32[]{:S(2)}) %collective-permute-start.7) | collective-permute-done | bytes 294944 | tf_op jit(solution)/shard_map/ppermute | solution.py:449
  81.3 0.4 collective-permute-done.8.refs_7_
  81.7 1.6 %shard_map.90 = (bf16[128,768]{1,0:T(8,128)(2,1)}, bf16[128,768]{1,0:T(8,128)(2,1)}) custom-call(s32[1]{0:T(128)} %bitcast.refs_0_, bf16[128,768]{1,0:T(8,128)(2,1)S(1)} %bitcast.8, bf16[128,768]{1,0:T(8,128)(2,1)S(1)} %bitcast.11, s32[768]{0:T(1024)S(1)} %copy-done.4, bf16[128,1152]{1,0:T(8,128)(2,1)S(1)} %get-tuple-element.42.refs_4_, ...), custom_call_target="tpu_custom_call" | custom-call | tf_op jit(solution)/shard_map/pallas_call | solution.py:24
  (1 shorter events, 0.0 us)
Async XLA Ops:
  0.6 3.6 %copy-start.1 = (bf16[1,128,768]{2,1,0:T(8,128)(2,1)S(1)}, bf16[1,128,768]{2,1,0:T(8,128)(2,1)}, u32[]{:S(2)}) copy-start(bf16[1,128,768]{2,1,0:T(8,128)(2,1)} %param.6) | copy-start | bytes 589828
  0.6 3.6 %copy-start = (bf16[1,128,768]{2,1,0:T(8,128)(2,1)S(1)}, bf16[1,128,768]{2,1,0:T(8,128)(2,1)}, u32[]{:S(2)}) copy-start(bf16[1,128,768]{2,1,0:T(8,128)(2,1)} %param.5) | copy-start | bytes 589828
  0.7 3.6 %copy-start.4 = (s32[768]{0:T(1024)S(1)}, s32[768]{0:T(1024)}, u32[]{:S(2)}) copy-start(s32[768]{0:T(1024)} %refs_3_.1) | copy-start | bytes 9220
  1.5 2.7 %collective-permute-start = (bf16[8,1536]{1,0:T(8,128)(2,1)S(1)}, bf16[8,1536]{1,0:T(8,128)(2,1)S(1)}, u32[]{:S(2)}, u32[]{:S(2)}) collective-permute-start(bf16[8,1536]{1,0:T(8,128)(2,1)S(1)} %fusion), channel_id=1, source_target_pairs={{6,8},{14,16},{22,24},{8,6},{16,14},{24,22},{7,9},{15,17},{23,25},... | collective-permute-start | bytes 73736 | tf_op jit(solution)/shard_map/ppermute | solution.py:362
  2.2 0.9 %copy-start.3 = (bf16[120,768]{1,0:T(8,128)(2,1)S(1)}, bf16[120,768]{1,0:T(8,128)(2,1)}, u32[]{:S(2)}) copy-start(bf16[120,768]{1,0:T(8,128)(2,1)} %refs_0_.1) | copy-start | bytes 552964
  5.9 13.2 %collective-permute-start.1 = (bf16[136,1152]{1,0:T(8,128)(2,1)S(1)}, bf16[136,1152]{1,0:T(8,128)(2,1)S(1)}, u32[]{:S(2)}, u32[]{:S(2)}) collective-permute-start(bf16[136,1152]{1,0:T(8,128)(2,1)S(1)} %get-tuple-element.30), channel_id=1, source_target_pairs={{0,5},{1,4},{2,7},{3,6},{4,1},{5,0},{6,3},{7,2},{8,13},{9,12},{10,... | collective-permute-start | bytes 940040 | tf_op jit(solution)/shard_map/ppermute | solution.py:398
  9.8 17.0 %collective-permute-start.2 = (bf16[136,1152]{1,0:T(8,128)(2,1)S(1)}, bf16[136,1152]{1,0:T(8,128)(2,1)S(1)}, u32[]{:S(2)}, u32[]{:S(2)}) collective-permute-start(bf16[136,1152]{1,0:T(8,128)(2,1)S(1)} %get-tuple-element.31), channel_id=1, source_target_pairs={{0,1},{1,0},{2,3},{3,2},{4,5},{5,4},{6,7},{7,6},{8,9},{9,8},{10,11... | collective-permute-start | bytes 940040 | tf_op jit(solution)/shard_map/ppermute | solution.py:398
  10.3 16.5 %collective-permute-start.3 = (bf16[136,1152]{1,0:T(8,128)(2,1)S(1)}, bf16[136,1152]{1,0:T(8,128)(2,1)S(1)}, u32[]{:S(2)}, u32[]{:S(2)}) collective-permute-start(bf16[136,1152]{1,0:T(8,128)(2,1)S(1)} %get-tuple-element.32), channel_id=1, source_target_pairs={{0,4},{1,5},{2,6},{3,7},{4,0},{5,1},{6,2},{7,3},{8,12},{9,13},{10,... | collective-permute-start | bytes 940040 | tf_op jit(solution)/shard_map/ppermute | solution.py:398
  10.4 29.3 %all-to-all-start = ((bf16[32,96,120]{2,1,0:T(8,128)(2,1)}), bf16[32,96,120]{2,1,0:T(8,128)(2,1)S(1)}, u32[]{:S(2)}, u32[]{:S(2)}) async-start(bf16[32,96,120]{2,1,0:T(8,128)(2,1)} %shard_map.84), calls=%async_computation | async-start | bytes 1572864 | tf_op jit(solution)/shard_map/all_to_all | solution.py:384
  19.1 11.2 %copy-start.5 = (f32[768]{0:T(1024)S(1)}, f32[768]{0:T(1024)}, u32[]{:S(2)}) copy-start(f32[768]{0:T(1024)} %param.8) | copy-start | bytes 9220
  28.0 11.8 %collective-permute-start.4 = (bf16[4,136,1152]{2,1,0:T(8,128)(2,1)}, bf16[4,136,1152]{2,1,0:T(8,128)(2,1)S(1)}, u32[]{:S(2)}, u32[]{:S(2)}) collective-permute-start(bf16[4,136,1152]{2,1,0:T(8,128)(2,1)} %shard_map.86), channel_id=1, source_target_pairs={{0,2},{1,3},{2,0},{3,1},{4,6},{5,7},{6,4},{7,5},{8,10},{9,11},{10,... | collective-permute-start | bytes 3760136 | tf_op jit(solution)/shard_map/ppermute | solution.py:404
  52.2 6.6 %copy-start.2 = (bf16[4,128,1024]{2,1,0:T(8,128)(2,1)S(1)}, bf16[4,128,1024]{2,1,0:T(8,128)(2,1)}, u32[]{:S(2)}) copy-start(bf16[4,128,1024]{2,1,0:T(8,128)(2,1)} %get-tuple-element.36.refs_0_) | copy-start | bytes 3145732
  52.2 24.3 %all-to-all-start.1 = ((bf16[32,96,122]{2,1,0:T(8,128)(2,1)}), bf16[32,96,122]{2,1,0:T(8,128)(2,1)S(1)}, u32[]{:S(2)}, u32[]{:S(2)}) async-start(bf16[32,96,122]{2,1,0:T(8,128)(2,1)} %get-tuple-element.34), calls=%async_computation.1 | async-start | bytes 1572864 | tf_op jit(solution)/shard_map/all_to_all | solution.py:440
  55.8 2.9 %collective-permute-start.5 = (bf16[4,128,1024]{2,1,0:T(8,128)(2,1)}, bf16[4,128,1024]{2,1,0:T(8,128)(2,1)S(1)}, u32[]{:S(2)}, u32[]{:S(2)}) collective-permute-start(bf16[4,128,1024]{2,1,0:T(8,128)(2,1)} %get-tuple-element.37), channel_id=1, source_target_pairs={{0,2},{1,3},{2,0},{3,1},{4,6},{5,7},{6,4},{7,5},{8,10},{9,11},{10,... | collective-permute-start | bytes 3145736 | tf_op jit(solution)/shard_map/ppermute | solution.py:441
  59.9 17.6 %collective-permute-start.6 = (bf16[128,1152]{1,0:T(8,128)(2,1)}, bf16[128,1152]{1,0:T(8,128)(2,1)S(1)}, u32[]{:S(2)}, u32[]{:S(2)}) collective-permute-start(bf16[128,1152]{1,0:T(8,128)(2,1)} %get-tuple-element.39), channel_id=1, source_target_pairs={{0,5},{1,4},{2,7},{3,6},{4,1},{5,0},{6,3},{7,2},{8,13},{9,12},{10,... | collective-permute-start | bytes 884744 | tf_op jit(solution)/shard_map/ppermute | solution.py:449
  62.5 18.8 %collective-permute-start.7 = (bf16[128,1152]{1,0:T(8,128)(2,1)S(1)}, bf16[128,1152]{1,0:T(8,128)(2,1)S(1)}, u32[]{:S(2)}, u32[]{:S(2)}) collective-permute-start(bf16[128,1152]{1,0:T(8,128)(2,1)S(1)} %get-tuple-element.40), channel_id=1, source_target_pairs={{0,1},{1,0},{2,3},{3,2},{4,5},{5,4},{6,7},{7,6},{8,9},{9,8},{10,11... | collective-permute-start | bytes 884744 | tf_op jit(solution)/shard_map/ppermute | solution.py:449
  63.1 18.6 %collective-permute-start.8 = (bf16[128,1152]{1,0:T(8,128)(2,1)S(1)}, bf16[128,1152]{1,0:T(8,128)(2,1)S(1)}, u32[]{:S(2)}, u32[]{:S(2)}) collective-permute-start(bf16[128,1152]{1,0:T(8,128)(2,1)S(1)} %get-tuple-element.41), channel_id=1, source_target_pairs={{0,4},{1,5},{2,6},{3,7},{4,0},{5,1},{6,2},{7,3},{8,12},{9,13},{10,... | collective-permute-start | bytes 884744 | tf_op jit(solution)/shard_map/ppermute | solution.py:449

commit v19 on v15

--- a/solution.py
+++ b/solution.py
@@ -152,8 +152,7 @@
     got_blocks += [moves.start(block, arrived.at[m]) for m, block in enumerate(arrived_in)]
     per = chips // groups
     got_blocks += [moves.start(crossed_in[m // per].at[m % per], crossed.at[m]) for m in range(chips)]
-    got_pieces = moves.start(pieces_in, pieces)
-    arrivals = len(moves.copies)
+    got_pieces = None
     masks = chip_masks(2 * chips, core)
     seq_ranks = 2 * chips // dp_ranks
     positions = home.shape[0] - HALO
@@ -165,6 +164,8 @@
     blocks += [(mask | core, crossed.at[m], channels) for m, mask in enumerate(masks)]
     for got, (flip, ref, lane) in zip(got_blocks, blocks):
         got.wait()
+        if got is got_blocks[1]:
+            got_pieces = moves.start(pieces_in, pieces)
         source = lax.bitwise_xor(rank_ref[0], flip)
         b, i = lax.rem(source, dp_ranks), lax.div(source, dp_ranks)
         start = pl.multiple_of(i * positions, positions)
@@ -193,6 +194,7 @@
             first += count
 
     got_pieces.wait()
+    arrivals = len(moves.copies)
     for owner in range(owners):
         for tap, channel, count, offset in runs(owner):
             kernel_ref[tap * part : (tap + 1) * part, channel : channel + count] = pieces[
@@ -259,8 +261,9 @@
             dot(shifted_ref[b], kernels[0], ((1,), (0,))) * gains[0]
             + dot(shifted_ref[dp_ranks + b], kernels[1], ((1,), (0,))) * gains[1]
         ).astype(bf16)
+    order = [*range(1, chips), 0]
     for out, target_out, flip in ((cross, cross_out, core), (own, own_out, 0)):
-        for m, mask in enumerate(masks):
+        for m, mask in [(m, masks[m]) for m in order]:
             target = lax.bitwise_xor(rank_ref[0], mask | flip)
             b = lax.rem(target, dp_ranks)
             start = pl.multiple_of(lax.div(target, dp_ranks) * positions, positions)
@@ -268,7 +271,7 @@
             for n in range(2):
                 lane = channels + n * LANES
                 out[m, :, lane : lane + LANES] = gelu_ref[n * dp_ranks + b, pl.ds(start, positions), :]
-        moves.start(out, target_out)
+            moves.start(out.at[m], target_out.at[m])
     for copy in moves.copies[arrivals:]:
         copy.wait()
 
@@ -430,7 +433,7 @@
             pltpu.VMEM((dp_ranks, span, channels), bf16),
         ]
         + [pltpu.VMEM(shape, bf16) for shape in shapes]
-        + [pltpu.SemaphoreType.DMA((ranks + 4,))],
+        + [pltpu.SemaphoreType.DMA((2 * ranks + 4,))],
         specs=[SMEM, ANY, HBM] + [ANY] * (len(held) - 2) + [VMEM] * 2,
         out_specs=(HBM,) * 3,
     )

time: 84.1 us -> 84 us (level)
  no operation moved by 1% of the time
where the time goes in v19:
time: 84 us; the launch traced here: 83.7 us
  waiting for transfers between devices  37 us (44%)
  starting transfers between devices  24 us (29%)
  Pallas kernels  20.1 us (24%)
  local copies, waits for them, and re-layouts  0.94 us (1%)
  other arithmetic  0.86 us (1%)
    pallas_call x7, Pallas kernels, called(): pl.pallas_call(body, out_shape=outs, in_specs=specs or [VMEM] * len(args)...  20.1 us
    ppermute x6, waiting for transfers between devices, per_device(): lax.ppermute(message, RANK, flipped_pairs(ranks, mask))  13.4 us
    all_to_all x1, waiting for transfers between devices, per_device(): terms = lax.all_to_all(outgoing, EVERY, 0, 0, tiled=True)  13.1 us
    all_to_all x1, starting transfers between devices, per_device(): pieces = lax.all_to_all(slices, EVERY, 0, 0, tiled=True)  8.99 us
    ppermute x6, starting transfers between devices, per_device(): lax.ppermute(message, RANK, flipped_pairs(ranks, mask))  7.96 us
    all_to_all x1, waiting for transfers between devices, per_device(): pieces = lax.all_to_all(slices, EVERY, 0, 0, tiled=True)  7.9 us
    all_to_all x1, starting transfers between devices, per_device(): terms = lax.all_to_all(outgoing, EVERY, 0, 0, tiled=True)  3.62 us
    ppermute x1, waiting for transfers between devices, per_device(): crossed = lax.ppermute(cross, RANK, flipped_pairs(ranks, core))  2.62 us
  transfers between devices with their start and end apart: 11, of which 6 were waited for; matrix products, arithmetic and copies ran while one was open for 0% of the time, Pallas kernels for 5%

profile of v19, /device:TPU:0, one launch (start us, length us, event | category | flops | bytes accessed | tf_op | source)
XLA Modules:
  0.0 83.7 jit_solution(2530419018975525086)
XLA Ops:
  0.6 0.0 copy-start.1
  0.6 0.0 copy-start
  0.7 0.0 copy-start.4
  0.7 0.9 %fusion = bf16[16,1536]{1,0:T(8,128)(2,1)S(1)} fusion(bf16[128,768]{1,0:T(8,128)(2,1)} %bitcast.9, bf16[128,768]{1,0:T(8,128)(2,1)} %bitcast.6, pred[]{:T(512)S(6)} %eq.3), kind=kLoop, calls=%fused_computation.1 | loop fusion | flops 221184 | bytes 442369 | tf_op jit(solution)/shard_map/jit(_where)/select_n | solution.py:361
  1.5 0.7 collective-permute-start
  2.2 0.0 copy-start.3
  2.2 0.9 %copy-done.3 = bf16[120,768]{1,0:T(8,128)(2,1)S(1)} copy-done((bf16[120,768]{1,0:T(8,128)(2,1)S(1)}, bf16[120,768]{1,0:T(8,128)(2,1)}, u32[]{:S(2)}) %copy-start.3) | copy-done | bytes 184344
  3.1 1.1 %shard_map.84 = bf16[32,96,120]{2,1,0:T(8,128)(2,1)} custom-call(bf16[120,768]{1,0:T(8,128)(2,1)S(1)} %copy-done.3), custom_call_target="tpu_custom_call" | custom-call | tf_op jit(solution)/shard_map/pallas_call | solution.py:23
  4.2 0.0 collective-permute-done.refs_3_
  4.2 0.0 copy-done.1
  4.2 0.0 copy-done
  4.2 0.0 copy-done.4
  4.3 1.8 %shard_map.85 = (bf16[144,960]{1,0:T(8,128)(2,1)}, bf16[144,960]{1,0:T(8,128)(2,1)S(1)}, bf16[144,1152]{1,0:T(8,128)(2,1)}, bf16[144,1152]{1,0:T(8,128)(2,1)S(1)}, bf16[144,1152]{1,0:T(8,128)(2,1)S(1)}) custom-call(s32[1]{0:T(128)} %bitcast.refs_0_, bf16[128,768]{1,0:T(8,128)(2,1)S(1)} %bitcast.7, bf16[128,768]{1,0:T(8,128)(2,1)S(1)} %bitcast.10, ...), custom_call_target="tpu_custom_call" | custom-call | tf_op jit(solution)/shard_map/pallas_call | solution.py:23
  6.1 3.9 %collective-permute-start.1 = (bf16[144,1152]{1,0:T(8,128)(2,1)}, bf16[144,1152]{1,0:T(8,128)(2,1)S(1)}, u32[]{:S(2)}, u32[]{:S(2)}) collective-permute-start(bf16[144,1152]{1,0:T(8,128)(2,1)} %get-tuple-element.30), channel_id=1, source_target_pairs={{0,5},{1,4},{2,7},{3,6},{4,1},{5,0},{6,3},{7,2},{8,13},{9,12},{10,... | collective-permute-start | bytes 995336 | tf_op jit(solution)/shard_map/ppermute | solution.py:398
  10.0 0.5 collective-permute-start.2
  10.5 0.1 collective-permute-start.3
  10.5 9.0 %all-to-all-start = ((bf16[32,96,120]{2,1,0:T(8,128)(2,1)}), bf16[32,96,120]{2,1,0:T(8,128)(2,1)S(1)}, u32[]{:S(2)}, u32[]{:S(2)}) async-start(bf16[32,96,120]{2,1,0:T(8,128)(2,1)} %shard_map.84), calls=%async_computation | async-start | bytes 1572864 | tf_op jit(solution)/shard_map/all_to_all | solution.py:384
  19.5 0.0 collective-permute-done.1.refs_1_.refs_3_
  19.5 9.1 %collective-permute-done.2.refs_2_.refs_4_ = bf16[144,1152]{1,0:T(8,128)(2,1)S(1)} collective-permute-done((bf16[144,1152]{1,0:T(8,128)(2,1)S(1)}, bf16[144,1152]{1,0:T(8,128)(2,1)S(1)}, u32[]{:S(2)}, u32[]{:S(2)}) %collective-permute-start.2) | collective-permute-done | bytes 331808 | tf_op jit(solution)/shard_map/ppermute | solution.py:398
  28.7 0.0 collective-permute-done.3.refs_3_.refs_5_
  28.7 0.0 copy-start.5
  28.7 1.1 %shard_map.86 = bf16[4,144,960]{2,1,0:T(8,128)(2,1)} custom-call(bf16[144,960]{1,0:T(8,128)(2,1)S(1)} %get-tuple-element.33.refs_0_, bf16[144,1152]{1,0:T(8,128)(2,1)S(1)} %collective-permute-done.1.refs_1_.refs_3_, bf16[144,1152]{1,0:T(8,128)(2,1)S(1)} %collective-permute-done.2.refs_2_.refs_4_, bf16[144,1152]{1,0:T(8,128)(2,1)S(1)} %collective-permute-done.3.refs_3_.refs_5_), custom_call_target="tpu_custom_call" | custom-call | tf_op jit(solution)/shard_map/pallas_call | solution.py:23
  29.8 2.5 %collective-permute-start.4 = (bf16[4,144,960]{2,1,0:T(8,128)(2,1)}, bf16[4,144,960]{2,1,0:T(8,128)(2,1)S(1)}, u32[]{:S(2)}, u32[]{:S(2)}) collective-permute-start(bf16[4,144,960]{2,1,0:T(8,128)(2,1)} %shard_map.86), channel_id=1, source_target_pairs={{0,2},{1,3},{2,0},{3,1},{4,6},{5,7},{6,4},{7,5},{8,10},{9,11},{10,... | collective-permute-start | bytes 3317768 | tf_op jit(solution)/shard_map/ppermute | solution.py:404
  32.2 0.0 copy-done.5
  32.2 7.9 %all-to-all-done.refs_1_ = bf16[32,96,120]{2,1,0:T(8,128)(2,1)S(1)} async-done(((bf16[32,96,120]{2,1,0:T(8,128)(2,1)}), bf16[32,96,120]{2,1,0:T(8,128)(2,1)S(1)}, u32[]{:S(2)}, u32[]{:S(2)}) %all-to-all-start) | async-done | bytes 737312 | tf_op jit(solution)/shard_map/all_to_all | solution.py:384
  40.1 0.0 collective-permute-done.4.refs_6_
  40.1 12.5 %shard_map.87 = (bf16[32,96,122]{2,1,0:T(8,128)(2,1)}, bf16[4,128,1024]{2,1,0:T(8,128)(2,1)}, bf16[4,128,1024]{2,1,0:T(8,128)(2,1)}) custom-call(s32[1]{0:T(128)} %bitcast.refs_0_, bf16[32,96,120]{2,1,0:T(8,128)(2,1)S(1)} %all-to-all-done.refs_1_, bf16[144,960]{1,0:T(8,128)(2,1)} %get-tuple-element.29.refs_2_, ...), custom_call_target="tpu_custom_call" | custom-call | tf_op jit(solution)/shard_map/pallas_call | solution.py:23
  52.7 0.0 copy-start.2
  52.7 3.6 %all-to-all-start.1 = ((bf16[32,96,122]{2,1,0:T(8,128)(2,1)}), bf16[32,96,122]{2,1,0:T(8,128)(2,1)S(1)}, u32[]{:S(2)}, u32[]{:S(2)}) async-start(bf16[32,96,122]{2,1,0:T(8,128)(2,1)} %get-tuple-element.34), calls=%async_computation.1 | async-start | bytes 1572864 | tf_op jit(solution)/shard_map/all_to_all | solution.py:440
  56.3 0.3 collective-permute-start.5
  56.6 2.6 %collective-permute-done.5.refs_1_ = bf16[4,128,1024]{2,1,0:T(8,128)(2,1)S(1)} collective-permute-done((bf16[4,128,1024]{2,1,0:T(8,128)(2,1)}, bf16[4,128,1024]{2,1,0:T(8,128)(2,1)S(1)}, u32[]{:S(2)}, u32[]{:S(2)}) %collective-permute-start.5) | collective-permute-done | bytes 1048608 | tf_op jit(solution)/shard_map/ppermute | solution.py:441
  59.2 0.0 copy-done.2
  59.2 1.1 %shard_map.89 = (bf16[128,1152]{1,0:T(8,128)(2,1)S(1)}, bf16[128,1152]{1,0:T(8,128)(2,1)}, bf16[128,1152]{1,0:T(8,128)(2,1)S(1)}, bf16[128,1152]{1,0:T(8,128)(2,1)S(1)}) custom-call(bf16[4,128,1024]{2,1,0:T(8,128)(2,1)S(1)} %copy-done.2, bf16[4,128,1024]{2,1,0:T(8,128)(2,1)S(1)} %collective-permute-done.5.refs_1_), custom_call_target="tpu_custom_call" | custom-call | tf_op jit(solution)/shard_map/pallas_call | solution.py:23
  60.3 2.7 %collective-permute-start.6 = (bf16[128,1152]{1,0:T(8,128)(2,1)}, bf16[128,1152]{1,0:T(8,128)(2,1)S(1)}, u32[]{:S(2)}, u32[]{:S(2)}) collective-permute-start(bf16[128,1152]{1,0:T(8,128)(2,1)} %get-tuple-element.39), channel_id=1, source_target_pairs={{0,5},{1,4},{2,7},{3,6},{4,1},{5,0},{6,3},{7,2},{8,13},{9,12},{10,... | collective-permute-start | bytes 884744 | tf_op jit(solution)/shard_map/ppermute | solution.py:449
  63.0 0.6 collective-permute-start.7
  63.6 0.3 collective-permute-start.8
  63.8 13.1 %all-to-all-done.1.refs_0_ = bf16[32,96,122]{2,1,0:T(8,128)(2,1)S(1)} async-done(((bf16[32,96,122]{2,1,0:T(8,128)(2,1)}), bf16[32,96,122]{2,1,0:T(8,128)(2,1)S(1)}, u32[]{:S(2)}, u32[]{:S(2)}) %all-to-all-start.1) | async-done | bytes 749600 | tf_op jit(solution)/shard_map/all_to_all | solution.py:440
  76.9 1.0 %shard_map.88 = (f32[120,768]{1,0:T(8,128)}, f32[1,24]{1,0:T(1,128)}) custom-call(bf16[32,96,122]{2,1,0:T(8,128)(2,1)S(1)} %all-to-all-done.1.refs_0_), custom_call_target="tpu_custom_call" | custom-call | tf_op jit(solution)/shard_map/pallas_call | solution.py:23
  77.9 0.0 collective-permute-done.6.refs_5_
  77.9 3.9 %collective-permute-done.7.refs_6_ = bf16[128,1152]{1,0:T(8,128)(2,1)S(1)} collective-permute-done((bf16[128,1152]{1,0:T(8,128)(2,1)S(1)}, bf16[128,1152]{1,0:T(8,128)(2,1)S(1)}, u32[]{:S(2)}, u32[]{:S(2)}) %collective-permute-start.7) | collective-permute-done | bytes 294944 | tf_op jit(solution)/shard_map/ppermute | solution.py:449
  81.8 0.4 collective-permute-done.8.refs_7_
  82.1 1.6 %shard_map.90 = (bf16[128,768]{1,0:T(8,128)(2,1)}, bf16[128,768]{1,0:T(8,128)(2,1)}) custom-call(s32[1]{0:T(128)} %bitcast.refs_0_, bf16[128,768]{1,0:T(8,128)(2,1)S(1)} %bitcast.8, bf16[128,768]{1,0:T(8,128)(2,1)S(1)} %bitcast.11, s32[768]{0:T(1024)S(1)} %copy-done.4, bf16[128,1152]{1,0:T(8,128)(2,1)S(1)} %get-tuple-element.42.refs_4_, ...), custom_call_target="tpu_custom_call" | custom-call | tf_op jit(solution)/shard_map/pallas_call | solution.py:23
  (1 shorter events, 0.0 us)
Async XLA Ops:
  0.6 3.6 %copy-start.1 = (bf16[1,128,768]{2,1,0:T(8,128)(2,1)S(1)}, bf16[1,128,768]{2,1,0:T(8,128)(2,1)}, u32[]{:S(2)}) copy-start(bf16[1,128,768]{2,1,0:T(8,128)(2,1)} %param.6) | copy-start | bytes 589828
  0.6 3.6 %copy-start = (bf16[1,128,768]{2,1,0:T(8,128)(2,1)S(1)}, bf16[1,128,768]{2,1,0:T(8,128)(2,1)}, u32[]{:S(2)}) copy-start(bf16[1,128,768]{2,1,0:T(8,128)(2,1)} %param.5) | copy-start | bytes 589828
  0.7 3.6 %copy-start.4 = (s32[768]{0:T(1024)S(1)}, s32[768]{0:T(1024)}, u32[]{:S(2)}) copy-start(s32[768]{0:T(1024)} %refs_3_.1) | copy-start | bytes 9220
  1.5 2.7 %collective-permute-start = (bf16[16,1536]{1,0:T(8,128)(2,1)S(1)}, bf16[16,1536]{1,0:T(8,128)(2,1)S(1)}, u32[]{:S(2)}, u32[]{:S(2)}) collective-permute-start(bf16[16,1536]{1,0:T(8,128)(2,1)S(1)} %fusion), channel_id=1, source_target_pairs={{6,8},{14,16},{22,24},{8,6},{16,14},{24,22},{7,9},{15,17},{23,25},... | collective-permute-start | bytes 147464 | tf_op jit(solution)/shard_map/ppermute | solution.py:362
  2.2 0.9 %copy-start.3 = (bf16[120,768]{1,0:T(8,128)(2,1)S(1)}, bf16[120,768]{1,0:T(8,128)(2,1)}, u32[]{:S(2)}) copy-start(bf16[120,768]{1,0:T(8,128)(2,1)} %refs_0_.1) | copy-start | bytes 552964
  6.1 13.5 %collective-permute-start.1 = (bf16[144,1152]{1,0:T(8,128)(2,1)}, bf16[144,1152]{1,0:T(8,128)(2,1)S(1)}, u32[]{:S(2)}, u32[]{:S(2)}) collective-permute-start(bf16[144,1152]{1,0:T(8,128)(2,1)} %get-tuple-element.30), channel_id=1, source_target_pairs={{0,5},{1,4},{2,7},{3,6},{4,1},{5,0},{6,3},{7,2},{8,13},{9,12},{10,... | collective-permute-start | bytes 995336 | tf_op jit(solution)/shard_map/ppermute | solution.py:398
  10.0 18.7 %collective-permute-start.2 = (bf16[144,1152]{1,0:T(8,128)(2,1)S(1)}, bf16[144,1152]{1,0:T(8,128)(2,1)S(1)}, u32[]{:S(2)}, u32[]{:S(2)}) collective-permute-start(bf16[144,1152]{1,0:T(8,128)(2,1)S(1)} %get-tuple-element.31), channel_id=1, source_target_pairs={{0,1},{1,0},{2,3},{3,2},{4,5},{5,4},{6,7},{7,6},{8,9},{9,8},{10,11... | collective-permute-start | bytes 995336 | tf_op jit(solution)/shard_map/ppermute | solution.py:398
  10.5 18.2 %collective-permute-start.3 = (bf16[144,1152]{1,0:T(8,128)(2,1)S(1)}, bf16[144,1152]{1,0:T(8,128)(2,1)S(1)}, u32[]{:S(2)}, u32[]{:S(2)}) collective-permute-start(bf16[144,1152]{1,0:T(8,128)(2,1)S(1)} %get-tuple-element.32), channel_id=1, source_target_pairs={{0,4},{1,5},{2,6},{3,7},{4,0},{5,1},{6,2},{7,3},{8,12},{9,13},{10,... | collective-permute-start | bytes 995336 | tf_op jit(solution)/shard_map/ppermute | solution.py:398
  10.5 29.6 %all-to-all-start = ((bf16[32,96,120]{2,1,0:T(8,128)(2,1)}), bf16[32,96,120]{2,1,0:T(8,128)(2,1)S(1)}, u32[]{:S(2)}, u32[]{:S(2)}) async-start(bf16[32,96,120]{2,1,0:T(8,128)(2,1)} %shard_map.84), calls=%async_computation | async-start | bytes 1572864 | tf_op jit(solution)/shard_map/all_to_all | solution.py:384
  28.7 3.6 %copy-start.5 = (f32[768]{0:T(1024)S(1)}, f32[768]{0:T(1024)}, u32[]{:S(2)}) copy-start(f32[768]{0:T(1024)} %param.8) | copy-start | bytes 9220
  29.8 10.4 %collective-permute-start.4 = (bf16[4,144,960]{2,1,0:T(8,128)(2,1)}, bf16[4,144,960]{2,1,0:T(8,128)(2,1)S(1)}, u32[]{:S(2)}, u32[]{:S(2)}) collective-permute-start(bf16[4,144,960]{2,1,0:T(8,128)(2,1)} %shard_map.86), channel_id=1, source_target_pairs={{0,2},{1,3},{2,0},{3,1},{4,6},{5,7},{6,4},{7,5},{8,10},{9,11},{10,... | collective-permute-start | bytes 3317768 | tf_op jit(solution)/shard_map/ppermute | solution.py:404
  52.7 6.6 %copy-start.2 = (bf16[4,128,1024]{2,1,0:T(8,128)(2,1)S(1)}, bf16[4,128,1024]{2,1,0:T(8,128)(2,1)}, u32[]{:S(2)}) copy-start(bf16[4,128,1024]{2,1,0:T(8,128)(2,1)} %get-tuple-element.36.refs_0_) | copy-start | bytes 3145732
  52.7 24.2 %all-to-all-start.1 = ((bf16[32,96,122]{2,1,0:T(8,128)(2,1)}), bf16[32,96,122]{2,1,0:T(8,128)(2,1)S(1)}, u32[]{:S(2)}, u32[]{:S(2)}) async-start(bf16[32,96,122]{2,1,0:T(8,128)(2,1)} %get-tuple-element.34), calls=%async_computation.1 | async-start | bytes 1572864 | tf_op jit(solution)/shard_map/all_to_all | solution.py:440
  56.3 2.9 %collective-permute-start.5 = (bf16[4,128,1024]{2,1,0:T(8,128)(2,1)}, bf16[4,128,1024]{2,1,0:T(8,128)(2,1)S(1)}, u32[]{:S(2)}, u32[]{:S(2)}) collective-permute-start(bf16[4,128,1024]{2,1,0:T(8,128)(2,1)} %get-tuple-element.37), channel_id=1, source_target_pairs={{0,2},{1,3},{2,0},{3,1},{4,6},{5,7},{6,4},{7,5},{8,10},{9,11},{10,... | collective-permute-start | bytes 3145736 | tf_op jit(solution)/shard_map/ppermute | solution.py:441
  60.3 17.6 %collective-permute-start.6 = (bf16[128,1152]{1,0:T(8,128)(2,1)}, bf16[128,1152]{1,0:T(8,128)(2,1)S(1)}, u32[]{:S(2)}, u32[]{:S(2)}) collective-permute-start(bf16[128,1152]{1,0:T(8,128)(2,1)} %get-tuple-element.39), channel_id=1, source_target_pairs={{0,5},{1,4},{2,7},{3,6},{4,1},{5,0},{6,3},{7,2},{8,13},{9,12},{10,... | collective-permute-start | bytes 884744 | tf_op jit(solution)/shard_map/ppermute | solution.py:449
  63.0 18.8 %collective-permute-start.7 = (bf16[128,1152]{1,0:T(8,128)(2,1)S(1)}, bf16[128,1152]{1,0:T(8,128)(2,1)S(1)}, u32[]{:S(2)}, u32[]{:S(2)}) collective-permute-start(bf16[128,1152]{1,0:T(8,128)(2,1)S(1)} %get-tuple-element.40), channel_id=1, source_target_pairs={{0,1},{1,0},{2,3},{3,2},{4,5},{5,4},{6,7},{7,6},{8,9},{9,8},{10,11... | collective-permute-start | bytes 884744 | tf_op jit(solution)/shard_map/ppermute | solution.py:449
  63.6 18.6 %collective-permute-start.8 = (bf16[128,1152]{1,0:T(8,128)(2,1)S(1)}, bf16[128,1152]{1,0:T(8,128)(2,1)S(1)}, u32[]{:S(2)}, u32[]{:S(2)}) collective-permute-start(bf16[128,1152]{1,0:T(8,128)(2,1)S(1)} %get-tuple-element.41), channel_id=1, source_target_pairs={{0,4},{1,5},{2,6},{3,7},{4,0},{5,1},{6,2},{7,3},{8,12},{9,13},{10,... | collective-permute-start | bytes 884744 | tf_op jit(solution)/shard_map/ppermute | solution.py:449
